TPU v7x, 32 devices: a whole 2x2x4 slice. The times are simulated.
32 devices in a mesh: grp: 4 (over x, core), tp: 4 (over z), ex: 2 (over y).
Axes of the slice: x: 2, y: 2, z: 4, core: 2. Of those that a mesh axis runs over, the one named last changes fastest.
Arguments:
- tokens: bfloat16 [128, 7168], P(('grp', 'tp'), 'ex'), may hold values from -6 to 6
- expert_ids: int32 [128, 1], P(('grp', 'tp')), may hold values from 0 to 1; in each aligned block of 8 rows (0 to 7, 8 to 15, ...) at most 6 rows name the same one
- gate_levels: int32 [128, 1], P(('grp', 'tp')), may hold values from 1 to 4095
- gate_weight: bfloat16 [4, 7168, 1024], P('grp', 'ex', 'tp'), may hold values from -0.0625 to 0.0625
- up_weight: bfloat16 [4, 7168, 1024], P('grp', 'ex', 'tp'), may hold values from -0.0625 to 0.0625
- down_weight: bfloat16 [4, 1024, 7168], P('grp', 'tp', 'ex'), may hold values from -0.125 to 0.125
Outputs:
- mixed: bfloat16 [128, 7168], P(('grp', 'tp'), 'ex')
Inputs may be any that keep to these rules, and one draw needn't show every extreme that they name: `expert_ids`: each row names 1 different experts. In each aligned block of 8 rows (the tokens of one index pair of grp and tp) no expert is named by more than 6 rows.
All inputs are finite; a program needn't handle non-finite values.
Results may differ from a plain program's by a relative error of at most 0.0057.
Values may be sent and summed in bfloat16 or wider, within the bound.
No kernel may reach another device: no remote copies, remote signals or barrier semaphores. Data moves between devices by JAX's collectives and lax.ppermute only.
A program may use at most 64 MiB of HBM per device.

v0:
```python
import functools

import jax
import jax.numpy as jnp
from jax import lax
from jax.experimental import pallas as pl
from jax.experimental.pallas import tpu as pltpu
from jax.sharding import PartitionSpec as P

ROUTED_SCALE = 2.5
MIB = 1024 * 1024


def shift(value, axis, by):
    size = lax.axis_size(axis)
    return lax.ppermute(value, axis, [(i, (i + by) % size) for i in range(size)])


def shift_expert(value, by_expert, by_tp=0):
    groups, n_tp = lax.axis_size("grp"), lax.axis_size("tp")
    pairs = []
    for g in range(groups):
        for t in range(n_tp):
            to = (g + 2 * by_expert) % groups * n_tp + (t + by_tp) % n_tp
            pairs.append((g * n_tp + t, to))
    return lax.ppermute(value, ("grp", "tp"), pairs)


def swap_half(value):
    return lax.ppermute(value, "grp", [(i, i ^ 1) for i in range(lax.axis_size("grp"))])


def hand_on(*refs):
    del refs


def after(value, *earlier, flops=0):
    return pl.pallas_call(
        hand_on,
        out_shape=jax.ShapeDtypeStruct(value.shape, value.dtype),
        in_specs=[pl.BlockSpec(memory_space=pl.ANY)] * (1 + len(earlier)),
        out_specs=pl.BlockSpec(memory_space=pl.ANY),
        input_output_aliases={0: 0},
        cost_estimate=pl.CostEstimate(flops=flops, bytes_accessed=0, transcendentals=0),
        compiler_params=pltpu.CompilerParams(vmem_limit_bytes=MIB),
    )(value, *earlier)


def copy_kernel(from_ref, to_ref):
    to_ref[...] = from_ref[...]


def copied(value):
    return pl.pallas_call(
        copy_kernel,
        out_shape=jax.ShapeDtypeStruct(value.shape, value.dtype),
        compiler_params=pltpu.CompilerParams(vmem_limit_bytes=2 * MIB),
    )(value)


def mix_kernel(n_tp, experts, ids_ref, levels_ref, *refs):
    *piece_refs, mixed_ref = refs
    count = mixed_ref.shape[0]
    expert = lax.axis_index("grp") // 2
    row = lax.broadcasted_iota(jnp.int32, (count, count), 0)
    column = lax.broadcasted_iota(jnp.int32, (count, count), 1)
    ids = ids_ref[...]
    levels = levels_ref[...].astype(jnp.float32)
    whole = jnp.sum(levels, axis=0, keepdims=True)
    mixed = jnp.zeros(mixed_ref.shape, jnp.float32)
    for s in range(experts):
        source = lax.rem(expert - s + experts, experts)
        weight = ROUTED_SCALE * jnp.sum(jnp.where(ids == source, levels, 0.0), axis=0, keepdims=True) / whole
        upright = jnp.sum(jnp.where(row == column, weight, 0.0), axis=1, keepdims=True)
        total = piece_refs[s * n_tp][...].astype(jnp.float32)
        for t in range(1, n_tp):
            total = total + piece_refs[s * n_tp + t][...].astype(jnp.float32)
        mixed = mixed + upright * total.astype(jnp.bfloat16).astype(jnp.float32)
    mixed_ref[...] = mixed.astype(mixed_ref.dtype)


def mix(expert_ids, gate_levels, pieces, n_tp, experts):
    return pl.pallas_call(
        functools.partial(mix_kernel, n_tp, experts),
        out_shape=jax.ShapeDtypeStruct(pieces[0].shape, jnp.bfloat16),
        compiler_params=pltpu.CompilerParams(vmem_limit_bytes=12 * MIB),
    )(expert_ids.T, gate_levels.T, *pieces)


def per_device(tokens, expert_ids, gate_levels, gate_weight, up_weight, down_weight):
    bf16, f32 = jnp.bfloat16, jnp.float32
    experts = lax.axis_size("grp") // 2
    n_tp, n_ex = lax.axis_size("tp"), lax.axis_size("ex")
    count, width = tokens.shape
    w_gate, w_up, w_down = gate_weight[0], up_weight[0], down_weight[0]
    inner = w_down.shape[0]

    def partial_sums(rows):
        parts = [jnp.dot(rows, w, preferred_element_type=f32) for w in (w_gate, w_up)]
        part = jnp.concatenate(parts, axis=1)
        sent = part.astype(bf16)
        return part, sent, [shift(sent, "ex", s) for s in range(1, n_ex)]

    def partial_out(part, others, kept_flops):
        for other in others:
            part = part + other.astype(f32)
        hidden = (jax.nn.silu(part[:, :inner]) * part[:, inner:]).astype(bf16)
        out = jnp.dot(hidden, w_down, preferred_element_type=f32)
        kept = out.shape[0] // 2
        swapped = swap_half(out[kept:].astype(bf16)).astype(f32)
        if kept_flops:
            out = after(out, flops=kept_flops)
        return out[:kept] + swapped

    held = copied(tokens)
    places = tuple(range(n_tp))
    blocks = [held] + [shift(tokens, "tp", t) for t in places[1:]]
    far = [[shift_expert(rows, s) for rows in blocks] for s in range(1, experts)]
    near = jnp.concatenate(blocks, axis=0)
    near_swapped = swap_half(after(near, *(line[1] for line in far)))
    near = jnp.concatenate([near, near_swapped], axis=0)
    near_part, near_sent, near_others = partial_sums(near)
    far = [after(rows, near_sent) if i == n_tp - 1 else rows for line in far for i, rows in enumerate(line)]
    far = jnp.concatenate(far, axis=0)
    far_swapped = swap_half(far)
    far = jnp.concatenate([after(far, flops=3450000000), far_swapped], axis=0)
    far_part, far_sent, far_others = partial_sums(far)
    near_out = partial_out(near_part, [after(other, far_sent) for other in near_others], 3450000000)
    near_out = near_out.reshape(n_tp, count, width)
    near_sent = near_out[1:].astype(bf16)
    pieces = [near_out[0]] + [shift(near_sent[i], "tp", -t) for i, t in enumerate(places[1:])]
    far_out = partial_out(far_part, [after(other, near_sent) for other in far_others], 0)
    far_out = far_out.reshape(experts - 1, n_tp, count, width).astype(bf16)
    for s in range(1, experts):
        pieces += [shift_expert(far_out[experts - 1 - s, i], s, -t) for i, t in enumerate(places)]
    return mix(expert_ids, gate_levels, pieces, n_tp, experts)


def solution(mesh):
    return jax.shard_map(
        per_device,
        mesh=mesh,
        in_specs=(
            P(("grp", "tp"), "ex"),
            P(("grp", "tp"), None),
            P(("grp", "tp"), None),
            P("grp", "ex", "tp"),
            P("grp", "ex", "tp"),
            P("grp", "tp", "ex"),
        ),
        out_specs=P(("grp", "tp"), "ex"),
        check_vma=False,
    )
```

profile of v0, /device:TPU:0, one launch (start us, length us, event | category | flops | bytes accessed | tf_op | source)
XLA Modules:
  0.0 39.2 jit_solution(14385407924584763693)
XLA Ops:
  0.0 0.0 copy-start
  0.0 3.0 %collective-permute-start = (bf16[8,3584]{1,0:T(8,128)(2,1)}, bf16[8,3584]{1,0:T(8,128)(2,1)S(1)}, u32[]{:S(2)}, u32[]{:S(2)}) collective-permute-start(bf16[8,3584]{1,0:T(8,128)(2,1)} %from_ref.1), channel_id=1, source_target_pairs={{0,2},{2,4},{4,6},{6,0},{1,3},{3,5},{5,7},{7,1},{8,10},{10,12},{12... | collective-permute-start | bytes 172040 | tf_op jit(solution)/shard_map/ppermute | solution.py:16
  3.0 2.1 %collective-permute-start.2 = (bf16[8,3584]{1,0:T(8,128)(2,1)}, bf16[8,3584]{1,0:T(8,128)(2,1)S(1)}, u32[]{:S(2)}, u32[]{:S(2)}) collective-permute-start(bf16[8,3584]{1,0:T(8,128)(2,1)} %from_ref.1), channel_id=1, source_target_pairs={{0,6},{2,0},{4,2},{6,4},{1,7},{3,1},{5,3},{7,5},{8,14},{10,8},{12,... | collective-permute-start | bytes 172040 | tf_op jit(solution)/shard_map/ppermute | solution.py:16
  5.1 1.0 %collective-permute-start.1 = (bf16[8,3584]{1,0:T(8,128)(2,1)}, bf16[8,3584]{1,0:T(8,128)(2,1)S(1)}, u32[]{:S(2)}, u32[]{:S(2)}) collective-permute-start(bf16[8,3584]{1,0:T(8,128)(2,1)} %from_ref.1), channel_id=1, source_target_pairs={{0,4},{2,6},{4,0},{6,2},{1,5},{3,7},{5,1},{7,3},{8,12},{10,14},{12... | collective-permute-start | bytes 172040 | tf_op jit(solution)/shard_map/ppermute | solution.py:16
  6.1 0.0 copy-start.1
  6.1 0.9 %copy-done.1 = bf16[8,3584]{1,0:T(8,128)(2,1)S(1)} copy-done((bf16[8,3584]{1,0:T(8,128)(2,1)S(1)}, bf16[8,3584]{1,0:T(8,128)(2,1)}, u32[]{:S(2)}) %copy-start.1) | copy-done | bytes 57368
  6.9 0.0 copy-start.4
  6.9 1.5 %collective-permute-start.6 = (bf16[8,3584]{1,0:T(8,128)(2,1)S(1)}, bf16[8,3584]{1,0:T(8,128)(2,1)S(1)}, u32[]{:S(2)}, u32[]{:S(2)}) collective-permute-start(bf16[8,3584]{1,0:T(8,128)(2,1)S(1)} %shard_map.64), channel_id=1, source_target_pairs={{0,16},{2,18},{4,20},{6,22},{8,24},{10,26},{12,28},{14,30},{16,0},... | collective-permute-start | bytes 172040 | tf_op jit(solution)/shard_map/ppermute | solution.py:26
  8.4 0.0 collective-permute-done
  8.4 1.0 %collective-permute-start.3 = (bf16[8,3584]{1,0:T(8,128)(2,1)S(1)}, bf16[8,3584]{1,0:T(8,128)(2,1)S(1)}, u32[]{:S(2)}, u32[]{:S(2)}) collective-permute-start(bf16[8,3584]{1,0:T(8,128)(2,1)S(1)} %collective-permute-done), channel_id=1, source_target_pairs={{0,16},{2,18},{4,20},{6,22},{8,24},{10,26},{12,28},{14,30},{16,0},... | collective-permute-start | bytes 172040 | tf_op jit(solution)/shard_map/ppermute | solution.py:26
  9.4 0.0 collective-permute-done.2
  9.4 1.1 %collective-permute-start.8 = (bf16[8,3584]{1,0:T(8,128)(2,1)S(1)}, bf16[8,3584]{1,0:T(8,128)(2,1)S(1)}, u32[]{:S(2)}, u32[]{:S(2)}) collective-permute-start(bf16[8,3584]{1,0:T(8,128)(2,1)S(1)} %collective-permute-done.2), channel_id=1, source_target_pairs={{0,16},{2,18},{4,20},{6,22},{8,24},{10,26},{12,28},{14,30},{16,0},... | collective-permute-start | bytes 172040 | tf_op jit(solution)/shard_map/ppermute | solution.py:26
  10.5 0.4 collective-permute-done.1
  10.9 1.6 %collective-permute-start.7 = (bf16[8,3584]{1,0:T(8,128)(2,1)S(1)}, bf16[8,3584]{1,0:T(8,128)(2,1)S(1)}, u32[]{:S(2)}, u32[]{:S(2)}) collective-permute-start(bf16[8,3584]{1,0:T(8,128)(2,1)S(1)} %collective-permute-done.1), channel_id=1, source_target_pairs={{0,16},{2,18},{4,20},{6,22},{8,24},{10,26},{12,28},{14,30},{16,0},... | collective-permute-start | bytes 172040 | tf_op jit(solution)/shard_map/ppermute | solution.py:26
  12.5 0.0 copy-start.5
  12.5 0.2 collective-permute-done.3.refs_1_
  12.7 0.0 collective-permute-start.4
  12.7 1.5 %collective-permute-done.4 = bf16[32,3584]{1,0:T(8,128)(2,1)S(1)} collective-permute-done((bf16[32,3584]{1,0:T(8,128)(2,1)S(1)}, bf16[32,3584]{1,0:T(8,128)(2,1)S(1)}, u32[]{:S(2)}, u32[]{:S(2)}) %collective-permute-start.4) | collective-permute-done | bytes 229408 | tf_op jit(solution)/shard_map/ppermute | solution.py:30
  14.2 0.0 copy-done.4
  14.2 0.4 %fusion.6 = f32[64,256]{1,0:T(8,128)S(1)} fusion(bf16[64,3584]{1,0:T(8,128)(2,1)S(1)} %constant_dynamic-update-slice_fusion, bf16[1,3584,256]{2,1,0:T(8,128)(2,1)S(1)} %copy-done.4), kind=kOutput, calls=%fused_computation.6 | convolution fusion | flops 117440512 | bytes 2359296 | tf_op jit(solution)/shard_map/dot_general | solution.py:99
  14.6 0.0 copy-done.5
  14.6 0.4 %fusion.10 = f32[64,256]{1,0:T(8,128)S(1)} fusion(bf16[64,3584]{1,0:T(8,128)(2,1)S(1)} %constant_dynamic-update-slice_fusion, bf16[1,3584,256]{2,1,0:T(8,128)(2,1)S(1)} %copy-done.5), kind=kOutput, calls=%fused_computation.10 | convolution fusion | flops 117440512 | bytes 2359296 | tf_op jit(solution)/shard_map/dot_general | solution.py:99
  15.1 0.0 collective-permute-done.8.refs_0_
  15.1 0.0 collective-permute-done.6
  15.1 0.0 collective-permute-done.7
  15.2 0.2 collective-permute-start.9
  15.4 1.5 %collective-permute-start.5 = (bf16[64,512]{1,0:T(8,128)(2,1)S(1)}, bf16[64,512]{1,0:T(8,128)(2,1)S(1)}, u32[]{:S(2)}, u32[]{:S(2)}) collective-permute-start(bf16[64,512]{1,0:T(8,128)(2,1)S(1)} %fusion.15.refs_1_), channel_id=1, source_target_pairs={{0,1},{1,0},{2,3},{3,2},{4,5},{5,4},{6,7},{7,6},{8,9},{9,8},{10,11... | collective-permute-start | bytes 196616 | tf_op jit(solution)/shard_map/ppermute | solution.py:16
  16.9 0.0 collective-permute-done.9
  16.9 0.4 %fusion.4 = f32[64,256]{1,0:T(8,128)S(1)} fusion(bf16[1,3584,256]{2,1,0:T(8,128)(2,1)S(1)} %copy-done.4, bf16[32,3584]{1,0:T(8,128)(2,1)S(1)} %collective-permute-done.9, bf16[32,3584]{1,0:T(8,128)(2,1)S(1)} %shard_map.67), kind=kOutput, calls=%fused_computation.4 | convolution fusion | flops 118358016 | bytes 2359296 | tf_op jit(solution)/shard_map/dot_general | solution.py:99
  17.4 0.4 %fusion.8 = f32[64,256]{1,0:T(8,128)S(1)} fusion(bf16[1,3584,256]{2,1,0:T(8,128)(2,1)S(1)} %copy-done.5, bf16[32,3584]{1,0:T(8,128)(2,1)S(1)} %collective-permute-done.9, bf16[32,3584]{1,0:T(8,128)(2,1)S(1)} %shard_map.67), kind=kOutput, calls=%fused_computation.8 | convolution fusion | flops 118358016 | bytes 2359296 | tf_op jit(solution)/shard_map/dot_general | solution.py:99
  17.8 1.4 %collective-permute-start.14 = (bf16[64,512]{1,0:T(8,128)(2,1)S(1)}, bf16[64,512]{1,0:T(8,128)(2,1)S(1)}, u32[]{:S(2)}, u32[]{:S(2)}) collective-permute-start(bf16[64,512]{1,0:T(8,128)(2,1)S(1)} %fusion.14.refs_1_), channel_id=1, source_target_pairs={{0,1},{1,0},{2,3},{3,2},{4,5},{5,4},{6,7},{7,6},{8,9},{9,8},{10,11... | collective-permute-start | bytes 196616 | tf_op jit(solution)/shard_map/ppermute | solution.py:16
  19.2 0.5 %collective-permute-done.5.refs_0_ = bf16[64,512]{1,0:T(8,128)(2,1)S(1)} collective-permute-done((bf16[64,512]{1,0:T(8,128)(2,1)S(1)}, bf16[64,512]{1,0:T(8,128)(2,1)S(1)}, u32[]{:S(2)}, u32[]{:S(2)}) %collective-permute-start.5) | collective-permute-done | bytes 65568 | tf_op jit(solution)/shard_map/ppermute | solution.py:16
  19.8 0.0 copy-done
  19.8 0.4 %fusion.2.refs_0_ = f32[64,3584]{1,0:T(8,128)S(1)} fusion(bf16[1,256,3584]{2,1,0:T(8,128)(2,1)S(1)} %copy-done, f32[64,512]{1,0:T(8,128)S(1)} %convert_add_fusion.1), kind=kOutput, calls=%fused_computation.2 | convolution fusion | flops 117538816 | bytes 2883584 | tf_op jit(solution)/shard_map/dot_general | solution.py:108
  20.2 0.1 collective-permute-start.10
  20.3 1.5 %collective-permute-done.10 = bf16[32,3584]{1,0:T(8,128)(2,1)S(1)} collective-permute-done((bf16[32,3584]{1,0:T(8,128)(2,1)S(1)}, bf16[32,3584]{1,0:T(8,128)(2,1)S(1)}, u32[]{:S(2)}, u32[]{:S(2)}) %collective-permute-start.10) | collective-permute-done | bytes 229408 | tf_op jit(solution)/shard_map/ppermute | solution.py:30
  21.8 0.1 fusion.26
  21.9 0.3 collective-permute-done.14.refs_0_
  22.2 0.4 %fusion = f32[64,3584]{1,0:T(8,128)S(1)} fusion(bf16[1,256,3584]{2,1,0:T(8,128)(2,1)S(1)} %copy-done, f32[64,512]{1,0:T(8,128)S(1)} %convert_add_fusion), kind=kOutput, calls=%fused_computation | convolution fusion | flops 117538816 | bytes 2883584 | tf_op jit(solution)/shard_map/dot_general | solution.py:108
  22.6 0.0 copy-start.2
  22.6 0.0 copy-start.3
  22.6 0.1 collective-permute-start.15
  22.7 1.8 %collective-permute-start.13 = (bf16[8,3584]{1,0:T(8,128)(2,1)S(1)}, bf16[8,3584]{1,0:T(8,128)(2,1)S(1)}, u32[]{:S(2)}, u32[]{:S(2)}) collective-permute-start(bf16[8,3584]{1,0:T(8,128)(2,1)S(1)} %get-tuple-element.11), channel_id=1, source_target_pairs={{0,2},{2,4},{4,6},{6,0},{1,3},{3,5},{5,7},{7,1},{8,10},{10,12},{12... | collective-permute-start | bytes 172040 | tf_op jit(solution)/shard_map/ppermute | solution.py:16
  24.6 1.0 %collective-permute-start.12 = (bf16[8,3584]{1,0:T(8,128)(2,1)S(1)}, bf16[8,3584]{1,0:T(8,128)(2,1)S(1)}, u32[]{:S(2)}, u32[]{:S(2)}) collective-permute-start(bf16[8,3584]{1,0:T(8,128)(2,1)S(1)} %get-tuple-element.12), channel_id=1, source_target_pairs={{0,4},{2,6},{4,0},{6,2},{1,5},{3,7},{5,1},{7,3},{8,12},{10,14},{12... | collective-permute-start | bytes 172040 | tf_op jit(solution)/shard_map/ppermute | solution.py:16
  25.5 2.7 %collective-permute-start.11 = (bf16[8,3584]{1,0:T(8,128)(2,1)S(1)}, bf16[8,3584]{1,0:T(8,128)(2,1)S(1)}, u32[]{:S(2)}, u32[]{:S(2)}) collective-permute-start(bf16[8,3584]{1,0:T(8,128)(2,1)S(1)} %get-tuple-element.13), channel_id=1, source_target_pairs={{0,6},{2,0},{4,2},{6,4},{1,7},{3,1},{5,3},{7,5},{8,14},{10,8},{12,... | collective-permute-start | bytes 172040 | tf_op jit(solution)/shard_map/ppermute | solution.py:16
  28.2 0.0 collective-permute-done.15
  28.3 0.4 collective-permute-start.19
  28.6 1.9 %collective-permute-start.18 = (bf16[8,3584]{1,0:T(8,128)(2,1)S(1)}, bf16[8,3584]{1,0:T(8,128)(2,1)S(1)}, u32[]{:S(2)}, u32[]{:S(2)}) collective-permute-start(bf16[8,3584]{1,0:T(8,128)(2,1)S(1)} %get-tuple-element.8), channel_id=1, source_target_pairs={{0,20},{2,22},{4,16},{6,18},{8,28},{10,30},{12,24},{14,26},{16,4},... | collective-permute-start | bytes 172040 | tf_op jit(solution)/shard_map/ppermute | solution.py:26
  30.6 0.0 collective-permute-done.13.refs_3_
  30.6 2.9 %collective-permute-start.17 = (bf16[8,3584]{1,0:T(8,128)(2,1)S(1)}, bf16[8,3584]{1,0:T(8,128)(2,1)S(1)}, u32[]{:S(2)}, u32[]{:S(2)}) collective-permute-start(bf16[8,3584]{1,0:T(8,128)(2,1)S(1)} %get-tuple-element.9), channel_id=1, source_target_pairs={{0,22},{2,16},{4,18},{6,20},{8,30},{10,24},{12,26},{14,28},{16,6},... | collective-permute-start | bytes 172040 | tf_op jit(solution)/shard_map/ppermute | solution.py:26
  33.4 0.0 collective-permute-done.12.refs_2_
  33.5 0.8 %collective-permute-start.16 = (bf16[8,3584]{1,0:T(8,128)(2,1)S(1)}, bf16[8,3584]{1,0:T(8,128)(2,1)S(1)}, u32[]{:S(2)}, u32[]{:S(2)}) collective-permute-start(bf16[8,3584]{1,0:T(8,128)(2,1)S(1)} %get-tuple-element.10), channel_id=1, source_target_pairs={{0,16},{2,18},{4,20},{6,22},{8,24},{10,26},{12,28},{14,30},{16,0},... | collective-permute-start | bytes 172040 | tf_op jit(solution)/shard_map/ppermute | solution.py:26
  34.2 0.0 collective-permute-done.11.refs_1_
  34.2 1.7 %collective-permute-done.19.refs_7_ = bf16[8,3584]{1,0:T(8,128)(2,1)S(1)} collective-permute-done((bf16[8,3584]{1,0:T(8,128)(2,1)S(1)}, bf16[8,3584]{1,0:T(8,128)(2,1)S(1)}, u32[]{:S(2)}, u32[]{:S(2)}) %collective-permute-start.19) | collective-permute-done | bytes 57376 | tf_op jit(solution)/shard_map/ppermute | solution.py:26
  35.9 1.4 %collective-permute-done.18.refs_6_ = bf16[8,3584]{1,0:T(8,128)(2,1)S(1)} collective-permute-done((bf16[8,3584]{1,0:T(8,128)(2,1)S(1)}, bf16[8,3584]{1,0:T(8,128)(2,1)S(1)}, u32[]{:S(2)}, u32[]{:S(2)}) %collective-permute-start.18) | collective-permute-done | bytes 57376 | tf_op jit(solution)/shard_map/ppermute | solution.py:26
  37.3 0.0 collective-permute-done.17.refs_5_
  37.3 1.1 %collective-permute-done.16.refs_4_ = bf16[8,3584]{1,0:T(8,128)(2,1)S(1)} collective-permute-done((bf16[8,3584]{1,0:T(8,128)(2,1)S(1)}, bf16[8,3584]{1,0:T(8,128)(2,1)S(1)}, u32[]{:S(2)}, u32[]{:S(2)}) %collective-permute-start.16) | collective-permute-done | bytes 57376 | tf_op jit(solution)/shard_map/ppermute | solution.py:26
  38.4 0.0 copy-done.2
  38.4 0.0 copy-done.3
  38.4 0.7 %shard_map.71 = bf16[8,3584]{1,0:T(8,128)(2,1)} custom-call(s32[1,8]{1,0:T(1,128)S(1)} %bitcast.31, s32[1,8]{1,0:T(1,128)S(1)} %bitcast.32, f32[8,3584]{1,0:T(8,128)S(1)} %slice.83.refs_0_, bf16[8,3584]{1,0:T(8,128)(2,1)S(1)} %collective-permute-done.11.refs_1_, bf16[8,3584]{1,0:T(8,128)(2,1)S(1)} %collective-permute-done.12.refs_2_, ...), custom_call_target="tpu_custom_call" | custom-call | tf_op jit(solution)/shard_map/pallas_call | solution.py:83
  (25 shorter events, 0.3 us)
Async XLA Ops:
  0.0 19.8 %copy-start = (bf16[1,256,3584]{2,1,0:T(8,128)(2,1)S(1)}, bf16[1,256,3584]{2,1,0:T(8,128)(2,1)}, u32[]{:S(2)}) copy-start(bf16[1,256,3584]{2,1,0:T(8,128)(2,1)} %param.11) | copy-start | bytes 5505028
  0.0 8.4 %collective-permute-start = (bf16[8,3584]{1,0:T(8,128)(2,1)}, bf16[8,3584]{1,0:T(8,128)(2,1)S(1)}, u32[]{:S(2)}, u32[]{:S(2)}) collective-permute-start(bf16[8,3584]{1,0:T(8,128)(2,1)} %from_ref.1), channel_id=1, source_target_pairs={{0,2},{2,4},{4,6},{6,0},{1,3},{3,5},{5,7},{7,1},{8,10},{10,12},{12... | collective-permute-start | bytes 172040 | tf_op jit(solution)/shard_map/ppermute | solution.py:16
  3.0 6.4 %collective-permute-start.2 = (bf16[8,3584]{1,0:T(8,128)(2,1)}, bf16[8,3584]{1,0:T(8,128)(2,1)S(1)}, u32[]{:S(2)}, u32[]{:S(2)}) collective-permute-start(bf16[8,3584]{1,0:T(8,128)(2,1)} %from_ref.1), channel_id=1, source_target_pairs={{0,6},{2,0},{4,2},{6,4},{1,7},{3,1},{5,3},{7,5},{8,14},{10,8},{12,... | collective-permute-start | bytes 172040 | tf_op jit(solution)/shard_map/ppermute | solution.py:16
  5.1 5.8 %collective-permute-start.1 = (bf16[8,3584]{1,0:T(8,128)(2,1)}, bf16[8,3584]{1,0:T(8,128)(2,1)S(1)}, u32[]{:S(2)}, u32[]{:S(2)}) collective-permute-start(bf16[8,3584]{1,0:T(8,128)(2,1)} %from_ref.1), channel_id=1, source_target_pairs={{0,4},{2,6},{4,0},{6,2},{1,5},{3,7},{5,1},{7,3},{8,12},{10,14},{12... | collective-permute-start | bytes 172040 | tf_op jit(solution)/shard_map/ppermute | solution.py:16
  6.1 0.9 %copy-start.1 = (bf16[8,3584]{1,0:T(8,128)(2,1)S(1)}, bf16[8,3584]{1,0:T(8,128)(2,1)}, u32[]{:S(2)}) copy-start(bf16[8,3584]{1,0:T(8,128)(2,1)} %from_ref.1) | copy-start | bytes 172036
  6.9 7.3 %copy-start.4 = (bf16[1,3584,256]{2,1,0:T(8,128)(2,1)S(1)}, bf16[1,3584,256]{2,1,0:T(8,128)(2,1)}, u32[]{:S(2)}) copy-start(bf16[1,3584,256]{2,1,0:T(8,128)(2,1)} %param.10) | copy-start | bytes 5505028
  6.9 8.2 %collective-permute-start.6 = (bf16[8,3584]{1,0:T(8,128)(2,1)S(1)}, bf16[8,3584]{1,0:T(8,128)(2,1)S(1)}, u32[]{:S(2)}, u32[]{:S(2)}) collective-permute-start(bf16[8,3584]{1,0:T(8,128)(2,1)S(1)} %shard_map.64), channel_id=1, source_target_pairs={{0,16},{2,18},{4,20},{6,22},{8,24},{10,26},{12,28},{14,30},{16,0},... | collective-permute-start | bytes 172040 | tf_op jit(solution)/shard_map/ppermute | solution.py:26
  8.4 4.2 %collective-permute-start.3 = (bf16[8,3584]{1,0:T(8,128)(2,1)S(1)}, bf16[8,3584]{1,0:T(8,128)(2,1)S(1)}, u32[]{:S(2)}, u32[]{:S(2)}) collective-permute-start(bf16[8,3584]{1,0:T(8,128)(2,1)S(1)} %collective-permute-done), channel_id=1, source_target_pairs={{0,16},{2,18},{4,20},{6,22},{8,24},{10,26},{12,28},{14,30},{16,0},... | collective-permute-start | bytes 172040 | tf_op jit(solution)/shard_map/ppermute | solution.py:26
  9.4 5.7 %collective-permute-start.8 = (bf16[8,3584]{1,0:T(8,128)(2,1)S(1)}, bf16[8,3584]{1,0:T(8,128)(2,1)S(1)}, u32[]{:S(2)}, u32[]{:S(2)}) collective-permute-start(bf16[8,3584]{1,0:T(8,128)(2,1)S(1)} %collective-permute-done.2), channel_id=1, source_target_pairs={{0,16},{2,18},{4,20},{6,22},{8,24},{10,26},{12,28},{14,30},{16,0},... | collective-permute-start | bytes 172040 | tf_op jit(solution)/shard_map/ppermute | solution.py:26
  10.9 4.2 %collective-permute-start.7 = (bf16[8,3584]{1,0:T(8,128)(2,1)S(1)}, bf16[8,3584]{1,0:T(8,128)(2,1)S(1)}, u32[]{:S(2)}, u32[]{:S(2)}) collective-permute-start(bf16[8,3584]{1,0:T(8,128)(2,1)S(1)} %collective-permute-done.1), channel_id=1, source_target_pairs={{0,16},{2,18},{4,20},{6,22},{8,24},{10,26},{12,28},{14,30},{16,0},... | collective-permute-start | bytes 172040 | tf_op jit(solution)/shard_map/ppermute | solution.py:26
  12.5 2.2 %copy-start.5 = (bf16[1,3584,256]{2,1,0:T(8,128)(2,1)S(1)}, bf16[1,3584,256]{2,1,0:T(8,128)(2,1)}, u32[]{:S(2)}) copy-start(bf16[1,3584,256]{2,1,0:T(8,128)(2,1)} %param.9) | copy-start | bytes 5505028
  12.7 1.5 %collective-permute-start.4 = (bf16[32,3584]{1,0:T(8,128)(2,1)S(1)}, bf16[32,3584]{1,0:T(8,128)(2,1)S(1)}, u32[]{:S(2)}, u32[]{:S(2)}) collective-permute-start(bf16[32,3584]{1,0:T(8,128)(2,1)S(1)} %shard_map.65), channel_id=1, source_target_pairs={{0,8},{8,0},{16,24},{24,16},{1,9},{9,1},{17,25},{25,17},{2,10},{10... | collective-permute-start | bytes 688136 | tf_op jit(solution)/shard_map/ppermute | solution.py:30
  15.2 1.7 %collective-permute-start.9 = (bf16[32,3584]{1,0:T(8,128)(2,1)S(1)}, bf16[32,3584]{1,0:T(8,128)(2,1)S(1)}, u32[]{:S(2)}, u32[]{:S(2)}) collective-permute-start(bf16[32,3584]{1,0:T(8,128)(2,1)S(1)} %pad_maximum_fusion.4.refs_0_), channel_id=1, source_target_pairs={{0,8},{8,0},{16,24},{24,16},{1,9},{9,1},{17,25},{25,17},{2,10},{10... | collective-permute-start | bytes 688136 | tf_op jit(solution)/shard_map/ppermute | solution.py:30
  15.4 4.4 %collective-permute-start.5 = (bf16[64,512]{1,0:T(8,128)(2,1)S(1)}, bf16[64,512]{1,0:T(8,128)(2,1)S(1)}, u32[]{:S(2)}, u32[]{:S(2)}) collective-permute-start(bf16[64,512]{1,0:T(8,128)(2,1)S(1)} %fusion.15.refs_1_), channel_id=1, source_target_pairs={{0,1},{1,0},{2,3},{3,2},{4,5},{5,4},{6,7},{7,6},{8,9},{9,8},{10,11... | collective-permute-start | bytes 196616 | tf_op jit(solution)/shard_map/ppermute | solution.py:16
  17.8 4.3 %collective-permute-start.14 = (bf16[64,512]{1,0:T(8,128)(2,1)S(1)}, bf16[64,512]{1,0:T(8,128)(2,1)S(1)}, u32[]{:S(2)}, u32[]{:S(2)}) collective-permute-start(bf16[64,512]{1,0:T(8,128)(2,1)S(1)} %fusion.14.refs_1_), channel_id=1, source_target_pairs={{0,1},{1,0},{2,3},{3,2},{4,5},{5,4},{6,7},{7,6},{8,9},{9,8},{10,11... | collective-permute-start | bytes 196616 | tf_op jit(solution)/shard_map/ppermute | solution.py:16
  20.2 1.6 %collective-permute-start.10 = (bf16[32,3584]{1,0:T(8,128)(2,1)S(1)}, bf16[32,3584]{1,0:T(8,128)(2,1)S(1)}, u32[]{:S(2)}, u32[]{:S(2)}) collective-permute-start(bf16[32,3584]{1,0:T(8,128)(2,1)S(1)} %slice.122), channel_id=1, source_target_pairs={{0,8},{8,0},{16,24},{24,16},{1,9},{9,1},{17,25},{25,17},{2,10},{10... | collective-permute-start | bytes 688136 | tf_op jit(solution)/shard_map/ppermute | solution.py:30
  22.6 15.8 %copy-start.2 = (s32[8,1]{0,1:T(1,128)S(1)}, s32[8,1]{0,1:T(1,128)}, u32[]{:S(2)}) copy-start(s32[8,1]{0,1:T(1,128)} %param.7) | copy-start | bytes 100
  22.6 15.8 %copy-start.3 = (s32[8,1]{0,1:T(1,128)S(1)}, s32[8,1]{0,1:T(1,128)}, u32[]{:S(2)}) copy-start(s32[8,1]{0,1:T(1,128)} %param.8) | copy-start | bytes 100
  22.6 5.6 %collective-permute-start.15 = (bf16[32,3584]{1,0:T(8,128)(2,1)S(1)}, bf16[32,3584]{1,0:T(8,128)(2,1)S(1)}, u32[]{:S(2)}, u32[]{:S(2)}) collective-permute-start(bf16[32,3584]{1,0:T(8,128)(2,1)S(1)} %slice.121), channel_id=1, source_target_pairs={{0,8},{8,0},{16,24},{24,16},{1,9},{9,1},{17,25},{25,17},{2,10},{10... | collective-permute-start | bytes 688136 | tf_op jit(solution)/shard_map/ppermute | solution.py:30
  22.7 7.8 %collective-permute-start.13 = (bf16[8,3584]{1,0:T(8,128)(2,1)S(1)}, bf16[8,3584]{1,0:T(8,128)(2,1)S(1)}, u32[]{:S(2)}, u32[]{:S(2)}) collective-permute-start(bf16[8,3584]{1,0:T(8,128)(2,1)S(1)} %get-tuple-element.11), channel_id=1, source_target_pairs={{0,2},{2,4},{4,6},{6,0},{1,3},{3,5},{5,7},{7,1},{8,10},{10,12},{12... | collective-permute-start | bytes 172040 | tf_op jit(solution)/shard_map/ppermute | solution.py:16
  24.6 8.9 %collective-permute-start.12 = (bf16[8,3584]{1,0:T(8,128)(2,1)S(1)}, bf16[8,3584]{1,0:T(8,128)(2,1)S(1)}, u32[]{:S(2)}, u32[]{:S(2)}) collective-permute-start(bf16[8,3584]{1,0:T(8,128)(2,1)S(1)} %get-tuple-element.12), channel_id=1, source_target_pairs={{0,4},{2,6},{4,0},{6,2},{1,5},{3,7},{5,1},{7,3},{8,12},{10,14},{12... | collective-permute-start | bytes 172040 | tf_op jit(solution)/shard_map/ppermute | solution.py:16
  25.5 8.7 %collective-permute-start.11 = (bf16[8,3584]{1,0:T(8,128)(2,1)S(1)}, bf16[8,3584]{1,0:T(8,128)(2,1)S(1)}, u32[]{:S(2)}, u32[]{:S(2)}) collective-permute-start(bf16[8,3584]{1,0:T(8,128)(2,1)S(1)} %get-tuple-element.13), channel_id=1, source_target_pairs={{0,6},{2,0},{4,2},{6,4},{1,7},{3,1},{5,3},{7,5},{8,14},{10,8},{12,... | collective-permute-start | bytes 172040 | tf_op jit(solution)/shard_map/ppermute | solution.py:16
  28.3 7.7 %collective-permute-start.19 = (bf16[8,3584]{1,0:T(8,128)(2,1)S(1)}, bf16[8,3584]{1,0:T(8,128)(2,1)S(1)}, u32[]{:S(2)}, u32[]{:S(2)}) collective-permute-start(bf16[8,3584]{1,0:T(8,128)(2,1)S(1)} %get-tuple-element.7), channel_id=1, source_target_pairs={{0,18},{2,20},{4,22},{6,16},{8,26},{10,28},{12,30},{14,24},{16,2},... | collective-permute-start | bytes 172040 | tf_op jit(solution)/shard_map/ppermute | solution.py:26
  28.6 8.7 %collective-permute-start.18 = (bf16[8,3584]{1,0:T(8,128)(2,1)S(1)}, bf16[8,3584]{1,0:T(8,128)(2,1)S(1)}, u32[]{:S(2)}, u32[]{:S(2)}) collective-permute-start(bf16[8,3584]{1,0:T(8,128)(2,1)S(1)} %get-tuple-element.8), channel_id=1, source_target_pairs={{0,20},{2,22},{4,16},{6,18},{8,28},{10,30},{12,24},{14,26},{16,4},... | collective-permute-start | bytes 172040 | tf_op jit(solution)/shard_map/ppermute | solution.py:26
  30.6 6.7 %collective-permute-start.17 = (bf16[8,3584]{1,0:T(8,128)(2,1)S(1)}, bf16[8,3584]{1,0:T(8,128)(2,1)S(1)}, u32[]{:S(2)}, u32[]{:S(2)}) collective-permute-start(bf16[8,3584]{1,0:T(8,128)(2,1)S(1)} %get-tuple-element.9), channel_id=1, source_target_pairs={{0,22},{2,16},{4,18},{6,20},{8,30},{10,24},{12,26},{14,28},{16,6},... | collective-permute-start | bytes 172040 | tf_op jit(solution)/shard_map/ppermute | solution.py:26
  33.5 5.0 %collective-permute-start.16 = (bf16[8,3584]{1,0:T(8,128)(2,1)S(1)}, bf16[8,3584]{1,0:T(8,128)(2,1)S(1)}, u32[]{:S(2)}, u32[]{:S(2)}) collective-permute-start(bf16[8,3584]{1,0:T(8,128)(2,1)S(1)} %get-tuple-element.10), channel_id=1, source_target_pairs={{0,16},{2,18},{4,20},{6,22},{8,24},{10,26},{12,28},{14,30},{16,0},... | collective-permute-start | bytes 172040 | tf_op jit(solution)/shard_map/ppermute | solution.py:26
where the time goes:
time: 39.3 us; the launch traced here: 39.2 us
  starting transfers between devices  25.9 us (66%)
  waiting for transfers between devices  8.51 us (22%)
  matrix products  2.6 us (7%)
  local copies, waits for them, and re-layouts  1.02 us (3%)
  Pallas kernels  0.74 us (2%)
    ppermute x8, starting transfers between devices, shift(): lax.ppermute(value, axis, [(i, (i + by) % size) for i in range(size)])  14.5 us
    ppermute x8, starting transfers between devices, shift_expert(): return lax.ppermute(value, ('grp', 'tp'), pairs)  11.1 us
    ppermute x8, waiting for transfers between devices, shift_expert(): return lax.ppermute(value, ('grp', 'tp'), pairs)  4.37 us
    ppermute x4, waiting for transfers between devices, swap_half(): lax.ppermute(value, 'grp', [(i, i ^ 1) for i in range(lax.axis_size('grp'...  2.95 us
    dot_general x4, matrix products, partial_sums(): jnp.dot(rows, w, preferred_element_type=f32)  1.76 us
    ppermute x8, waiting for transfers between devices, shift(): lax.ppermute(value, axis, [(i, (i + by) % size) for i in range(size)])  1.19 us
    unnamed x16, local copies, waits for them, and re-layouts  0.9 us
    dot_general x2, matrix products, partial_out(): out = jnp.dot(hidden, w_down, preferred_element_type=f32)  0.83 us
  transfers between devices with their start and end apart: 20, of which 9 were waited for; matrix products, arithmetic and copies ran while one was open for 6% of the time, Pallas kernels for 0%

commit v1 on v0

--- a/solution.py
+++ b/solution.py
@@ -28,6 +28,10 @@
 
 def swap_half(value):
     return lax.ppermute(value, "grp", [(i, i ^ 1) for i in range(lax.axis_size("grp"))])
+
+
+def joined(parts):
+    return parts[0] if len(parts) == 1 else jnp.concatenate(parts, axis=0)
 
 
 def hand_on(*refs):
@@ -101,38 +105,41 @@
         sent = part.astype(bf16)
         return part, sent, [shift(sent, "ex", s) for s in range(1, n_ex)]
 
-    def partial_out(part, others, kept_flops):
+    def partial_out(part, others, part_flops, kept_flops):
+        if part_flops:
+            part = after(part, flops=part_flops)
         for other in others:
             part = part + other.astype(f32)
         hidden = (jax.nn.silu(part[:, :inner]) * part[:, inner:]).astype(bf16)
         out = jnp.dot(hidden, w_down, preferred_element_type=f32)
         kept = out.shape[0] // 2
         swapped = swap_half(out[kept:].astype(bf16)).astype(f32)
-        if kept_flops:
-            out = after(out, flops=kept_flops)
-        return out[:kept] + swapped
+        kept_out = after(out, flops=kept_flops) if kept_flops else out
+        return out, kept_out[:kept] + swapped
 
     held = copied(tokens)
-    places = tuple(range(n_tp))
+    places = (0, 1, *range(n_tp - 1, 1, -1))
     blocks = [held] + [shift(tokens, "tp", t) for t in places[1:]]
     far = [[shift_expert(rows, s) for rows in blocks] for s in range(1, experts)]
-    near = jnp.concatenate(blocks, axis=0)
-    near_swapped = swap_half(after(near, *(line[1] for line in far)))
-    near = jnp.concatenate([near, near_swapped], axis=0)
-    near_part, near_sent, near_others = partial_sums(near)
-    far = [after(rows, near_sent) if i == n_tp - 1 else rows for line in far for i, rows in enumerate(line)]
-    far = jnp.concatenate(far, axis=0)
-    far_swapped = swap_half(far)
-    far = jnp.concatenate([after(far, flops=3450000000), far_swapped], axis=0)
-    far_part, far_sent, far_others = partial_sums(far)
-    near_out = partial_out(near_part, [after(other, far_sent) for other in near_others], 3450000000)
-    near_out = near_out.reshape(n_tp, count, width)
-    near_sent = near_out[1:].astype(bf16)
-    pieces = [near_out[0]] + [shift(near_sent[i], "tp", -t) for i, t in enumerate(places[1:])]
-    far_out = partial_out(far_part, [after(other, near_sent) for other in far_others], 0)
-    far_out = far_out.reshape(experts - 1, n_tp, count, width).astype(bf16)
+    first = joined(blocks[:-1])
+    first_swapped = swap_half(after(first, *(line[0] for line in far)))
+    first = joined([first, first_swapped])
+    a_part, a_sent, a_others = partial_sums(first)
+    second = [blocks[-1]] + [after(rows, a_sent) for line in far for i, rows in enumerate(line)]
+    second = joined(second)
+    second_swapped = swap_half(second)
+    a_whole, a_out = partial_out(a_part, [other for other in a_others], 3450000000, 3450000000)
+    second = joined([after(second, a_whole, flops=3450000000), second_swapped])
+    b_part, b_sent, b_others = partial_sums(second)
+    a_out = a_out.reshape(n_tp - 1, count, width)
+    a_back = a_out[1:].astype(bf16)
+    near = [a_out[0]] + [shift(a_back[i], "tp", -t) for i, t in enumerate(places[1:-1])]
+    _, b_out = partial_out(b_part, [after(other, a_back) for other in b_others], 0, 3450000000)
+    b_out = b_out.astype(bf16).reshape(-1, count, width)
+    near.append(shift(b_out[0], "tp", -places[-1]))
+    pieces = near
     for s in range(1, experts):
-        pieces += [shift_expert(far_out[experts - 1 - s, i], s, -t) for i, t in enumerate(places)]
+        pieces = pieces + [shift_expert(b_out[1 + (experts - 1 - s) * n_tp + i], s, -t) for i, t in enumerate(places)]
     return mix(expert_ids, gate_levels, pieces, n_tp, experts)
 
 

time: 39.3 us -> 45.3 us (1.15)
  waiting for transfers between devices: 8.51 us -> 11.6 us
  matrix products: 2.6 us -> 4.1 us
  local copies, waits for them, and re-layouts: 1.02 us -> 2.4 us
    ppermute x8, waiting for transfers between devices: 1.19 us -> 4.71 us  [shift(): lax.ppermute(value, axis, [(i, (i + by) % size) for i in range(size)])]
    dot_general x4, matrix products: 1.76 us -> 3.25 us  [partial_sums(): jnp.dot(rows, w, preferred_element_type=f32)]
    ppermute x4, waiting for transfers between devices: 2.95 us -> 1.53 us  [swap_half(): lax.ppermute(value, 'grp', [(i, i ^ 1) for i in range(lax.axis_size('grp'...]
    unnamed x16, local copies, waits for them, and re-layouts: 0.9 us -> 2.29 us
    ppermute x8, starting transfers between devices: 14.5 us -> 13.1 us  [shift(): lax.ppermute(value, axis, [(i, (i + by) % size) for i in range(size)])]
    ppermute x8, starting transfers between devices: 11.1 us -> 12.4 us  [shift_expert(): return lax.ppermute(value, ('grp', 'tp'), pairs)]
    ppermute x8, waiting for transfers between devices: 4.37 us -> 5.37 us  [shift_expert(): return lax.ppermute(value, ('grp', 'tp'), pairs)]
  transfers between devices with their start and end apart: 20 -> 20, of which waited for: 9 -> 6; matrix products, arithmetic and copies ran while one was open for 6% -> 10% of each run, Pallas kernels for 0% -> 0%
where the time goes in v1:
time: 45.3 us; the launch traced here: 45 us
  starting transfers between devices  25.7 us (57%)
  waiting for transfers between devices  11.6 us (26%)
  matrix products  4.1 us (9%)
  local copies, waits for them, and re-layouts  2.4 us (5%)
  Pallas kernels  0.75 us (2%)
    ppermute x8, starting transfers between devices, shift(): lax.ppermute(value, axis, [(i, (i + by) % size) for i in range(size)])  13.1 us
    ppermute x8, starting transfers between devices, shift_expert(): return lax.ppermute(value, ('grp', 'tp'), pairs)  12.4 us
    ppermute x8, waiting for transfers between devices, shift_expert(): return lax.ppermute(value, ('grp', 'tp'), pairs)  5.37 us
    ppermute x8, waiting for transfers between devices, shift(): lax.ppermute(value, axis, [(i, (i + by) % size) for i in range(size)])  4.71 us
    dot_general x4, matrix products, partial_sums(): jnp.dot(rows, w, preferred_element_type=f32)  3.25 us
    unnamed x16, local copies, waits for them, and re-layouts  2.29 us
    ppermute x4, waiting for transfers between devices, swap_half(): lax.ppermute(value, 'grp', [(i, i ^ 1) for i in range(lax.axis_size('grp'...  1.53 us
  transfers between devices with their start and end apart: 20, of which 6 were waited for; matrix products, arithmetic and copies ran while one was open for 10% of the time, Pallas kernels for 0%

profile of v1, /device:TPU:0, one launch (start us, length us, event | category | flops | bytes accessed | tf_op | source)
XLA Modules:
  0.0 45.0 jit_solution(6406601650606542623)
XLA Ops:
  0.0 0.0 copy-start
  0.0 3.0 %collective-permute-start = (bf16[8,3584]{1,0:T(8,128)(2,1)}, bf16[8,3584]{1,0:T(8,128)(2,1)S(1)}, u32[]{:S(2)}, u32[]{:S(2)}) collective-permute-start(bf16[8,3584]{1,0:T(8,128)(2,1)} %from_ref.1), channel_id=1, source_target_pairs={{0,2},{2,4},{4,6},{6,0},{1,3},{3,5},{5,7},{7,1},{8,10},{10,12},{12... | collective-permute-start | bytes 172040 | tf_op jit(solution)/shard_map/ppermute | solution.py:16
  3.0 2.1 %collective-permute-start.1 = (bf16[8,3584]{1,0:T(8,128)(2,1)}, bf16[8,3584]{1,0:T(8,128)(2,1)S(1)}, u32[]{:S(2)}, u32[]{:S(2)}) collective-permute-start(bf16[8,3584]{1,0:T(8,128)(2,1)} %from_ref.1), channel_id=1, source_target_pairs={{0,6},{2,0},{4,2},{6,4},{1,7},{3,1},{5,3},{7,5},{8,14},{10,8},{12,... | collective-permute-start | bytes 172040 | tf_op jit(solution)/shard_map/ppermute | solution.py:16
  5.1 1.0 %collective-permute-start.8 = (bf16[8,3584]{1,0:T(8,128)(2,1)}, bf16[8,3584]{1,0:T(8,128)(2,1)S(1)}, u32[]{:S(2)}, u32[]{:S(2)}) collective-permute-start(bf16[8,3584]{1,0:T(8,128)(2,1)} %from_ref.1), channel_id=1, source_target_pairs={{0,4},{2,6},{4,0},{6,2},{1,5},{3,7},{5,1},{7,3},{8,12},{10,14},{12... | collective-permute-start | bytes 172040 | tf_op jit(solution)/shard_map/ppermute | solution.py:16
  6.1 0.0 copy-start.1
  6.1 0.9 %copy-done.1 = bf16[8,3584]{1,0:T(8,128)(2,1)S(1)} copy-done((bf16[8,3584]{1,0:T(8,128)(2,1)S(1)}, bf16[8,3584]{1,0:T(8,128)(2,1)}, u32[]{:S(2)}) %copy-start.1) | copy-done | bytes 57368
  6.9 0.0 copy-start.5
  6.9 1.5 %collective-permute-start.2 = (bf16[8,3584]{1,0:T(8,128)(2,1)S(1)}, bf16[8,3584]{1,0:T(8,128)(2,1)S(1)}, u32[]{:S(2)}, u32[]{:S(2)}) collective-permute-start(bf16[8,3584]{1,0:T(8,128)(2,1)S(1)} %shard_map.64), channel_id=1, source_target_pairs={{0,16},{2,18},{4,20},{6,22},{8,24},{10,26},{12,28},{14,30},{16,0},... | collective-permute-start | bytes 172040 | tf_op jit(solution)/shard_map/ppermute | solution.py:26
  8.4 0.0 collective-permute-done
  8.4 0.0 collective-permute-done.1
  8.4 2.7 %collective-permute-done.2.refs_1_.refs_0_ = bf16[8,3584]{1,0:T(8,128)(2,1)S(1)} collective-permute-done((bf16[8,3584]{1,0:T(8,128)(2,1)S(1)}, bf16[8,3584]{1,0:T(8,128)(2,1)S(1)}, u32[]{:S(2)}, u32[]{:S(2)}) %collective-permute-start.2) | collective-permute-done | bytes 57376 | tf_op jit(solution)/shard_map/ppermute | solution.py:26
  11.1 0.0 collective-permute-start.3
  11.1 1.5 %collective-permute-start.9 = (bf16[8,3584]{1,0:T(8,128)(2,1)S(1)}, bf16[8,3584]{1,0:T(8,128)(2,1)S(1)}, u32[]{:S(2)}, u32[]{:S(2)}) collective-permute-start(bf16[8,3584]{1,0:T(8,128)(2,1)S(1)} %collective-permute-done), channel_id=1, source_target_pairs={{0,16},{2,18},{4,20},{6,22},{8,24},{10,26},{12,28},{14,30},{16,0},... | collective-permute-start | bytes 172040 | tf_op jit(solution)/shard_map/ppermute | solution.py:26
  12.6 0.5 %collective-permute-start.10 = (bf16[8,3584]{1,0:T(8,128)(2,1)S(1)}, bf16[8,3584]{1,0:T(8,128)(2,1)S(1)}, u32[]{:S(2)}, u32[]{:S(2)}) collective-permute-start(bf16[8,3584]{1,0:T(8,128)(2,1)S(1)} %collective-permute-done.1), channel_id=1, source_target_pairs={{0,16},{2,18},{4,20},{6,22},{8,24},{10,26},{12,28},{14,30},{16,0},... | collective-permute-start | bytes 172040 | tf_op jit(solution)/shard_map/ppermute | solution.py:26
  13.1 0.0 collective-permute-done.8
  13.1 1.5 %collective-permute-start.11 = (bf16[8,3584]{1,0:T(8,128)(2,1)S(1)}, bf16[8,3584]{1,0:T(8,128)(2,1)S(1)}, u32[]{:S(2)}, u32[]{:S(2)}) collective-permute-start(bf16[8,3584]{1,0:T(8,128)(2,1)S(1)} %collective-permute-done.8), channel_id=1, source_target_pairs={{0,16},{2,18},{4,20},{6,22},{8,24},{10,26},{12,28},{14,30},{16,0},... | collective-permute-start | bytes 172040 | tf_op jit(solution)/shard_map/ppermute | solution.py:26
  14.6 0.0 collective-permute-done.3
  14.6 1.9 %fusion.6 = f32[48,256]{1,0:T(8,128)S(1)} fusion(bf16[1,3584,256]{2,1,0:T(8,128)(2,1)} %param.10, bf16[24,3584]{1,0:T(8,128)(2,1)S(1)} %collective-permute-done.3, bf16[8,3584]{1,0:T(8,128)(2,1)S(1)} %collective-permute-done.1, bf16[8,3584]{1,0:T(8,128)(2,1)S(1)} %collective-permute-done, bf16[8,3584]{1,0:T(8,128)(2,1)S(1)} %shard_map.64), kind=kOutput, calls=%fused_computation.6 | convolution fusion | flops 89456640 | bytes 2228224 | tf_op jit(solution)/shard_map/dot_general | solution.py:103
  16.6 0.0 copy-done.5
  16.6 0.4 fusion.10
  17.1 1.6 %collective-permute-start.4 = (bf16[48,512]{1,0:T(8,128)(2,1)S(1)}, bf16[48,512]{1,0:T(8,128)(2,1)S(1)}, u32[]{:S(2)}, u32[]{:S(2)}) collective-permute-start(bf16[48,512]{1,0:T(8,128)(2,1)S(1)} %fusion.26.refs_1_), channel_id=1, source_target_pairs={{0,1},{1,0},{2,3},{3,2},{4,5},{5,4},{6,7},{7,6},{8,9},{9,8},{10,11... | collective-permute-start | bytes 147464 | tf_op jit(solution)/shard_map/ppermute | solution.py:16
  18.6 0.0 collective-permute-done.9.refs_0_
  18.7 0.0 collective-permute-done.10.refs_0_
  18.7 0.0 collective-permute-done.11.refs_0_
  18.8 0.1 collective-permute-start.12
  18.8 2.4 %collective-permute-done.4 = bf16[48,512]{1,0:T(8,128)(2,1)S(1)} collective-permute-done((bf16[48,512]{1,0:T(8,128)(2,1)S(1)}, bf16[48,512]{1,0:T(8,128)(2,1)S(1)}, u32[]{:S(2)}, u32[]{:S(2)}) %collective-permute-start.4) | collective-permute-done | bytes 49184 | tf_op jit(solution)/shard_map/ppermute | solution.py:16
  21.2 0.0 copy-done
  21.2 0.4 fusion.2.refs_0_.refs_1_
  21.7 0.0 copy-start.4
  21.7 0.1 collective-permute-start.5
  21.8 0.0 collective-permute-done.12
  21.8 1.4 %copy-done.4 = bf16[1,3584,256]{2,1,0:T(8,128)(2,1)S(1)} copy-done((bf16[1,3584,256]{2,1,0:T(8,128)(2,1)S(1)}, bf16[1,3584,256]{2,1,0:T(8,128)(2,1)}, u32[]{:S(2)}) %copy-start.4) | copy-done | bytes 1835032
  23.2 0.4 fusion.4
  23.6 0.4 fusion.8
  24.1 1.6 %collective-permute-start.13 = (bf16[80,512]{1,0:T(8,128)(2,1)S(1)}, bf16[80,512]{1,0:T(8,128)(2,1)S(1)}, u32[]{:S(2)}, u32[]{:S(2)}) collective-permute-start(bf16[80,512]{1,0:T(8,128)(2,1)S(1)} %fusion.13), channel_id=1, source_target_pairs={{0,1},{1,0},{2,3},{3,2},{4,5},{5,4},{6,7},{7,6},{8,9},{9,8},{10,11... | collective-permute-start | bytes 245768 | tf_op jit(solution)/shard_map/ppermute | solution.py:16
  25.7 0.0 collective-permute-done.5
  25.8 1.6 %collective-permute-start.7 = (bf16[8,3584]{1,0:T(8,128)(2,1)S(1)}, bf16[8,3584]{1,0:T(8,128)(2,1)S(1)}, u32[]{:S(2)}, u32[]{:S(2)}) collective-permute-start(bf16[8,3584]{1,0:T(8,128)(2,1)S(1)} %get-tuple-element.12), channel_id=1, source_target_pairs={{0,2},{2,4},{4,6},{6,0},{1,3},{3,5},{5,7},{7,1},{8,10},{10,12},{12... | collective-permute-start | bytes 172040 | tf_op jit(solution)/shard_map/ppermute | solution.py:16
  27.4 2.2 %collective-permute-start.6 = (bf16[8,3584]{1,0:T(8,128)(2,1)S(1)}, bf16[8,3584]{1,0:T(8,128)(2,1)S(1)}, u32[]{:S(2)}, u32[]{:S(2)}) collective-permute-start(bf16[8,3584]{1,0:T(8,128)(2,1)S(1)} %get-tuple-element.13), channel_id=1, source_target_pairs={{0,6},{2,0},{4,2},{6,4},{1,7},{3,1},{5,3},{7,5},{8,14},{10,8},{12,... | collective-permute-start | bytes 172040 | tf_op jit(solution)/shard_map/ppermute | solution.py:16
  29.6 0.0 collective-permute-done.13.refs_0_
  29.7 0.4 fusion.refs_0_
  30.1 0.1 collective-permute-start.14
  30.2 0.0 copy-start.2
  30.2 0.0 copy-start.3
  30.2 1.5 %collective-permute-done.14 = bf16[40,3584]{1,0:T(8,128)(2,1)S(1)} collective-permute-done((bf16[40,3584]{1,0:T(8,128)(2,1)S(1)}, bf16[40,3584]{1,0:T(8,128)(2,1)S(1)}, u32[]{:S(2)}, u32[]{:S(2)}) %collective-permute-start.14) | collective-permute-done | bytes 286752 | tf_op jit(solution)/shard_map/ppermute | solution.py:30
  31.8 0.1 fusion.12
  31.9 1.0 %collective-permute-start.19 = (bf16[8,3584]{1,0:T(8,128)(2,1)S(1)}, bf16[8,3584]{1,0:T(8,128)(2,1)S(1)}, u32[]{:S(2)}, u32[]{:S(2)}) collective-permute-start(bf16[8,3584]{1,0:T(8,128)(2,1)S(1)} %get-tuple-element.7), channel_id=1, source_target_pairs={{0,20},{2,22},{4,16},{6,18},{8,28},{10,30},{12,24},{14,26},{16,4},... | collective-permute-start | bytes 172040 | tf_op jit(solution)/shard_map/ppermute | solution.py:26
  32.8 0.9 %collective-permute-start.18 = (bf16[8,3584]{1,0:T(8,128)(2,1)S(1)}, bf16[8,3584]{1,0:T(8,128)(2,1)S(1)}, u32[]{:S(2)}, u32[]{:S(2)}) collective-permute-start(bf16[8,3584]{1,0:T(8,128)(2,1)S(1)} %get-tuple-element.8), channel_id=1, source_target_pairs={{0,18},{2,20},{4,22},{6,16},{8,26},{10,28},{12,30},{14,24},{16,2},... | collective-permute-start | bytes 172040 | tf_op jit(solution)/shard_map/ppermute | solution.py:26
  33.7 3.9 %collective-permute-start.17 = (bf16[8,3584]{1,0:T(8,128)(2,1)S(1)}, bf16[8,3584]{1,0:T(8,128)(2,1)S(1)}, u32[]{:S(2)}, u32[]{:S(2)}) collective-permute-start(bf16[8,3584]{1,0:T(8,128)(2,1)S(1)} %get-tuple-element.9), channel_id=1, source_target_pairs={{0,22},{2,16},{4,18},{6,20},{8,30},{10,24},{12,26},{14,28},{16,6},... | collective-permute-start | bytes 172040 | tf_op jit(solution)/shard_map/ppermute | solution.py:26
  37.6 0.0 collective-permute-done.7.refs_2_
  37.6 1.7 %collective-permute-start.16 = (bf16[8,3584]{1,0:T(8,128)(2,1)S(1)}, bf16[8,3584]{1,0:T(8,128)(2,1)S(1)}, u32[]{:S(2)}, u32[]{:S(2)}) collective-permute-start(bf16[8,3584]{1,0:T(8,128)(2,1)S(1)} %get-tuple-element.10), channel_id=1, source_target_pairs={{0,16},{2,18},{4,20},{6,22},{8,24},{10,26},{12,28},{14,30},{16,0},... | collective-permute-start | bytes 172040 | tf_op jit(solution)/shard_map/ppermute | solution.py:26
  39.2 0.0 collective-permute-done.6.refs_1_
  39.2 0.0 collective-permute-start.15
  39.3 1.6 %collective-permute-done.19.refs_7_ = bf16[8,3584]{1,0:T(8,128)(2,1)S(1)} collective-permute-done((bf16[8,3584]{1,0:T(8,128)(2,1)S(1)}, bf16[8,3584]{1,0:T(8,128)(2,1)S(1)}, u32[]{:S(2)}, u32[]{:S(2)}) %collective-permute-start.19) | collective-permute-done | bytes 57376 | tf_op jit(solution)/shard_map/ppermute | solution.py:26
  40.8 0.0 collective-permute-done.18.refs_6_
  40.8 0.0 collective-permute-done.17.refs_5_
  40.8 1.1 %collective-permute-done.16.refs_4_ = bf16[8,3584]{1,0:T(8,128)(2,1)S(1)} collective-permute-done((bf16[8,3584]{1,0:T(8,128)(2,1)S(1)}, bf16[8,3584]{1,0:T(8,128)(2,1)S(1)}, u32[]{:S(2)}, u32[]{:S(2)}) %collective-permute-start.16) | collective-permute-done | bytes 57376 | tf_op jit(solution)/shard_map/ppermute | solution.py:26
  42.0 2.3 %collective-permute-done.15.refs_3_ = bf16[8,3584]{1,0:T(8,128)(2,1)S(1)} collective-permute-done((bf16[8,3584]{1,0:T(8,128)(2,1)S(1)}, bf16[8,3584]{1,0:T(8,128)(2,1)S(1)}, u32[]{:S(2)}, u32[]{:S(2)}) %collective-permute-start.15) | collective-permute-done | bytes 57376 | tf_op jit(solution)/shard_map/ppermute | solution.py:16
  44.3 0.0 copy-done.2
  44.3 0.0 copy-done.3
  44.3 0.7 %shard_map.75 = bf16[8,3584]{1,0:T(8,128)(2,1)} custom-call(s32[1,8]{1,0:T(1,128)S(1)} %bitcast.19, s32[1,8]{1,0:T(1,128)S(1)} %bitcast.20, f32[8,3584]{1,0:T(8,128)S(1)} %slice.86.refs_0_, bf16[8,3584]{1,0:T(8,128)(2,1)S(1)} %collective-permute-done.6.refs_1_, bf16[8,3584]{1,0:T(8,128)(2,1)S(1)} %collective-permute-done.7.refs_2_, ...), custom_call_target="tpu_custom_call" | custom-call | tf_op jit(solution)/shard_map/pallas_call | solution.py:87
  (29 shorter events, 0.3 us)
Async XLA Ops:
  0.0 21.2 %copy-start = (bf16[1,256,3584]{2,1,0:T(8,128)(2,1)S(1)}, bf16[1,256,3584]{2,1,0:T(8,128)(2,1)}, u32[]{:S(2)}) copy-start(bf16[1,256,3584]{2,1,0:T(8,128)(2,1)} %param.11) | copy-start | bytes 5505028
  0.0 8.4 %collective-permute-start = (bf16[8,3584]{1,0:T(8,128)(2,1)}, bf16[8,3584]{1,0:T(8,128)(2,1)S(1)}, u32[]{:S(2)}, u32[]{:S(2)}) collective-permute-start(bf16[8,3584]{1,0:T(8,128)(2,1)} %from_ref.1), channel_id=1, source_target_pairs={{0,2},{2,4},{4,6},{6,0},{1,3},{3,5},{5,7},{7,1},{8,10},{10,12},{12... | collective-permute-start | bytes 172040 | tf_op jit(solution)/shard_map/ppermute | solution.py:16
  3.0 5.4 %collective-permute-start.1 = (bf16[8,3584]{1,0:T(8,128)(2,1)}, bf16[8,3584]{1,0:T(8,128)(2,1)S(1)}, u32[]{:S(2)}, u32[]{:S(2)}) collective-permute-start(bf16[8,3584]{1,0:T(8,128)(2,1)} %from_ref.1), channel_id=1, source_target_pairs={{0,6},{2,0},{4,2},{6,4},{1,7},{3,1},{5,3},{7,5},{8,14},{10,8},{12,... | collective-permute-start | bytes 172040 | tf_op jit(solution)/shard_map/ppermute | solution.py:16
  5.1 8.0 %collective-permute-start.8 = (bf16[8,3584]{1,0:T(8,128)(2,1)}, bf16[8,3584]{1,0:T(8,128)(2,1)S(1)}, u32[]{:S(2)}, u32[]{:S(2)}) collective-permute-start(bf16[8,3584]{1,0:T(8,128)(2,1)} %from_ref.1), channel_id=1, source_target_pairs={{0,4},{2,6},{4,0},{6,2},{1,5},{3,7},{5,1},{7,3},{8,12},{10,14},{12... | collective-permute-start | bytes 172040 | tf_op jit(solution)/shard_map/ppermute | solution.py:16
  6.1 0.9 %copy-start.1 = (bf16[8,3584]{1,0:T(8,128)(2,1)S(1)}, bf16[8,3584]{1,0:T(8,128)(2,1)}, u32[]{:S(2)}) copy-start(bf16[8,3584]{1,0:T(8,128)(2,1)} %from_ref.1) | copy-start | bytes 172036
  6.9 9.7 %copy-start.5 = (bf16[1,3584,256]{2,1,0:T(8,128)(2,1)S(1)}, bf16[1,3584,256]{2,1,0:T(8,128)(2,1)}, u32[]{:S(2)}) copy-start(bf16[1,3584,256]{2,1,0:T(8,128)(2,1)} %param.9) | copy-start | bytes 5505028
  6.9 4.2 %collective-permute-start.2 = (bf16[8,3584]{1,0:T(8,128)(2,1)S(1)}, bf16[8,3584]{1,0:T(8,128)(2,1)S(1)}, u32[]{:S(2)}, u32[]{:S(2)}) collective-permute-start(bf16[8,3584]{1,0:T(8,128)(2,1)S(1)} %shard_map.64), channel_id=1, source_target_pairs={{0,16},{2,18},{4,20},{6,22},{8,24},{10,26},{12,28},{14,30},{16,0},... | collective-permute-start | bytes 172040 | tf_op jit(solution)/shard_map/ppermute | solution.py:26
  11.1 3.5 %collective-permute-start.3 = (bf16[24,3584]{1,0:T(8,128)(2,1)S(1)}, bf16[24,3584]{1,0:T(8,128)(2,1)S(1)}, u32[]{:S(2)}, u32[]{:S(2)}) collective-permute-start(bf16[24,3584]{1,0:T(8,128)(2,1)S(1)} %shard_map.65), channel_id=1, source_target_pairs={{0,8},{8,0},{16,24},{24,16},{1,9},{9,1},{17,25},{25,17},{2,10},{10... | collective-permute-start | bytes 516104 | tf_op jit(solution)/shard_map/ppermute | solution.py:30
  11.1 7.5 %collective-permute-start.9 = (bf16[8,3584]{1,0:T(8,128)(2,1)S(1)}, bf16[8,3584]{1,0:T(8,128)(2,1)S(1)}, u32[]{:S(2)}, u32[]{:S(2)}) collective-permute-start(bf16[8,3584]{1,0:T(8,128)(2,1)S(1)} %collective-permute-done), channel_id=1, source_target_pairs={{0,16},{2,18},{4,20},{6,22},{8,24},{10,26},{12,28},{14,30},{16,0},... | collective-permute-start | bytes 172040 | tf_op jit(solution)/shard_map/ppermute | solution.py:26
  12.6 6.1 %collective-permute-start.10 = (bf16[8,3584]{1,0:T(8,128)(2,1)S(1)}, bf16[8,3584]{1,0:T(8,128)(2,1)S(1)}, u32[]{:S(2)}, u32[]{:S(2)}) collective-permute-start(bf16[8,3584]{1,0:T(8,128)(2,1)S(1)} %collective-permute-done.1), channel_id=1, source_target_pairs={{0,16},{2,18},{4,20},{6,22},{8,24},{10,26},{12,28},{14,30},{16,0},... | collective-permute-start | bytes 172040 | tf_op jit(solution)/shard_map/ppermute | solution.py:26
  13.1 5.6 %collective-permute-start.11 = (bf16[8,3584]{1,0:T(8,128)(2,1)S(1)}, bf16[8,3584]{1,0:T(8,128)(2,1)S(1)}, u32[]{:S(2)}, u32[]{:S(2)}) collective-permute-start(bf16[8,3584]{1,0:T(8,128)(2,1)S(1)} %collective-permute-done.8), channel_id=1, source_target_pairs={{0,16},{2,18},{4,20},{6,22},{8,24},{10,26},{12,28},{14,30},{16,0},... | collective-permute-start | bytes 172040 | tf_op jit(solution)/shard_map/ppermute | solution.py:26
  17.1 4.2 %collective-permute-start.4 = (bf16[48,512]{1,0:T(8,128)(2,1)S(1)}, bf16[48,512]{1,0:T(8,128)(2,1)S(1)}, u32[]{:S(2)}, u32[]{:S(2)}) collective-permute-start(bf16[48,512]{1,0:T(8,128)(2,1)S(1)} %fusion.26.refs_1_), channel_id=1, source_target_pairs={{0,1},{1,0},{2,3},{3,2},{4,5},{5,4},{6,7},{7,6},{8,9},{9,8},{10,11... | collective-permute-start | bytes 147464 | tf_op jit(solution)/shard_map/ppermute | solution.py:16
  18.8 3.0 %collective-permute-start.12 = (bf16[40,3584]{1,0:T(8,128)(2,1)S(1)}, bf16[40,3584]{1,0:T(8,128)(2,1)S(1)}, u32[]{:S(2)}, u32[]{:S(2)}) collective-permute-start(bf16[40,3584]{1,0:T(8,128)(2,1)S(1)} %constant_dynamic-update-slice_fusion.refs_0_), channel_id=1, source_target_pairs={{0,8},{8,0},{16,24},{24,16},{1,9},{9,1},{17,25},{25,17},{2,10},{10... | collective-permute-start | bytes 860168 | tf_op jit(solution)/shard_map/ppermute | solution.py:30
  21.7 1.5 %copy-start.4 = (bf16[1,3584,256]{2,1,0:T(8,128)(2,1)S(1)}, bf16[1,3584,256]{2,1,0:T(8,128)(2,1)}, u32[]{:S(2)}) copy-start(bf16[1,3584,256]{2,1,0:T(8,128)(2,1)} %param.10) | copy-start | bytes 5505028
  21.7 4.0 %collective-permute-start.5 = (bf16[24,3584]{1,0:T(8,128)(2,1)S(1)}, bf16[24,3584]{1,0:T(8,128)(2,1)S(1)}, u32[]{:S(2)}, u32[]{:S(2)}) collective-permute-start(bf16[24,3584]{1,0:T(8,128)(2,1)S(1)} %slice.119), channel_id=1, source_target_pairs={{0,8},{8,0},{16,24},{24,16},{1,9},{9,1},{17,25},{25,17},{2,10},{10... | collective-permute-start | bytes 516104 | tf_op jit(solution)/shard_map/ppermute | solution.py:30
  24.1 5.6 %collective-permute-start.13 = (bf16[80,512]{1,0:T(8,128)(2,1)S(1)}, bf16[80,512]{1,0:T(8,128)(2,1)S(1)}, u32[]{:S(2)}, u32[]{:S(2)}) collective-permute-start(bf16[80,512]{1,0:T(8,128)(2,1)S(1)} %fusion.13), channel_id=1, source_target_pairs={{0,1},{1,0},{2,3},{3,2},{4,5},{5,4},{6,7},{7,6},{8,9},{9,8},{10,11... | collective-permute-start | bytes 245768 | tf_op jit(solution)/shard_map/ppermute | solution.py:16
  25.8 11.8 %collective-permute-start.7 = (bf16[8,3584]{1,0:T(8,128)(2,1)S(1)}, bf16[8,3584]{1,0:T(8,128)(2,1)S(1)}, u32[]{:S(2)}, u32[]{:S(2)}) collective-permute-start(bf16[8,3584]{1,0:T(8,128)(2,1)S(1)} %get-tuple-element.12), channel_id=1, source_target_pairs={{0,2},{2,4},{4,6},{6,0},{1,3},{3,5},{5,7},{7,1},{8,10},{10,12},{12... | collective-permute-start | bytes 172040 | tf_op jit(solution)/shard_map/ppermute | solution.py:16
  27.4 11.8 %collective-permute-start.6 = (bf16[8,3584]{1,0:T(8,128)(2,1)S(1)}, bf16[8,3584]{1,0:T(8,128)(2,1)S(1)}, u32[]{:S(2)}, u32[]{:S(2)}) collective-permute-start(bf16[8,3584]{1,0:T(8,128)(2,1)S(1)} %get-tuple-element.13), channel_id=1, source_target_pairs={{0,6},{2,0},{4,2},{6,4},{1,7},{3,1},{5,3},{7,5},{8,14},{10,8},{12,... | collective-permute-start | bytes 172040 | tf_op jit(solution)/shard_map/ppermute | solution.py:16
  30.1 1.6 %collective-permute-start.14 = (bf16[40,3584]{1,0:T(8,128)(2,1)S(1)}, bf16[40,3584]{1,0:T(8,128)(2,1)S(1)}, u32[]{:S(2)}, u32[]{:S(2)}) collective-permute-start(bf16[40,3584]{1,0:T(8,128)(2,1)S(1)} %slice.118), channel_id=1, source_target_pairs={{0,8},{8,0},{16,24},{24,16},{1,9},{9,1},{17,25},{25,17},{2,10},{10... | collective-permute-start | bytes 860168 | tf_op jit(solution)/shard_map/ppermute | solution.py:30
  30.2 14.1 %copy-start.2 = (s32[8,1]{0,1:T(1,128)S(1)}, s32[8,1]{0,1:T(1,128)}, u32[]{:S(2)}) copy-start(s32[8,1]{0,1:T(1,128)} %param.7) | copy-start | bytes 100
  30.2 14.1 %copy-start.3 = (s32[8,1]{0,1:T(1,128)S(1)}, s32[8,1]{0,1:T(1,128)}, u32[]{:S(2)}) copy-start(s32[8,1]{0,1:T(1,128)} %param.8) | copy-start | bytes 100
  31.9 9.0 %collective-permute-start.19 = (bf16[8,3584]{1,0:T(8,128)(2,1)S(1)}, bf16[8,3584]{1,0:T(8,128)(2,1)S(1)}, u32[]{:S(2)}, u32[]{:S(2)}) collective-permute-start(bf16[8,3584]{1,0:T(8,128)(2,1)S(1)} %get-tuple-element.7), channel_id=1, source_target_pairs={{0,20},{2,22},{4,16},{6,18},{8,28},{10,30},{12,24},{14,26},{16,4},... | collective-permute-start | bytes 172040 | tf_op jit(solution)/shard_map/ppermute | solution.py:26
  32.8 8.0 %collective-permute-start.18 = (bf16[8,3584]{1,0:T(8,128)(2,1)S(1)}, bf16[8,3584]{1,0:T(8,128)(2,1)S(1)}, u32[]{:S(2)}, u32[]{:S(2)}) collective-permute-start(bf16[8,3584]{1,0:T(8,128)(2,1)S(1)} %get-tuple-element.8), channel_id=1, source_target_pairs={{0,18},{2,20},{4,22},{6,16},{8,26},{10,28},{12,30},{14,24},{16,2},... | collective-permute-start | bytes 172040 | tf_op jit(solution)/shard_map/ppermute | solution.py:26
  33.7 7.1 %collective-permute-start.17 = (bf16[8,3584]{1,0:T(8,128)(2,1)S(1)}, bf16[8,3584]{1,0:T(8,128)(2,1)S(1)}, u32[]{:S(2)}, u32[]{:S(2)}) collective-permute-start(bf16[8,3584]{1,0:T(8,128)(2,1)S(1)} %get-tuple-element.9), channel_id=1, source_target_pairs={{0,22},{2,16},{4,18},{6,20},{8,30},{10,24},{12,26},{14,28},{16,6},... | collective-permute-start | bytes 172040 | tf_op jit(solution)/shard_map/ppermute | solution.py:26
  37.6 4.4 %collective-permute-start.16 = (bf16[8,3584]{1,0:T(8,128)(2,1)S(1)}, bf16[8,3584]{1,0:T(8,128)(2,1)S(1)}, u32[]{:S(2)}, u32[]{:S(2)}) collective-permute-start(bf16[8,3584]{1,0:T(8,128)(2,1)S(1)} %get-tuple-element.10), channel_id=1, source_target_pairs={{0,16},{2,18},{4,20},{6,22},{8,24},{10,26},{12,28},{14,30},{16,0},... | collective-permute-start | bytes 172040 | tf_op jit(solution)/shard_map/ppermute | solution.py:26
  39.2 5.1 %collective-permute-start.15 = (bf16[8,3584]{1,0:T(8,128)(2,1)S(1)}, bf16[8,3584]{1,0:T(8,128)(2,1)S(1)}, u32[]{:S(2)}, u32[]{:S(2)}) collective-permute-start(bf16[8,3584]{1,0:T(8,128)(2,1)S(1)} %get-tuple-element.11), channel_id=1, source_target_pairs={{0,4},{2,6},{4,0},{6,2},{1,5},{3,7},{5,1},{7,3},{8,12},{10,14},{12... | collective-permute-start | bytes 172040 | tf_op jit(solution)/shard_map/ppermute | solution.py:16

commit v2 on v0

--- a/solution.py
+++ b/solution.py
@@ -60,6 +60,7 @@
 
 def mix_kernel(n_tp, experts, ids_ref, levels_ref, *refs):
     *piece_refs, mixed_ref = refs
+    piece_refs = piece_refs[::-1]
     count = mixed_ref.shape[0]
     expert = lax.axis_index("grp") // 2
     row = lax.broadcasted_iota(jnp.int32, (count, count), 0)
@@ -101,16 +102,17 @@
         sent = part.astype(bf16)
         return part, sent, [shift(sent, "ex", s) for s in range(1, n_ex)]
 
-    def partial_out(part, others, kept_flops):
+    def partial_out(part, others, kept_flops, part_flops=0, *earlier):
+        if part_flops:
+            part = after(part, flops=part_flops)
         for other in others:
             part = part + other.astype(f32)
         hidden = (jax.nn.silu(part[:, :inner]) * part[:, inner:]).astype(bf16)
         out = jnp.dot(hidden, w_down, preferred_element_type=f32)
         kept = out.shape[0] // 2
         swapped = swap_half(out[kept:].astype(bf16)).astype(f32)
-        if kept_flops:
-            out = after(out, flops=kept_flops)
-        return out[:kept] + swapped
+        kept_out = after(out, flops=kept_flops) if kept_flops else out
+        return kept_out, kept_out[:kept] + swapped
 
     held = copied(tokens)
     places = tuple(range(n_tp))
@@ -125,15 +127,16 @@
     far_swapped = swap_half(far)
     far = jnp.concatenate([after(far, flops=3450000000), far_swapped], axis=0)
     far_part, far_sent, far_others = partial_sums(far)
-    near_out = partial_out(near_part, [after(other, far_sent) for other in near_others], 3450000000)
+    _, near_out = partial_out(near_part, [after(other, far_sent) for other in near_others], 3450000000, 3450000000)
     near_out = near_out.reshape(n_tp, count, width)
     near_sent = near_out[1:].astype(bf16)
+    far_whole, far_out = partial_out(far_part, [after(other, near_sent) for other in far_others], 3450000000, 3450000000)
+    near_sent = [after(near_sent[i], far_whole) if i in (1, 2) else near_sent[i] for i in range(n_tp - 1)]
     pieces = [near_out[0]] + [shift(near_sent[i], "tp", -t) for i, t in enumerate(places[1:])]
-    far_out = partial_out(far_part, [after(other, near_sent) for other in far_others], 0)
     far_out = far_out.reshape(experts - 1, n_tp, count, width).astype(bf16)
     for s in range(1, experts):
         pieces += [shift_expert(far_out[experts - 1 - s, i], s, -t) for i, t in enumerate(places)]
-    return mix(expert_ids, gate_levels, pieces, n_tp, experts)
+    return mix(expert_ids, gate_levels, pieces[::-1], n_tp, experts)
 
 
 def solution(mesh):

time: 39.3 us -> 40.5 us (1.031)
  waiting for transfers between devices: 8.51 us -> 11.2 us
  starting transfers between devices: 25.9 us -> 24.4 us
    ppermute x8, waiting for transfers between devices: 4.37 us -> 6.33 us  [shift_expert(): return lax.ppermute(value, ('grp', 'tp'), pairs)]
    ppermute x8, starting transfers between devices: 14.5 us -> 12.8 us  [shift(): lax.ppermute(value, axis, [(i, (i + by) % size) for i in range(size)])]
    ppermute x4, waiting for transfers between devices: 2.95 us -> 4.41 us  [swap_half(): lax.ppermute(value, 'grp', [(i, i ^ 1) for i in range(lax.axis_size('grp'...]
    ppermute x8, waiting for transfers between devices: 1.19 us -> 0.41 us  [shift(): lax.ppermute(value, axis, [(i, (i + by) % size) for i in range(size)])]
  transfers between devices with their start and end apart: 20 -> 20, of which waited for: 9 -> 8; matrix products, arithmetic and copies ran while one was open for 6% -> 7% of each run, Pallas kernels for 0% -> 0%
where the time goes in v2:
time: 40.5 us; the launch traced here: 40.4 us
  starting transfers between devices  24.4 us (60%)
  waiting for transfers between devices  11.2 us (28%)
  matrix products  2.6 us (6%)
  local copies, waits for them, and re-layouts  1.02 us (3%)
  Pallas kernels  0.76 us (2%)
    ppermute x8, starting transfers between devices, shift(): lax.ppermute(value, axis, [(i, (i + by) % size) for i in range(size)])  12.8 us
    ppermute x8, starting transfers between devices, shift_expert(): return lax.ppermute(value, ('grp', 'tp'), pairs)  11.3 us
    ppermute x8, waiting for transfers between devices, shift_expert(): return lax.ppermute(value, ('grp', 'tp'), pairs)  6.33 us
    ppermute x4, waiting for transfers between devices, swap_half(): lax.ppermute(value, 'grp', [(i, i ^ 1) for i in range(lax.axis_size('grp'...  4.41 us
    dot_general x4, matrix products, partial_sums(): jnp.dot(rows, w, preferred_element_type=f32)  1.76 us
    unnamed x16, local copies, waits for them, and re-layouts  0.9 us
    dot_general x2, matrix products, partial_out(): out = jnp.dot(hidden, w_down, preferred_element_type=f32)  0.83 us
  transfers between devices with their start and end apart: 20, of which 8 were waited for; matrix products, arithmetic and copies ran while one was open for 7% of the time, Pallas kernels for 0%

profile of v2, /device:TPU:0, one launch (start us, length us, event | category | flops | bytes accessed | tf_op | source)
XLA Modules:
  0.0 40.4 jit_solution(38129730909182429)
XLA Ops:
  0.0 0.0 copy-start
  0.0 3.0 %collective-permute-start.1 = (bf16[8,3584]{1,0:T(8,128)(2,1)}, bf16[8,3584]{1,0:T(8,128)(2,1)S(1)}, u32[]{:S(2)}, u32[]{:S(2)}) collective-permute-start(bf16[8,3584]{1,0:T(8,128)(2,1)} %from_ref.1), channel_id=1, source_target_pairs={{0,2},{2,4},{4,6},{6,0},{1,3},{3,5},{5,7},{7,1},{8,10},{10,12},{12... | collective-permute-start | bytes 172040 | tf_op jit(solution)/shard_map/ppermute | solution.py:16
  3.0 2.1 %collective-permute-start.5 = (bf16[8,3584]{1,0:T(8,128)(2,1)}, bf16[8,3584]{1,0:T(8,128)(2,1)S(1)}, u32[]{:S(2)}, u32[]{:S(2)}) collective-permute-start(bf16[8,3584]{1,0:T(8,128)(2,1)} %from_ref.1), channel_id=1, source_target_pairs={{0,6},{2,0},{4,2},{6,4},{1,7},{3,1},{5,3},{7,5},{8,14},{10,8},{12,... | collective-permute-start | bytes 172040 | tf_op jit(solution)/shard_map/ppermute | solution.py:16
  5.1 1.0 %collective-permute-start.3 = (bf16[8,3584]{1,0:T(8,128)(2,1)}, bf16[8,3584]{1,0:T(8,128)(2,1)S(1)}, u32[]{:S(2)}, u32[]{:S(2)}) collective-permute-start(bf16[8,3584]{1,0:T(8,128)(2,1)} %from_ref.1), channel_id=1, source_target_pairs={{0,4},{2,6},{4,0},{6,2},{1,5},{3,7},{5,1},{7,3},{8,12},{10,14},{12... | collective-permute-start | bytes 172040 | tf_op jit(solution)/shard_map/ppermute | solution.py:16
  6.1 0.0 copy-start.1
  6.1 0.9 %copy-done.1 = bf16[8,3584]{1,0:T(8,128)(2,1)S(1)} copy-done((bf16[8,3584]{1,0:T(8,128)(2,1)S(1)}, bf16[8,3584]{1,0:T(8,128)(2,1)}, u32[]{:S(2)}) %copy-start.1) | copy-done | bytes 57368
  6.9 0.0 copy-start.4
  6.9 1.5 %collective-permute-start = (bf16[8,3584]{1,0:T(8,128)(2,1)S(1)}, bf16[8,3584]{1,0:T(8,128)(2,1)S(1)}, u32[]{:S(2)}, u32[]{:S(2)}) collective-permute-start(bf16[8,3584]{1,0:T(8,128)(2,1)S(1)} %shard_map.64), channel_id=1, source_target_pairs={{0,16},{2,18},{4,20},{6,22},{8,24},{10,26},{12,28},{14,30},{16,0},... | collective-permute-start | bytes 172040 | tf_op jit(solution)/shard_map/ppermute | solution.py:26
  8.4 0.0 collective-permute-done.1
  8.4 1.0 %collective-permute-start.2 = (bf16[8,3584]{1,0:T(8,128)(2,1)S(1)}, bf16[8,3584]{1,0:T(8,128)(2,1)S(1)}, u32[]{:S(2)}, u32[]{:S(2)}) collective-permute-start(bf16[8,3584]{1,0:T(8,128)(2,1)S(1)} %collective-permute-done.1), channel_id=1, source_target_pairs={{0,16},{2,18},{4,20},{6,22},{8,24},{10,26},{12,28},{14,30},{16,0},... | collective-permute-start | bytes 172040 | tf_op jit(solution)/shard_map/ppermute | solution.py:26
  9.4 0.0 collective-permute-done.5
  9.4 1.1 %collective-permute-start.6 = (bf16[8,3584]{1,0:T(8,128)(2,1)S(1)}, bf16[8,3584]{1,0:T(8,128)(2,1)S(1)}, u32[]{:S(2)}, u32[]{:S(2)}) collective-permute-start(bf16[8,3584]{1,0:T(8,128)(2,1)S(1)} %collective-permute-done.5), channel_id=1, source_target_pairs={{0,16},{2,18},{4,20},{6,22},{8,24},{10,26},{12,28},{14,30},{16,0},... | collective-permute-start | bytes 172040 | tf_op jit(solution)/shard_map/ppermute | solution.py:26
  10.5 0.4 collective-permute-done.3
  10.9 1.6 %collective-permute-start.4 = (bf16[8,3584]{1,0:T(8,128)(2,1)S(1)}, bf16[8,3584]{1,0:T(8,128)(2,1)S(1)}, u32[]{:S(2)}, u32[]{:S(2)}) collective-permute-start(bf16[8,3584]{1,0:T(8,128)(2,1)S(1)} %collective-permute-done.3), channel_id=1, source_target_pairs={{0,16},{2,18},{4,20},{6,22},{8,24},{10,26},{12,28},{14,30},{16,0},... | collective-permute-start | bytes 172040 | tf_op jit(solution)/shard_map/ppermute | solution.py:26
  12.5 0.0 copy-start.5
  12.5 0.2 collective-permute-done.2.refs_1_
  12.7 0.0 collective-permute-start.7
  12.7 1.5 %collective-permute-done.7 = bf16[32,3584]{1,0:T(8,128)(2,1)S(1)} collective-permute-done((bf16[32,3584]{1,0:T(8,128)(2,1)S(1)}, bf16[32,3584]{1,0:T(8,128)(2,1)S(1)}, u32[]{:S(2)}, u32[]{:S(2)}) %collective-permute-start.7) | collective-permute-done | bytes 229408 | tf_op jit(solution)/shard_map/ppermute | solution.py:30
  14.2 0.0 copy-done.4
  14.2 0.4 %fusion.6 = f32[64,256]{1,0:T(8,128)S(1)} fusion(bf16[64,3584]{1,0:T(8,128)(2,1)S(1)} %constant_dynamic-update-slice_fusion, bf16[1,3584,256]{2,1,0:T(8,128)(2,1)S(1)} %copy-done.4), kind=kOutput, calls=%fused_computation.6 | convolution fusion | flops 117440512 | bytes 2359296 | tf_op jit(solution)/shard_map/dot_general | solution.py:100
  14.6 0.0 copy-done.5
  14.6 0.4 %fusion.10 = f32[64,256]{1,0:T(8,128)S(1)} fusion(bf16[64,3584]{1,0:T(8,128)(2,1)S(1)} %constant_dynamic-update-slice_fusion, bf16[1,3584,256]{2,1,0:T(8,128)(2,1)S(1)} %copy-done.5), kind=kOutput, calls=%fused_computation.10 | convolution fusion | flops 117440512 | bytes 2359296 | tf_op jit(solution)/shard_map/dot_general | solution.py:100
  15.1 1.6 %collective-permute-start.10 = (bf16[64,512]{1,0:T(8,128)(2,1)S(1)}, bf16[64,512]{1,0:T(8,128)(2,1)S(1)}, u32[]{:S(2)}, u32[]{:S(2)}) collective-permute-start(bf16[64,512]{1,0:T(8,128)(2,1)S(1)} %fusion.25.refs_1_), channel_id=1, source_target_pairs={{0,1},{1,0},{2,3},{3,2},{4,5},{5,4},{6,7},{7,6},{8,9},{9,8},{10,11... | collective-permute-start | bytes 196616 | tf_op jit(solution)/shard_map/ppermute | solution.py:16
  16.7 0.0 collective-permute-done.6.refs_0_
  16.7 0.0 collective-permute-done
  16.7 0.0 collective-permute-done.4
  16.7 0.1 collective-permute-start.8
  16.8 1.5 %collective-permute-done.8 = bf16[32,3584]{1,0:T(8,128)(2,1)S(1)} collective-permute-done((bf16[32,3584]{1,0:T(8,128)(2,1)S(1)}, bf16[32,3584]{1,0:T(8,128)(2,1)S(1)}, u32[]{:S(2)}, u32[]{:S(2)}) %collective-permute-start.8) | collective-permute-done | bytes 229408 | tf_op jit(solution)/shard_map/ppermute | solution.py:30
  18.3 0.4 %fusion.4 = f32[64,256]{1,0:T(8,128)S(1)} fusion(bf16[1,3584,256]{2,1,0:T(8,128)(2,1)S(1)} %copy-done.4, bf16[32,3584]{1,0:T(8,128)(2,1)S(1)} %collective-permute-done.8, bf16[32,3584]{1,0:T(8,128)(2,1)S(1)} %shard_map.67), kind=kOutput, calls=%fused_computation.4 | convolution fusion | flops 118358016 | bytes 2359296 | tf_op jit(solution)/shard_map/dot_general | solution.py:100
  18.7 0.4 %fusion.8 = f32[64,256]{1,0:T(8,128)S(1)} fusion(bf16[1,3584,256]{2,1,0:T(8,128)(2,1)S(1)} %copy-done.5, bf16[32,3584]{1,0:T(8,128)(2,1)S(1)} %collective-permute-done.8, bf16[32,3584]{1,0:T(8,128)(2,1)S(1)} %shard_map.67), kind=kOutput, calls=%fused_computation.8 | convolution fusion | flops 118358016 | bytes 2359296 | tf_op jit(solution)/shard_map/dot_general | solution.py:100
  19.2 0.6 %collective-permute-start.9 = (bf16[64,512]{1,0:T(8,128)(2,1)S(1)}, bf16[64,512]{1,0:T(8,128)(2,1)S(1)}, u32[]{:S(2)}, u32[]{:S(2)}) collective-permute-start(bf16[64,512]{1,0:T(8,128)(2,1)S(1)} %fusion.24.refs_1_), channel_id=1, source_target_pairs={{0,1},{1,0},{2,3},{3,2},{4,5},{5,4},{6,7},{7,6},{8,9},{9,8},{10,11... | collective-permute-start | bytes 196616 | tf_op jit(solution)/shard_map/ppermute | solution.py:16
  19.8 0.0 collective-permute-done.10.refs_0_
  19.8 0.0 copy-done
  19.8 0.4 %fusion.2.refs_0_ = f32[64,3584]{1,0:T(8,128)S(1)} fusion(bf16[1,256,3584]{2,1,0:T(8,128)(2,1)S(1)} %copy-done, f32[64,512]{1,0:T(8,128)S(1)} %convert_add_fusion.1), kind=kOutput, calls=%fused_computation.2 | convolution fusion | flops 117538816 | bytes 2883584 | tf_op jit(solution)/shard_map/dot_general | solution.py:111
  20.3 0.1 collective-permute-start.11
  20.4 1.5 %collective-permute-done.11 = bf16[32,3584]{1,0:T(8,128)(2,1)S(1)} collective-permute-done((bf16[32,3584]{1,0:T(8,128)(2,1)S(1)}, bf16[32,3584]{1,0:T(8,128)(2,1)S(1)}, u32[]{:S(2)}, u32[]{:S(2)}) %collective-permute-start.11) | collective-permute-done | bytes 229408 | tf_op jit(solution)/shard_map/ppermute | solution.py:30
  21.9 0.1 fusion.26
  22.0 2.2 %collective-permute-start.19 = (bf16[8,3584]{1,0:T(8,128)(2,1)S(1)}, bf16[8,3584]{1,0:T(8,128)(2,1)S(1)}, u32[]{:S(2)}, u32[]{:S(2)}) collective-permute-start(bf16[8,3584]{1,0:T(8,128)(2,1)S(1)} %get-tuple-element.7), channel_id=1, source_target_pairs={{0,6},{2,0},{4,2},{6,4},{1,7},{3,1},{5,3},{7,5},{8,14},{10,8},{12,... | collective-permute-start | bytes 172040 | tf_op jit(solution)/shard_map/ppermute | solution.py:16
  24.2 0.0 collective-permute-done.9.refs_0_
  24.2 0.4 %fusion.refs_0_ = f32[64,3584]{1,0:T(8,128)S(1)} fusion(bf16[1,256,3584]{2,1,0:T(8,128)(2,1)S(1)} %copy-done, f32[64,512]{1,0:T(8,128)S(1)} %convert_add_fusion), kind=kOutput, calls=%fused_computation | convolution fusion | flops 117538816 | bytes 2883584 | tf_op jit(solution)/shard_map/dot_general | solution.py:111
  24.7 0.1 collective-permute-start.12
  24.8 0.0 copy-start.2
  24.8 0.0 copy-start.3
  24.8 1.2 %collective-permute-start.17 = (bf16[8,3584]{1,0:T(8,128)(2,1)S(1)}, bf16[8,3584]{1,0:T(8,128)(2,1)S(1)}, u32[]{:S(2)}, u32[]{:S(2)}) collective-permute-start(bf16[8,3584]{1,0:T(8,128)(2,1)S(1)} %shard_map.74), channel_id=1, source_target_pairs={{0,2},{2,4},{4,6},{6,0},{1,3},{3,5},{5,7},{7,1},{8,10},{10,12},{12... | collective-permute-start | bytes 172040 | tf_op jit(solution)/shard_map/ppermute | solution.py:16
  26.0 1.2 %collective-permute-start.18 = (bf16[8,3584]{1,0:T(8,128)(2,1)S(1)}, bf16[8,3584]{1,0:T(8,128)(2,1)S(1)}, u32[]{:S(2)}, u32[]{:S(2)}) collective-permute-start(bf16[8,3584]{1,0:T(8,128)(2,1)S(1)} %shard_map.75), channel_id=1, source_target_pairs={{0,4},{2,6},{4,0},{6,2},{1,5},{3,7},{5,1},{7,3},{8,12},{10,14},{12... | collective-permute-start | bytes 172040 | tf_op jit(solution)/shard_map/ppermute | solution.py:16
  27.2 0.0 collective-permute-done.12
  27.2 1.2 %collective-permute-start.16 = (bf16[8,3584]{1,0:T(8,128)(2,1)S(1)}, bf16[8,3584]{1,0:T(8,128)(2,1)S(1)}, u32[]{:S(2)}, u32[]{:S(2)}) collective-permute-start(bf16[8,3584]{1,0:T(8,128)(2,1)S(1)} %get-tuple-element.10), channel_id=1, source_target_pairs={{0,16},{2,18},{4,20},{6,22},{8,24},{10,26},{12,28},{14,30},{16,0},... | collective-permute-start | bytes 172040 | tf_op jit(solution)/shard_map/ppermute | solution.py:26
  28.4 2.8 %collective-permute-start.15 = (bf16[8,3584]{1,0:T(8,128)(2,1)S(1)}, bf16[8,3584]{1,0:T(8,128)(2,1)S(1)}, u32[]{:S(2)}, u32[]{:S(2)}) collective-permute-start(bf16[8,3584]{1,0:T(8,128)(2,1)S(1)} %get-tuple-element.11), channel_id=1, source_target_pairs={{0,22},{2,16},{4,18},{6,20},{8,30},{10,24},{12,26},{14,28},{16,6},... | collective-permute-start | bytes 172040 | tf_op jit(solution)/shard_map/ppermute | solution.py:26
  31.2 0.0 collective-permute-done.19.refs_6_
  31.2 1.6 %collective-permute-start.14 = (bf16[8,3584]{1,0:T(8,128)(2,1)S(1)}, bf16[8,3584]{1,0:T(8,128)(2,1)S(1)}, u32[]{:S(2)}, u32[]{:S(2)}) collective-permute-start(bf16[8,3584]{1,0:T(8,128)(2,1)S(1)} %get-tuple-element.12), channel_id=1, source_target_pairs={{0,20},{2,22},{4,16},{6,18},{8,28},{10,30},{12,24},{14,26},{16,4},... | collective-permute-start | bytes 172040 | tf_op jit(solution)/shard_map/ppermute | solution.py:26
  32.8 0.0 collective-permute-done.17.refs_4_
  32.8 0.7 %collective-permute-start.13 = (bf16[8,3584]{1,0:T(8,128)(2,1)S(1)}, bf16[8,3584]{1,0:T(8,128)(2,1)S(1)}, u32[]{:S(2)}, u32[]{:S(2)}) collective-permute-start(bf16[8,3584]{1,0:T(8,128)(2,1)S(1)} %get-tuple-element.13), channel_id=1, source_target_pairs={{0,18},{2,20},{4,22},{6,16},{8,26},{10,28},{12,30},{14,24},{16,2},... | collective-permute-start | bytes 172040 | tf_op jit(solution)/shard_map/ppermute | solution.py:26
  33.4 0.0 collective-permute-done.18.refs_5_
  33.5 0.0 collective-permute-done.16.refs_3_
  33.5 0.9 %collective-permute-done.15.refs_2_ = bf16[8,3584]{1,0:T(8,128)(2,1)S(1)} collective-permute-done((bf16[8,3584]{1,0:T(8,128)(2,1)S(1)}, bf16[8,3584]{1,0:T(8,128)(2,1)S(1)}, u32[]{:S(2)}, u32[]{:S(2)}) %collective-permute-start.15) | collective-permute-done | bytes 57376 | tf_op jit(solution)/shard_map/ppermute | solution.py:26
  34.4 3.7 %collective-permute-done.14.refs_1_ = bf16[8,3584]{1,0:T(8,128)(2,1)S(1)} collective-permute-done((bf16[8,3584]{1,0:T(8,128)(2,1)S(1)}, bf16[8,3584]{1,0:T(8,128)(2,1)S(1)}, u32[]{:S(2)}, u32[]{:S(2)}) %collective-permute-start.14) | collective-permute-done | bytes 57376 | tf_op jit(solution)/shard_map/ppermute | solution.py:26
  38.1 1.5 %collective-permute-done.13.refs_0_ = bf16[8,3584]{1,0:T(8,128)(2,1)S(1)} collective-permute-done((bf16[8,3584]{1,0:T(8,128)(2,1)S(1)}, bf16[8,3584]{1,0:T(8,128)(2,1)S(1)}, u32[]{:S(2)}, u32[]{:S(2)}) %collective-permute-start.13) | collective-permute-done | bytes 57376 | tf_op jit(solution)/shard_map/ppermute | solution.py:26
  39.6 0.0 copy-done.2
  39.6 0.0 copy-done.3
  39.6 0.7 %shard_map.76 = bf16[8,3584]{1,0:T(8,128)(2,1)} custom-call(s32[1,8]{1,0:T(1,128)S(1)} %bitcast.31, s32[1,8]{1,0:T(1,128)S(1)} %bitcast.32, bf16[8,3584]{1,0:T(8,128)(2,1)S(1)} %collective-permute-done.13.refs_0_, bf16[8,3584]{1,0:T(8,128)(2,1)S(1)} %collective-permute-done.14.refs_1_, bf16[8,3584]{1,0:T(8,128)(2,1)S(1)} %collective-permute-done.15.refs_2_, ...), custom_call_target="tpu_custom_call" | custom-call | tf_op jit(solution)/shard_map/pallas_call | solution.py:84
  (32 shorter events, 0.3 us)
Async XLA Ops:
  0.0 19.8 %copy-start = (bf16[1,256,3584]{2,1,0:T(8,128)(2,1)S(1)}, bf16[1,256,3584]{2,1,0:T(8,128)(2,1)}, u32[]{:S(2)}) copy-start(bf16[1,256,3584]{2,1,0:T(8,128)(2,1)} %param.11) | copy-start | bytes 5505028
  0.0 8.4 %collective-permute-start.1 = (bf16[8,3584]{1,0:T(8,128)(2,1)}, bf16[8,3584]{1,0:T(8,128)(2,1)S(1)}, u32[]{:S(2)}, u32[]{:S(2)}) collective-permute-start(bf16[8,3584]{1,0:T(8,128)(2,1)} %from_ref.1), channel_id=1, source_target_pairs={{0,2},{2,4},{4,6},{6,0},{1,3},{3,5},{5,7},{7,1},{8,10},{10,12},{12... | collective-permute-start | bytes 172040 | tf_op jit(solution)/shard_map/ppermute | solution.py:16
  3.0 6.4 %collective-permute-start.5 = (bf16[8,3584]{1,0:T(8,128)(2,1)}, bf16[8,3584]{1,0:T(8,128)(2,1)S(1)}, u32[]{:S(2)}, u32[]{:S(2)}) collective-permute-start(bf16[8,3584]{1,0:T(8,128)(2,1)} %from_ref.1), channel_id=1, source_target_pairs={{0,6},{2,0},{4,2},{6,4},{1,7},{3,1},{5,3},{7,5},{8,14},{10,8},{12,... | collective-permute-start | bytes 172040 | tf_op jit(solution)/shard_map/ppermute | solution.py:16
  5.1 5.8 %collective-permute-start.3 = (bf16[8,3584]{1,0:T(8,128)(2,1)}, bf16[8,3584]{1,0:T(8,128)(2,1)S(1)}, u32[]{:S(2)}, u32[]{:S(2)}) collective-permute-start(bf16[8,3584]{1,0:T(8,128)(2,1)} %from_ref.1), channel_id=1, source_target_pairs={{0,4},{2,6},{4,0},{6,2},{1,5},{3,7},{5,1},{7,3},{8,12},{10,14},{12... | collective-permute-start | bytes 172040 | tf_op jit(solution)/shard_map/ppermute | solution.py:16
  6.1 0.9 %copy-start.1 = (bf16[8,3584]{1,0:T(8,128)(2,1)S(1)}, bf16[8,3584]{1,0:T(8,128)(2,1)}, u32[]{:S(2)}) copy-start(bf16[8,3584]{1,0:T(8,128)(2,1)} %from_ref.1) | copy-start | bytes 172036
  6.9 7.3 %copy-start.4 = (bf16[1,3584,256]{2,1,0:T(8,128)(2,1)S(1)}, bf16[1,3584,256]{2,1,0:T(8,128)(2,1)}, u32[]{:S(2)}) copy-start(bf16[1,3584,256]{2,1,0:T(8,128)(2,1)} %param.10) | copy-start | bytes 5505028
  6.9 9.8 %collective-permute-start = (bf16[8,3584]{1,0:T(8,128)(2,1)S(1)}, bf16[8,3584]{1,0:T(8,128)(2,1)S(1)}, u32[]{:S(2)}, u32[]{:S(2)}) collective-permute-start(bf16[8,3584]{1,0:T(8,128)(2,1)S(1)} %shard_map.64), channel_id=1, source_target_pairs={{0,16},{2,18},{4,20},{6,22},{8,24},{10,26},{12,28},{14,30},{16,0},... | collective-permute-start | bytes 172040 | tf_op jit(solution)/shard_map/ppermute | solution.py:26
  8.4 4.2 %collective-permute-start.2 = (bf16[8,3584]{1,0:T(8,128)(2,1)S(1)}, bf16[8,3584]{1,0:T(8,128)(2,1)S(1)}, u32[]{:S(2)}, u32[]{:S(2)}) collective-permute-start(bf16[8,3584]{1,0:T(8,128)(2,1)S(1)} %collective-permute-done.1), channel_id=1, source_target_pairs={{0,16},{2,18},{4,20},{6,22},{8,24},{10,26},{12,28},{14,30},{16,0},... | collective-permute-start | bytes 172040 | tf_op jit(solution)/shard_map/ppermute | solution.py:26
  9.4 7.3 %collective-permute-start.6 = (bf16[8,3584]{1,0:T(8,128)(2,1)S(1)}, bf16[8,3584]{1,0:T(8,128)(2,1)S(1)}, u32[]{:S(2)}, u32[]{:S(2)}) collective-permute-start(bf16[8,3584]{1,0:T(8,128)(2,1)S(1)} %collective-permute-done.5), channel_id=1, source_target_pairs={{0,16},{2,18},{4,20},{6,22},{8,24},{10,26},{12,28},{14,30},{16,0},... | collective-permute-start | bytes 172040 | tf_op jit(solution)/shard_map/ppermute | solution.py:26
  10.9 5.8 %collective-permute-start.4 = (bf16[8,3584]{1,0:T(8,128)(2,1)S(1)}, bf16[8,3584]{1,0:T(8,128)(2,1)S(1)}, u32[]{:S(2)}, u32[]{:S(2)}) collective-permute-start(bf16[8,3584]{1,0:T(8,128)(2,1)S(1)} %collective-permute-done.3), channel_id=1, source_target_pairs={{0,16},{2,18},{4,20},{6,22},{8,24},{10,26},{12,28},{14,30},{16,0},... | collective-permute-start | bytes 172040 | tf_op jit(solution)/shard_map/ppermute | solution.py:26
  12.5 2.2 %copy-start.5 = (bf16[1,3584,256]{2,1,0:T(8,128)(2,1)S(1)}, bf16[1,3584,256]{2,1,0:T(8,128)(2,1)}, u32[]{:S(2)}) copy-start(bf16[1,3584,256]{2,1,0:T(8,128)(2,1)} %param.9) | copy-start | bytes 5505028
  12.7 1.5 %collective-permute-start.7 = (bf16[32,3584]{1,0:T(8,128)(2,1)S(1)}, bf16[32,3584]{1,0:T(8,128)(2,1)S(1)}, u32[]{:S(2)}, u32[]{:S(2)}) collective-permute-start(bf16[32,3584]{1,0:T(8,128)(2,1)S(1)} %shard_map.65), channel_id=1, source_target_pairs={{0,8},{8,0},{16,24},{24,16},{1,9},{9,1},{17,25},{25,17},{2,10},{10... | collective-permute-start | bytes 688136 | tf_op jit(solution)/shard_map/ppermute | solution.py:30
  15.1 4.7 %collective-permute-start.10 = (bf16[64,512]{1,0:T(8,128)(2,1)S(1)}, bf16[64,512]{1,0:T(8,128)(2,1)S(1)}, u32[]{:S(2)}, u32[]{:S(2)}) collective-permute-start(bf16[64,512]{1,0:T(8,128)(2,1)S(1)} %fusion.25.refs_1_), channel_id=1, source_target_pairs={{0,1},{1,0},{2,3},{3,2},{4,5},{5,4},{6,7},{7,6},{8,9},{9,8},{10,11... | collective-permute-start | bytes 196616 | tf_op jit(solution)/shard_map/ppermute | solution.py:16
  16.7 1.6 %collective-permute-start.8 = (bf16[32,3584]{1,0:T(8,128)(2,1)S(1)}, bf16[32,3584]{1,0:T(8,128)(2,1)S(1)}, u32[]{:S(2)}, u32[]{:S(2)}) collective-permute-start(bf16[32,3584]{1,0:T(8,128)(2,1)S(1)} %pad_maximum_fusion.4.refs_0_), channel_id=1, source_target_pairs={{0,8},{8,0},{16,24},{24,16},{1,9},{9,1},{17,25},{25,17},{2,10},{10... | collective-permute-start | bytes 688136 | tf_op jit(solution)/shard_map/ppermute | solution.py:30
  19.2 5.0 %collective-permute-start.9 = (bf16[64,512]{1,0:T(8,128)(2,1)S(1)}, bf16[64,512]{1,0:T(8,128)(2,1)S(1)}, u32[]{:S(2)}, u32[]{:S(2)}) collective-permute-start(bf16[64,512]{1,0:T(8,128)(2,1)S(1)} %fusion.24.refs_1_), channel_id=1, source_target_pairs={{0,1},{1,0},{2,3},{3,2},{4,5},{5,4},{6,7},{7,6},{8,9},{9,8},{10,11... | collective-permute-start | bytes 196616 | tf_op jit(solution)/shard_map/ppermute | solution.py:16
  20.3 1.6 %collective-permute-start.11 = (bf16[32,3584]{1,0:T(8,128)(2,1)S(1)}, bf16[32,3584]{1,0:T(8,128)(2,1)S(1)}, u32[]{:S(2)}, u32[]{:S(2)}) collective-permute-start(bf16[32,3584]{1,0:T(8,128)(2,1)S(1)} %slice.122), channel_id=1, source_target_pairs={{0,8},{8,0},{16,24},{24,16},{1,9},{9,1},{17,25},{25,17},{2,10},{10... | collective-permute-start | bytes 688136 | tf_op jit(solution)/shard_map/ppermute | solution.py:30
  22.0 9.2 %collective-permute-start.19 = (bf16[8,3584]{1,0:T(8,128)(2,1)S(1)}, bf16[8,3584]{1,0:T(8,128)(2,1)S(1)}, u32[]{:S(2)}, u32[]{:S(2)}) collective-permute-start(bf16[8,3584]{1,0:T(8,128)(2,1)S(1)} %get-tuple-element.7), channel_id=1, source_target_pairs={{0,6},{2,0},{4,2},{6,4},{1,7},{3,1},{5,3},{7,5},{8,14},{10,8},{12,... | collective-permute-start | bytes 172040 | tf_op jit(solution)/shard_map/ppermute | solution.py:16
  24.7 2.5 %collective-permute-start.12 = (bf16[32,3584]{1,0:T(8,128)(2,1)S(1)}, bf16[32,3584]{1,0:T(8,128)(2,1)S(1)}, u32[]{:S(2)}, u32[]{:S(2)}) collective-permute-start(bf16[32,3584]{1,0:T(8,128)(2,1)S(1)} %slice.121), channel_id=1, source_target_pairs={{0,8},{8,0},{16,24},{24,16},{1,9},{9,1},{17,25},{25,17},{2,10},{10... | collective-permute-start | bytes 688136 | tf_op jit(solution)/shard_map/ppermute | solution.py:30
  24.8 14.9 %copy-start.2 = (s32[8,1]{0,1:T(1,128)S(1)}, s32[8,1]{0,1:T(1,128)}, u32[]{:S(2)}) copy-start(s32[8,1]{0,1:T(1,128)} %param.7) | copy-start | bytes 100
  24.8 14.9 %copy-start.3 = (s32[8,1]{0,1:T(1,128)S(1)}, s32[8,1]{0,1:T(1,128)}, u32[]{:S(2)}) copy-start(s32[8,1]{0,1:T(1,128)} %param.8) | copy-start | bytes 100
  24.8 7.9 %collective-permute-start.17 = (bf16[8,3584]{1,0:T(8,128)(2,1)S(1)}, bf16[8,3584]{1,0:T(8,128)(2,1)S(1)}, u32[]{:S(2)}, u32[]{:S(2)}) collective-permute-start(bf16[8,3584]{1,0:T(8,128)(2,1)S(1)} %shard_map.74), channel_id=1, source_target_pairs={{0,2},{2,4},{4,6},{6,0},{1,3},{3,5},{5,7},{7,1},{8,10},{10,12},{12... | collective-permute-start | bytes 172040 | tf_op jit(solution)/shard_map/ppermute | solution.py:16
  26.0 7.5 %collective-permute-start.18 = (bf16[8,3584]{1,0:T(8,128)(2,1)S(1)}, bf16[8,3584]{1,0:T(8,128)(2,1)S(1)}, u32[]{:S(2)}, u32[]{:S(2)}) collective-permute-start(bf16[8,3584]{1,0:T(8,128)(2,1)S(1)} %shard_map.75), channel_id=1, source_target_pairs={{0,4},{2,6},{4,0},{6,2},{1,5},{3,7},{5,1},{7,3},{8,12},{10,14},{12... | collective-permute-start | bytes 172040 | tf_op jit(solution)/shard_map/ppermute | solution.py:16
  27.2 6.2 %collective-permute-start.16 = (bf16[8,3584]{1,0:T(8,128)(2,1)S(1)}, bf16[8,3584]{1,0:T(8,128)(2,1)S(1)}, u32[]{:S(2)}, u32[]{:S(2)}) collective-permute-start(bf16[8,3584]{1,0:T(8,128)(2,1)S(1)} %get-tuple-element.10), channel_id=1, source_target_pairs={{0,16},{2,18},{4,20},{6,22},{8,24},{10,26},{12,28},{14,30},{16,0},... | collective-permute-start | bytes 172040 | tf_op jit(solution)/shard_map/ppermute | solution.py:26
  28.4 6.0 %collective-permute-start.15 = (bf16[8,3584]{1,0:T(8,128)(2,1)S(1)}, bf16[8,3584]{1,0:T(8,128)(2,1)S(1)}, u32[]{:S(2)}, u32[]{:S(2)}) collective-permute-start(bf16[8,3584]{1,0:T(8,128)(2,1)S(1)} %get-tuple-element.11), channel_id=1, source_target_pairs={{0,22},{2,16},{4,18},{6,20},{8,30},{10,24},{12,26},{14,28},{16,6},... | collective-permute-start | bytes 172040 | tf_op jit(solution)/shard_map/ppermute | solution.py:26
  31.2 6.9 %collective-permute-start.14 = (bf16[8,3584]{1,0:T(8,128)(2,1)S(1)}, bf16[8,3584]{1,0:T(8,128)(2,1)S(1)}, u32[]{:S(2)}, u32[]{:S(2)}) collective-permute-start(bf16[8,3584]{1,0:T(8,128)(2,1)S(1)} %get-tuple-element.12), channel_id=1, source_target_pairs={{0,20},{2,22},{4,16},{6,18},{8,28},{10,30},{12,24},{14,26},{16,4},... | collective-permute-start | bytes 172040 | tf_op jit(solution)/shard_map/ppermute | solution.py:26
  32.8 6.9 %collective-permute-start.13 = (bf16[8,3584]{1,0:T(8,128)(2,1)S(1)}, bf16[8,3584]{1,0:T(8,128)(2,1)S(1)}, u32[]{:S(2)}, u32[]{:S(2)}) collective-permute-start(bf16[8,3584]{1,0:T(8,128)(2,1)S(1)} %get-tuple-element.13), channel_id=1, source_target_pairs={{0,18},{2,20},{4,22},{6,16},{8,26},{10,28},{12,30},{14,24},{16,2},... | collective-permute-start | bytes 172040 | tf_op jit(solution)/shard_map/ppermute | solution.py:26

commit v3 on v2

--- a/solution.py
+++ b/solution.py
@@ -60,7 +60,7 @@
 
 def mix_kernel(n_tp, experts, ids_ref, levels_ref, *refs):
     *piece_refs, mixed_ref = refs
-    piece_refs = piece_refs[::-1]
+    piece_refs = piece_refs[: n_tp] + [r for s in range(1, experts) for r in piece_refs[s * n_tp : (s + 1) * n_tp][::-1]]
     count = mixed_ref.shape[0]
     expert = lax.axis_index("grp") // 2
     row = lax.broadcasted_iota(jnp.int32, (count, count), 0)
@@ -130,13 +130,15 @@
     _, near_out = partial_out(near_part, [after(other, far_sent) for other in near_others], 3450000000, 3450000000)
     near_out = near_out.reshape(n_tp, count, width)
     near_sent = near_out[1:].astype(bf16)
-    far_whole, far_out = partial_out(far_part, [after(other, near_sent) for other in far_others], 3450000000, 3450000000)
-    near_sent = [after(near_sent[i], far_whole) if i in (1, 2) else near_sent[i] for i in range(n_tp - 1)]
-    pieces = [near_out[0]] + [shift(near_sent[i], "tp", -t) for i, t in enumerate(places[1:])]
+    far_whole, far_out = partial_out(far_part, [after(other, near_sent) for other in far_others], 0, 0)
     far_out = far_out.reshape(experts - 1, n_tp, count, width).astype(bf16)
+    far_back = []
     for s in range(1, experts):
-        pieces += [shift_expert(far_out[experts - 1 - s, i], s, -t) for i, t in enumerate(places)]
-    return mix(expert_ids, gate_levels, pieces[::-1], n_tp, experts)
+        far_back += [shift_expert(far_out[experts - 1 - s, i], s, -t) for i, t in enumerate(places)]
+    near_sent = after(near_sent, *far_back[::n_tp])
+    near_back = [near_out[0]] + [shift(near_sent[i], "tp", -t) for i, t in enumerate(places[1:])]
+    pieces = near_back + [piece for s in range(experts - 1) for piece in far_back[s * n_tp : (s + 1) * n_tp][::-1]]
+    return mix(expert_ids, gate_levels, pieces, n_tp, experts)
 
 
 def solution(mesh):

time: 40.5 us -> 41.6 us (1.027)
  waiting for transfers between devices: 11.2 us -> 12.2 us
    ppermute x8, waiting for transfers between devices: 6.33 us -> 2.1 us  [shift_expert(): return lax.ppermute(value, ('grp', 'tp'), pairs)]
    ppermute x8, waiting for transfers between devices: 0.41 us -> 4.22 us  [shift(): lax.ppermute(value, axis, [(i, (i + by) % size) for i in range(size)])]
    ppermute x4, waiting for transfers between devices: 4.41 us -> 5.88 us  [swap_half(): lax.ppermute(value, 'grp', [(i, i ^ 1) for i in range(lax.axis_size('grp'...]
    ppermute x8, starting transfers between devices: 11.3 us -> 12.1 us  [shift_expert(): return lax.ppermute(value, ('grp', 'tp'), pairs)]
    ppermute x8, starting transfers between devices: 12.8 us -> 12.1 us  [shift(): lax.ppermute(value, axis, [(i, (i + by) % size) for i in range(size)])]
  transfers between devices with their start and end apart: 20 -> 20, of which waited for: 8 -> 10; matrix products, arithmetic and copies ran while one was open for 7% -> 6% of each run, Pallas kernels for 0% -> 0%
where the time goes in v3:
time: 41.6 us; the launch traced here: 41.4 us
  starting transfers between devices  24.4 us (59%)
  waiting for transfers between devices  12.2 us (29%)
  matrix products  2.59 us (6%)
  local copies, waits for them, and re-layouts  1.03 us (2%)
  Pallas kernels  0.75 us (2%)
    ppermute x8, starting transfers between devices, shift(): lax.ppermute(value, axis, [(i, (i + by) % size) for i in range(size)])  12.1 us
    ppermute x8, starting transfers between devices, shift_expert(): return lax.ppermute(value, ('grp', 'tp'), pairs)  12.1 us
    ppermute x4, waiting for transfers between devices, swap_half(): lax.ppermute(value, 'grp', [(i, i ^ 1) for i in range(lax.axis_size('grp'...  5.88 us
    ppermute x8, waiting for transfers between devices, shift(): lax.ppermute(value, axis, [(i, (i + by) % size) for i in range(size)])  4.22 us
    ppermute x8, waiting for transfers between devices, shift_expert(): return lax.ppermute(value, ('grp', 'tp'), pairs)  2.1 us
    dot_general x4, matrix products, partial_sums(): jnp.dot(rows, w, preferred_element_type=f32)  1.76 us
    unnamed x16, local copies, waits for them, and re-layouts  0.9 us
    dot_general x2, matrix products, partial_out(): out = jnp.dot(hidden, w_down, preferred_element_type=f32)  0.83 us
  transfers between devices with their start and end apart: 20, of which 10 were waited for; matrix products, arithmetic and copies ran while one was open for 6% of the time, Pallas kernels for 0%

profile of v3, /device:TPU:0, one launch (start us, length us, event | category | flops | bytes accessed | tf_op | source)
XLA Modules:
  0.0 41.4 jit_solution(5938839350453447135)
XLA Ops:
  0.0 0.0 copy-start
  0.0 3.0 %collective-permute-start = (bf16[8,3584]{1,0:T(8,128)(2,1)}, bf16[8,3584]{1,0:T(8,128)(2,1)S(1)}, u32[]{:S(2)}, u32[]{:S(2)}) collective-permute-start(bf16[8,3584]{1,0:T(8,128)(2,1)} %from_ref.1), channel_id=1, source_target_pairs={{0,2},{2,4},{4,6},{6,0},{1,3},{3,5},{5,7},{7,1},{8,10},{10,12},{12... | collective-permute-start | bytes 172040 | tf_op jit(solution)/shard_map/ppermute | solution.py:16
  3.0 2.1 %collective-permute-start.2 = (bf16[8,3584]{1,0:T(8,128)(2,1)}, bf16[8,3584]{1,0:T(8,128)(2,1)S(1)}, u32[]{:S(2)}, u32[]{:S(2)}) collective-permute-start(bf16[8,3584]{1,0:T(8,128)(2,1)} %from_ref.1), channel_id=1, source_target_pairs={{0,6},{2,0},{4,2},{6,4},{1,7},{3,1},{5,3},{7,5},{8,14},{10,8},{12,... | collective-permute-start | bytes 172040 | tf_op jit(solution)/shard_map/ppermute | solution.py:16
  5.1 1.0 %collective-permute-start.1 = (bf16[8,3584]{1,0:T(8,128)(2,1)}, bf16[8,3584]{1,0:T(8,128)(2,1)S(1)}, u32[]{:S(2)}, u32[]{:S(2)}) collective-permute-start(bf16[8,3584]{1,0:T(8,128)(2,1)} %from_ref.1), channel_id=1, source_target_pairs={{0,4},{2,6},{4,0},{6,2},{1,5},{3,7},{5,1},{7,3},{8,12},{10,14},{12... | collective-permute-start | bytes 172040 | tf_op jit(solution)/shard_map/ppermute | solution.py:16
  6.1 0.0 copy-start.1
  6.1 0.9 %copy-done.1 = bf16[8,3584]{1,0:T(8,128)(2,1)S(1)} copy-done((bf16[8,3584]{1,0:T(8,128)(2,1)S(1)}, bf16[8,3584]{1,0:T(8,128)(2,1)}, u32[]{:S(2)}) %copy-start.1) | copy-done | bytes 57368
  6.9 0.0 copy-start.4
  6.9 1.5 %collective-permute-start.6 = (bf16[8,3584]{1,0:T(8,128)(2,1)S(1)}, bf16[8,3584]{1,0:T(8,128)(2,1)S(1)}, u32[]{:S(2)}, u32[]{:S(2)}) collective-permute-start(bf16[8,3584]{1,0:T(8,128)(2,1)S(1)} %shard_map.64), channel_id=1, source_target_pairs={{0,16},{2,18},{4,20},{6,22},{8,24},{10,26},{12,28},{14,30},{16,0},... | collective-permute-start | bytes 172040 | tf_op jit(solution)/shard_map/ppermute | solution.py:26
  8.4 0.0 collective-permute-done
  8.4 1.0 %collective-permute-start.3 = (bf16[8,3584]{1,0:T(8,128)(2,1)S(1)}, bf16[8,3584]{1,0:T(8,128)(2,1)S(1)}, u32[]{:S(2)}, u32[]{:S(2)}) collective-permute-start(bf16[8,3584]{1,0:T(8,128)(2,1)S(1)} %collective-permute-done), channel_id=1, source_target_pairs={{0,16},{2,18},{4,20},{6,22},{8,24},{10,26},{12,28},{14,30},{16,0},... | collective-permute-start | bytes 172040 | tf_op jit(solution)/shard_map/ppermute | solution.py:26
  9.4 0.0 collective-permute-done.2
  9.4 1.1 %collective-permute-start.8 = (bf16[8,3584]{1,0:T(8,128)(2,1)S(1)}, bf16[8,3584]{1,0:T(8,128)(2,1)S(1)}, u32[]{:S(2)}, u32[]{:S(2)}) collective-permute-start(bf16[8,3584]{1,0:T(8,128)(2,1)S(1)} %collective-permute-done.2), channel_id=1, source_target_pairs={{0,16},{2,18},{4,20},{6,22},{8,24},{10,26},{12,28},{14,30},{16,0},... | collective-permute-start | bytes 172040 | tf_op jit(solution)/shard_map/ppermute | solution.py:26
  10.5 0.4 collective-permute-done.1
  10.9 1.6 %collective-permute-start.7 = (bf16[8,3584]{1,0:T(8,128)(2,1)S(1)}, bf16[8,3584]{1,0:T(8,128)(2,1)S(1)}, u32[]{:S(2)}, u32[]{:S(2)}) collective-permute-start(bf16[8,3584]{1,0:T(8,128)(2,1)S(1)} %collective-permute-done.1), channel_id=1, source_target_pairs={{0,16},{2,18},{4,20},{6,22},{8,24},{10,26},{12,28},{14,30},{16,0},... | collective-permute-start | bytes 172040 | tf_op jit(solution)/shard_map/ppermute | solution.py:26
  12.5 0.0 copy-start.5
  12.5 0.2 collective-permute-done.3.refs_1_
  12.7 0.0 collective-permute-start.4
  12.7 1.5 %collective-permute-done.4 = bf16[32,3584]{1,0:T(8,128)(2,1)S(1)} collective-permute-done((bf16[32,3584]{1,0:T(8,128)(2,1)S(1)}, bf16[32,3584]{1,0:T(8,128)(2,1)S(1)}, u32[]{:S(2)}, u32[]{:S(2)}) %collective-permute-start.4) | collective-permute-done | bytes 229408 | tf_op jit(solution)/shard_map/ppermute | solution.py:30
  14.2 0.0 copy-done.4
  14.2 0.4 %fusion.6 = f32[64,256]{1,0:T(8,128)S(1)} fusion(bf16[64,3584]{1,0:T(8,128)(2,1)S(1)} %constant_dynamic-update-slice_fusion, bf16[1,3584,256]{2,1,0:T(8,128)(2,1)S(1)} %copy-done.4), kind=kOutput, calls=%fused_computation.6 | convolution fusion | flops 117440512 | bytes 2359296 | tf_op jit(solution)/shard_map/dot_general | solution.py:100
  14.6 0.0 copy-done.5
  14.6 0.4 %fusion.10 = f32[64,256]{1,0:T(8,128)S(1)} fusion(bf16[64,3584]{1,0:T(8,128)(2,1)S(1)} %constant_dynamic-update-slice_fusion, bf16[1,3584,256]{2,1,0:T(8,128)(2,1)S(1)} %copy-done.5), kind=kOutput, calls=%fused_computation.10 | convolution fusion | flops 117440512 | bytes 2359296 | tf_op jit(solution)/shard_map/dot_general | solution.py:100
  15.1 1.6 %collective-permute-start.5 = (bf16[64,512]{1,0:T(8,128)(2,1)S(1)}, bf16[64,512]{1,0:T(8,128)(2,1)S(1)}, u32[]{:S(2)}, u32[]{:S(2)}) collective-permute-start(bf16[64,512]{1,0:T(8,128)(2,1)S(1)} %fusion.26.refs_1_), channel_id=1, source_target_pairs={{0,1},{1,0},{2,3},{3,2},{4,5},{5,4},{6,7},{7,6},{8,9},{9,8},{10,11... | collective-permute-start | bytes 196616 | tf_op jit(solution)/shard_map/ppermute | solution.py:16
  16.7 0.0 collective-permute-done.8.refs_0_
  16.7 0.0 collective-permute-done.6
  16.7 0.0 collective-permute-done.7
  16.7 0.1 collective-permute-start.9
  16.8 1.5 %collective-permute-done.9 = bf16[32,3584]{1,0:T(8,128)(2,1)S(1)} collective-permute-done((bf16[32,3584]{1,0:T(8,128)(2,1)S(1)}, bf16[32,3584]{1,0:T(8,128)(2,1)S(1)}, u32[]{:S(2)}, u32[]{:S(2)}) %collective-permute-start.9) | collective-permute-done | bytes 229408 | tf_op jit(solution)/shard_map/ppermute | solution.py:30
  18.3 0.4 %fusion.4 = f32[64,256]{1,0:T(8,128)S(1)} fusion(bf16[1,3584,256]{2,1,0:T(8,128)(2,1)S(1)} %copy-done.4, bf16[32,3584]{1,0:T(8,128)(2,1)S(1)} %collective-permute-done.9, bf16[32,3584]{1,0:T(8,128)(2,1)S(1)} %shard_map.68), kind=kOutput, calls=%fused_computation.4 | convolution fusion | flops 118358016 | bytes 2359296 | tf_op jit(solution)/shard_map/dot_general | solution.py:100
  18.7 0.4 %fusion.8 = f32[64,256]{1,0:T(8,128)S(1)} fusion(bf16[1,3584,256]{2,1,0:T(8,128)(2,1)S(1)} %copy-done.5, bf16[32,3584]{1,0:T(8,128)(2,1)S(1)} %collective-permute-done.9, bf16[32,3584]{1,0:T(8,128)(2,1)S(1)} %shard_map.68), kind=kOutput, calls=%fused_computation.8 | convolution fusion | flops 118358016 | bytes 2359296 | tf_op jit(solution)/shard_map/dot_general | solution.py:100
  19.2 0.6 %collective-permute-start.11 = (bf16[64,512]{1,0:T(8,128)(2,1)S(1)}, bf16[64,512]{1,0:T(8,128)(2,1)S(1)}, u32[]{:S(2)}, u32[]{:S(2)}) collective-permute-start(bf16[64,512]{1,0:T(8,128)(2,1)S(1)} %fusion.15.refs_1_), channel_id=1, source_target_pairs={{0,1},{1,0},{2,3},{3,2},{4,5},{5,4},{6,7},{7,6},{8,9},{9,8},{10,11... | collective-permute-start | bytes 196616 | tf_op jit(solution)/shard_map/ppermute | solution.py:16
  19.8 0.0 collective-permute-done.5.refs_0_
  19.8 0.0 copy-done
  19.8 0.4 %fusion.2.refs_0_ = f32[64,3584]{1,0:T(8,128)S(1)} fusion(bf16[1,256,3584]{2,1,0:T(8,128)(2,1)S(1)} %copy-done, f32[64,512]{1,0:T(8,128)S(1)} %convert_add_fusion.1), kind=kOutput, calls=%fused_computation.2 | convolution fusion | flops 117538816 | bytes 2883584 | tf_op jit(solution)/shard_map/dot_general | solution.py:111
  20.3 0.1 collective-permute-start.10
  20.4 1.5 %collective-permute-done.10 = bf16[32,3584]{1,0:T(8,128)(2,1)S(1)} collective-permute-done((bf16[32,3584]{1,0:T(8,128)(2,1)S(1)}, bf16[32,3584]{1,0:T(8,128)(2,1)S(1)}, u32[]{:S(2)}, u32[]{:S(2)}) %collective-permute-start.10) | collective-permute-done | bytes 229408 | tf_op jit(solution)/shard_map/ppermute | solution.py:30
  21.8 0.1 slice_add_fusion.1
  21.9 1.6 %collective-permute-done.11.refs_0_ = bf16[64,512]{1,0:T(8,128)(2,1)S(1)} collective-permute-done((bf16[64,512]{1,0:T(8,128)(2,1)S(1)}, bf16[64,512]{1,0:T(8,128)(2,1)S(1)}, u32[]{:S(2)}, u32[]{:S(2)}) %collective-permute-start.11) | collective-permute-done | bytes 65568 | tf_op jit(solution)/shard_map/ppermute | solution.py:16
  23.6 0.4 %fusion = f32[64,3584]{1,0:T(8,128)S(1)} fusion(bf16[1,256,3584]{2,1,0:T(8,128)(2,1)S(1)} %copy-done, f32[64,512]{1,0:T(8,128)S(1)} %convert_add_fusion), kind=kOutput, calls=%fused_computation | convolution fusion | flops 117538816 | bytes 2883584 | tf_op jit(solution)/shard_map/dot_general | solution.py:111
  24.0 0.0 copy-start.2
  24.0 0.0 copy-start.3
  24.0 0.1 collective-permute-start.12
  24.1 1.5 %collective-permute-done.12 = bf16[32,3584]{1,0:T(8,128)(2,1)S(1)} collective-permute-done((bf16[32,3584]{1,0:T(8,128)(2,1)S(1)}, bf16[32,3584]{1,0:T(8,128)(2,1)S(1)}, u32[]{:S(2)}, u32[]{:S(2)}) %collective-permute-start.12) | collective-permute-done | bytes 229408 | tf_op jit(solution)/shard_map/ppermute | solution.py:30
  25.7 1.0 %collective-permute-start.13 = (bf16[8,3584]{1,0:T(8,128)(2,1)S(1)}, bf16[8,3584]{1,0:T(8,128)(2,1)S(1)}, u32[]{:S(2)}, u32[]{:S(2)}) collective-permute-start(bf16[8,3584]{1,0:T(8,128)(2,1)S(1)} %get-tuple-element.8), channel_id=1, source_target_pairs={{0,16},{2,18},{4,20},{6,22},{8,24},{10,26},{12,28},{14,30},{16,0},... | collective-permute-start | bytes 172040 | tf_op jit(solution)/shard_map/ppermute | solution.py:26
  26.7 2.7 %collective-permute-start.19 = (bf16[8,3584]{1,0:T(8,128)(2,1)S(1)}, bf16[8,3584]{1,0:T(8,128)(2,1)S(1)}, u32[]{:S(2)}, u32[]{:S(2)}) collective-permute-start(bf16[8,3584]{1,0:T(8,128)(2,1)S(1)} %get-tuple-element.5), channel_id=1, source_target_pairs={{0,22},{2,16},{4,18},{6,20},{8,30},{10,24},{12,26},{14,28},{16,6},... | collective-permute-start | bytes 172040 | tf_op jit(solution)/shard_map/ppermute | solution.py:26
  29.4 1.6 %collective-permute-start.18 = (bf16[8,3584]{1,0:T(8,128)(2,1)S(1)}, bf16[8,3584]{1,0:T(8,128)(2,1)S(1)}, u32[]{:S(2)}, u32[]{:S(2)}) collective-permute-start(bf16[8,3584]{1,0:T(8,128)(2,1)S(1)} %get-tuple-element.6), channel_id=1, source_target_pairs={{0,20},{2,22},{4,16},{6,18},{8,28},{10,30},{12,24},{14,26},{16,4},... | collective-permute-start | bytes 172040 | tf_op jit(solution)/shard_map/ppermute | solution.py:26
  31.0 1.6 %collective-permute-start.17 = (bf16[8,3584]{1,0:T(8,128)(2,1)S(1)}, bf16[8,3584]{1,0:T(8,128)(2,1)S(1)}, u32[]{:S(2)}, u32[]{:S(2)}) collective-permute-start(bf16[8,3584]{1,0:T(8,128)(2,1)S(1)} %get-tuple-element.7), channel_id=1, source_target_pairs={{0,18},{2,20},{4,22},{6,16},{8,26},{10,28},{12,30},{14,24},{16,2},... | collective-permute-start | bytes 172040 | tf_op jit(solution)/shard_map/ppermute | solution.py:26
  32.6 0.0 collective-permute-done.13.refs_1_.refs_7_
  32.6 1.2 %collective-permute-start.16 = (bf16[8,3584]{1,0:T(8,128)(2,1)S(1)}, bf16[8,3584]{1,0:T(8,128)(2,1)S(1)}, u32[]{:S(2)}, u32[]{:S(2)}) collective-permute-start(bf16[8,3584]{1,0:T(8,128)(2,1)S(1)} %get-tuple-element.9), channel_id=1, source_target_pairs={{0,2},{2,4},{4,6},{6,0},{1,3},{3,5},{5,7},{7,1},{8,10},{10,12},{12... | collective-permute-start | bytes 172040 | tf_op jit(solution)/shard_map/ppermute | solution.py:16
  33.8 1.9 %collective-permute-start.15 = (bf16[8,3584]{1,0:T(8,128)(2,1)S(1)}, bf16[8,3584]{1,0:T(8,128)(2,1)S(1)}, u32[]{:S(2)}, u32[]{:S(2)}) collective-permute-start(bf16[8,3584]{1,0:T(8,128)(2,1)S(1)} %get-tuple-element.10), channel_id=1, source_target_pairs={{0,4},{2,6},{4,0},{6,2},{1,5},{3,7},{5,1},{7,3},{8,12},{10,14},{12... | collective-permute-start | bytes 172040 | tf_op jit(solution)/shard_map/ppermute | solution.py:16
  35.8 0.0 collective-permute-done.19.refs_6_
  35.8 0.7 %collective-permute-start.14 = (bf16[8,3584]{1,0:T(8,128)(2,1)S(1)}, bf16[8,3584]{1,0:T(8,128)(2,1)S(1)}, u32[]{:S(2)}, u32[]{:S(2)}) collective-permute-start(bf16[8,3584]{1,0:T(8,128)(2,1)S(1)} %get-tuple-element.11), channel_id=1, source_target_pairs={{0,6},{2,0},{4,2},{6,4},{1,7},{3,1},{5,3},{7,5},{8,14},{10,8},{12,... | collective-permute-start | bytes 172040 | tf_op jit(solution)/shard_map/ppermute | solution.py:16
  36.5 0.0 collective-permute-done.18.refs_5_
  36.5 1.9 %collective-permute-done.17.refs_4_ = bf16[8,3584]{1,0:T(8,128)(2,1)S(1)} collective-permute-done((bf16[8,3584]{1,0:T(8,128)(2,1)S(1)}, bf16[8,3584]{1,0:T(8,128)(2,1)S(1)}, u32[]{:S(2)}, u32[]{:S(2)}) %collective-permute-start.17) | collective-permute-done | bytes 57376 | tf_op jit(solution)/shard_map/ppermute | solution.py:26
  38.4 0.7 %collective-permute-done.16.refs_3_ = bf16[8,3584]{1,0:T(8,128)(2,1)S(1)} collective-permute-done((bf16[8,3584]{1,0:T(8,128)(2,1)S(1)}, bf16[8,3584]{1,0:T(8,128)(2,1)S(1)}, u32[]{:S(2)}, u32[]{:S(2)}) %collective-permute-start.16) | collective-permute-done | bytes 57376 | tf_op jit(solution)/shard_map/ppermute | solution.py:16
  39.2 1.5 %collective-permute-done.15.refs_2_ = bf16[8,3584]{1,0:T(8,128)(2,1)S(1)} collective-permute-done((bf16[8,3584]{1,0:T(8,128)(2,1)S(1)}, bf16[8,3584]{1,0:T(8,128)(2,1)S(1)}, u32[]{:S(2)}, u32[]{:S(2)}) %collective-permute-start.15) | collective-permute-done | bytes 57376 | tf_op jit(solution)/shard_map/ppermute | solution.py:16
  40.7 0.0 collective-permute-done.14.refs_1_
  40.7 0.0 copy-done.2
  40.7 0.0 copy-done.3
  40.7 0.7 %shard_map.73 = bf16[8,3584]{1,0:T(8,128)(2,1)} custom-call(s32[1,8]{1,0:T(1,128)S(1)} %bitcast.37, s32[1,8]{1,0:T(1,128)S(1)} %bitcast.38, f32[8,3584]{1,0:T(8,128)S(1)} %slice.77.refs_0_, bf16[8,3584]{1,0:T(8,128)(2,1)S(1)} %collective-permute-done.14.refs_1_, bf16[8,3584]{1,0:T(8,128)(2,1)S(1)} %collective-permute-done.15.refs_2_, ...), custom_call_target="tpu_custom_call" | custom-call | tf_op jit(solution)/shard_map/pallas_call | solution.py:84
  (28 shorter events, 0.3 us)
Async XLA Ops:
  0.0 19.8 %copy-start = (bf16[1,256,3584]{2,1,0:T(8,128)(2,1)S(1)}, bf16[1,256,3584]{2,1,0:T(8,128)(2,1)}, u32[]{:S(2)}) copy-start(bf16[1,256,3584]{2,1,0:T(8,128)(2,1)} %param.11) | copy-start | bytes 5505028
  0.0 8.4 %collective-permute-start = (bf16[8,3584]{1,0:T(8,128)(2,1)}, bf16[8,3584]{1,0:T(8,128)(2,1)S(1)}, u32[]{:S(2)}, u32[]{:S(2)}) collective-permute-start(bf16[8,3584]{1,0:T(8,128)(2,1)} %from_ref.1), channel_id=1, source_target_pairs={{0,2},{2,4},{4,6},{6,0},{1,3},{3,5},{5,7},{7,1},{8,10},{10,12},{12... | collective-permute-start | bytes 172040 | tf_op jit(solution)/shard_map/ppermute | solution.py:16
  3.0 6.4 %collective-permute-start.2 = (bf16[8,3584]{1,0:T(8,128)(2,1)}, bf16[8,3584]{1,0:T(8,128)(2,1)S(1)}, u32[]{:S(2)}, u32[]{:S(2)}) collective-permute-start(bf16[8,3584]{1,0:T(8,128)(2,1)} %from_ref.1), channel_id=1, source_target_pairs={{0,6},{2,0},{4,2},{6,4},{1,7},{3,1},{5,3},{7,5},{8,14},{10,8},{12,... | collective-permute-start | bytes 172040 | tf_op jit(solution)/shard_map/ppermute | solution.py:16
  5.1 5.8 %collective-permute-start.1 = (bf16[8,3584]{1,0:T(8,128)(2,1)}, bf16[8,3584]{1,0:T(8,128)(2,1)S(1)}, u32[]{:S(2)}, u32[]{:S(2)}) collective-permute-start(bf16[8,3584]{1,0:T(8,128)(2,1)} %from_ref.1), channel_id=1, source_target_pairs={{0,4},{2,6},{4,0},{6,2},{1,5},{3,7},{5,1},{7,3},{8,12},{10,14},{12... | collective-permute-start | bytes 172040 | tf_op jit(solution)/shard_map/ppermute | solution.py:16
  6.1 0.9 %copy-start.1 = (bf16[8,3584]{1,0:T(8,128)(2,1)S(1)}, bf16[8,3584]{1,0:T(8,128)(2,1)}, u32[]{:S(2)}) copy-start(bf16[8,3584]{1,0:T(8,128)(2,1)} %from_ref.1) | copy-start | bytes 172036
  6.9 7.3 %copy-start.4 = (bf16[1,3584,256]{2,1,0:T(8,128)(2,1)S(1)}, bf16[1,3584,256]{2,1,0:T(8,128)(2,1)}, u32[]{:S(2)}) copy-start(bf16[1,3584,256]{2,1,0:T(8,128)(2,1)} %param.10) | copy-start | bytes 5505028
  6.9 9.8 %collective-permute-start.6 = (bf16[8,3584]{1,0:T(8,128)(2,1)S(1)}, bf16[8,3584]{1,0:T(8,128)(2,1)S(1)}, u32[]{:S(2)}, u32[]{:S(2)}) collective-permute-start(bf16[8,3584]{1,0:T(8,128)(2,1)S(1)} %shard_map.64), channel_id=1, source_target_pairs={{0,16},{2,18},{4,20},{6,22},{8,24},{10,26},{12,28},{14,30},{16,0},... | collective-permute-start | bytes 172040 | tf_op jit(solution)/shard_map/ppermute | solution.py:26
  8.4 4.2 %collective-permute-start.3 = (bf16[8,3584]{1,0:T(8,128)(2,1)S(1)}, bf16[8,3584]{1,0:T(8,128)(2,1)S(1)}, u32[]{:S(2)}, u32[]{:S(2)}) collective-permute-start(bf16[8,3584]{1,0:T(8,128)(2,1)S(1)} %collective-permute-done), channel_id=1, source_target_pairs={{0,16},{2,18},{4,20},{6,22},{8,24},{10,26},{12,28},{14,30},{16,0},... | collective-permute-start | bytes 172040 | tf_op jit(solution)/shard_map/ppermute | solution.py:26
  9.4 7.3 %collective-permute-start.8 = (bf16[8,3584]{1,0:T(8,128)(2,1)S(1)}, bf16[8,3584]{1,0:T(8,128)(2,1)S(1)}, u32[]{:S(2)}, u32[]{:S(2)}) collective-permute-start(bf16[8,3584]{1,0:T(8,128)(2,1)S(1)} %collective-permute-done.2), channel_id=1, source_target_pairs={{0,16},{2,18},{4,20},{6,22},{8,24},{10,26},{12,28},{14,30},{16,0},... | collective-permute-start | bytes 172040 | tf_op jit(solution)/shard_map/ppermute | solution.py:26
  10.9 5.8 %collective-permute-start.7 = (bf16[8,3584]{1,0:T(8,128)(2,1)S(1)}, bf16[8,3584]{1,0:T(8,128)(2,1)S(1)}, u32[]{:S(2)}, u32[]{:S(2)}) collective-permute-start(bf16[8,3584]{1,0:T(8,128)(2,1)S(1)} %collective-permute-done.1), channel_id=1, source_target_pairs={{0,16},{2,18},{4,20},{6,22},{8,24},{10,26},{12,28},{14,30},{16,0},... | collective-permute-start | bytes 172040 | tf_op jit(solution)/shard_map/ppermute | solution.py:26
  12.5 2.2 %copy-start.5 = (bf16[1,3584,256]{2,1,0:T(8,128)(2,1)S(1)}, bf16[1,3584,256]{2,1,0:T(8,128)(2,1)}, u32[]{:S(2)}) copy-start(bf16[1,3584,256]{2,1,0:T(8,128)(2,1)} %param.9) | copy-start | bytes 5505028
  12.7 1.5 %collective-permute-start.4 = (bf16[32,3584]{1,0:T(8,128)(2,1)S(1)}, bf16[32,3584]{1,0:T(8,128)(2,1)S(1)}, u32[]{:S(2)}, u32[]{:S(2)}) collective-permute-start(bf16[32,3584]{1,0:T(8,128)(2,1)S(1)} %shard_map.65), channel_id=1, source_target_pairs={{0,8},{8,0},{16,24},{24,16},{1,9},{9,1},{17,25},{25,17},{2,10},{10... | collective-permute-start | bytes 688136 | tf_op jit(solution)/shard_map/ppermute | solution.py:30
  15.1 4.7 %collective-permute-start.5 = (bf16[64,512]{1,0:T(8,128)(2,1)S(1)}, bf16[64,512]{1,0:T(8,128)(2,1)S(1)}, u32[]{:S(2)}, u32[]{:S(2)}) collective-permute-start(bf16[64,512]{1,0:T(8,128)(2,1)S(1)} %fusion.26.refs_1_), channel_id=1, source_target_pairs={{0,1},{1,0},{2,3},{3,2},{4,5},{5,4},{6,7},{7,6},{8,9},{9,8},{10,11... | collective-permute-start | bytes 196616 | tf_op jit(solution)/shard_map/ppermute | solution.py:16
  16.7 1.6 %collective-permute-start.9 = (bf16[32,3584]{1,0:T(8,128)(2,1)S(1)}, bf16[32,3584]{1,0:T(8,128)(2,1)S(1)}, u32[]{:S(2)}, u32[]{:S(2)}) collective-permute-start(bf16[32,3584]{1,0:T(8,128)(2,1)S(1)} %pad_maximum_fusion.4.refs_0_), channel_id=1, source_target_pairs={{0,8},{8,0},{16,24},{24,16},{1,9},{9,1},{17,25},{25,17},{2,10},{10... | collective-permute-start | bytes 688136 | tf_op jit(solution)/shard_map/ppermute | solution.py:30
  19.2 4.3 %collective-permute-start.11 = (bf16[64,512]{1,0:T(8,128)(2,1)S(1)}, bf16[64,512]{1,0:T(8,128)(2,1)S(1)}, u32[]{:S(2)}, u32[]{:S(2)}) collective-permute-start(bf16[64,512]{1,0:T(8,128)(2,1)S(1)} %fusion.15.refs_1_), channel_id=1, source_target_pairs={{0,1},{1,0},{2,3},{3,2},{4,5},{5,4},{6,7},{7,6},{8,9},{9,8},{10,11... | collective-permute-start | bytes 196616 | tf_op jit(solution)/shard_map/ppermute | solution.py:16
  20.3 1.6 %collective-permute-start.10 = (bf16[32,3584]{1,0:T(8,128)(2,1)S(1)}, bf16[32,3584]{1,0:T(8,128)(2,1)S(1)}, u32[]{:S(2)}, u32[]{:S(2)}) collective-permute-start(bf16[32,3584]{1,0:T(8,128)(2,1)S(1)} %slice.121), channel_id=1, source_target_pairs={{0,8},{8,0},{16,24},{24,16},{1,9},{9,1},{17,25},{25,17},{2,10},{10... | collective-permute-start | bytes 688136 | tf_op jit(solution)/shard_map/ppermute | solution.py:30
  24.0 16.7 %copy-start.2 = (s32[8,1]{0,1:T(1,128)S(1)}, s32[8,1]{0,1:T(1,128)}, u32[]{:S(2)}) copy-start(s32[8,1]{0,1:T(1,128)} %param.7) | copy-start | bytes 100
  24.0 16.7 %copy-start.3 = (s32[8,1]{0,1:T(1,128)S(1)}, s32[8,1]{0,1:T(1,128)}, u32[]{:S(2)}) copy-start(s32[8,1]{0,1:T(1,128)} %param.8) | copy-start | bytes 100
  24.0 1.6 %collective-permute-start.12 = (bf16[32,3584]{1,0:T(8,128)(2,1)S(1)}, bf16[32,3584]{1,0:T(8,128)(2,1)S(1)}, u32[]{:S(2)}, u32[]{:S(2)}) collective-permute-start(bf16[32,3584]{1,0:T(8,128)(2,1)S(1)} %slice.120), channel_id=1, source_target_pairs={{0,8},{8,0},{16,24},{24,16},{1,9},{9,1},{17,25},{25,17},{2,10},{10... | collective-permute-start | bytes 688136 | tf_op jit(solution)/shard_map/ppermute | solution.py:30
  25.7 6.9 %collective-permute-start.13 = (bf16[8,3584]{1,0:T(8,128)(2,1)S(1)}, bf16[8,3584]{1,0:T(8,128)(2,1)S(1)}, u32[]{:S(2)}, u32[]{:S(2)}) collective-permute-start(bf16[8,3584]{1,0:T(8,128)(2,1)S(1)} %get-tuple-element.8), channel_id=1, source_target_pairs={{0,16},{2,18},{4,20},{6,22},{8,24},{10,26},{12,28},{14,30},{16,0},... | collective-permute-start | bytes 172040 | tf_op jit(solution)/shard_map/ppermute | solution.py:26
  26.7 9.1 %collective-permute-start.19 = (bf16[8,3584]{1,0:T(8,128)(2,1)S(1)}, bf16[8,3584]{1,0:T(8,128)(2,1)S(1)}, u32[]{:S(2)}, u32[]{:S(2)}) collective-permute-start(bf16[8,3584]{1,0:T(8,128)(2,1)S(1)} %get-tuple-element.5), channel_id=1, source_target_pairs={{0,22},{2,16},{4,18},{6,20},{8,30},{10,24},{12,26},{14,28},{16,6},... | collective-permute-start | bytes 172040 | tf_op jit(solution)/shard_map/ppermute | solution.py:26
  29.4 7.1 %collective-permute-start.18 = (bf16[8,3584]{1,0:T(8,128)(2,1)S(1)}, bf16[8,3584]{1,0:T(8,128)(2,1)S(1)}, u32[]{:S(2)}, u32[]{:S(2)}) collective-permute-start(bf16[8,3584]{1,0:T(8,128)(2,1)S(1)} %get-tuple-element.6), channel_id=1, source_target_pairs={{0,20},{2,22},{4,16},{6,18},{8,28},{10,30},{12,24},{14,26},{16,4},... | collective-permute-start | bytes 172040 | tf_op jit(solution)/shard_map/ppermute | solution.py:26
  31.0 7.4 %collective-permute-start.17 = (bf16[8,3584]{1,0:T(8,128)(2,1)S(1)}, bf16[8,3584]{1,0:T(8,128)(2,1)S(1)}, u32[]{:S(2)}, u32[]{:S(2)}) collective-permute-start(bf16[8,3584]{1,0:T(8,128)(2,1)S(1)} %get-tuple-element.7), channel_id=1, source_target_pairs={{0,18},{2,20},{4,22},{6,16},{8,26},{10,28},{12,30},{14,24},{16,2},... | collective-permute-start | bytes 172040 | tf_op jit(solution)/shard_map/ppermute | solution.py:26
  32.6 6.6 %collective-permute-start.16 = (bf16[8,3584]{1,0:T(8,128)(2,1)S(1)}, bf16[8,3584]{1,0:T(8,128)(2,1)S(1)}, u32[]{:S(2)}, u32[]{:S(2)}) collective-permute-start(bf16[8,3584]{1,0:T(8,128)(2,1)S(1)} %get-tuple-element.9), channel_id=1, source_target_pairs={{0,2},{2,4},{4,6},{6,0},{1,3},{3,5},{5,7},{7,1},{8,10},{10,12},{12... | collective-permute-start | bytes 172040 | tf_op jit(solution)/shard_map/ppermute | solution.py:16
  33.8 6.8 %collective-permute-start.15 = (bf16[8,3584]{1,0:T(8,128)(2,1)S(1)}, bf16[8,3584]{1,0:T(8,128)(2,1)S(1)}, u32[]{:S(2)}, u32[]{:S(2)}) collective-permute-start(bf16[8,3584]{1,0:T(8,128)(2,1)S(1)} %get-tuple-element.10), channel_id=1, source_target_pairs={{0,4},{2,6},{4,0},{6,2},{1,5},{3,7},{5,1},{7,3},{8,12},{10,14},{12... | collective-permute-start | bytes 172040 | tf_op jit(solution)/shard_map/ppermute | solution.py:16
  35.8 4.9 %collective-permute-start.14 = (bf16[8,3584]{1,0:T(8,128)(2,1)S(1)}, bf16[8,3584]{1,0:T(8,128)(2,1)S(1)}, u32[]{:S(2)}, u32[]{:S(2)}) collective-permute-start(bf16[8,3584]{1,0:T(8,128)(2,1)S(1)} %get-tuple-element.11), channel_id=1, source_target_pairs={{0,6},{2,0},{4,2},{6,4},{1,7},{3,1},{5,3},{7,5},{8,14},{10,8},{12,... | collective-permute-start | bytes 172040 | tf_op jit(solution)/shard_map/ppermute | solution.py:16

commit v4 on v0

--- a/solution.py
+++ b/solution.py
@@ -101,7 +101,9 @@
         sent = part.astype(bf16)
         return part, sent, [shift(sent, "ex", s) for s in range(1, n_ex)]
 
-    def partial_out(part, others, kept_flops):
+    def partial_out(part, others, kept_flops, part_flops=0, *earlier):
+        if part_flops:
+            part = after(part, flops=part_flops)
         for other in others:
             part = part + other.astype(f32)
         hidden = (jax.nn.silu(part[:, :inner]) * part[:, inner:]).astype(bf16)
@@ -109,7 +111,7 @@
         kept = out.shape[0] // 2
         swapped = swap_half(out[kept:].astype(bf16)).astype(f32)
         if kept_flops:
-            out = after(out, flops=kept_flops)
+            out = after(after(out, *earlier) if earlier else out, flops=kept_flops)
         return out[:kept] + swapped
 
     held = copied(tokens)
@@ -120,19 +122,24 @@
     near_swapped = swap_half(after(near, *(line[1] for line in far)))
     near = jnp.concatenate([near, near_swapped], axis=0)
     near_part, near_sent, near_others = partial_sums(near)
-    far = [after(rows, near_sent) if i == n_tp - 1 else rows for line in far for i, rows in enumerate(line)]
-    far = jnp.concatenate(far, axis=0)
-    far_swapped = swap_half(far)
-    far = jnp.concatenate([after(far, flops=3450000000), far_swapped], axis=0)
+    early = jnp.concatenate([rows for line in far for rows in line[:-1]], axis=0)
+    early_swapped = swap_half(after(early, near_swapped))
+    late = jnp.concatenate([after(line[-1], near_sent) for line in far], axis=0)
+    late_swapped = swap_half(late)
+    far = jnp.concatenate([early, after(late, flops=3450000000), early_swapped, late_swapped], axis=0)
     far_part, far_sent, far_others = partial_sums(far)
-    near_out = partial_out(near_part, [after(other, far_sent) for other in near_others], 3450000000)
+    near_out = partial_out(near_part, [after(other, far_sent) for other in near_others], 3450000000, 3450000000)
     near_out = near_out.reshape(n_tp, count, width)
     near_sent = near_out[1:].astype(bf16)
     pieces = [near_out[0]] + [shift(near_sent[i], "tp", -t) for i, t in enumerate(places[1:])]
-    far_out = partial_out(far_part, [after(other, near_sent) for other in far_others], 0)
-    far_out = far_out.reshape(experts - 1, n_tp, count, width).astype(bf16)
+    far_out = partial_out(far_part, [after(other, near_sent) for other in far_others], 0, 0)
+    far_out = far_out.astype(bf16)
+    split = early.shape[0]
     for s in range(1, experts):
-        pieces += [shift_expert(far_out[experts - 1 - s, i], s, -t) for i, t in enumerate(places)]
+        line = experts - 1 - s
+        for i, t in enumerate(places):
+            start = (line * (n_tp - 1) + i) * count if i < n_tp - 1 else split + line * count
+            pieces.append(shift_expert(far_out[start : start + count], s, -t))
     return mix(expert_ids, gate_levels, pieces, n_tp, experts)
 
 

time: 39.3 us -> 41.8 us (1.064)
  waiting for transfers between devices: 8.51 us -> 11 us
  starting transfers between devices: 25.9 us -> 24.8 us
  local copies, waits for them, and re-layouts: 1.02 us -> 1.95 us
    ppermute x8, waiting for transfers between devices: 4.37 us -> 6.15 us  [shift_expert(): return lax.ppermute(value, ('grp', 'tp'), pairs)]
    ppermute x8, starting transfers between devices: 14.5 us -> 12.9 us  [shift(): lax.ppermute(value, axis, [(i, (i + by) % size) for i in range(size)])]
    unnamed x16 -> x21, local copies, waits for them, and re-layouts: 0.9 us -> 1.82 us
    ppermute x8, waiting for transfers between devices: 1.19 us -> 2.1 us  [shift(): lax.ppermute(value, axis, [(i, (i + by) % size) for i in range(size)])]
    ppermute x8, starting transfers between devices: 11.1 us -> 11.7 us  [shift_expert(): return lax.ppermute(value, ('grp', 'tp'), pairs)]
    ppermute x4 -> x5, waiting for transfers between devices: 2.95 us -> 2.71 us  [swap_half(): lax.ppermute(value, 'grp', [(i, i ^ 1) for i in range(lax.axis_size('grp'...]
  transfers between devices with their start and end apart: 20 -> 21, of which waited for: 9 -> 9; matrix products, arithmetic and copies ran while one was open for 6% -> 6% of each run, Pallas kernels for 0% -> 0%
where the time goes in v4:
time: 41.8 us; the launch traced here: 41.6 us
  starting transfers between devices  24.8 us (59%)
  waiting for transfers between devices  11 us (26%)
  matrix products  2.59 us (6%)
  local copies, waits for them, and re-layouts  1.95 us (5%)
  Pallas kernels  0.75 us (2%)
    ppermute x8, starting transfers between devices, shift(): lax.ppermute(value, axis, [(i, (i + by) % size) for i in range(size)])  12.9 us
    ppermute x8, starting transfers between devices, shift_expert(): return lax.ppermute(value, ('grp', 'tp'), pairs)  11.7 us
    ppermute x8, waiting for transfers between devices, shift_expert(): return lax.ppermute(value, ('grp', 'tp'), pairs)  6.15 us
    ppermute x5, waiting for transfers between devices, swap_half(): lax.ppermute(value, 'grp', [(i, i ^ 1) for i in range(lax.axis_size('grp'...  2.71 us
    ppermute x8, waiting for transfers between devices, shift(): lax.ppermute(value, axis, [(i, (i + by) % size) for i in range(size)])  2.1 us
    unnamed x21, local copies, waits for them, and re-layouts  1.82 us
    dot_general x4, matrix products, partial_sums(): jnp.dot(rows, w, preferred_element_type=f32)  1.76 us
  transfers between devices with their start and end apart: 21, of which 9 were waited for; matrix products, arithmetic and copies ran while one was open for 6% of the time, Pallas kernels for 0%

profile of v4, /device:TPU:0, one launch (start us, length us, event | category | flops | bytes accessed | tf_op | source)
XLA Modules:
  0.0 41.6 jit_solution(16280158836110435135)
XLA Ops:
  0.0 0.0 copy-start
  0.0 3.0 %collective-permute-start = (bf16[8,3584]{1,0:T(8,128)(2,1)}, bf16[8,3584]{1,0:T(8,128)(2,1)S(1)}, u32[]{:S(2)}, u32[]{:S(2)}) collective-permute-start(bf16[8,3584]{1,0:T(8,128)(2,1)} %from_ref.1), channel_id=1, source_target_pairs={{0,2},{2,4},{4,6},{6,0},{1,3},{3,5},{5,7},{7,1},{8,10},{10,12},{12... | collective-permute-start | bytes 172040 | tf_op jit(solution)/shard_map/ppermute | solution.py:16
  3.0 2.1 %collective-permute-start.2 = (bf16[8,3584]{1,0:T(8,128)(2,1)}, bf16[8,3584]{1,0:T(8,128)(2,1)S(1)}, u32[]{:S(2)}, u32[]{:S(2)}) collective-permute-start(bf16[8,3584]{1,0:T(8,128)(2,1)} %from_ref.1), channel_id=1, source_target_pairs={{0,6},{2,0},{4,2},{6,4},{1,7},{3,1},{5,3},{7,5},{8,14},{10,8},{12,... | collective-permute-start | bytes 172040 | tf_op jit(solution)/shard_map/ppermute | solution.py:16
  5.1 1.0 %collective-permute-start.1 = (bf16[8,3584]{1,0:T(8,128)(2,1)}, bf16[8,3584]{1,0:T(8,128)(2,1)S(1)}, u32[]{:S(2)}, u32[]{:S(2)}) collective-permute-start(bf16[8,3584]{1,0:T(8,128)(2,1)} %from_ref.1), channel_id=1, source_target_pairs={{0,4},{2,6},{4,0},{6,2},{1,5},{3,7},{5,1},{7,3},{8,12},{10,14},{12... | collective-permute-start | bytes 172040 | tf_op jit(solution)/shard_map/ppermute | solution.py:16
  6.1 0.0 copy-start.1
  6.1 0.9 %copy-done.1 = bf16[8,3584]{1,0:T(8,128)(2,1)S(1)} copy-done((bf16[8,3584]{1,0:T(8,128)(2,1)S(1)}, bf16[8,3584]{1,0:T(8,128)(2,1)}, u32[]{:S(2)}) %copy-start.1) | copy-done | bytes 57368
  6.9 0.0 copy-start.4
  6.9 1.5 %collective-permute-start.6 = (bf16[8,3584]{1,0:T(8,128)(2,1)S(1)}, bf16[8,3584]{1,0:T(8,128)(2,1)S(1)}, u32[]{:S(2)}, u32[]{:S(2)}) collective-permute-start(bf16[8,3584]{1,0:T(8,128)(2,1)S(1)} %shard_map.64), channel_id=1, source_target_pairs={{0,16},{2,18},{4,20},{6,22},{8,24},{10,26},{12,28},{14,30},{16,0},... | collective-permute-start | bytes 172040 | tf_op jit(solution)/shard_map/ppermute | solution.py:26
  8.4 0.0 collective-permute-done
  8.4 1.0 %collective-permute-start.3 = (bf16[8,3584]{1,0:T(8,128)(2,1)S(1)}, bf16[8,3584]{1,0:T(8,128)(2,1)S(1)}, u32[]{:S(2)}, u32[]{:S(2)}) collective-permute-start(bf16[8,3584]{1,0:T(8,128)(2,1)S(1)} %collective-permute-done), channel_id=1, source_target_pairs={{0,16},{2,18},{4,20},{6,22},{8,24},{10,26},{12,28},{14,30},{16,0},... | collective-permute-start | bytes 172040 | tf_op jit(solution)/shard_map/ppermute | solution.py:26
  9.4 0.0 collective-permute-done.2
  9.4 1.1 %collective-permute-start.8 = (bf16[8,3584]{1,0:T(8,128)(2,1)S(1)}, bf16[8,3584]{1,0:T(8,128)(2,1)S(1)}, u32[]{:S(2)}, u32[]{:S(2)}) collective-permute-start(bf16[8,3584]{1,0:T(8,128)(2,1)S(1)} %collective-permute-done.2), channel_id=1, source_target_pairs={{0,16},{2,18},{4,20},{6,22},{8,24},{10,26},{12,28},{14,30},{16,0},... | collective-permute-start | bytes 172040 | tf_op jit(solution)/shard_map/ppermute | solution.py:26
  10.5 0.4 collective-permute-done.1
  10.9 1.6 %collective-permute-start.7 = (bf16[8,3584]{1,0:T(8,128)(2,1)S(1)}, bf16[8,3584]{1,0:T(8,128)(2,1)S(1)}, u32[]{:S(2)}, u32[]{:S(2)}) collective-permute-start(bf16[8,3584]{1,0:T(8,128)(2,1)S(1)} %collective-permute-done.1), channel_id=1, source_target_pairs={{0,16},{2,18},{4,20},{6,22},{8,24},{10,26},{12,28},{14,30},{16,0},... | collective-permute-start | bytes 172040 | tf_op jit(solution)/shard_map/ppermute | solution.py:26
  12.5 0.0 collective-permute-done.6
  12.5 0.1 collective-permute-done.3.refs_1_
  12.7 0.0 collective-permute-start.4
  12.7 2.4 %collective-permute-done.7 = bf16[8,3584]{1,0:T(8,128)(2,1)S(1)} collective-permute-done((bf16[8,3584]{1,0:T(8,128)(2,1)S(1)}, bf16[8,3584]{1,0:T(8,128)(2,1)S(1)}, u32[]{:S(2)}, u32[]{:S(2)}) %collective-permute-start.7) | collective-permute-done | bytes 57376 | tf_op jit(solution)/shard_map/ppermute | solution.py:26
  15.1 0.0 copy-start.5
  15.1 0.0 collective-permute-done.4.refs_1_
  15.1 0.1 collective-permute-start.9
  15.2 0.0 copy-done.4
  15.3 0.4 %fusion.6 = f32[64,256]{1,0:T(8,128)S(1)} fusion(bf16[64,3584]{1,0:T(8,128)(2,1)S(1)} %constant_dynamic-update-slice_fusion, bf16[1,3584,256]{2,1,0:T(8,128)(2,1)S(1)} %copy-done.4), kind=kOutput, calls=%fused_computation.6 | convolution fusion | flops 117440512 | bytes 2359296 | tf_op jit(solution)/shard_map/dot_general | solution.py:99
  15.7 0.9 %copy-done.5 = bf16[1,3584,256]{2,1,0:T(8,128)(2,1)S(1)} copy-done((bf16[1,3584,256]{2,1,0:T(8,128)(2,1)S(1)}, bf16[1,3584,256]{2,1,0:T(8,128)(2,1)}, u32[]{:S(2)}) %copy-start.5) | copy-done | bytes 1835032
  16.6 0.4 %fusion.10 = f32[64,256]{1,0:T(8,128)S(1)} fusion(bf16[64,3584]{1,0:T(8,128)(2,1)S(1)} %constant_dynamic-update-slice_fusion, bf16[1,3584,256]{2,1,0:T(8,128)(2,1)S(1)} %copy-done.5), kind=kOutput, calls=%fused_computation.10 | convolution fusion | flops 117440512 | bytes 2359296 | tf_op jit(solution)/shard_map/dot_general | solution.py:99
  17.1 1.7 %collective-permute-start.5 = (bf16[64,512]{1,0:T(8,128)(2,1)S(1)}, bf16[64,512]{1,0:T(8,128)(2,1)S(1)}, u32[]{:S(2)}, u32[]{:S(2)}) collective-permute-start(bf16[64,512]{1,0:T(8,128)(2,1)S(1)} %fusion.22.refs_1_), channel_id=1, source_target_pairs={{0,1},{1,0},{2,3},{3,2},{4,5},{5,4},{6,7},{7,6},{8,9},{9,8},{10,11... | collective-permute-start | bytes 196616 | tf_op jit(solution)/shard_map/ppermute | solution.py:16
  18.7 0.0 collective-permute-done.8.refs_0_
  18.7 0.0 collective-permute-start.10
  18.7 1.2 %collective-permute-done.10 = bf16[8,3584]{1,0:T(8,128)(2,1)S(1)} collective-permute-done((bf16[8,3584]{1,0:T(8,128)(2,1)S(1)}, bf16[8,3584]{1,0:T(8,128)(2,1)S(1)}, u32[]{:S(2)}, u32[]{:S(2)}) %collective-permute-start.10) | collective-permute-done | bytes 57376 | tf_op jit(solution)/shard_map/ppermute | solution.py:30
  20.0 0.0 collective-permute-done.9
  20.0 0.4 %fusion.4 = f32[64,256]{1,0:T(8,128)S(1)} fusion(bf16[64,3584]{1,0:T(8,128)(2,1)S(1)} %constant_dynamic-update-slice_fusion.5, bf16[1,3584,256]{2,1,0:T(8,128)(2,1)S(1)} %copy-done.4), kind=kOutput, calls=%fused_computation.4 | convolution fusion | flops 117440512 | bytes 2359296 | tf_op jit(solution)/shard_map/dot_general | solution.py:99
  20.5 0.4 %fusion.8 = f32[64,256]{1,0:T(8,128)S(1)} fusion(bf16[64,3584]{1,0:T(8,128)(2,1)S(1)} %constant_dynamic-update-slice_fusion.5, bf16[1,3584,256]{2,1,0:T(8,128)(2,1)S(1)} %copy-done.5), kind=kOutput, calls=%fused_computation.8 | convolution fusion | flops 117440512 | bytes 2359296 | tf_op jit(solution)/shard_map/dot_general | solution.py:99
  20.9 0.5 %collective-permute-start.15 = (bf16[64,512]{1,0:T(8,128)(2,1)S(1)}, bf16[64,512]{1,0:T(8,128)(2,1)S(1)}, u32[]{:S(2)}, u32[]{:S(2)}) collective-permute-start(bf16[64,512]{1,0:T(8,128)(2,1)S(1)} %fusion.13.refs_1_), channel_id=1, source_target_pairs={{0,1},{1,0},{2,3},{3,2},{4,5},{5,4},{6,7},{7,6},{8,9},{9,8},{10,11... | collective-permute-start | bytes 196616 | tf_op jit(solution)/shard_map/ppermute | solution.py:16
  21.4 0.0 collective-permute-done.5.refs_0_
  21.4 0.0 copy-done
  21.5 0.4 fusion.2.refs_0_
  21.9 0.1 collective-permute-start.11
  22.0 1.5 %collective-permute-done.11 = bf16[32,3584]{1,0:T(8,128)(2,1)S(1)} collective-permute-done((bf16[32,3584]{1,0:T(8,128)(2,1)S(1)}, bf16[32,3584]{1,0:T(8,128)(2,1)S(1)}, u32[]{:S(2)}, u32[]{:S(2)}) %collective-permute-start.11) | collective-permute-done | bytes 229408 | tf_op jit(solution)/shard_map/ppermute | solution.py:30
  23.5 1.7 %collective-permute-done.15.refs_0_ = bf16[64,512]{1,0:T(8,128)(2,1)S(1)} collective-permute-done((bf16[64,512]{1,0:T(8,128)(2,1)S(1)}, bf16[64,512]{1,0:T(8,128)(2,1)S(1)}, u32[]{:S(2)}, u32[]{:S(2)}) %collective-permute-start.15) | collective-permute-done | bytes 65568 | tf_op jit(solution)/shard_map/ppermute | solution.py:16
  25.3 0.4 fusion
  25.7 0.0 copy-start.2
  25.7 0.0 copy-start.3
  25.7 0.1 collective-permute-start.16
  25.8 1.2 %collective-permute-start.14 = (bf16[8,3584]{1,0:T(8,128)(2,1)S(1)}, bf16[8,3584]{1,0:T(8,128)(2,1)S(1)}, u32[]{:S(2)}, u32[]{:S(2)}) collective-permute-start(bf16[8,3584]{1,0:T(8,128)(2,1)S(1)} %get-tuple-element.11), channel_id=1, source_target_pairs={{0,2},{2,4},{4,6},{6,0},{1,3},{3,5},{5,7},{7,1},{8,10},{10,12},{12... | collective-permute-start | bytes 172040 | tf_op jit(solution)/shard_map/ppermute | solution.py:16
  27.1 1.7 %collective-permute-start.13 = (bf16[8,3584]{1,0:T(8,128)(2,1)S(1)}, bf16[8,3584]{1,0:T(8,128)(2,1)S(1)}, u32[]{:S(2)}, u32[]{:S(2)}) collective-permute-start(bf16[8,3584]{1,0:T(8,128)(2,1)S(1)} %get-tuple-element.12), channel_id=1, source_target_pairs={{0,4},{2,6},{4,0},{6,2},{1,5},{3,7},{5,1},{7,3},{8,12},{10,14},{12... | collective-permute-start | bytes 172040 | tf_op jit(solution)/shard_map/ppermute | solution.py:16
  28.7 1.8 %collective-permute-start.12 = (bf16[8,3584]{1,0:T(8,128)(2,1)S(1)}, bf16[8,3584]{1,0:T(8,128)(2,1)S(1)}, u32[]{:S(2)}, u32[]{:S(2)}) collective-permute-start(bf16[8,3584]{1,0:T(8,128)(2,1)S(1)} %get-tuple-element.13), channel_id=1, source_target_pairs={{0,6},{2,0},{4,2},{6,4},{1,7},{3,1},{5,3},{7,5},{8,14},{10,8},{12,... | collective-permute-start | bytes 172040 | tf_op jit(solution)/shard_map/ppermute | solution.py:16
  30.5 0.0 collective-permute-done.16
  30.6 1.2 %collective-permute-start.20 = (bf16[8,3584]{1,0:T(8,128)(2,1)S(1)}, bf16[8,3584]{1,0:T(8,128)(2,1)S(1)}, u32[]{:S(2)}, u32[]{:S(2)}) collective-permute-start(bf16[8,3584]{1,0:T(8,128)(2,1)S(1)} %get-tuple-element.7), channel_id=1, source_target_pairs={{0,18},{2,20},{4,22},{6,16},{8,26},{10,28},{12,30},{14,24},{16,2},... | collective-permute-start | bytes 172040 | tf_op jit(solution)/shard_map/ppermute | solution.py:26
  31.8 1.2 %collective-permute-start.19 = (bf16[8,3584]{1,0:T(8,128)(2,1)S(1)}, bf16[8,3584]{1,0:T(8,128)(2,1)S(1)}, u32[]{:S(2)}, u32[]{:S(2)}) collective-permute-start(bf16[8,3584]{1,0:T(8,128)(2,1)S(1)} %get-tuple-element.8), channel_id=1, source_target_pairs={{0,20},{2,22},{4,16},{6,18},{8,28},{10,30},{12,24},{14,26},{16,4},... | collective-permute-start | bytes 172040 | tf_op jit(solution)/shard_map/ppermute | solution.py:26
  33.0 0.0 collective-permute-done.14.refs_3_
  33.0 3.6 %collective-permute-start.18 = (bf16[8,3584]{1,0:T(8,128)(2,1)S(1)}, bf16[8,3584]{1,0:T(8,128)(2,1)S(1)}, u32[]{:S(2)}, u32[]{:S(2)}) collective-permute-start(bf16[8,3584]{1,0:T(8,128)(2,1)S(1)} %get-tuple-element.9), channel_id=1, source_target_pairs={{0,22},{2,16},{4,18},{6,20},{8,30},{10,24},{12,26},{14,28},{16,6},... | collective-permute-start | bytes 172040 | tf_op jit(solution)/shard_map/ppermute | solution.py:26
  36.6 0.0 collective-permute-done.13.refs_2_
  36.6 0.5 %collective-permute-start.17 = (bf16[8,3584]{1,0:T(8,128)(2,1)S(1)}, bf16[8,3584]{1,0:T(8,128)(2,1)S(1)}, u32[]{:S(2)}, u32[]{:S(2)}) collective-permute-start(bf16[8,3584]{1,0:T(8,128)(2,1)S(1)} %get-tuple-element.10), channel_id=1, source_target_pairs={{0,16},{2,18},{4,20},{6,22},{8,24},{10,26},{12,28},{14,30},{16,0},... | collective-permute-start | bytes 172040 | tf_op jit(solution)/shard_map/ppermute | solution.py:26
  37.2 0.0 collective-permute-done.12.refs_1_
  37.2 0.9 %collective-permute-done.20.refs_7_ = bf16[8,3584]{1,0:T(8,128)(2,1)S(1)} collective-permute-done((bf16[8,3584]{1,0:T(8,128)(2,1)S(1)}, bf16[8,3584]{1,0:T(8,128)(2,1)S(1)}, u32[]{:S(2)}, u32[]{:S(2)}) %collective-permute-start.20) | collective-permute-done | bytes 57376 | tf_op jit(solution)/shard_map/ppermute | solution.py:26
  38.1 1.7 %collective-permute-done.19.refs_6_ = bf16[8,3584]{1,0:T(8,128)(2,1)S(1)} collective-permute-done((bf16[8,3584]{1,0:T(8,128)(2,1)S(1)}, bf16[8,3584]{1,0:T(8,128)(2,1)S(1)}, u32[]{:S(2)}, u32[]{:S(2)}) %collective-permute-start.19) | collective-permute-done | bytes 57376 | tf_op jit(solution)/shard_map/ppermute | solution.py:26
  39.7 0.0 collective-permute-done.18.refs_5_
  39.7 1.1 %collective-permute-done.17.refs_4_ = bf16[8,3584]{1,0:T(8,128)(2,1)S(1)} collective-permute-done((bf16[8,3584]{1,0:T(8,128)(2,1)S(1)}, bf16[8,3584]{1,0:T(8,128)(2,1)S(1)}, u32[]{:S(2)}, u32[]{:S(2)}) %collective-permute-start.17) | collective-permute-done | bytes 57376 | tf_op jit(solution)/shard_map/ppermute | solution.py:26
  40.8 0.0 copy-done.2
  40.8 0.0 copy-done.3
  40.8 0.7 %shard_map.73 = bf16[8,3584]{1,0:T(8,128)(2,1)} custom-call(s32[1,8]{1,0:T(1,128)S(1)} %bitcast.23, s32[1,8]{1,0:T(1,128)S(1)} %bitcast.24, f32[8,3584]{1,0:T(8,128)S(1)} %slice.83.refs_0_, bf16[8,3584]{1,0:T(8,128)(2,1)S(1)} %collective-permute-done.12.refs_1_, bf16[8,3584]{1,0:T(8,128)(2,1)S(1)} %collective-permute-done.13.refs_2_, ...), custom_call_target="tpu_custom_call" | custom-call | tf_op jit(solution)/shard_map/pallas_call | solution.py:83
  (35 shorter events, 0.4 us)
Async XLA Ops:
  0.0 21.4 %copy-start = (bf16[1,256,3584]{2,1,0:T(8,128)(2,1)S(1)}, bf16[1,256,3584]{2,1,0:T(8,128)(2,1)}, u32[]{:S(2)}) copy-start(bf16[1,256,3584]{2,1,0:T(8,128)(2,1)} %param.11) | copy-start | bytes 5505028
  0.0 8.4 %collective-permute-start = (bf16[8,3584]{1,0:T(8,128)(2,1)}, bf16[8,3584]{1,0:T(8,128)(2,1)S(1)}, u32[]{:S(2)}, u32[]{:S(2)}) collective-permute-start(bf16[8,3584]{1,0:T(8,128)(2,1)} %from_ref.1), channel_id=1, source_target_pairs={{0,2},{2,4},{4,6},{6,0},{1,3},{3,5},{5,7},{7,1},{8,10},{10,12},{12... | collective-permute-start | bytes 172040 | tf_op jit(solution)/shard_map/ppermute | solution.py:16
  3.0 6.4 %collective-permute-start.2 = (bf16[8,3584]{1,0:T(8,128)(2,1)}, bf16[8,3584]{1,0:T(8,128)(2,1)S(1)}, u32[]{:S(2)}, u32[]{:S(2)}) collective-permute-start(bf16[8,3584]{1,0:T(8,128)(2,1)} %from_ref.1), channel_id=1, source_target_pairs={{0,6},{2,0},{4,2},{6,4},{1,7},{3,1},{5,3},{7,5},{8,14},{10,8},{12,... | collective-permute-start | bytes 172040 | tf_op jit(solution)/shard_map/ppermute | solution.py:16
  5.1 5.8 %collective-permute-start.1 = (bf16[8,3584]{1,0:T(8,128)(2,1)}, bf16[8,3584]{1,0:T(8,128)(2,1)S(1)}, u32[]{:S(2)}, u32[]{:S(2)}) collective-permute-start(bf16[8,3584]{1,0:T(8,128)(2,1)} %from_ref.1), channel_id=1, source_target_pairs={{0,4},{2,6},{4,0},{6,2},{1,5},{3,7},{5,1},{7,3},{8,12},{10,14},{12... | collective-permute-start | bytes 172040 | tf_op jit(solution)/shard_map/ppermute | solution.py:16
  6.1 0.9 %copy-start.1 = (bf16[8,3584]{1,0:T(8,128)(2,1)S(1)}, bf16[8,3584]{1,0:T(8,128)(2,1)}, u32[]{:S(2)}) copy-start(bf16[8,3584]{1,0:T(8,128)(2,1)} %from_ref.1) | copy-start | bytes 172036
  6.9 8.3 %copy-start.4 = (bf16[1,3584,256]{2,1,0:T(8,128)(2,1)S(1)}, bf16[1,3584,256]{2,1,0:T(8,128)(2,1)}, u32[]{:S(2)}) copy-start(bf16[1,3584,256]{2,1,0:T(8,128)(2,1)} %param.10) | copy-start | bytes 5505028
  6.9 5.6 %collective-permute-start.6 = (bf16[8,3584]{1,0:T(8,128)(2,1)S(1)}, bf16[8,3584]{1,0:T(8,128)(2,1)S(1)}, u32[]{:S(2)}, u32[]{:S(2)}) collective-permute-start(bf16[8,3584]{1,0:T(8,128)(2,1)S(1)} %shard_map.64), channel_id=1, source_target_pairs={{0,16},{2,18},{4,20},{6,22},{8,24},{10,26},{12,28},{14,30},{16,0},... | collective-permute-start | bytes 172040 | tf_op jit(solution)/shard_map/ppermute | solution.py:26
  8.4 4.2 %collective-permute-start.3 = (bf16[8,3584]{1,0:T(8,128)(2,1)S(1)}, bf16[8,3584]{1,0:T(8,128)(2,1)S(1)}, u32[]{:S(2)}, u32[]{:S(2)}) collective-permute-start(bf16[8,3584]{1,0:T(8,128)(2,1)S(1)} %collective-permute-done), channel_id=1, source_target_pairs={{0,16},{2,18},{4,20},{6,22},{8,24},{10,26},{12,28},{14,30},{16,0},... | collective-permute-start | bytes 172040 | tf_op jit(solution)/shard_map/ppermute | solution.py:26
  9.4 9.3 %collective-permute-start.8 = (bf16[8,3584]{1,0:T(8,128)(2,1)S(1)}, bf16[8,3584]{1,0:T(8,128)(2,1)S(1)}, u32[]{:S(2)}, u32[]{:S(2)}) collective-permute-start(bf16[8,3584]{1,0:T(8,128)(2,1)S(1)} %collective-permute-done.2), channel_id=1, source_target_pairs={{0,16},{2,18},{4,20},{6,22},{8,24},{10,26},{12,28},{14,30},{16,0},... | collective-permute-start | bytes 172040 | tf_op jit(solution)/shard_map/ppermute | solution.py:26
  10.9 4.2 %collective-permute-start.7 = (bf16[8,3584]{1,0:T(8,128)(2,1)S(1)}, bf16[8,3584]{1,0:T(8,128)(2,1)S(1)}, u32[]{:S(2)}, u32[]{:S(2)}) collective-permute-start(bf16[8,3584]{1,0:T(8,128)(2,1)S(1)} %collective-permute-done.1), channel_id=1, source_target_pairs={{0,16},{2,18},{4,20},{6,22},{8,24},{10,26},{12,28},{14,30},{16,0},... | collective-permute-start | bytes 172040 | tf_op jit(solution)/shard_map/ppermute | solution.py:26
  12.7 2.4 %collective-permute-start.4 = (bf16[32,3584]{1,0:T(8,128)(2,1)S(1)}, bf16[32,3584]{1,0:T(8,128)(2,1)S(1)}, u32[]{:S(2)}, u32[]{:S(2)}) collective-permute-start(bf16[32,3584]{1,0:T(8,128)(2,1)S(1)} %shard_map.65), channel_id=1, source_target_pairs={{0,8},{8,0},{16,24},{24,16},{1,9},{9,1},{17,25},{25,17},{2,10},{10... | collective-permute-start | bytes 688136 | tf_op jit(solution)/shard_map/ppermute | solution.py:30
  15.1 1.5 %copy-start.5 = (bf16[1,3584,256]{2,1,0:T(8,128)(2,1)S(1)}, bf16[1,3584,256]{2,1,0:T(8,128)(2,1)}, u32[]{:S(2)}) copy-start(bf16[1,3584,256]{2,1,0:T(8,128)(2,1)} %param.9) | copy-start | bytes 5505028
  15.1 4.8 %collective-permute-start.9 = (bf16[24,3584]{1,0:T(8,128)(2,1)S(1)}, bf16[24,3584]{1,0:T(8,128)(2,1)S(1)}, u32[]{:S(2)}, u32[]{:S(2)}) collective-permute-start(bf16[24,3584]{1,0:T(8,128)(2,1)S(1)} %shard_map.69), channel_id=1, source_target_pairs={{0,8},{8,0},{16,24},{24,16},{1,9},{9,1},{17,25},{25,17},{2,10},{10... | collective-permute-start | bytes 516104 | tf_op jit(solution)/shard_map/ppermute | solution.py:30
  17.1 4.4 %collective-permute-start.5 = (bf16[64,512]{1,0:T(8,128)(2,1)S(1)}, bf16[64,512]{1,0:T(8,128)(2,1)S(1)}, u32[]{:S(2)}, u32[]{:S(2)}) collective-permute-start(bf16[64,512]{1,0:T(8,128)(2,1)S(1)} %fusion.22.refs_1_), channel_id=1, source_target_pairs={{0,1},{1,0},{2,3},{3,2},{4,5},{5,4},{6,7},{7,6},{8,9},{9,8},{10,11... | collective-permute-start | bytes 196616 | tf_op jit(solution)/shard_map/ppermute | solution.py:16
  18.7 1.2 %collective-permute-start.10 = (bf16[8,3584]{1,0:T(8,128)(2,1)S(1)}, bf16[8,3584]{1,0:T(8,128)(2,1)S(1)}, u32[]{:S(2)}, u32[]{:S(2)}) collective-permute-start(bf16[8,3584]{1,0:T(8,128)(2,1)S(1)} %shard_map.67.refs_0_), channel_id=1, source_target_pairs={{0,8},{8,0},{16,24},{24,16},{1,9},{9,1},{17,25},{25,17},{2,10},{10... | collective-permute-start | bytes 172040 | tf_op jit(solution)/shard_map/ppermute | solution.py:30
  20.9 4.3 %collective-permute-start.15 = (bf16[64,512]{1,0:T(8,128)(2,1)S(1)}, bf16[64,512]{1,0:T(8,128)(2,1)S(1)}, u32[]{:S(2)}, u32[]{:S(2)}) collective-permute-start(bf16[64,512]{1,0:T(8,128)(2,1)S(1)} %fusion.13.refs_1_), channel_id=1, source_target_pairs={{0,1},{1,0},{2,3},{3,2},{4,5},{5,4},{6,7},{7,6},{8,9},{9,8},{10,11... | collective-permute-start | bytes 196616 | tf_op jit(solution)/shard_map/ppermute | solution.py:16
  21.9 1.6 %collective-permute-start.11 = (bf16[32,3584]{1,0:T(8,128)(2,1)S(1)}, bf16[32,3584]{1,0:T(8,128)(2,1)S(1)}, u32[]{:S(2)}, u32[]{:S(2)}) collective-permute-start(bf16[32,3584]{1,0:T(8,128)(2,1)S(1)} %slice.116), channel_id=1, source_target_pairs={{0,8},{8,0},{16,24},{24,16},{1,9},{9,1},{17,25},{25,17},{2,10},{10... | collective-permute-start | bytes 688136 | tf_op jit(solution)/shard_map/ppermute | solution.py:30
  25.7 15.1 %copy-start.2 = (s32[8,1]{0,1:T(1,128)S(1)}, s32[8,1]{0,1:T(1,128)}, u32[]{:S(2)}) copy-start(s32[8,1]{0,1:T(1,128)} %param.7) | copy-start | bytes 100
  25.7 15.1 %copy-start.3 = (s32[8,1]{0,1:T(1,128)S(1)}, s32[8,1]{0,1:T(1,128)}, u32[]{:S(2)}) copy-start(s32[8,1]{0,1:T(1,128)} %param.8) | copy-start | bytes 100
  25.7 4.8 %collective-permute-start.16 = (bf16[32,3584]{1,0:T(8,128)(2,1)S(1)}, bf16[32,3584]{1,0:T(8,128)(2,1)S(1)}, u32[]{:S(2)}, u32[]{:S(2)}) collective-permute-start(bf16[32,3584]{1,0:T(8,128)(2,1)S(1)} %slice.115), channel_id=1, source_target_pairs={{0,8},{8,0},{16,24},{24,16},{1,9},{9,1},{17,25},{25,17},{2,10},{10... | collective-permute-start | bytes 688136 | tf_op jit(solution)/shard_map/ppermute | solution.py:30
  25.8 7.2 %collective-permute-start.14 = (bf16[8,3584]{1,0:T(8,128)(2,1)S(1)}, bf16[8,3584]{1,0:T(8,128)(2,1)S(1)}, u32[]{:S(2)}, u32[]{:S(2)}) collective-permute-start(bf16[8,3584]{1,0:T(8,128)(2,1)S(1)} %get-tuple-element.11), channel_id=1, source_target_pairs={{0,2},{2,4},{4,6},{6,0},{1,3},{3,5},{5,7},{7,1},{8,10},{10,12},{12... | collective-permute-start | bytes 172040 | tf_op jit(solution)/shard_map/ppermute | solution.py:16
  27.1 9.6 %collective-permute-start.13 = (bf16[8,3584]{1,0:T(8,128)(2,1)S(1)}, bf16[8,3584]{1,0:T(8,128)(2,1)S(1)}, u32[]{:S(2)}, u32[]{:S(2)}) collective-permute-start(bf16[8,3584]{1,0:T(8,128)(2,1)S(1)} %get-tuple-element.12), channel_id=1, source_target_pairs={{0,4},{2,6},{4,0},{6,2},{1,5},{3,7},{5,1},{7,3},{8,12},{10,14},{12... | collective-permute-start | bytes 172040 | tf_op jit(solution)/shard_map/ppermute | solution.py:16
  28.7 8.5 %collective-permute-start.12 = (bf16[8,3584]{1,0:T(8,128)(2,1)S(1)}, bf16[8,3584]{1,0:T(8,128)(2,1)S(1)}, u32[]{:S(2)}, u32[]{:S(2)}) collective-permute-start(bf16[8,3584]{1,0:T(8,128)(2,1)S(1)} %get-tuple-element.13), channel_id=1, source_target_pairs={{0,6},{2,0},{4,2},{6,4},{1,7},{3,1},{5,3},{7,5},{8,14},{10,8},{12,... | collective-permute-start | bytes 172040 | tf_op jit(solution)/shard_map/ppermute | solution.py:16
  30.6 7.5 %collective-permute-start.20 = (bf16[8,3584]{1,0:T(8,128)(2,1)S(1)}, bf16[8,3584]{1,0:T(8,128)(2,1)S(1)}, u32[]{:S(2)}, u32[]{:S(2)}) collective-permute-start(bf16[8,3584]{1,0:T(8,128)(2,1)S(1)} %get-tuple-element.7), channel_id=1, source_target_pairs={{0,18},{2,20},{4,22},{6,16},{8,26},{10,28},{12,30},{14,24},{16,2},... | collective-permute-start | bytes 172040 | tf_op jit(solution)/shard_map/ppermute | solution.py:26
  31.8 7.9 %collective-permute-start.19 = (bf16[8,3584]{1,0:T(8,128)(2,1)S(1)}, bf16[8,3584]{1,0:T(8,128)(2,1)S(1)}, u32[]{:S(2)}, u32[]{:S(2)}) collective-permute-start(bf16[8,3584]{1,0:T(8,128)(2,1)S(1)} %get-tuple-element.8), channel_id=1, source_target_pairs={{0,20},{2,22},{4,16},{6,18},{8,28},{10,30},{12,24},{14,26},{16,4},... | collective-permute-start | bytes 172040 | tf_op jit(solution)/shard_map/ppermute | solution.py:26
  33.0 6.7 %collective-permute-start.18 = (bf16[8,3584]{1,0:T(8,128)(2,1)S(1)}, bf16[8,3584]{1,0:T(8,128)(2,1)S(1)}, u32[]{:S(2)}, u32[]{:S(2)}) collective-permute-start(bf16[8,3584]{1,0:T(8,128)(2,1)S(1)} %get-tuple-element.9), channel_id=1, source_target_pairs={{0,22},{2,16},{4,18},{6,20},{8,30},{10,24},{12,26},{14,28},{16,6},... | collective-permute-start | bytes 172040 | tf_op jit(solution)/shard_map/ppermute | solution.py:26
  36.6 4.2 %collective-permute-start.17 = (bf16[8,3584]{1,0:T(8,128)(2,1)S(1)}, bf16[8,3584]{1,0:T(8,128)(2,1)S(1)}, u32[]{:S(2)}, u32[]{:S(2)}) collective-permute-start(bf16[8,3584]{1,0:T(8,128)(2,1)S(1)} %get-tuple-element.10), channel_id=1, source_target_pairs={{0,16},{2,18},{4,20},{6,22},{8,24},{10,26},{12,28},{14,30},{16,0},... | collective-permute-start | bytes 172040 | tf_op jit(solution)/shard_map/ppermute | solution.py:26

commit v5 on v4

--- a/solution.py
+++ b/solution.py
@@ -122,9 +122,10 @@
     near_swapped = swap_half(after(near, *(line[1] for line in far)))
     near = jnp.concatenate([near, near_swapped], axis=0)
     near_part, near_sent, near_others = partial_sums(near)
-    early = jnp.concatenate([rows for line in far for rows in line[:-1]], axis=0)
+    last = n_tp - 2
+    early = jnp.concatenate([rows for line in far for i, rows in enumerate(line) if i != last], axis=0)
     early_swapped = swap_half(after(early, near_swapped))
-    late = jnp.concatenate([after(line[-1], near_sent) for line in far], axis=0)
+    late = jnp.concatenate([after(line[last], near_sent) for line in far], axis=0)
     late_swapped = swap_half(late)
     far = jnp.concatenate([early, after(late, flops=3450000000), early_swapped, late_swapped], axis=0)
     far_part, far_sent, far_others = partial_sums(far)
@@ -138,7 +139,7 @@
     for s in range(1, experts):
         line = experts - 1 - s
         for i, t in enumerate(places):
-            start = (line * (n_tp - 1) + i) * count if i < n_tp - 1 else split + line * count
+            start = split + line * count if i == last else (line * (n_tp - 1) + i - (i > last)) * count
             pieces.append(shift_expert(far_out[start : start + count], s, -t))
     return mix(expert_ids, gate_levels, pieces, n_tp, experts)
 

time: 41.8 us -> 40.7 us (0.974)
  waiting for transfers between devices: 11 us -> 9.86 us
    ppermute x8, waiting for transfers between devices: 6.15 us -> 5.22 us  [shift_expert(): return lax.ppermute(value, ('grp', 'tp'), pairs)]
where the time goes in v5:
time: 40.7 us; the launch traced here: 40.5 us
  starting transfers between devices  24.8 us (61%)
  waiting for transfers between devices  9.86 us (24%)
  matrix products  2.6 us (6%)
  local copies, waits for them, and re-layouts  1.95 us (5%)
  Pallas kernels  0.75 us (2%)
    ppermute x8, starting transfers between devices, shift(): lax.ppermute(value, axis, [(i, (i + by) % size) for i in range(size)])  12.8 us
    ppermute x8, starting transfers between devices, shift_expert(): return lax.ppermute(value, ('grp', 'tp'), pairs)  11.8 us
    ppermute x8, waiting for transfers between devices, shift_expert(): return lax.ppermute(value, ('grp', 'tp'), pairs)  5.22 us
    ppermute x5, waiting for transfers between devices, swap_half(): lax.ppermute(value, 'grp', [(i, i ^ 1) for i in range(lax.axis_size('grp'...  2.71 us
    ppermute x8, waiting for transfers between devices, shift(): lax.ppermute(value, axis, [(i, (i + by) % size) for i in range(size)])  1.93 us
    unnamed x21, local copies, waits for them, and re-layouts  1.82 us
    dot_general x4, matrix products, partial_sums(): jnp.dot(rows, w, preferred_element_type=f32)  1.77 us
    dot_general x2, matrix products, partial_out(): out = jnp.dot(hidden, w_down, preferred_element_type=f32)  0.83 us
  transfers between devices with their start and end apart: 21, of which 9 were waited for; matrix products, arithmetic and copies ran while one was open for 6% of the time, Pallas kernels for 0%

profile of v5, /device:TPU:0, one launch (start us, length us, event | category | flops | bytes accessed | tf_op | source)
XLA Modules:
  0.0 40.5 jit_solution(10735587330986385066)
XLA Ops:
  0.0 0.0 copy-start
  0.0 3.0 %collective-permute-start = (bf16[8,3584]{1,0:T(8,128)(2,1)}, bf16[8,3584]{1,0:T(8,128)(2,1)S(1)}, u32[]{:S(2)}, u32[]{:S(2)}) collective-permute-start(bf16[8,3584]{1,0:T(8,128)(2,1)} %from_ref.1), channel_id=1, source_target_pairs={{0,2},{2,4},{4,6},{6,0},{1,3},{3,5},{5,7},{7,1},{8,10},{10,12},{12... | collective-permute-start | bytes 172040 | tf_op jit(solution)/shard_map/ppermute | solution.py:16
  3.0 2.1 %collective-permute-start.2 = (bf16[8,3584]{1,0:T(8,128)(2,1)}, bf16[8,3584]{1,0:T(8,128)(2,1)S(1)}, u32[]{:S(2)}, u32[]{:S(2)}) collective-permute-start(bf16[8,3584]{1,0:T(8,128)(2,1)} %from_ref.1), channel_id=1, source_target_pairs={{0,6},{2,0},{4,2},{6,4},{1,7},{3,1},{5,3},{7,5},{8,14},{10,8},{12,... | collective-permute-start | bytes 172040 | tf_op jit(solution)/shard_map/ppermute | solution.py:16
  5.1 1.0 %collective-permute-start.1 = (bf16[8,3584]{1,0:T(8,128)(2,1)}, bf16[8,3584]{1,0:T(8,128)(2,1)S(1)}, u32[]{:S(2)}, u32[]{:S(2)}) collective-permute-start(bf16[8,3584]{1,0:T(8,128)(2,1)} %from_ref.1), channel_id=1, source_target_pairs={{0,4},{2,6},{4,0},{6,2},{1,5},{3,7},{5,1},{7,3},{8,12},{10,14},{12... | collective-permute-start | bytes 172040 | tf_op jit(solution)/shard_map/ppermute | solution.py:16
  6.1 0.0 copy-start.1
  6.1 0.9 %copy-done.1 = bf16[8,3584]{1,0:T(8,128)(2,1)S(1)} copy-done((bf16[8,3584]{1,0:T(8,128)(2,1)S(1)}, bf16[8,3584]{1,0:T(8,128)(2,1)}, u32[]{:S(2)}) %copy-start.1) | copy-done | bytes 57368
  6.9 0.0 copy-start.4
  6.9 1.5 %collective-permute-start.6 = (bf16[8,3584]{1,0:T(8,128)(2,1)S(1)}, bf16[8,3584]{1,0:T(8,128)(2,1)S(1)}, u32[]{:S(2)}, u32[]{:S(2)}) collective-permute-start(bf16[8,3584]{1,0:T(8,128)(2,1)S(1)} %shard_map.64), channel_id=1, source_target_pairs={{0,16},{2,18},{4,20},{6,22},{8,24},{10,26},{12,28},{14,30},{16,0},... | collective-permute-start | bytes 172040 | tf_op jit(solution)/shard_map/ppermute | solution.py:26
  8.4 0.0 collective-permute-done
  8.4 1.0 %collective-permute-start.3 = (bf16[8,3584]{1,0:T(8,128)(2,1)S(1)}, bf16[8,3584]{1,0:T(8,128)(2,1)S(1)}, u32[]{:S(2)}, u32[]{:S(2)}) collective-permute-start(bf16[8,3584]{1,0:T(8,128)(2,1)S(1)} %collective-permute-done), channel_id=1, source_target_pairs={{0,16},{2,18},{4,20},{6,22},{8,24},{10,26},{12,28},{14,30},{16,0},... | collective-permute-start | bytes 172040 | tf_op jit(solution)/shard_map/ppermute | solution.py:26
  9.4 0.0 collective-permute-done.2
  9.4 1.1 %collective-permute-start.7 = (bf16[8,3584]{1,0:T(8,128)(2,1)S(1)}, bf16[8,3584]{1,0:T(8,128)(2,1)S(1)}, u32[]{:S(2)}, u32[]{:S(2)}) collective-permute-start(bf16[8,3584]{1,0:T(8,128)(2,1)S(1)} %collective-permute-done.2), channel_id=1, source_target_pairs={{0,16},{2,18},{4,20},{6,22},{8,24},{10,26},{12,28},{14,30},{16,0},... | collective-permute-start | bytes 172040 | tf_op jit(solution)/shard_map/ppermute | solution.py:26
  10.5 0.4 collective-permute-done.1
  10.9 1.6 %collective-permute-start.8 = (bf16[8,3584]{1,0:T(8,128)(2,1)S(1)}, bf16[8,3584]{1,0:T(8,128)(2,1)S(1)}, u32[]{:S(2)}, u32[]{:S(2)}) collective-permute-start(bf16[8,3584]{1,0:T(8,128)(2,1)S(1)} %collective-permute-done.1), channel_id=1, source_target_pairs={{0,16},{2,18},{4,20},{6,22},{8,24},{10,26},{12,28},{14,30},{16,0},... | collective-permute-start | bytes 172040 | tf_op jit(solution)/shard_map/ppermute | solution.py:26
  12.5 0.0 collective-permute-done.6
  12.5 0.1 collective-permute-done.3.refs_1_
  12.7 0.0 collective-permute-start.4
  12.7 1.5 %collective-permute-done.7 = bf16[8,3584]{1,0:T(8,128)(2,1)S(1)} collective-permute-done((bf16[8,3584]{1,0:T(8,128)(2,1)S(1)}, bf16[8,3584]{1,0:T(8,128)(2,1)S(1)}, u32[]{:S(2)}, u32[]{:S(2)}) %collective-permute-start.7) | collective-permute-done | bytes 57376 | tf_op jit(solution)/shard_map/ppermute | solution.py:26
  14.2 0.0 copy-start.5
  14.3 0.0 collective-permute-done.4.refs_1_
  14.3 0.1 collective-permute-start.9
  14.4 0.0 copy-done.4
  14.4 0.4 %fusion.6 = f32[64,256]{1,0:T(8,128)S(1)} fusion(bf16[64,3584]{1,0:T(8,128)(2,1)S(1)} %constant_dynamic-update-slice_fusion, bf16[1,3584,256]{2,1,0:T(8,128)(2,1)S(1)} %copy-done.4), kind=kOutput, calls=%fused_computation.6 | convolution fusion | flops 117440512 | bytes 2359296 | tf_op jit(solution)/shard_map/dot_general | solution.py:99
  14.8 0.9 %copy-done.5 = bf16[1,3584,256]{2,1,0:T(8,128)(2,1)S(1)} copy-done((bf16[1,3584,256]{2,1,0:T(8,128)(2,1)S(1)}, bf16[1,3584,256]{2,1,0:T(8,128)(2,1)}, u32[]{:S(2)}) %copy-start.5) | copy-done | bytes 1835032
  15.7 0.4 %fusion.10 = f32[64,256]{1,0:T(8,128)S(1)} fusion(bf16[64,3584]{1,0:T(8,128)(2,1)S(1)} %constant_dynamic-update-slice_fusion, bf16[1,3584,256]{2,1,0:T(8,128)(2,1)S(1)} %copy-done.5), kind=kOutput, calls=%fused_computation.10 | convolution fusion | flops 117440512 | bytes 2359296 | tf_op jit(solution)/shard_map/dot_general | solution.py:99
  16.2 1.5 %collective-permute-start.5 = (bf16[64,512]{1,0:T(8,128)(2,1)S(1)}, bf16[64,512]{1,0:T(8,128)(2,1)S(1)}, u32[]{:S(2)}, u32[]{:S(2)}) collective-permute-start(bf16[64,512]{1,0:T(8,128)(2,1)S(1)} %fusion.22.refs_1_), channel_id=1, source_target_pairs={{0,1},{1,0},{2,3},{3,2},{4,5},{5,4},{6,7},{7,6},{8,9},{9,8},{10,11... | collective-permute-start | bytes 196616 | tf_op jit(solution)/shard_map/ppermute | solution.py:16
  17.7 0.0 collective-permute-done.8.refs_0_
  17.7 0.0 collective-permute-start.10
  17.7 1.2 %collective-permute-done.10 = bf16[8,3584]{1,0:T(8,128)(2,1)S(1)} collective-permute-done((bf16[8,3584]{1,0:T(8,128)(2,1)S(1)}, bf16[8,3584]{1,0:T(8,128)(2,1)S(1)}, u32[]{:S(2)}, u32[]{:S(2)}) %collective-permute-start.10) | collective-permute-done | bytes 57376 | tf_op jit(solution)/shard_map/ppermute | solution.py:30
  19.0 0.0 collective-permute-done.9
  19.0 0.4 %fusion.4 = f32[64,256]{1,0:T(8,128)S(1)} fusion(bf16[64,3584]{1,0:T(8,128)(2,1)S(1)} %constant_dynamic-update-slice_fusion.5, bf16[1,3584,256]{2,1,0:T(8,128)(2,1)S(1)} %copy-done.4), kind=kOutput, calls=%fused_computation.4 | convolution fusion | flops 117440512 | bytes 2359296 | tf_op jit(solution)/shard_map/dot_general | solution.py:99
  19.4 0.4 %fusion.8 = f32[64,256]{1,0:T(8,128)S(1)} fusion(bf16[64,3584]{1,0:T(8,128)(2,1)S(1)} %constant_dynamic-update-slice_fusion.5, bf16[1,3584,256]{2,1,0:T(8,128)(2,1)S(1)} %copy-done.5), kind=kOutput, calls=%fused_computation.8 | convolution fusion | flops 117440512 | bytes 2359296 | tf_op jit(solution)/shard_map/dot_general | solution.py:99
  19.9 0.7 %collective-permute-start.15 = (bf16[64,512]{1,0:T(8,128)(2,1)S(1)}, bf16[64,512]{1,0:T(8,128)(2,1)S(1)}, u32[]{:S(2)}, u32[]{:S(2)}) collective-permute-start(bf16[64,512]{1,0:T(8,128)(2,1)S(1)} %fusion.13.refs_1_), channel_id=1, source_target_pairs={{0,1},{1,0},{2,3},{3,2},{4,5},{5,4},{6,7},{7,6},{8,9},{9,8},{10,11... | collective-permute-start | bytes 196616 | tf_op jit(solution)/shard_map/ppermute | solution.py:16
  20.6 0.0 collective-permute-done.5.refs_0_
  20.6 0.0 copy-done
  20.6 0.4 %fusion.2.refs_0_ = f32[64,3584]{1,0:T(8,128)S(1)} fusion(bf16[1,256,3584]{2,1,0:T(8,128)(2,1)S(1)} %copy-done, f32[64,512]{1,0:T(8,128)S(1)} %convert_add_fusion.1), kind=kOutput, calls=%fused_computation.2 | convolution fusion | flops 117538816 | bytes 2883584 | tf_op jit(solution)/shard_map/dot_general | solution.py:110
  21.1 0.1 collective-permute-start.11
  21.1 1.5 %collective-permute-done.11 = bf16[32,3584]{1,0:T(8,128)(2,1)S(1)} collective-permute-done((bf16[32,3584]{1,0:T(8,128)(2,1)S(1)}, bf16[32,3584]{1,0:T(8,128)(2,1)S(1)}, u32[]{:S(2)}, u32[]{:S(2)}) %collective-permute-start.11) | collective-permute-done | bytes 229408 | tf_op jit(solution)/shard_map/ppermute | solution.py:30
  22.7 1.6 %collective-permute-done.15.refs_0_ = bf16[64,512]{1,0:T(8,128)(2,1)S(1)} collective-permute-done((bf16[64,512]{1,0:T(8,128)(2,1)S(1)}, bf16[64,512]{1,0:T(8,128)(2,1)S(1)}, u32[]{:S(2)}, u32[]{:S(2)}) %collective-permute-start.15) | collective-permute-done | bytes 65568 | tf_op jit(solution)/shard_map/ppermute | solution.py:16
  24.3 0.4 %fusion = f32[64,3584]{1,0:T(8,128)S(1)} fusion(bf16[1,256,3584]{2,1,0:T(8,128)(2,1)S(1)} %copy-done, f32[64,512]{1,0:T(8,128)S(1)} %convert_add_fusion), kind=kOutput, calls=%fused_computation | convolution fusion | flops 117538816 | bytes 2883584 | tf_op jit(solution)/shard_map/dot_general | solution.py:110
  24.7 0.0 copy-start.2
  24.7 0.0 copy-start.3
  24.7 0.1 collective-permute-start.16
  24.8 1.0 %collective-permute-start.14 = (bf16[8,3584]{1,0:T(8,128)(2,1)S(1)}, bf16[8,3584]{1,0:T(8,128)(2,1)S(1)}, u32[]{:S(2)}, u32[]{:S(2)}) collective-permute-start(bf16[8,3584]{1,0:T(8,128)(2,1)S(1)} %get-tuple-element.11), channel_id=1, source_target_pairs={{0,2},{2,4},{4,6},{6,0},{1,3},{3,5},{5,7},{7,1},{8,10},{10,12},{12... | collective-permute-start | bytes 172040 | tf_op jit(solution)/shard_map/ppermute | solution.py:16
  25.8 1.2 %collective-permute-start.13 = (bf16[8,3584]{1,0:T(8,128)(2,1)S(1)}, bf16[8,3584]{1,0:T(8,128)(2,1)S(1)}, u32[]{:S(2)}, u32[]{:S(2)}) collective-permute-start(bf16[8,3584]{1,0:T(8,128)(2,1)S(1)} %get-tuple-element.12), channel_id=1, source_target_pairs={{0,4},{2,6},{4,0},{6,2},{1,5},{3,7},{5,1},{7,3},{8,12},{10,14},{12... | collective-permute-start | bytes 172040 | tf_op jit(solution)/shard_map/ppermute | solution.py:16
  27.0 2.5 %collective-permute-start.12 = (bf16[8,3584]{1,0:T(8,128)(2,1)S(1)}, bf16[8,3584]{1,0:T(8,128)(2,1)S(1)}, u32[]{:S(2)}, u32[]{:S(2)}) collective-permute-start(bf16[8,3584]{1,0:T(8,128)(2,1)S(1)} %get-tuple-element.13), channel_id=1, source_target_pairs={{0,6},{2,0},{4,2},{6,4},{1,7},{3,1},{5,3},{7,5},{8,14},{10,8},{12,... | collective-permute-start | bytes 172040 | tf_op jit(solution)/shard_map/ppermute | solution.py:16
  29.5 0.0 collective-permute-done.16
  29.5 0.5 %collective-permute-start.20 = (bf16[8,3584]{1,0:T(8,128)(2,1)S(1)}, bf16[8,3584]{1,0:T(8,128)(2,1)S(1)}, u32[]{:S(2)}, u32[]{:S(2)}) collective-permute-start(bf16[8,3584]{1,0:T(8,128)(2,1)S(1)} %get-tuple-element.7), channel_id=1, source_target_pairs={{0,18},{2,20},{4,22},{6,16},{8,26},{10,28},{12,30},{14,24},{16,2},... | collective-permute-start | bytes 172040 | tf_op jit(solution)/shard_map/ppermute | solution.py:26
  30.1 1.7 %collective-permute-start.19 = (bf16[8,3584]{1,0:T(8,128)(2,1)S(1)}, bf16[8,3584]{1,0:T(8,128)(2,1)S(1)}, u32[]{:S(2)}, u32[]{:S(2)}) collective-permute-start(bf16[8,3584]{1,0:T(8,128)(2,1)S(1)} %get-tuple-element.8), channel_id=1, source_target_pairs={{0,20},{2,22},{4,16},{6,18},{8,28},{10,30},{12,24},{14,26},{16,4},... | collective-permute-start | bytes 172040 | tf_op jit(solution)/shard_map/ppermute | solution.py:26
  31.8 0.0 collective-permute-done.14.refs_3_
  31.8 3.0 %collective-permute-start.18 = (bf16[8,3584]{1,0:T(8,128)(2,1)S(1)}, bf16[8,3584]{1,0:T(8,128)(2,1)S(1)}, u32[]{:S(2)}, u32[]{:S(2)}) collective-permute-start(bf16[8,3584]{1,0:T(8,128)(2,1)S(1)} %get-tuple-element.9), channel_id=1, source_target_pairs={{0,22},{2,16},{4,18},{6,20},{8,30},{10,24},{12,26},{14,28},{16,6},... | collective-permute-start | bytes 172040 | tf_op jit(solution)/shard_map/ppermute | solution.py:26
  34.9 0.0 collective-permute-done.13.refs_2_
  34.9 1.3 %collective-permute-start.17 = (bf16[8,3584]{1,0:T(8,128)(2,1)S(1)}, bf16[8,3584]{1,0:T(8,128)(2,1)S(1)}, u32[]{:S(2)}, u32[]{:S(2)}) collective-permute-start(bf16[8,3584]{1,0:T(8,128)(2,1)S(1)} %get-tuple-element.10), channel_id=1, source_target_pairs={{0,16},{2,18},{4,20},{6,22},{8,24},{10,26},{12,28},{14,30},{16,0},... | collective-permute-start | bytes 172040 | tf_op jit(solution)/shard_map/ppermute | solution.py:26
  36.2 0.0 collective-permute-done.12.refs_1_
  36.2 0.9 %collective-permute-done.20.refs_7_ = bf16[8,3584]{1,0:T(8,128)(2,1)S(1)} collective-permute-done((bf16[8,3584]{1,0:T(8,128)(2,1)S(1)}, bf16[8,3584]{1,0:T(8,128)(2,1)S(1)}, u32[]{:S(2)}, u32[]{:S(2)}) %collective-permute-start.20) | collective-permute-done | bytes 57376 | tf_op jit(solution)/shard_map/ppermute | solution.py:26
  37.1 1.5 %collective-permute-done.19.refs_6_ = bf16[8,3584]{1,0:T(8,128)(2,1)S(1)} collective-permute-done((bf16[8,3584]{1,0:T(8,128)(2,1)S(1)}, bf16[8,3584]{1,0:T(8,128)(2,1)S(1)}, u32[]{:S(2)}, u32[]{:S(2)}) %collective-permute-start.19) | collective-permute-done | bytes 57376 | tf_op jit(solution)/shard_map/ppermute | solution.py:26
  38.6 0.0 collective-permute-done.18.refs_5_
  38.6 1.1 %collective-permute-done.17.refs_4_ = bf16[8,3584]{1,0:T(8,128)(2,1)S(1)} collective-permute-done((bf16[8,3584]{1,0:T(8,128)(2,1)S(1)}, bf16[8,3584]{1,0:T(8,128)(2,1)S(1)}, u32[]{:S(2)}, u32[]{:S(2)}) %collective-permute-start.17) | collective-permute-done | bytes 57376 | tf_op jit(solution)/shard_map/ppermute | solution.py:26
  39.7 0.0 copy-done.2
  39.7 0.0 copy-done.3
  39.7 0.7 %shard_map.73 = bf16[8,3584]{1,0:T(8,128)(2,1)} custom-call(s32[1,8]{1,0:T(1,128)S(1)} %bitcast.23, s32[1,8]{1,0:T(1,128)S(1)} %bitcast.24, f32[8,3584]{1,0:T(8,128)S(1)} %slice.83.refs_0_, bf16[8,3584]{1,0:T(8,128)(2,1)S(1)} %collective-permute-done.12.refs_1_, bf16[8,3584]{1,0:T(8,128)(2,1)S(1)} %collective-permute-done.13.refs_2_, ...), custom_call_target="tpu_custom_call" | custom-call | tf_op jit(solution)/shard_map/pallas_call | solution.py:83
  (35 shorter events, 0.4 us)
Async XLA Ops:
  0.0 20.6 %copy-start = (bf16[1,256,3584]{2,1,0:T(8,128)(2,1)S(1)}, bf16[1,256,3584]{2,1,0:T(8,128)(2,1)}, u32[]{:S(2)}) copy-start(bf16[1,256,3584]{2,1,0:T(8,128)(2,1)} %param.11) | copy-start | bytes 5505028
  0.0 8.4 %collective-permute-start = (bf16[8,3584]{1,0:T(8,128)(2,1)}, bf16[8,3584]{1,0:T(8,128)(2,1)S(1)}, u32[]{:S(2)}, u32[]{:S(2)}) collective-permute-start(bf16[8,3584]{1,0:T(8,128)(2,1)} %from_ref.1), channel_id=1, source_target_pairs={{0,2},{2,4},{4,6},{6,0},{1,3},{3,5},{5,7},{7,1},{8,10},{10,12},{12... | collective-permute-start | bytes 172040 | tf_op jit(solution)/shard_map/ppermute | solution.py:16
  3.0 6.4 %collective-permute-start.2 = (bf16[8,3584]{1,0:T(8,128)(2,1)}, bf16[8,3584]{1,0:T(8,128)(2,1)S(1)}, u32[]{:S(2)}, u32[]{:S(2)}) collective-permute-start(bf16[8,3584]{1,0:T(8,128)(2,1)} %from_ref.1), channel_id=1, source_target_pairs={{0,6},{2,0},{4,2},{6,4},{1,7},{3,1},{5,3},{7,5},{8,14},{10,8},{12,... | collective-permute-start | bytes 172040 | tf_op jit(solution)/shard_map/ppermute | solution.py:16
  5.1 5.8 %collective-permute-start.1 = (bf16[8,3584]{1,0:T(8,128)(2,1)}, bf16[8,3584]{1,0:T(8,128)(2,1)S(1)}, u32[]{:S(2)}, u32[]{:S(2)}) collective-permute-start(bf16[8,3584]{1,0:T(8,128)(2,1)} %from_ref.1), channel_id=1, source_target_pairs={{0,4},{2,6},{4,0},{6,2},{1,5},{3,7},{5,1},{7,3},{8,12},{10,14},{12... | collective-permute-start | bytes 172040 | tf_op jit(solution)/shard_map/ppermute | solution.py:16
  6.1 0.9 %copy-start.1 = (bf16[8,3584]{1,0:T(8,128)(2,1)S(1)}, bf16[8,3584]{1,0:T(8,128)(2,1)}, u32[]{:S(2)}) copy-start(bf16[8,3584]{1,0:T(8,128)(2,1)} %from_ref.1) | copy-start | bytes 172036
  6.9 7.5 %copy-start.4 = (bf16[1,3584,256]{2,1,0:T(8,128)(2,1)S(1)}, bf16[1,3584,256]{2,1,0:T(8,128)(2,1)}, u32[]{:S(2)}) copy-start(bf16[1,3584,256]{2,1,0:T(8,128)(2,1)} %param.10) | copy-start | bytes 5505028
  6.9 5.6 %collective-permute-start.6 = (bf16[8,3584]{1,0:T(8,128)(2,1)S(1)}, bf16[8,3584]{1,0:T(8,128)(2,1)S(1)}, u32[]{:S(2)}, u32[]{:S(2)}) collective-permute-start(bf16[8,3584]{1,0:T(8,128)(2,1)S(1)} %shard_map.64), channel_id=1, source_target_pairs={{0,16},{2,18},{4,20},{6,22},{8,24},{10,26},{12,28},{14,30},{16,0},... | collective-permute-start | bytes 172040 | tf_op jit(solution)/shard_map/ppermute | solution.py:26
  8.4 4.2 %collective-permute-start.3 = (bf16[8,3584]{1,0:T(8,128)(2,1)S(1)}, bf16[8,3584]{1,0:T(8,128)(2,1)S(1)}, u32[]{:S(2)}, u32[]{:S(2)}) collective-permute-start(bf16[8,3584]{1,0:T(8,128)(2,1)S(1)} %collective-permute-done), channel_id=1, source_target_pairs={{0,16},{2,18},{4,20},{6,22},{8,24},{10,26},{12,28},{14,30},{16,0},... | collective-permute-start | bytes 172040 | tf_op jit(solution)/shard_map/ppermute | solution.py:26
  9.4 4.8 %collective-permute-start.7 = (bf16[8,3584]{1,0:T(8,128)(2,1)S(1)}, bf16[8,3584]{1,0:T(8,128)(2,1)S(1)}, u32[]{:S(2)}, u32[]{:S(2)}) collective-permute-start(bf16[8,3584]{1,0:T(8,128)(2,1)S(1)} %collective-permute-done.2), channel_id=1, source_target_pairs={{0,16},{2,18},{4,20},{6,22},{8,24},{10,26},{12,28},{14,30},{16,0},... | collective-permute-start | bytes 172040 | tf_op jit(solution)/shard_map/ppermute | solution.py:26
  10.9 6.8 %collective-permute-start.8 = (bf16[8,3584]{1,0:T(8,128)(2,1)S(1)}, bf16[8,3584]{1,0:T(8,128)(2,1)S(1)}, u32[]{:S(2)}, u32[]{:S(2)}) collective-permute-start(bf16[8,3584]{1,0:T(8,128)(2,1)S(1)} %collective-permute-done.1), channel_id=1, source_target_pairs={{0,16},{2,18},{4,20},{6,22},{8,24},{10,26},{12,28},{14,30},{16,0},... | collective-permute-start | bytes 172040 | tf_op jit(solution)/shard_map/ppermute | solution.py:26
  12.7 1.6 %collective-permute-start.4 = (bf16[32,3584]{1,0:T(8,128)(2,1)S(1)}, bf16[32,3584]{1,0:T(8,128)(2,1)S(1)}, u32[]{:S(2)}, u32[]{:S(2)}) collective-permute-start(bf16[32,3584]{1,0:T(8,128)(2,1)S(1)} %shard_map.65), channel_id=1, source_target_pairs={{0,8},{8,0},{16,24},{24,16},{1,9},{9,1},{17,25},{25,17},{2,10},{10... | collective-permute-start | bytes 688136 | tf_op jit(solution)/shard_map/ppermute | solution.py:30
  14.2 1.5 %copy-start.5 = (bf16[1,3584,256]{2,1,0:T(8,128)(2,1)S(1)}, bf16[1,3584,256]{2,1,0:T(8,128)(2,1)}, u32[]{:S(2)}) copy-start(bf16[1,3584,256]{2,1,0:T(8,128)(2,1)} %param.9) | copy-start | bytes 5505028
  14.3 4.7 %collective-permute-start.9 = (bf16[24,3584]{1,0:T(8,128)(2,1)S(1)}, bf16[24,3584]{1,0:T(8,128)(2,1)S(1)}, u32[]{:S(2)}, u32[]{:S(2)}) collective-permute-start(bf16[24,3584]{1,0:T(8,128)(2,1)S(1)} %shard_map.69), channel_id=1, source_target_pairs={{0,8},{8,0},{16,24},{24,16},{1,9},{9,1},{17,25},{25,17},{2,10},{10... | collective-permute-start | bytes 516104 | tf_op jit(solution)/shard_map/ppermute | solution.py:30
  16.2 4.4 %collective-permute-start.5 = (bf16[64,512]{1,0:T(8,128)(2,1)S(1)}, bf16[64,512]{1,0:T(8,128)(2,1)S(1)}, u32[]{:S(2)}, u32[]{:S(2)}) collective-permute-start(bf16[64,512]{1,0:T(8,128)(2,1)S(1)} %fusion.22.refs_1_), channel_id=1, source_target_pairs={{0,1},{1,0},{2,3},{3,2},{4,5},{5,4},{6,7},{7,6},{8,9},{9,8},{10,11... | collective-permute-start | bytes 196616 | tf_op jit(solution)/shard_map/ppermute | solution.py:16
  17.7 1.2 %collective-permute-start.10 = (bf16[8,3584]{1,0:T(8,128)(2,1)S(1)}, bf16[8,3584]{1,0:T(8,128)(2,1)S(1)}, u32[]{:S(2)}, u32[]{:S(2)}) collective-permute-start(bf16[8,3584]{1,0:T(8,128)(2,1)S(1)} %shard_map.67.refs_0_), channel_id=1, source_target_pairs={{0,8},{8,0},{16,24},{24,16},{1,9},{9,1},{17,25},{25,17},{2,10},{10... | collective-permute-start | bytes 172040 | tf_op jit(solution)/shard_map/ppermute | solution.py:30
  19.9 4.3 %collective-permute-start.15 = (bf16[64,512]{1,0:T(8,128)(2,1)S(1)}, bf16[64,512]{1,0:T(8,128)(2,1)S(1)}, u32[]{:S(2)}, u32[]{:S(2)}) collective-permute-start(bf16[64,512]{1,0:T(8,128)(2,1)S(1)} %fusion.13.refs_1_), channel_id=1, source_target_pairs={{0,1},{1,0},{2,3},{3,2},{4,5},{5,4},{6,7},{7,6},{8,9},{9,8},{10,11... | collective-permute-start | bytes 196616 | tf_op jit(solution)/shard_map/ppermute | solution.py:16
  21.1 1.6 %collective-permute-start.11 = (bf16[32,3584]{1,0:T(8,128)(2,1)S(1)}, bf16[32,3584]{1,0:T(8,128)(2,1)S(1)}, u32[]{:S(2)}, u32[]{:S(2)}) collective-permute-start(bf16[32,3584]{1,0:T(8,128)(2,1)S(1)} %slice.116), channel_id=1, source_target_pairs={{0,8},{8,0},{16,24},{24,16},{1,9},{9,1},{17,25},{25,17},{2,10},{10... | collective-permute-start | bytes 688136 | tf_op jit(solution)/shard_map/ppermute | solution.py:30
  24.7 15.1 %copy-start.2 = (s32[8,1]{0,1:T(1,128)S(1)}, s32[8,1]{0,1:T(1,128)}, u32[]{:S(2)}) copy-start(s32[8,1]{0,1:T(1,128)} %param.7) | copy-start | bytes 100
  24.7 15.1 %copy-start.3 = (s32[8,1]{0,1:T(1,128)S(1)}, s32[8,1]{0,1:T(1,128)}, u32[]{:S(2)}) copy-start(s32[8,1]{0,1:T(1,128)} %param.8) | copy-start | bytes 100
  24.7 4.7 %collective-permute-start.16 = (bf16[32,3584]{1,0:T(8,128)(2,1)S(1)}, bf16[32,3584]{1,0:T(8,128)(2,1)S(1)}, u32[]{:S(2)}, u32[]{:S(2)}) collective-permute-start(bf16[32,3584]{1,0:T(8,128)(2,1)S(1)} %slice.115), channel_id=1, source_target_pairs={{0,8},{8,0},{16,24},{24,16},{1,9},{9,1},{17,25},{25,17},{2,10},{10... | collective-permute-start | bytes 688136 | tf_op jit(solution)/shard_map/ppermute | solution.py:30
  24.8 7.0 %collective-permute-start.14 = (bf16[8,3584]{1,0:T(8,128)(2,1)S(1)}, bf16[8,3584]{1,0:T(8,128)(2,1)S(1)}, u32[]{:S(2)}, u32[]{:S(2)}) collective-permute-start(bf16[8,3584]{1,0:T(8,128)(2,1)S(1)} %get-tuple-element.11), channel_id=1, source_target_pairs={{0,2},{2,4},{4,6},{6,0},{1,3},{3,5},{5,7},{7,1},{8,10},{10,12},{12... | collective-permute-start | bytes 172040 | tf_op jit(solution)/shard_map/ppermute | solution.py:16
  25.8 9.0 %collective-permute-start.13 = (bf16[8,3584]{1,0:T(8,128)(2,1)S(1)}, bf16[8,3584]{1,0:T(8,128)(2,1)S(1)}, u32[]{:S(2)}, u32[]{:S(2)}) collective-permute-start(bf16[8,3584]{1,0:T(8,128)(2,1)S(1)} %get-tuple-element.12), channel_id=1, source_target_pairs={{0,4},{2,6},{4,0},{6,2},{1,5},{3,7},{5,1},{7,3},{8,12},{10,14},{12... | collective-permute-start | bytes 172040 | tf_op jit(solution)/shard_map/ppermute | solution.py:16
  27.0 9.2 %collective-permute-start.12 = (bf16[8,3584]{1,0:T(8,128)(2,1)S(1)}, bf16[8,3584]{1,0:T(8,128)(2,1)S(1)}, u32[]{:S(2)}, u32[]{:S(2)}) collective-permute-start(bf16[8,3584]{1,0:T(8,128)(2,1)S(1)} %get-tuple-element.13), channel_id=1, source_target_pairs={{0,6},{2,0},{4,2},{6,4},{1,7},{3,1},{5,3},{7,5},{8,14},{10,8},{12,... | collective-permute-start | bytes 172040 | tf_op jit(solution)/shard_map/ppermute | solution.py:16
  29.5 7.6 %collective-permute-start.20 = (bf16[8,3584]{1,0:T(8,128)(2,1)S(1)}, bf16[8,3584]{1,0:T(8,128)(2,1)S(1)}, u32[]{:S(2)}, u32[]{:S(2)}) collective-permute-start(bf16[8,3584]{1,0:T(8,128)(2,1)S(1)} %get-tuple-element.7), channel_id=1, source_target_pairs={{0,18},{2,20},{4,22},{6,16},{8,26},{10,28},{12,30},{14,24},{16,2},... | collective-permute-start | bytes 172040 | tf_op jit(solution)/shard_map/ppermute | solution.py:26
  30.1 8.5 %collective-permute-start.19 = (bf16[8,3584]{1,0:T(8,128)(2,1)S(1)}, bf16[8,3584]{1,0:T(8,128)(2,1)S(1)}, u32[]{:S(2)}, u32[]{:S(2)}) collective-permute-start(bf16[8,3584]{1,0:T(8,128)(2,1)S(1)} %get-tuple-element.8), channel_id=1, source_target_pairs={{0,20},{2,22},{4,16},{6,18},{8,28},{10,30},{12,24},{14,26},{16,4},... | collective-permute-start | bytes 172040 | tf_op jit(solution)/shard_map/ppermute | solution.py:26
  31.8 6.8 %collective-permute-start.18 = (bf16[8,3584]{1,0:T(8,128)(2,1)S(1)}, bf16[8,3584]{1,0:T(8,128)(2,1)S(1)}, u32[]{:S(2)}, u32[]{:S(2)}) collective-permute-start(bf16[8,3584]{1,0:T(8,128)(2,1)S(1)} %get-tuple-element.9), channel_id=1, source_target_pairs={{0,22},{2,16},{4,18},{6,20},{8,30},{10,24},{12,26},{14,28},{16,6},... | collective-permute-start | bytes 172040 | tf_op jit(solution)/shard_map/ppermute | solution.py:26
  34.9 4.9 %collective-permute-start.17 = (bf16[8,3584]{1,0:T(8,128)(2,1)S(1)}, bf16[8,3584]{1,0:T(8,128)(2,1)S(1)}, u32[]{:S(2)}, u32[]{:S(2)}) collective-permute-start(bf16[8,3584]{1,0:T(8,128)(2,1)S(1)} %get-tuple-element.10), channel_id=1, source_target_pairs={{0,16},{2,18},{4,20},{6,22},{8,24},{10,26},{12,28},{14,30},{16,0},... | collective-permute-start | bytes 172040 | tf_op jit(solution)/shard_map/ppermute | solution.py:26

commit v6 on v0

--- a/solution.py
+++ b/solution.py
@@ -101,7 +101,9 @@
         sent = part.astype(bf16)
         return part, sent, [shift(sent, "ex", s) for s in range(1, n_ex)]
 
-    def partial_out(part, others, kept_flops):
+    def partial_out(part, others, kept_flops, part_flops=0, *earlier):
+        if part_flops:
+            part = after(part, flops=part_flops)
         for other in others:
             part = part + other.astype(f32)
         hidden = (jax.nn.silu(part[:, :inner]) * part[:, inner:]).astype(bf16)
@@ -109,27 +111,28 @@
         kept = out.shape[0] // 2
         swapped = swap_half(out[kept:].astype(bf16)).astype(f32)
         if kept_flops:
-            out = after(out, flops=kept_flops)
+            out = after(after(out, *earlier) if earlier else out, flops=kept_flops)
         return out[:kept] + swapped
 
     held = copied(tokens)
-    places = tuple(range(n_tp))
+    places = (0, n_tp - 1, *range(1, n_tp - 1))
     blocks = [held] + [shift(tokens, "tp", t) for t in places[1:]]
-    far = [[shift_expert(rows, s) for rows in blocks] for s in range(1, experts)]
+    straight = n_tp // 2
+    far = [[shift_expert(tokens, s, t) if t == straight else shift_expert(rows, s) for t, rows in zip(places, blocks)] for s in range(1, experts)]
     near = jnp.concatenate(blocks, axis=0)
-    near_swapped = swap_half(after(near, *(line[1] for line in far)))
+    near_swapped = swap_half(after(near, *(line[places.index(1)] for line in far)))
     near = jnp.concatenate([near, near_swapped], axis=0)
     near_part, near_sent, near_others = partial_sums(near)
-    far = [after(rows, near_sent) if i == n_tp - 1 else rows for line in far for i, rows in enumerate(line)]
+    far = [after(rows, near_sent) if i > 1 else rows for line in far for i, rows in enumerate(line)]
     far = jnp.concatenate(far, axis=0)
     far_swapped = swap_half(far)
     far = jnp.concatenate([after(far, flops=3450000000), far_swapped], axis=0)
     far_part, far_sent, far_others = partial_sums(far)
-    near_out = partial_out(near_part, [after(other, far_sent) for other in near_others], 3450000000)
+    near_out = partial_out(near_part, [after(other, far_sent) for other in near_others], 3450000000, 3450000000)
     near_out = near_out.reshape(n_tp, count, width)
     near_sent = near_out[1:].astype(bf16)
     pieces = [near_out[0]] + [shift(near_sent[i], "tp", -t) for i, t in enumerate(places[1:])]
-    far_out = partial_out(far_part, [after(other, near_sent) for other in far_others], 0)
+    far_out = partial_out(far_part, [after(other, near_sent) for other in far_others], 0, 0)
     far_out = far_out.reshape(experts - 1, n_tp, count, width).astype(bf16)
     for s in range(1, experts):
         pieces += [shift_expert(far_out[experts - 1 - s, i], s, -t) for i, t in enumerate(places)]

time: 39.3 us -> 42.5 us (1.081)
  waiting for transfers between devices: 8.51 us -> 14.1 us
  starting transfers between devices: 25.9 us -> 23.4 us
    ppermute x8, waiting for transfers between devices: 4.37 us -> 6.89 us  [shift_expert(): return lax.ppermute(value, ('grp', 'tp'), pairs)]
    ppermute x8, starting transfers between devices: 14.5 us -> 12 us  [shift(): lax.ppermute(value, axis, [(i, (i + by) % size) for i in range(size)])]
    ppermute x8, waiting for transfers between devices: 1.19 us -> 2.79 us  [shift(): lax.ppermute(value, axis, [(i, (i + by) % size) for i in range(size)])]
    ppermute x4, waiting for transfers between devices: 2.95 us -> 4.41 us  [swap_half(): lax.ppermute(value, 'grp', [(i, i ^ 1) for i in range(lax.axis_size('grp'...]
where the time goes in v6:
time: 42.5 us; the launch traced here: 42.3 us
  starting transfers between devices  23.4 us (55%)
  waiting for transfers between devices  14.1 us (33%)
  matrix products  2.6 us (6%)
  local copies, waits for them, and re-layouts  1.02 us (2%)
  Pallas kernels  0.75 us (2%)
    ppermute x8, starting transfers between devices, shift(): lax.ppermute(value, axis, [(i, (i + by) % size) for i in range(size)])  12 us
    ppermute x8, starting transfers between devices, shift_expert(): return lax.ppermute(value, ('grp', 'tp'), pairs)  11.2 us
    ppermute x8, waiting for transfers between devices, shift_expert(): return lax.ppermute(value, ('grp', 'tp'), pairs)  6.89 us
    ppermute x4, waiting for transfers between devices, swap_half(): lax.ppermute(value, 'grp', [(i, i ^ 1) for i in range(lax.axis_size('grp'...  4.41 us
    ppermute x8, waiting for transfers between devices, shift(): lax.ppermute(value, axis, [(i, (i + by) % size) for i in range(size)])  2.79 us
    dot_general x4, matrix products, partial_sums(): jnp.dot(rows, w, preferred_element_type=f32)  1.76 us
    unnamed x16, local copies, waits for them, and re-layouts  0.9 us
  transfers between devices with their start and end apart: 20, of which 9 were waited for; matrix products, arithmetic and copies ran while one was open for 6% of the time, Pallas kernels for 0%

profile of v6, /device:TPU:0, one launch (start us, length us, event | category | flops | bytes accessed | tf_op | source)
XLA Modules:
  0.0 42.3 jit_solution(3273905819318270029)
XLA Ops:
  0.0 0.0 copy-start
  0.0 3.0 %collective-permute-start.1 = (bf16[8,3584]{1,0:T(8,128)(2,1)}, bf16[8,3584]{1,0:T(8,128)(2,1)S(1)}, u32[]{:S(2)}, u32[]{:S(2)}) collective-permute-start(bf16[8,3584]{1,0:T(8,128)(2,1)} %from_ref.1), channel_id=1, source_target_pairs={{0,2},{2,4},{4,6},{6,0},{1,3},{3,5},{5,7},{7,1},{8,10},{10,12},{12... | collective-permute-start | bytes 172040 | tf_op jit(solution)/shard_map/ppermute | solution.py:16
  3.0 2.1 %collective-permute-start = (bf16[8,3584]{1,0:T(8,128)(2,1)}, bf16[8,3584]{1,0:T(8,128)(2,1)S(1)}, u32[]{:S(2)}, u32[]{:S(2)}) collective-permute-start(bf16[8,3584]{1,0:T(8,128)(2,1)} %from_ref.1), channel_id=1, source_target_pairs={{0,6},{2,0},{4,2},{6,4},{1,7},{3,1},{5,3},{7,5},{8,14},{10,8},{12,... | collective-permute-start | bytes 172040 | tf_op jit(solution)/shard_map/ppermute | solution.py:16
  5.1 1.9 %collective-permute-start.8 = (bf16[8,3584]{1,0:T(8,128)(2,1)}, bf16[8,3584]{1,0:T(8,128)(2,1)S(1)}, u32[]{:S(2)}, u32[]{:S(2)}) collective-permute-start(bf16[8,3584]{1,0:T(8,128)(2,1)} %from_ref.1), channel_id=1, source_target_pairs={{0,20},{2,22},{4,16},{6,18},{8,28},{10,30},{12,24},{14,26},{16,4},... | collective-permute-start | bytes 172040 | tf_op jit(solution)/shard_map/ppermute | solution.py:26
  7.0 2.1 %collective-permute-start.2 = (bf16[8,3584]{1,0:T(8,128)(2,1)}, bf16[8,3584]{1,0:T(8,128)(2,1)S(1)}, u32[]{:S(2)}, u32[]{:S(2)}) collective-permute-start(bf16[8,3584]{1,0:T(8,128)(2,1)} %from_ref.1), channel_id=1, source_target_pairs={{0,4},{2,6},{4,0},{6,2},{1,5},{3,7},{5,1},{7,3},{8,12},{10,14},{12... | collective-permute-start | bytes 172040 | tf_op jit(solution)/shard_map/ppermute | solution.py:16
  9.1 0.0 copy-start.1
  9.1 0.9 %copy-done.1 = bf16[8,3584]{1,0:T(8,128)(2,1)S(1)} copy-done((bf16[8,3584]{1,0:T(8,128)(2,1)S(1)}, bf16[8,3584]{1,0:T(8,128)(2,1)}, u32[]{:S(2)}) %copy-start.1) | copy-done | bytes 57368
  10.0 0.0 copy-start.4
  10.0 0.4 collective-permute-start.6
  10.4 0.0 collective-permute-done.1
  10.4 1.7 %collective-permute-start.3 = (bf16[8,3584]{1,0:T(8,128)(2,1)S(1)}, bf16[8,3584]{1,0:T(8,128)(2,1)S(1)}, u32[]{:S(2)}, u32[]{:S(2)}) collective-permute-start(bf16[8,3584]{1,0:T(8,128)(2,1)S(1)} %collective-permute-done.1), channel_id=1, source_target_pairs={{0,16},{2,18},{4,20},{6,22},{8,24},{10,26},{12,28},{14,30},{16,0},... | collective-permute-start | bytes 172040 | tf_op jit(solution)/shard_map/ppermute | solution.py:26
  12.1 0.0 collective-permute-done
  12.1 0.4 collective-permute-start.7
  12.5 1.1 %collective-permute-done.2 = bf16[8,3584]{1,0:T(8,128)(2,1)S(1)} collective-permute-done((bf16[8,3584]{1,0:T(8,128)(2,1)}, bf16[8,3584]{1,0:T(8,128)(2,1)S(1)}, u32[]{:S(2)}, u32[]{:S(2)}) %collective-permute-start.2) | collective-permute-done | bytes 57376 | tf_op jit(solution)/shard_map/ppermute | solution.py:16
  13.6 0.0 copy-start.5
  13.7 1.6 %collective-permute-done.3.refs_1_.refs_0_ = bf16[8,3584]{1,0:T(8,128)(2,1)S(1)} collective-permute-done((bf16[8,3584]{1,0:T(8,128)(2,1)S(1)}, bf16[8,3584]{1,0:T(8,128)(2,1)S(1)}, u32[]{:S(2)}, u32[]{:S(2)}) %collective-permute-start.3) | collective-permute-done | bytes 57376 | tf_op jit(solution)/shard_map/ppermute | solution.py:26
  15.2 0.0 collective-permute-start.4
  15.3 1.5 %collective-permute-done.4 = bf16[32,3584]{1,0:T(8,128)(2,1)S(1)} collective-permute-done((bf16[32,3584]{1,0:T(8,128)(2,1)S(1)}, bf16[32,3584]{1,0:T(8,128)(2,1)S(1)}, u32[]{:S(2)}, u32[]{:S(2)}) %collective-permute-start.4) | collective-permute-done | bytes 229408 | tf_op jit(solution)/shard_map/ppermute | solution.py:30
  16.8 0.0 copy-done.4
  16.8 0.4 %fusion.6 = f32[64,256]{1,0:T(8,128)S(1)} fusion(bf16[64,3584]{1,0:T(8,128)(2,1)S(1)} %constant_dynamic-update-slice_fusion, bf16[1,3584,256]{2,1,0:T(8,128)(2,1)S(1)} %copy-done.4), kind=kOutput, calls=%fused_computation.6 | convolution fusion | flops 117440512 | bytes 2359296 | tf_op jit(solution)/shard_map/dot_general | solution.py:99
  17.2 0.0 copy-done.5
  17.2 0.4 %fusion.10 = f32[64,256]{1,0:T(8,128)S(1)} fusion(bf16[64,3584]{1,0:T(8,128)(2,1)S(1)} %constant_dynamic-update-slice_fusion, bf16[1,3584,256]{2,1,0:T(8,128)(2,1)S(1)} %copy-done.5), kind=kOutput, calls=%fused_computation.10 | convolution fusion | flops 117440512 | bytes 2359296 | tf_op jit(solution)/shard_map/dot_general | solution.py:99
  17.7 1.6 %collective-permute-start.5 = (bf16[64,512]{1,0:T(8,128)(2,1)S(1)}, bf16[64,512]{1,0:T(8,128)(2,1)S(1)}, u32[]{:S(2)}, u32[]{:S(2)}) collective-permute-start(bf16[64,512]{1,0:T(8,128)(2,1)S(1)} %fusion.25.refs_1_), channel_id=1, source_target_pairs={{0,1},{1,0},{2,3},{3,2},{4,5},{5,4},{6,7},{7,6},{8,9},{9,8},{10,11... | collective-permute-start | bytes 196616 | tf_op jit(solution)/shard_map/ppermute | solution.py:16
  19.3 0.0 collective-permute-done.8.refs_0_
  19.3 0.0 collective-permute-done.6
  19.3 0.0 collective-permute-done.7
  19.3 0.1 collective-permute-start.9
  19.4 1.5 %collective-permute-done.9 = bf16[32,3584]{1,0:T(8,128)(2,1)S(1)} collective-permute-done((bf16[32,3584]{1,0:T(8,128)(2,1)S(1)}, bf16[32,3584]{1,0:T(8,128)(2,1)S(1)}, u32[]{:S(2)}, u32[]{:S(2)}) %collective-permute-start.9) | collective-permute-done | bytes 229408 | tf_op jit(solution)/shard_map/ppermute | solution.py:30
  20.9 0.4 %fusion.4 = f32[64,256]{1,0:T(8,128)S(1)} fusion(bf16[1,3584,256]{2,1,0:T(8,128)(2,1)S(1)} %copy-done.4, bf16[32,3584]{1,0:T(8,128)(2,1)S(1)} %collective-permute-done.9, bf16[32,3584]{1,0:T(8,128)(2,1)S(1)} %shard_map.69), kind=kOutput, calls=%fused_computation.4 | convolution fusion | flops 118358016 | bytes 2359296 | tf_op jit(solution)/shard_map/dot_general | solution.py:99
  21.3 0.4 %fusion.8 = f32[64,256]{1,0:T(8,128)S(1)} fusion(bf16[1,3584,256]{2,1,0:T(8,128)(2,1)S(1)} %copy-done.5, bf16[32,3584]{1,0:T(8,128)(2,1)S(1)} %collective-permute-done.9, bf16[32,3584]{1,0:T(8,128)(2,1)S(1)} %shard_map.69), kind=kOutput, calls=%fused_computation.8 | convolution fusion | flops 118358016 | bytes 2359296 | tf_op jit(solution)/shard_map/dot_general | solution.py:99
  21.8 0.6 %collective-permute-start.14 = (bf16[64,512]{1,0:T(8,128)(2,1)S(1)}, bf16[64,512]{1,0:T(8,128)(2,1)S(1)}, u32[]{:S(2)}, u32[]{:S(2)}) collective-permute-start(bf16[64,512]{1,0:T(8,128)(2,1)S(1)} %fusion.14.refs_1_), channel_id=1, source_target_pairs={{0,1},{1,0},{2,3},{3,2},{4,5},{5,4},{6,7},{7,6},{8,9},{9,8},{10,11... | collective-permute-start | bytes 196616 | tf_op jit(solution)/shard_map/ppermute | solution.py:16
  22.4 0.0 collective-permute-done.5.refs_0_
  22.4 0.0 copy-done
  22.4 0.4 fusion.2.refs_0_
  22.8 0.1 collective-permute-start.10
  22.9 1.5 %collective-permute-done.10 = bf16[32,3584]{1,0:T(8,128)(2,1)S(1)} collective-permute-done((bf16[32,3584]{1,0:T(8,128)(2,1)S(1)}, bf16[32,3584]{1,0:T(8,128)(2,1)S(1)}, u32[]{:S(2)}, u32[]{:S(2)}) %collective-permute-start.10) | collective-permute-done | bytes 229408 | tf_op jit(solution)/shard_map/ppermute | solution.py:30
  24.4 0.1 fusion.26
  24.5 1.6 %collective-permute-done.14.refs_0_ = bf16[64,512]{1,0:T(8,128)(2,1)S(1)} collective-permute-done((bf16[64,512]{1,0:T(8,128)(2,1)S(1)}, bf16[64,512]{1,0:T(8,128)(2,1)S(1)}, u32[]{:S(2)}, u32[]{:S(2)}) %collective-permute-start.14) | collective-permute-done | bytes 65568 | tf_op jit(solution)/shard_map/ppermute | solution.py:16
  26.1 0.4 fusion
  26.6 0.0 copy-start.2
  26.6 0.0 copy-start.3
  26.6 0.1 collective-permute-start.15
  26.7 0.4 collective-permute-start.13
  27.1 1.7 %collective-permute-start.12 = (bf16[8,3584]{1,0:T(8,128)(2,1)S(1)}, bf16[8,3584]{1,0:T(8,128)(2,1)S(1)}, u32[]{:S(2)}, u32[]{:S(2)}) collective-permute-start(bf16[8,3584]{1,0:T(8,128)(2,1)S(1)} %get-tuple-element.12), channel_id=1, source_target_pairs={{0,6},{2,0},{4,2},{6,4},{1,7},{3,1},{5,3},{7,5},{8,14},{10,8},{12,... | collective-permute-start | bytes 172040 | tf_op jit(solution)/shard_map/ppermute | solution.py:16
  28.8 0.5 %collective-permute-start.11 = (bf16[8,3584]{1,0:T(8,128)(2,1)S(1)}, bf16[8,3584]{1,0:T(8,128)(2,1)S(1)}, u32[]{:S(2)}, u32[]{:S(2)}) collective-permute-start(bf16[8,3584]{1,0:T(8,128)(2,1)S(1)} %get-tuple-element.13), channel_id=1, source_target_pairs={{0,2},{2,4},{4,6},{6,0},{1,3},{3,5},{5,7},{7,1},{8,10},{10,12},{12... | collective-permute-start | bytes 172040 | tf_op jit(solution)/shard_map/ppermute | solution.py:16
  29.3 0.0 collective-permute-done.15
  29.4 3.0 %collective-permute-start.19 = (bf16[8,3584]{1,0:T(8,128)(2,1)S(1)}, bf16[8,3584]{1,0:T(8,128)(2,1)S(1)}, u32[]{:S(2)}, u32[]{:S(2)}) collective-permute-start(bf16[8,3584]{1,0:T(8,128)(2,1)S(1)} %get-tuple-element.7), channel_id=1, source_target_pairs={{0,20},{2,22},{4,16},{6,18},{8,28},{10,30},{12,24},{14,26},{16,4},... | collective-permute-start | bytes 172040 | tf_op jit(solution)/shard_map/ppermute | solution.py:26
  32.4 2.4 %collective-permute-start.18 = (bf16[8,3584]{1,0:T(8,128)(2,1)S(1)}, bf16[8,3584]{1,0:T(8,128)(2,1)S(1)}, u32[]{:S(2)}, u32[]{:S(2)}) collective-permute-start(bf16[8,3584]{1,0:T(8,128)(2,1)S(1)} %get-tuple-element.8), channel_id=1, source_target_pairs={{0,22},{2,16},{4,18},{6,20},{8,30},{10,24},{12,26},{14,28},{16,6},... | collective-permute-start | bytes 172040 | tf_op jit(solution)/shard_map/ppermute | solution.py:26
  34.7 0.0 collective-permute-done.13.refs_3_
  34.7 0.6 %collective-permute-start.17 = (bf16[8,3584]{1,0:T(8,128)(2,1)S(1)}, bf16[8,3584]{1,0:T(8,128)(2,1)S(1)}, u32[]{:S(2)}, u32[]{:S(2)}) collective-permute-start(bf16[8,3584]{1,0:T(8,128)(2,1)S(1)} %get-tuple-element.9), channel_id=1, source_target_pairs={{0,18},{2,20},{4,22},{6,16},{8,26},{10,28},{12,30},{14,24},{16,2},... | collective-permute-start | bytes 172040 | tf_op jit(solution)/shard_map/ppermute | solution.py:26
  35.3 0.0 collective-permute-done.12.refs_2_
  35.3 1.0 %collective-permute-start.16 = (bf16[8,3584]{1,0:T(8,128)(2,1)S(1)}, bf16[8,3584]{1,0:T(8,128)(2,1)S(1)}, u32[]{:S(2)}, u32[]{:S(2)}) collective-permute-start(bf16[8,3584]{1,0:T(8,128)(2,1)S(1)} %get-tuple-element.10), channel_id=1, source_target_pairs={{0,16},{2,18},{4,20},{6,22},{8,24},{10,26},{12,28},{14,30},{16,0},... | collective-permute-start | bytes 172040 | tf_op jit(solution)/shard_map/ppermute | solution.py:26
  36.3 0.0 collective-permute-done.11.refs_1_
  36.3 1.7 %collective-permute-done.19.refs_7_ = bf16[8,3584]{1,0:T(8,128)(2,1)S(1)} collective-permute-done((bf16[8,3584]{1,0:T(8,128)(2,1)S(1)}, bf16[8,3584]{1,0:T(8,128)(2,1)S(1)}, u32[]{:S(2)}, u32[]{:S(2)}) %collective-permute-start.19) | collective-permute-done | bytes 57376 | tf_op jit(solution)/shard_map/ppermute | solution.py:26
  38.0 0.3 collective-permute-done.18.refs_6_
  38.2 3.4 %collective-permute-done.17.refs_5_ = bf16[8,3584]{1,0:T(8,128)(2,1)S(1)} collective-permute-done((bf16[8,3584]{1,0:T(8,128)(2,1)S(1)}, bf16[8,3584]{1,0:T(8,128)(2,1)S(1)}, u32[]{:S(2)}, u32[]{:S(2)}) %collective-permute-start.17) | collective-permute-done | bytes 57376 | tf_op jit(solution)/shard_map/ppermute | solution.py:26
  41.6 0.0 collective-permute-done.16.refs_4_
  41.6 0.0 copy-done.2
  41.6 0.0 copy-done.3
  41.6 0.7 %shard_map.73 = bf16[8,3584]{1,0:T(8,128)(2,1)} custom-call(s32[1,8]{1,0:T(1,128)S(1)} %bitcast.31, s32[1,8]{1,0:T(1,128)S(1)} %bitcast.32, f32[8,3584]{1,0:T(8,128)S(1)} %slice.83.refs_0_, bf16[8,3584]{1,0:T(8,128)(2,1)S(1)} %collective-permute-done.11.refs_1_, bf16[8,3584]{1,0:T(8,128)(2,1)S(1)} %collective-permute-done.12.refs_2_, ...), custom_call_target="tpu_custom_call" | custom-call | tf_op jit(solution)/shard_map/pallas_call | solution.py:83
  (28 shorter events, 0.3 us)
Async XLA Ops:
  0.0 22.4 %copy-start = (bf16[1,256,3584]{2,1,0:T(8,128)(2,1)S(1)}, bf16[1,256,3584]{2,1,0:T(8,128)(2,1)}, u32[]{:S(2)}) copy-start(bf16[1,256,3584]{2,1,0:T(8,128)(2,1)} %param.11) | copy-start | bytes 5505028
  0.0 10.4 %collective-permute-start.1 = (bf16[8,3584]{1,0:T(8,128)(2,1)}, bf16[8,3584]{1,0:T(8,128)(2,1)S(1)}, u32[]{:S(2)}, u32[]{:S(2)}) collective-permute-start(bf16[8,3584]{1,0:T(8,128)(2,1)} %from_ref.1), channel_id=1, source_target_pairs={{0,2},{2,4},{4,6},{6,0},{1,3},{3,5},{5,7},{7,1},{8,10},{10,12},{12... | collective-permute-start | bytes 172040 | tf_op jit(solution)/shard_map/ppermute | solution.py:16
  3.0 9.1 %collective-permute-start = (bf16[8,3584]{1,0:T(8,128)(2,1)}, bf16[8,3584]{1,0:T(8,128)(2,1)S(1)}, u32[]{:S(2)}, u32[]{:S(2)}) collective-permute-start(bf16[8,3584]{1,0:T(8,128)(2,1)} %from_ref.1), channel_id=1, source_target_pairs={{0,6},{2,0},{4,2},{6,4},{1,7},{3,1},{5,3},{7,5},{8,14},{10,8},{12,... | collective-permute-start | bytes 172040 | tf_op jit(solution)/shard_map/ppermute | solution.py:16
  5.1 14.2 %collective-permute-start.8 = (bf16[8,3584]{1,0:T(8,128)(2,1)}, bf16[8,3584]{1,0:T(8,128)(2,1)S(1)}, u32[]{:S(2)}, u32[]{:S(2)}) collective-permute-start(bf16[8,3584]{1,0:T(8,128)(2,1)} %from_ref.1), channel_id=1, source_target_pairs={{0,20},{2,22},{4,16},{6,18},{8,28},{10,30},{12,24},{14,26},{16,4},... | collective-permute-start | bytes 172040 | tf_op jit(solution)/shard_map/ppermute | solution.py:26
  7.0 6.6 %collective-permute-start.2 = (bf16[8,3584]{1,0:T(8,128)(2,1)}, bf16[8,3584]{1,0:T(8,128)(2,1)S(1)}, u32[]{:S(2)}, u32[]{:S(2)}) collective-permute-start(bf16[8,3584]{1,0:T(8,128)(2,1)} %from_ref.1), channel_id=1, source_target_pairs={{0,4},{2,6},{4,0},{6,2},{1,5},{3,7},{5,1},{7,3},{8,12},{10,14},{12... | collective-permute-start | bytes 172040 | tf_op jit(solution)/shard_map/ppermute | solution.py:16
  9.1 0.9 %copy-start.1 = (bf16[8,3584]{1,0:T(8,128)(2,1)S(1)}, bf16[8,3584]{1,0:T(8,128)(2,1)}, u32[]{:S(2)}) copy-start(bf16[8,3584]{1,0:T(8,128)(2,1)} %from_ref.1) | copy-start | bytes 172036
  10.0 6.8 %copy-start.4 = (bf16[1,3584,256]{2,1,0:T(8,128)(2,1)S(1)}, bf16[1,3584,256]{2,1,0:T(8,128)(2,1)}, u32[]{:S(2)}) copy-start(bf16[1,3584,256]{2,1,0:T(8,128)(2,1)} %param.10) | copy-start | bytes 5505028
  10.0 9.3 %collective-permute-start.6 = (bf16[8,3584]{1,0:T(8,128)(2,1)S(1)}, bf16[8,3584]{1,0:T(8,128)(2,1)S(1)}, u32[]{:S(2)}, u32[]{:S(2)}) collective-permute-start(bf16[8,3584]{1,0:T(8,128)(2,1)S(1)} %shard_map.64), channel_id=1, source_target_pairs={{0,16},{2,18},{4,20},{6,22},{8,24},{10,26},{12,28},{14,30},{16,0},... | collective-permute-start | bytes 172040 | tf_op jit(solution)/shard_map/ppermute | solution.py:26
  10.4 4.9 %collective-permute-start.3 = (bf16[8,3584]{1,0:T(8,128)(2,1)S(1)}, bf16[8,3584]{1,0:T(8,128)(2,1)S(1)}, u32[]{:S(2)}, u32[]{:S(2)}) collective-permute-start(bf16[8,3584]{1,0:T(8,128)(2,1)S(1)} %collective-permute-done.1), channel_id=1, source_target_pairs={{0,16},{2,18},{4,20},{6,22},{8,24},{10,26},{12,28},{14,30},{16,0},... | collective-permute-start | bytes 172040 | tf_op jit(solution)/shard_map/ppermute | solution.py:26
  12.1 7.2 %collective-permute-start.7 = (bf16[8,3584]{1,0:T(8,128)(2,1)S(1)}, bf16[8,3584]{1,0:T(8,128)(2,1)S(1)}, u32[]{:S(2)}, u32[]{:S(2)}) collective-permute-start(bf16[8,3584]{1,0:T(8,128)(2,1)S(1)} %collective-permute-done), channel_id=1, source_target_pairs={{0,16},{2,18},{4,20},{6,22},{8,24},{10,26},{12,28},{14,30},{16,0},... | collective-permute-start | bytes 172040 | tf_op jit(solution)/shard_map/ppermute | solution.py:26
  13.6 3.6 %copy-start.5 = (bf16[1,3584,256]{2,1,0:T(8,128)(2,1)S(1)}, bf16[1,3584,256]{2,1,0:T(8,128)(2,1)}, u32[]{:S(2)}) copy-start(bf16[1,3584,256]{2,1,0:T(8,128)(2,1)} %param.9) | copy-start | bytes 5505028
  15.2 1.5 %collective-permute-start.4 = (bf16[32,3584]{1,0:T(8,128)(2,1)S(1)}, bf16[32,3584]{1,0:T(8,128)(2,1)S(1)}, u32[]{:S(2)}, u32[]{:S(2)}) collective-permute-start(bf16[32,3584]{1,0:T(8,128)(2,1)S(1)} %shard_map.65), channel_id=1, source_target_pairs={{0,8},{8,0},{16,24},{24,16},{1,9},{9,1},{17,25},{25,17},{2,10},{10... | collective-permute-start | bytes 688136 | tf_op jit(solution)/shard_map/ppermute | solution.py:30
  17.7 4.7 %collective-permute-start.5 = (bf16[64,512]{1,0:T(8,128)(2,1)S(1)}, bf16[64,512]{1,0:T(8,128)(2,1)S(1)}, u32[]{:S(2)}, u32[]{:S(2)}) collective-permute-start(bf16[64,512]{1,0:T(8,128)(2,1)S(1)} %fusion.25.refs_1_), channel_id=1, source_target_pairs={{0,1},{1,0},{2,3},{3,2},{4,5},{5,4},{6,7},{7,6},{8,9},{9,8},{10,11... | collective-permute-start | bytes 196616 | tf_op jit(solution)/shard_map/ppermute | solution.py:16
  19.3 1.6 %collective-permute-start.9 = (bf16[32,3584]{1,0:T(8,128)(2,1)S(1)}, bf16[32,3584]{1,0:T(8,128)(2,1)S(1)}, u32[]{:S(2)}, u32[]{:S(2)}) collective-permute-start(bf16[32,3584]{1,0:T(8,128)(2,1)S(1)} %pad_maximum_fusion.4.refs_0_), channel_id=1, source_target_pairs={{0,8},{8,0},{16,24},{24,16},{1,9},{9,1},{17,25},{25,17},{2,10},{10... | collective-permute-start | bytes 688136 | tf_op jit(solution)/shard_map/ppermute | solution.py:30
  21.8 4.3 %collective-permute-start.14 = (bf16[64,512]{1,0:T(8,128)(2,1)S(1)}, bf16[64,512]{1,0:T(8,128)(2,1)S(1)}, u32[]{:S(2)}, u32[]{:S(2)}) collective-permute-start(bf16[64,512]{1,0:T(8,128)(2,1)S(1)} %fusion.14.refs_1_), channel_id=1, source_target_pairs={{0,1},{1,0},{2,3},{3,2},{4,5},{5,4},{6,7},{7,6},{8,9},{9,8},{10,11... | collective-permute-start | bytes 196616 | tf_op jit(solution)/shard_map/ppermute | solution.py:16
  22.8 1.6 %collective-permute-start.10 = (bf16[32,3584]{1,0:T(8,128)(2,1)S(1)}, bf16[32,3584]{1,0:T(8,128)(2,1)S(1)}, u32[]{:S(2)}, u32[]{:S(2)}) collective-permute-start(bf16[32,3584]{1,0:T(8,128)(2,1)S(1)} %slice.122), channel_id=1, source_target_pairs={{0,8},{8,0},{16,24},{24,16},{1,9},{9,1},{17,25},{25,17},{2,10},{10... | collective-permute-start | bytes 688136 | tf_op jit(solution)/shard_map/ppermute | solution.py:30
  26.6 15.0 %copy-start.2 = (s32[8,1]{0,1:T(1,128)S(1)}, s32[8,1]{0,1:T(1,128)}, u32[]{:S(2)}) copy-start(s32[8,1]{0,1:T(1,128)} %param.7) | copy-start | bytes 100
  26.6 15.0 %copy-start.3 = (s32[8,1]{0,1:T(1,128)S(1)}, s32[8,1]{0,1:T(1,128)}, u32[]{:S(2)}) copy-start(s32[8,1]{0,1:T(1,128)} %param.8) | copy-start | bytes 100
  26.6 2.7 %collective-permute-start.15 = (bf16[32,3584]{1,0:T(8,128)(2,1)S(1)}, bf16[32,3584]{1,0:T(8,128)(2,1)S(1)}, u32[]{:S(2)}, u32[]{:S(2)}) collective-permute-start(bf16[32,3584]{1,0:T(8,128)(2,1)S(1)} %slice.121), channel_id=1, source_target_pairs={{0,8},{8,0},{16,24},{24,16},{1,9},{9,1},{17,25},{25,17},{2,10},{10... | collective-permute-start | bytes 688136 | tf_op jit(solution)/shard_map/ppermute | solution.py:30
  26.7 8.0 %collective-permute-start.13 = (bf16[8,3584]{1,0:T(8,128)(2,1)S(1)}, bf16[8,3584]{1,0:T(8,128)(2,1)S(1)}, u32[]{:S(2)}, u32[]{:S(2)}) collective-permute-start(bf16[8,3584]{1,0:T(8,128)(2,1)S(1)} %get-tuple-element.11), channel_id=1, source_target_pairs={{0,4},{2,6},{4,0},{6,2},{1,5},{3,7},{5,1},{7,3},{8,12},{10,14},{12... | collective-permute-start | bytes 172040 | tf_op jit(solution)/shard_map/ppermute | solution.py:16
  27.1 8.2 %collective-permute-start.12 = (bf16[8,3584]{1,0:T(8,128)(2,1)S(1)}, bf16[8,3584]{1,0:T(8,128)(2,1)S(1)}, u32[]{:S(2)}, u32[]{:S(2)}) collective-permute-start(bf16[8,3584]{1,0:T(8,128)(2,1)S(1)} %get-tuple-element.12), channel_id=1, source_target_pairs={{0,6},{2,0},{4,2},{6,4},{1,7},{3,1},{5,3},{7,5},{8,14},{10,8},{12,... | collective-permute-start | bytes 172040 | tf_op jit(solution)/shard_map/ppermute | solution.py:16
  28.8 7.5 %collective-permute-start.11 = (bf16[8,3584]{1,0:T(8,128)(2,1)S(1)}, bf16[8,3584]{1,0:T(8,128)(2,1)S(1)}, u32[]{:S(2)}, u32[]{:S(2)}) collective-permute-start(bf16[8,3584]{1,0:T(8,128)(2,1)S(1)} %get-tuple-element.13), channel_id=1, source_target_pairs={{0,2},{2,4},{4,6},{6,0},{1,3},{3,5},{5,7},{7,1},{8,10},{10,12},{12... | collective-permute-start | bytes 172040 | tf_op jit(solution)/shard_map/ppermute | solution.py:16
  29.4 8.6 %collective-permute-start.19 = (bf16[8,3584]{1,0:T(8,128)(2,1)S(1)}, bf16[8,3584]{1,0:T(8,128)(2,1)S(1)}, u32[]{:S(2)}, u32[]{:S(2)}) collective-permute-start(bf16[8,3584]{1,0:T(8,128)(2,1)S(1)} %get-tuple-element.7), channel_id=1, source_target_pairs={{0,20},{2,22},{4,16},{6,18},{8,28},{10,30},{12,24},{14,26},{16,4},... | collective-permute-start | bytes 172040 | tf_op jit(solution)/shard_map/ppermute | solution.py:26
  32.4 5.9 %collective-permute-start.18 = (bf16[8,3584]{1,0:T(8,128)(2,1)S(1)}, bf16[8,3584]{1,0:T(8,128)(2,1)S(1)}, u32[]{:S(2)}, u32[]{:S(2)}) collective-permute-start(bf16[8,3584]{1,0:T(8,128)(2,1)S(1)} %get-tuple-element.8), channel_id=1, source_target_pairs={{0,22},{2,16},{4,18},{6,20},{8,30},{10,24},{12,26},{14,28},{16,6},... | collective-permute-start | bytes 172040 | tf_op jit(solution)/shard_map/ppermute | solution.py:26
  34.7 6.9 %collective-permute-start.17 = (bf16[8,3584]{1,0:T(8,128)(2,1)S(1)}, bf16[8,3584]{1,0:T(8,128)(2,1)S(1)}, u32[]{:S(2)}, u32[]{:S(2)}) collective-permute-start(bf16[8,3584]{1,0:T(8,128)(2,1)S(1)} %get-tuple-element.9), channel_id=1, source_target_pairs={{0,18},{2,20},{4,22},{6,16},{8,26},{10,28},{12,30},{14,24},{16,2},... | collective-permute-start | bytes 172040 | tf_op jit(solution)/shard_map/ppermute | solution.py:26
  35.3 6.3 %collective-permute-start.16 = (bf16[8,3584]{1,0:T(8,128)(2,1)S(1)}, bf16[8,3584]{1,0:T(8,128)(2,1)S(1)}, u32[]{:S(2)}, u32[]{:S(2)}) collective-permute-start(bf16[8,3584]{1,0:T(8,128)(2,1)S(1)} %get-tuple-element.10), channel_id=1, source_target_pairs={{0,16},{2,18},{4,20},{6,22},{8,24},{10,26},{12,28},{14,30},{16,0},... | collective-permute-start | bytes 172040 | tf_op jit(solution)/shard_map/ppermute | solution.py:26

commit v7 on v6

--- a/solution.py
+++ b/solution.py
@@ -11,17 +11,26 @@
 MIB = 1024 * 1024
 
 
-def shift(value, axis, by):
+def rotate(value, axis, by):
     size = lax.axis_size(axis)
     return lax.ppermute(value, axis, [(i, (i + by) % size) for i in range(size)])
 
 
-def shift_expert(value, by_expert, by_tp=0):
+def rotate_experts(value, by):
+    groups = lax.axis_size("grp")
+    return lax.ppermute(value, "grp", [(i, (i + 2 * by) % groups) for i in range(groups)])
+
+
+def partner(place, step, size):
+    return place ^ abs(step) if size & (size - 1) == 0 else (place + step) % size
+
+
+def exchange(value, by_expert, step):
     groups, n_tp = lax.axis_size("grp"), lax.axis_size("tp")
     pairs = []
     for g in range(groups):
         for t in range(n_tp):
-            to = (g + 2 * by_expert) % groups * n_tp + (t + by_tp) % n_tp
+            to = (g + 2 * by_expert) % groups * n_tp + partner(t, step, n_tp)
             pairs.append((g * n_tp + t, to))
     return lax.ppermute(value, ("grp", "tp"), pairs)
 
@@ -99,7 +108,7 @@
         parts = [jnp.dot(rows, w, preferred_element_type=f32) for w in (w_gate, w_up)]
         part = jnp.concatenate(parts, axis=1)
         sent = part.astype(bf16)
-        return part, sent, [shift(sent, "ex", s) for s in range(1, n_ex)]
+        return part, sent, [rotate(sent, "ex", s) for s in range(1, n_ex)]
 
     def partial_out(part, others, kept_flops, part_flops=0, *earlier):
         if part_flops:
@@ -115,27 +124,26 @@
         return out[:kept] + swapped
 
     held = copied(tokens)
-    places = (0, n_tp - 1, *range(1, n_tp - 1))
-    blocks = [held] + [shift(tokens, "tp", t) for t in places[1:]]
-    straight = n_tp // 2
-    far = [[shift_expert(tokens, s, t) if t == straight else shift_expert(rows, s) for t, rows in zip(places, blocks)] for s in range(1, experts)]
+    places = tuple(range(n_tp))
+    blocks = [held] + [exchange(tokens, 0, t) for t in places[1:]]
+    far = [[rotate_experts(rows, s) for rows in blocks] for s in range(1, experts)]
     near = jnp.concatenate(blocks, axis=0)
-    near_swapped = swap_half(after(near, *(line[places.index(1)] for line in far)))
+    near_swapped = swap_half(after(near, *(line[1] for line in far)))
     near = jnp.concatenate([near, near_swapped], axis=0)
     near_part, near_sent, near_others = partial_sums(near)
-    far = [after(rows, near_sent) if i > 1 else rows for line in far for i, rows in enumerate(line)]
+    far = [after(rows, near_sent) if i == n_tp - 1 else rows for line in far for i, rows in enumerate(line)]
     far = jnp.concatenate(far, axis=0)
     far_swapped = swap_half(far)
     far = jnp.concatenate([after(far, flops=3450000000), far_swapped], axis=0)
     far_part, far_sent, far_others = partial_sums(far)
-    near_out = partial_out(near_part, [after(other, far_sent) for other in near_others], 3450000000, 3450000000)
+    near_out = partial_out(near_part, [after(other, far_sent) for other in near_others], 3450000000, 0)
     near_out = near_out.reshape(n_tp, count, width)
     near_sent = near_out[1:].astype(bf16)
-    pieces = [near_out[0]] + [shift(near_sent[i], "tp", -t) for i, t in enumerate(places[1:])]
+    pieces = [near_out[0]] + [exchange(near_sent[i], 0, -t) for i, t in enumerate(places[1:])]
     far_out = partial_out(far_part, [after(other, near_sent) for other in far_others], 0, 0)
     far_out = far_out.reshape(experts - 1, n_tp, count, width).astype(bf16)
     for s in range(1, experts):
-        pieces += [shift_expert(far_out[experts - 1 - s, i], s, -t) for i, t in enumerate(places)]
+        pieces += [exchange(far_out[experts - 1 - s, i], s, -t) for i, t in enumerate(places)]
     return mix(expert_ids, gate_levels, pieces, n_tp, experts)
 
 

time: 42.5 us -> 39.5 us (0.929)
  waiting for transfers between devices: 14.1 us -> 9.18 us
  starting transfers between devices: 23.4 us -> 25.3 us
    ppermute x16, waiting for transfers between devices: 9.68 us -> 6.24 us  [the longest x10 5.41 us: exchange(): return lax.ppermute(value, ('grp', 'tp'), pairs)]
    ppermute x16, starting transfers between devices: 23.2 us -> 25 us  [the longest x10 16.9 us: exchange(): return lax.ppermute(value, ('grp', 'tp'), pairs)]
    ppermute x4, waiting for transfers between devices: 4.41 us -> 2.93 us  [swap_half(): lax.ppermute(value, 'grp', [(i, i ^ 1) for i in range(lax.axis_size('grp'...]
  transfers between devices with their start and end apart: 20 -> 20, of which waited for: 9 -> 10; matrix products, arithmetic and copies ran while one was open for 6% -> 6% of each run, Pallas kernels for 0% -> 0%
where the time goes in v7:
time: 39.5 us; the launch traced here: 39.3 us
  starting transfers between devices  25.3 us (64%)
  waiting for transfers between devices  9.18 us (23%)
  matrix products  2.6 us (7%)
  local copies, waits for them, and re-layouts  1.02 us (3%)
  Pallas kernels  0.75 us (2%)
    ppermute x10, starting transfers between devices, exchange(): return lax.ppermute(value, ('grp', 'tp'), pairs)  16.9 us
    ppermute x10, waiting for transfers between devices, exchange(): return lax.ppermute(value, ('grp', 'tp'), pairs)  5.41 us
    ppermute x4, starting transfers between devices, rotate_experts(): lax.ppermute(value, 'grp', [(i, (i + 2 * by) % groups) for i in range(gro...  5.07 us
    ppermute x2, starting transfers between devices, rotate(): lax.ppermute(value, axis, [(i, (i + by) % size) for i in range(size)])  2.99 us
    ppermute x4, waiting for transfers between devices, swap_half(): lax.ppermute(value, 'grp', [(i, i ^ 1) for i in range(lax.axis_size('grp'...  2.93 us
    dot_general x4, matrix products, partial_sums(): jnp.dot(rows, w, preferred_element_type=f32)  1.76 us
    unnamed x16, local copies, waits for them, and re-layouts  0.9 us
    dot_general x2, matrix products, partial_out(): out = jnp.dot(hidden, w_down, preferred_element_type=f32)  0.83 us
  transfers between devices with their start and end apart: 20, of which 10 were waited for; matrix products, arithmetic and copies ran while one was open for 6% of the time, Pallas kernels for 0%

profile of v7, /device:TPU:0, one launch (start us, length us, event | category | flops | bytes accessed | tf_op | source)
XLA Modules:
  0.0 39.3 jit_solution(16101129036215110033)
XLA Ops:
  0.0 0.0 copy-start
  0.0 3.0 %collective-permute-start = (bf16[8,3584]{1,0:T(8,128)(2,1)}, bf16[8,3584]{1,0:T(8,128)(2,1)S(1)}, u32[]{:S(2)}, u32[]{:S(2)}) collective-permute-start(bf16[8,3584]{1,0:T(8,128)(2,1)} %from_ref.1), channel_id=1, source_target_pairs={{0,2},{2,0},{4,6},{6,4},{8,10},{10,8},{12,14},{14,12},{16,18},{18,... | collective-permute-start | bytes 172040 | tf_op jit(solution)/shard_map/ppermute | solution.py:35
  3.0 2.5 %collective-permute-start.2 = (bf16[8,3584]{1,0:T(8,128)(2,1)}, bf16[8,3584]{1,0:T(8,128)(2,1)S(1)}, u32[]{:S(2)}, u32[]{:S(2)}) collective-permute-start(bf16[8,3584]{1,0:T(8,128)(2,1)} %from_ref.1), channel_id=1, source_target_pairs={{0,6},{2,4},{4,2},{6,0},{8,14},{10,12},{12,10},{14,8},{16,22},{18,... | collective-permute-start | bytes 172040 | tf_op jit(solution)/shard_map/ppermute | solution.py:35
  5.5 0.1 collective-permute-start.1
  5.6 0.0 copy-start.1
  5.6 0.9 %copy-done.1 = bf16[8,3584]{1,0:T(8,128)(2,1)S(1)} copy-done((bf16[8,3584]{1,0:T(8,128)(2,1)S(1)}, bf16[8,3584]{1,0:T(8,128)(2,1)}, u32[]{:S(2)}) %copy-start.1) | copy-done | bytes 57368
  6.5 0.0 copy-start.4
  6.5 1.5 %collective-permute-start.6 = (bf16[8,3584]{1,0:T(8,128)(2,1)S(1)}, bf16[8,3584]{1,0:T(8,128)(2,1)S(1)}, u32[]{:S(2)}, u32[]{:S(2)}) collective-permute-start(bf16[8,3584]{1,0:T(8,128)(2,1)S(1)} %shard_map.64), channel_id=1, source_target_pairs={{0,16},{8,24},{16,0},{24,8},{1,17},{9,25},{17,1},{25,9},{2,18},{10... | collective-permute-start | bytes 172040 | tf_op jit(solution)/shard_map/ppermute | solution.py:21
  8.0 0.0 collective-permute-done
  8.0 0.6 %collective-permute-start.3 = (bf16[8,3584]{1,0:T(8,128)(2,1)S(1)}, bf16[8,3584]{1,0:T(8,128)(2,1)S(1)}, u32[]{:S(2)}, u32[]{:S(2)}) collective-permute-start(bf16[8,3584]{1,0:T(8,128)(2,1)S(1)} %collective-permute-done), channel_id=1, source_target_pairs={{0,16},{8,24},{16,0},{24,8},{1,17},{9,25},{17,1},{25,9},{2,18},{10... | collective-permute-start | bytes 172040 | tf_op jit(solution)/shard_map/ppermute | solution.py:21
  8.6 1.3 %collective-permute-done.2 = bf16[8,3584]{1,0:T(8,128)(2,1)S(1)} collective-permute-done((bf16[8,3584]{1,0:T(8,128)(2,1)}, bf16[8,3584]{1,0:T(8,128)(2,1)S(1)}, u32[]{:S(2)}, u32[]{:S(2)}) %collective-permute-start.2) | collective-permute-done | bytes 57376 | tf_op jit(solution)/shard_map/ppermute | solution.py:35
  9.9 1.5 %collective-permute-start.8 = (bf16[8,3584]{1,0:T(8,128)(2,1)S(1)}, bf16[8,3584]{1,0:T(8,128)(2,1)S(1)}, u32[]{:S(2)}, u32[]{:S(2)}) collective-permute-start(bf16[8,3584]{1,0:T(8,128)(2,1)S(1)} %collective-permute-done.2), channel_id=1, source_target_pairs={{0,16},{8,24},{16,0},{24,8},{1,17},{9,25},{17,1},{25,9},{2,18},{10... | collective-permute-start | bytes 172040 | tf_op jit(solution)/shard_map/ppermute | solution.py:21
  11.4 0.1 collective-permute-done.1
  11.6 1.5 %collective-permute-start.7 = (bf16[8,3584]{1,0:T(8,128)(2,1)S(1)}, bf16[8,3584]{1,0:T(8,128)(2,1)S(1)}, u32[]{:S(2)}, u32[]{:S(2)}) collective-permute-start(bf16[8,3584]{1,0:T(8,128)(2,1)S(1)} %collective-permute-done.1), channel_id=1, source_target_pairs={{0,16},{8,24},{16,0},{24,8},{1,17},{9,25},{17,1},{25,9},{2,18},{10... | collective-permute-start | bytes 172040 | tf_op jit(solution)/shard_map/ppermute | solution.py:21
  13.1 0.0 copy-start.5
  13.1 0.0 collective-permute-done.3.refs_1_
  13.1 0.1 collective-permute-start.4
  13.2 1.5 %collective-permute-done.4 = bf16[32,3584]{1,0:T(8,128)(2,1)S(1)} collective-permute-done((bf16[32,3584]{1,0:T(8,128)(2,1)S(1)}, bf16[32,3584]{1,0:T(8,128)(2,1)S(1)}, u32[]{:S(2)}, u32[]{:S(2)}) %collective-permute-start.4) | collective-permute-done | bytes 229408 | tf_op jit(solution)/shard_map/ppermute | solution.py:39
  14.7 0.0 copy-done.4
  14.7 0.4 %fusion.6 = f32[64,256]{1,0:T(8,128)S(1)} fusion(bf16[64,3584]{1,0:T(8,128)(2,1)S(1)} %constant_dynamic-update-slice_fusion, bf16[1,3584,256]{2,1,0:T(8,128)(2,1)S(1)} %copy-done.4), kind=kOutput, calls=%fused_computation.6 | convolution fusion | flops 117440512 | bytes 2359296 | tf_op jit(solution)/shard_map/dot_general | solution.py:108
  15.2 0.0 copy-done.5
  15.2 0.4 %fusion.10 = f32[64,256]{1,0:T(8,128)S(1)} fusion(bf16[64,3584]{1,0:T(8,128)(2,1)S(1)} %constant_dynamic-update-slice_fusion, bf16[1,3584,256]{2,1,0:T(8,128)(2,1)S(1)} %copy-done.5), kind=kOutput, calls=%fused_computation.10 | convolution fusion | flops 117440512 | bytes 2359296 | tf_op jit(solution)/shard_map/dot_general | solution.py:108
  15.6 0.0 collective-permute-done.8.refs_0_
  15.7 0.0 collective-permute-done.6
  15.7 0.1 collective-permute-done.7
  15.8 0.1 collective-permute-start.9
  15.9 1.5 %collective-permute-start.5 = (bf16[64,512]{1,0:T(8,128)(2,1)S(1)}, bf16[64,512]{1,0:T(8,128)(2,1)S(1)}, u32[]{:S(2)}, u32[]{:S(2)}) collective-permute-start(bf16[64,512]{1,0:T(8,128)(2,1)S(1)} %fusion.15.refs_1_), channel_id=1, source_target_pairs={{0,1},{1,0},{2,3},{3,2},{4,5},{5,4},{6,7},{7,6},{8,9},{9,8},{10,11... | collective-permute-start | bytes 196616 | tf_op jit(solution)/shard_map/ppermute | solution.py:16
  17.4 0.0 collective-permute-done.9
  17.4 0.4 %fusion.4 = f32[64,256]{1,0:T(8,128)S(1)} fusion(bf16[1,3584,256]{2,1,0:T(8,128)(2,1)S(1)} %copy-done.4, bf16[32,3584]{1,0:T(8,128)(2,1)S(1)} %collective-permute-done.9, bf16[32,3584]{1,0:T(8,128)(2,1)S(1)} %shard_map.67), kind=kOutput, calls=%fused_computation.4 | convolution fusion | flops 118358016 | bytes 2359296 | tf_op jit(solution)/shard_map/dot_general | solution.py:108
  17.9 0.4 %fusion.8 = f32[64,256]{1,0:T(8,128)S(1)} fusion(bf16[1,3584,256]{2,1,0:T(8,128)(2,1)S(1)} %copy-done.5, bf16[32,3584]{1,0:T(8,128)(2,1)S(1)} %collective-permute-done.9, bf16[32,3584]{1,0:T(8,128)(2,1)S(1)} %shard_map.67), kind=kOutput, calls=%fused_computation.8 | convolution fusion | flops 118358016 | bytes 2359296 | tf_op jit(solution)/shard_map/dot_general | solution.py:108
  18.3 1.5 %collective-permute-start.14 = (bf16[64,512]{1,0:T(8,128)(2,1)S(1)}, bf16[64,512]{1,0:T(8,128)(2,1)S(1)}, u32[]{:S(2)}, u32[]{:S(2)}) collective-permute-start(bf16[64,512]{1,0:T(8,128)(2,1)S(1)} %fusion.14.refs_1_), channel_id=1, source_target_pairs={{0,1},{1,0},{2,3},{3,2},{4,5},{5,4},{6,7},{7,6},{8,9},{9,8},{10,11... | collective-permute-start | bytes 196616 | tf_op jit(solution)/shard_map/ppermute | solution.py:16
  19.8 0.5 %collective-permute-done.5.refs_0_ = bf16[64,512]{1,0:T(8,128)(2,1)S(1)} collective-permute-done((bf16[64,512]{1,0:T(8,128)(2,1)S(1)}, bf16[64,512]{1,0:T(8,128)(2,1)S(1)}, u32[]{:S(2)}, u32[]{:S(2)}) %collective-permute-start.5) | collective-permute-done | bytes 65568 | tf_op jit(solution)/shard_map/ppermute | solution.py:16
  20.4 0.0 copy-done
  20.4 0.4 %fusion.2.refs_0_ = f32[64,3584]{1,0:T(8,128)S(1)} fusion(bf16[1,256,3584]{2,1,0:T(8,128)(2,1)S(1)} %copy-done, f32[64,512]{1,0:T(8,128)S(1)} %convert_add_fusion.1), kind=kOutput, calls=%fused_computation.2 | convolution fusion | flops 117538816 | bytes 2883584 | tf_op jit(solution)/shard_map/dot_general | solution.py:119
  20.8 0.1 collective-permute-start.10
  20.9 1.5 %collective-permute-done.10 = bf16[32,3584]{1,0:T(8,128)(2,1)S(1)} collective-permute-done((bf16[32,3584]{1,0:T(8,128)(2,1)S(1)}, bf16[32,3584]{1,0:T(8,128)(2,1)S(1)}, u32[]{:S(2)}, u32[]{:S(2)}) %collective-permute-start.10) | collective-permute-done | bytes 229408 | tf_op jit(solution)/shard_map/ppermute | solution.py:39
  22.4 0.1 fusion.26
  22.5 0.2 collective-permute-done.14.refs_0_
  22.7 0.4 %fusion = f32[64,3584]{1,0:T(8,128)S(1)} fusion(bf16[1,256,3584]{2,1,0:T(8,128)(2,1)S(1)} %copy-done, f32[64,512]{1,0:T(8,128)S(1)} %convert_add_fusion), kind=kOutput, calls=%fused_computation | convolution fusion | flops 117538816 | bytes 2883584 | tf_op jit(solution)/shard_map/dot_general | solution.py:119
  23.1 0.0 copy-start.2
  23.1 0.0 copy-start.3
  23.2 0.1 collective-permute-start.15
  23.3 2.5 %collective-permute-start.13 = (bf16[8,3584]{1,0:T(8,128)(2,1)S(1)}, bf16[8,3584]{1,0:T(8,128)(2,1)S(1)}, u32[]{:S(2)}, u32[]{:S(2)}) collective-permute-start(bf16[8,3584]{1,0:T(8,128)(2,1)S(1)} %get-tuple-element.11), channel_id=1, source_target_pairs={{0,6},{2,4},{4,2},{6,0},{8,14},{10,12},{12,10},{14,8},{16,22},{18,... | collective-permute-start | bytes 172040 | tf_op jit(solution)/shard_map/ppermute | solution.py:35
  25.7 0.4 %collective-permute-start.12 = (bf16[8,3584]{1,0:T(8,128)(2,1)S(1)}, bf16[8,3584]{1,0:T(8,128)(2,1)S(1)}, u32[]{:S(2)}, u32[]{:S(2)}) collective-permute-start(bf16[8,3584]{1,0:T(8,128)(2,1)S(1)} %get-tuple-element.12), channel_id=1, source_target_pairs={{0,4},{2,6},{4,0},{6,2},{8,12},{10,14},{12,8},{14,10},{16,20},{18,... | collective-permute-start | bytes 172040 | tf_op jit(solution)/shard_map/ppermute | solution.py:35
  26.1 1.6 %collective-permute-start.11 = (bf16[8,3584]{1,0:T(8,128)(2,1)S(1)}, bf16[8,3584]{1,0:T(8,128)(2,1)S(1)}, u32[]{:S(2)}, u32[]{:S(2)}) collective-permute-start(bf16[8,3584]{1,0:T(8,128)(2,1)S(1)} %get-tuple-element.13), channel_id=1, source_target_pairs={{0,2},{2,0},{4,6},{6,4},{8,10},{10,8},{12,14},{14,12},{16,18},{18,... | collective-permute-start | bytes 172040 | tf_op jit(solution)/shard_map/ppermute | solution.py:35
  27.7 0.0 collective-permute-done.15
  27.8 3.4 %collective-permute-start.19 = (bf16[8,3584]{1,0:T(8,128)(2,1)S(1)}, bf16[8,3584]{1,0:T(8,128)(2,1)S(1)}, u32[]{:S(2)}, u32[]{:S(2)}) collective-permute-start(bf16[8,3584]{1,0:T(8,128)(2,1)S(1)} %get-tuple-element.7), channel_id=1, source_target_pairs={{0,22},{2,20},{4,18},{6,16},{8,30},{10,28},{12,26},{14,24},{16,6},... | collective-permute-start | bytes 172040 | tf_op jit(solution)/shard_map/ppermute | solution.py:35
  31.2 0.0 collective-permute-start.18
  31.2 0.0 collective-permute-done.13.refs_3_
  31.2 2.9 %collective-permute-start.17 = (bf16[8,3584]{1,0:T(8,128)(2,1)S(1)}, bf16[8,3584]{1,0:T(8,128)(2,1)S(1)}, u32[]{:S(2)}, u32[]{:S(2)}) collective-permute-start(bf16[8,3584]{1,0:T(8,128)(2,1)S(1)} %get-tuple-element.9), channel_id=1, source_target_pairs={{0,18},{2,16},{4,22},{6,20},{8,26},{10,24},{12,30},{14,28},{16,2},... | collective-permute-start | bytes 172040 | tf_op jit(solution)/shard_map/ppermute | solution.py:35
  34.1 0.0 collective-permute-done.12.refs_2_
  34.1 0.5 %collective-permute-start.16 = (bf16[8,3584]{1,0:T(8,128)(2,1)S(1)}, bf16[8,3584]{1,0:T(8,128)(2,1)S(1)}, u32[]{:S(2)}, u32[]{:S(2)}) collective-permute-start(bf16[8,3584]{1,0:T(8,128)(2,1)S(1)} %get-tuple-element.10), channel_id=1, source_target_pairs={{0,16},{2,18},{4,20},{6,22},{8,24},{10,26},{12,28},{14,30},{16,0},... | collective-permute-start | bytes 172040 | tf_op jit(solution)/shard_map/ppermute | solution.py:35
  34.6 0.0 collective-permute-done.11.refs_1_
  34.6 0.5 %collective-permute-done.19.refs_7_ = bf16[8,3584]{1,0:T(8,128)(2,1)S(1)} collective-permute-done((bf16[8,3584]{1,0:T(8,128)(2,1)S(1)}, bf16[8,3584]{1,0:T(8,128)(2,1)S(1)}, u32[]{:S(2)}, u32[]{:S(2)}) %collective-permute-start.19) | collective-permute-done | bytes 57376 | tf_op jit(solution)/shard_map/ppermute | solution.py:35
  35.1 2.8 %collective-permute-done.18.refs_6_ = bf16[8,3584]{1,0:T(8,128)(2,1)S(1)} collective-permute-done((bf16[8,3584]{1,0:T(8,128)(2,1)S(1)}, bf16[8,3584]{1,0:T(8,128)(2,1)S(1)}, u32[]{:S(2)}, u32[]{:S(2)}) %collective-permute-start.18) | collective-permute-done | bytes 57376 | tf_op jit(solution)/shard_map/ppermute | solution.py:35
  37.9 0.0 collective-permute-done.17.refs_5_
  37.9 0.6 %collective-permute-done.16.refs_4_ = bf16[8,3584]{1,0:T(8,128)(2,1)S(1)} collective-permute-done((bf16[8,3584]{1,0:T(8,128)(2,1)S(1)}, bf16[8,3584]{1,0:T(8,128)(2,1)S(1)}, u32[]{:S(2)}, u32[]{:S(2)}) %collective-permute-start.16) | collective-permute-done | bytes 57376 | tf_op jit(solution)/shard_map/ppermute | solution.py:35
  38.6 0.0 copy-done.2
  38.6 0.0 copy-done.3
  38.6 0.7 %shard_map.71 = bf16[8,3584]{1,0:T(8,128)(2,1)} custom-call(s32[1,8]{1,0:T(1,128)S(1)} %bitcast.31, s32[1,8]{1,0:T(1,128)S(1)} %bitcast.32, f32[8,3584]{1,0:T(8,128)S(1)} %slice.83.refs_0_, bf16[8,3584]{1,0:T(8,128)(2,1)S(1)} %collective-permute-done.11.refs_1_, bf16[8,3584]{1,0:T(8,128)(2,1)S(1)} %collective-permute-done.12.refs_2_, ...), custom_call_target="tpu_custom_call" | custom-call | tf_op jit(solution)/shard_map/pallas_call | solution.py:92
  (25 shorter events, 0.3 us)
Async XLA Ops:
  0.0 20.4 %copy-start = (bf16[1,256,3584]{2,1,0:T(8,128)(2,1)S(1)}, bf16[1,256,3584]{2,1,0:T(8,128)(2,1)}, u32[]{:S(2)}) copy-start(bf16[1,256,3584]{2,1,0:T(8,128)(2,1)} %param.11) | copy-start | bytes 5505028
  0.0 8.0 %collective-permute-start = (bf16[8,3584]{1,0:T(8,128)(2,1)}, bf16[8,3584]{1,0:T(8,128)(2,1)S(1)}, u32[]{:S(2)}, u32[]{:S(2)}) collective-permute-start(bf16[8,3584]{1,0:T(8,128)(2,1)} %from_ref.1), channel_id=1, source_target_pairs={{0,2},{2,0},{4,6},{6,4},{8,10},{10,8},{12,14},{14,12},{16,18},{18,... | collective-permute-start | bytes 172040 | tf_op jit(solution)/shard_map/ppermute | solution.py:35
  3.0 6.9 %collective-permute-start.2 = (bf16[8,3584]{1,0:T(8,128)(2,1)}, bf16[8,3584]{1,0:T(8,128)(2,1)S(1)}, u32[]{:S(2)}, u32[]{:S(2)}) collective-permute-start(bf16[8,3584]{1,0:T(8,128)(2,1)} %from_ref.1), channel_id=1, source_target_pairs={{0,6},{2,4},{4,2},{6,0},{8,14},{10,12},{12,10},{14,8},{16,22},{18,... | collective-permute-start | bytes 172040 | tf_op jit(solution)/shard_map/ppermute | solution.py:35
  5.5 6.1 %collective-permute-start.1 = (bf16[8,3584]{1,0:T(8,128)(2,1)}, bf16[8,3584]{1,0:T(8,128)(2,1)S(1)}, u32[]{:S(2)}, u32[]{:S(2)}) collective-permute-start(bf16[8,3584]{1,0:T(8,128)(2,1)} %from_ref.1), channel_id=1, source_target_pairs={{0,4},{2,6},{4,0},{6,2},{8,12},{10,14},{12,8},{14,10},{16,20},{18,... | collective-permute-start | bytes 172040 | tf_op jit(solution)/shard_map/ppermute | solution.py:35
  5.6 0.9 %copy-start.1 = (bf16[8,3584]{1,0:T(8,128)(2,1)S(1)}, bf16[8,3584]{1,0:T(8,128)(2,1)}, u32[]{:S(2)}) copy-start(bf16[8,3584]{1,0:T(8,128)(2,1)} %from_ref.1) | copy-start | bytes 172036
  6.5 8.2 %copy-start.4 = (bf16[1,3584,256]{2,1,0:T(8,128)(2,1)S(1)}, bf16[1,3584,256]{2,1,0:T(8,128)(2,1)}, u32[]{:S(2)}) copy-start(bf16[1,3584,256]{2,1,0:T(8,128)(2,1)} %param.10) | copy-start | bytes 5505028
  6.5 9.2 %collective-permute-start.6 = (bf16[8,3584]{1,0:T(8,128)(2,1)S(1)}, bf16[8,3584]{1,0:T(8,128)(2,1)S(1)}, u32[]{:S(2)}, u32[]{:S(2)}) collective-permute-start(bf16[8,3584]{1,0:T(8,128)(2,1)S(1)} %shard_map.64), channel_id=1, source_target_pairs={{0,16},{8,24},{16,0},{24,8},{1,17},{9,25},{17,1},{25,9},{2,18},{10... | collective-permute-start | bytes 172040 | tf_op jit(solution)/shard_map/ppermute | solution.py:21
  8.0 5.1 %collective-permute-start.3 = (bf16[8,3584]{1,0:T(8,128)(2,1)S(1)}, bf16[8,3584]{1,0:T(8,128)(2,1)S(1)}, u32[]{:S(2)}, u32[]{:S(2)}) collective-permute-start(bf16[8,3584]{1,0:T(8,128)(2,1)S(1)} %collective-permute-done), channel_id=1, source_target_pairs={{0,16},{8,24},{16,0},{24,8},{1,17},{9,25},{17,1},{25,9},{2,18},{10... | collective-permute-start | bytes 172040 | tf_op jit(solution)/shard_map/ppermute | solution.py:21
  9.9 5.7 %collective-permute-start.8 = (bf16[8,3584]{1,0:T(8,128)(2,1)S(1)}, bf16[8,3584]{1,0:T(8,128)(2,1)S(1)}, u32[]{:S(2)}, u32[]{:S(2)}) collective-permute-start(bf16[8,3584]{1,0:T(8,128)(2,1)S(1)} %collective-permute-done.2), channel_id=1, source_target_pairs={{0,16},{8,24},{16,0},{24,8},{1,17},{9,25},{17,1},{25,9},{2,18},{10... | collective-permute-start | bytes 172040 | tf_op jit(solution)/shard_map/ppermute | solution.py:21
  11.6 4.2 %collective-permute-start.7 = (bf16[8,3584]{1,0:T(8,128)(2,1)S(1)}, bf16[8,3584]{1,0:T(8,128)(2,1)S(1)}, u32[]{:S(2)}, u32[]{:S(2)}) collective-permute-start(bf16[8,3584]{1,0:T(8,128)(2,1)S(1)} %collective-permute-done.1), channel_id=1, source_target_pairs={{0,16},{8,24},{16,0},{24,8},{1,17},{9,25},{17,1},{25,9},{2,18},{10... | collective-permute-start | bytes 172040 | tf_op jit(solution)/shard_map/ppermute | solution.py:21
  13.1 2.1 %copy-start.5 = (bf16[1,3584,256]{2,1,0:T(8,128)(2,1)S(1)}, bf16[1,3584,256]{2,1,0:T(8,128)(2,1)}, u32[]{:S(2)}) copy-start(bf16[1,3584,256]{2,1,0:T(8,128)(2,1)} %param.9) | copy-start | bytes 5505028
  13.1 1.6 %collective-permute-start.4 = (bf16[32,3584]{1,0:T(8,128)(2,1)S(1)}, bf16[32,3584]{1,0:T(8,128)(2,1)S(1)}, u32[]{:S(2)}, u32[]{:S(2)}) collective-permute-start(bf16[32,3584]{1,0:T(8,128)(2,1)S(1)} %shard_map.65), channel_id=1, source_target_pairs={{0,8},{8,0},{16,24},{24,16},{1,9},{9,1},{17,25},{25,17},{2,10},{10... | collective-permute-start | bytes 688136 | tf_op jit(solution)/shard_map/ppermute | solution.py:39
  15.8 1.7 %collective-permute-start.9 = (bf16[32,3584]{1,0:T(8,128)(2,1)S(1)}, bf16[32,3584]{1,0:T(8,128)(2,1)S(1)}, u32[]{:S(2)}, u32[]{:S(2)}) collective-permute-start(bf16[32,3584]{1,0:T(8,128)(2,1)S(1)} %pad_maximum_fusion.4.refs_0_), channel_id=1, source_target_pairs={{0,8},{8,0},{16,24},{24,16},{1,9},{9,1},{17,25},{25,17},{2,10},{10... | collective-permute-start | bytes 688136 | tf_op jit(solution)/shard_map/ppermute | solution.py:39
  15.9 4.4 %collective-permute-start.5 = (bf16[64,512]{1,0:T(8,128)(2,1)S(1)}, bf16[64,512]{1,0:T(8,128)(2,1)S(1)}, u32[]{:S(2)}, u32[]{:S(2)}) collective-permute-start(bf16[64,512]{1,0:T(8,128)(2,1)S(1)} %fusion.15.refs_1_), channel_id=1, source_target_pairs={{0,1},{1,0},{2,3},{3,2},{4,5},{5,4},{6,7},{7,6},{8,9},{9,8},{10,11... | collective-permute-start | bytes 196616 | tf_op jit(solution)/shard_map/ppermute | solution.py:16
  18.3 4.3 %collective-permute-start.14 = (bf16[64,512]{1,0:T(8,128)(2,1)S(1)}, bf16[64,512]{1,0:T(8,128)(2,1)S(1)}, u32[]{:S(2)}, u32[]{:S(2)}) collective-permute-start(bf16[64,512]{1,0:T(8,128)(2,1)S(1)} %fusion.14.refs_1_), channel_id=1, source_target_pairs={{0,1},{1,0},{2,3},{3,2},{4,5},{5,4},{6,7},{7,6},{8,9},{9,8},{10,11... | collective-permute-start | bytes 196616 | tf_op jit(solution)/shard_map/ppermute | solution.py:16
  20.8 1.6 %collective-permute-start.10 = (bf16[32,3584]{1,0:T(8,128)(2,1)S(1)}, bf16[32,3584]{1,0:T(8,128)(2,1)S(1)}, u32[]{:S(2)}, u32[]{:S(2)}) collective-permute-start(bf16[32,3584]{1,0:T(8,128)(2,1)S(1)} %slice.122), channel_id=1, source_target_pairs={{0,8},{8,0},{16,24},{24,16},{1,9},{9,1},{17,25},{25,17},{2,10},{10... | collective-permute-start | bytes 688136 | tf_op jit(solution)/shard_map/ppermute | solution.py:39
  23.1 15.5 %copy-start.2 = (s32[8,1]{0,1:T(1,128)S(1)}, s32[8,1]{0,1:T(1,128)}, u32[]{:S(2)}) copy-start(s32[8,1]{0,1:T(1,128)} %param.7) | copy-start | bytes 100
  23.1 15.5 %copy-start.3 = (s32[8,1]{0,1:T(1,128)S(1)}, s32[8,1]{0,1:T(1,128)}, u32[]{:S(2)}) copy-start(s32[8,1]{0,1:T(1,128)} %param.8) | copy-start | bytes 100
  23.2 4.6 %collective-permute-start.15 = (bf16[32,3584]{1,0:T(8,128)(2,1)S(1)}, bf16[32,3584]{1,0:T(8,128)(2,1)S(1)}, u32[]{:S(2)}, u32[]{:S(2)}) collective-permute-start(bf16[32,3584]{1,0:T(8,128)(2,1)S(1)} %slice.121), channel_id=1, source_target_pairs={{0,8},{8,0},{16,24},{24,16},{1,9},{9,1},{17,25},{25,17},{2,10},{10... | collective-permute-start | bytes 688136 | tf_op jit(solution)/shard_map/ppermute | solution.py:39
  23.3 7.9 %collective-permute-start.13 = (bf16[8,3584]{1,0:T(8,128)(2,1)S(1)}, bf16[8,3584]{1,0:T(8,128)(2,1)S(1)}, u32[]{:S(2)}, u32[]{:S(2)}) collective-permute-start(bf16[8,3584]{1,0:T(8,128)(2,1)S(1)} %get-tuple-element.11), channel_id=1, source_target_pairs={{0,6},{2,4},{4,2},{6,0},{8,14},{10,12},{12,10},{14,8},{16,22},{18,... | collective-permute-start | bytes 172040 | tf_op jit(solution)/shard_map/ppermute | solution.py:35
  25.7 8.4 %collective-permute-start.12 = (bf16[8,3584]{1,0:T(8,128)(2,1)S(1)}, bf16[8,3584]{1,0:T(8,128)(2,1)S(1)}, u32[]{:S(2)}, u32[]{:S(2)}) collective-permute-start(bf16[8,3584]{1,0:T(8,128)(2,1)S(1)} %get-tuple-element.12), channel_id=1, source_target_pairs={{0,4},{2,6},{4,0},{6,2},{8,12},{10,14},{12,8},{14,10},{16,20},{18,... | collective-permute-start | bytes 172040 | tf_op jit(solution)/shard_map/ppermute | solution.py:35
  26.1 8.5 %collective-permute-start.11 = (bf16[8,3584]{1,0:T(8,128)(2,1)S(1)}, bf16[8,3584]{1,0:T(8,128)(2,1)S(1)}, u32[]{:S(2)}, u32[]{:S(2)}) collective-permute-start(bf16[8,3584]{1,0:T(8,128)(2,1)S(1)} %get-tuple-element.13), channel_id=1, source_target_pairs={{0,2},{2,0},{4,6},{6,4},{8,10},{10,8},{12,14},{14,12},{16,18},{18,... | collective-permute-start | bytes 172040 | tf_op jit(solution)/shard_map/ppermute | solution.py:35
  27.8 7.3 %collective-permute-start.19 = (bf16[8,3584]{1,0:T(8,128)(2,1)S(1)}, bf16[8,3584]{1,0:T(8,128)(2,1)S(1)}, u32[]{:S(2)}, u32[]{:S(2)}) collective-permute-start(bf16[8,3584]{1,0:T(8,128)(2,1)S(1)} %get-tuple-element.7), channel_id=1, source_target_pairs={{0,22},{2,20},{4,18},{6,16},{8,30},{10,28},{12,26},{14,24},{16,6},... | collective-permute-start | bytes 172040 | tf_op jit(solution)/shard_map/ppermute | solution.py:35
  31.2 6.7 %collective-permute-start.18 = (bf16[8,3584]{1,0:T(8,128)(2,1)S(1)}, bf16[8,3584]{1,0:T(8,128)(2,1)S(1)}, u32[]{:S(2)}, u32[]{:S(2)}) collective-permute-start(bf16[8,3584]{1,0:T(8,128)(2,1)S(1)} %get-tuple-element.8), channel_id=1, source_target_pairs={{0,20},{2,22},{4,16},{6,18},{8,28},{10,30},{12,24},{14,26},{16,4},... | collective-permute-start | bytes 172040 | tf_op jit(solution)/shard_map/ppermute | solution.py:35
  31.2 6.7 %collective-permute-start.17 = (bf16[8,3584]{1,0:T(8,128)(2,1)S(1)}, bf16[8,3584]{1,0:T(8,128)(2,1)S(1)}, u32[]{:S(2)}, u32[]{:S(2)}) collective-permute-start(bf16[8,3584]{1,0:T(8,128)(2,1)S(1)} %get-tuple-element.9), channel_id=1, source_target_pairs={{0,18},{2,16},{4,22},{6,20},{8,26},{10,24},{12,30},{14,28},{16,2},... | collective-permute-start | bytes 172040 | tf_op jit(solution)/shard_map/ppermute | solution.py:35
  34.1 4.5 %collective-permute-start.16 = (bf16[8,3584]{1,0:T(8,128)(2,1)S(1)}, bf16[8,3584]{1,0:T(8,128)(2,1)S(1)}, u32[]{:S(2)}, u32[]{:S(2)}) collective-permute-start(bf16[8,3584]{1,0:T(8,128)(2,1)S(1)} %get-tuple-element.10), channel_id=1, source_target_pairs={{0,16},{2,18},{4,20},{6,22},{8,24},{10,26},{12,28},{14,30},{16,0},... | collective-permute-start | bytes 172040 | tf_op jit(solution)/shard_map/ppermute | solution.py:35

commit v8 on v7

--- a/solution.py
+++ b/solution.py
@@ -136,7 +136,7 @@
     far_swapped = swap_half(far)
     far = jnp.concatenate([after(far, flops=3450000000), far_swapped], axis=0)
     far_part, far_sent, far_others = partial_sums(far)
-    near_out = partial_out(near_part, [after(other, far_sent) for other in near_others], 3450000000, 0)
+    near_out = partial_out(near_part, [after(other, far_sent) for other in near_others], 3450000000, 3450000000)
     near_out = near_out.reshape(n_tp, count, width)
     near_sent = near_out[1:].astype(bf16)
     pieces = [near_out[0]] + [exchange(near_sent[i], 0, -t) for i, t in enumerate(places[1:])]

time: 39.5 us -> 40.3 us (1.020)
  waiting for transfers between devices: 9.18 us -> 10.9 us
  starting transfers between devices: 25.3 us -> 24.4 us
    ppermute x4, waiting for transfers between devices: 2.93 us -> 4.39 us  [swap_half(): lax.ppermute(value, 'grp', [(i, i ^ 1) for i in range(lax.axis_size('grp'...]
    ppermute x2, waiting for transfers between devices: 0.74 us -> 1.64 us  [rotate(): lax.ppermute(value, axis, [(i, (i + by) % size) for i in range(size)])]
    ppermute x2, starting transfers between devices: 2.99 us -> 2.16 us  [rotate(): lax.ppermute(value, axis, [(i, (i + by) % size) for i in range(size)])]
    ppermute x10, waiting for transfers between devices: 5.41 us -> 4.86 us  [exchange(): return lax.ppermute(value, ('grp', 'tp'), pairs)]
  transfers between devices with their start and end apart: 20 -> 20, of which waited for: 10 -> 9; matrix products, arithmetic and copies ran while one was open for 6% -> 6% of each run, Pallas kernels for 0% -> 0%
where the time goes in v8:
time: 40.3 us; the launch traced here: 40.1 us
  starting transfers between devices  24.4 us (61%)
  waiting for transfers between devices  10.9 us (27%)
  matrix products  2.6 us (6%)
  local copies, waits for them, and re-layouts  1.02 us (3%)
  Pallas kernels  0.75 us (2%)
    ppermute x10, starting transfers between devices, exchange(): return lax.ppermute(value, ('grp', 'tp'), pairs)  16.9 us
    ppermute x4, starting transfers between devices, rotate_experts(): lax.ppermute(value, 'grp', [(i, (i + 2 * by) % groups) for i in range(gro...  5.07 us
    ppermute x10, waiting for transfers between devices, exchange(): return lax.ppermute(value, ('grp', 'tp'), pairs)  4.86 us
    ppermute x4, waiting for transfers between devices, swap_half(): lax.ppermute(value, 'grp', [(i, i ^ 1) for i in range(lax.axis_size('grp'...  4.39 us
    ppermute x2, starting transfers between devices, rotate(): lax.ppermute(value, axis, [(i, (i + by) % size) for i in range(size)])  2.16 us
    dot_general x4, matrix products, partial_sums(): jnp.dot(rows, w, preferred_element_type=f32)  1.76 us
    ppermute x2, waiting for transfers between devices, rotate(): lax.ppermute(value, axis, [(i, (i + by) % size) for i in range(size)])  1.64 us
    unnamed x16, local copies, waits for them, and re-layouts  0.9 us
  transfers between devices with their start and end apart: 20, of which 9 were waited for; matrix products, arithmetic and copies ran while one was open for 6% of the time, Pallas kernels for 0%

profile of v8, /device:TPU:0, one launch (start us, length us, event | category | flops | bytes accessed | tf_op | source)
XLA Modules:
  0.0 40.1 jit_solution(15156864104174254095)
XLA Ops:
  0.0 0.0 copy-start
  0.0 3.0 %collective-permute-start = (bf16[8,3584]{1,0:T(8,128)(2,1)}, bf16[8,3584]{1,0:T(8,128)(2,1)S(1)}, u32[]{:S(2)}, u32[]{:S(2)}) collective-permute-start(bf16[8,3584]{1,0:T(8,128)(2,1)} %from_ref.1), channel_id=1, source_target_pairs={{0,2},{2,0},{4,6},{6,4},{8,10},{10,8},{12,14},{14,12},{16,18},{18,... | collective-permute-start | bytes 172040 | tf_op jit(solution)/shard_map/ppermute | solution.py:35
  3.0 2.5 %collective-permute-start.2 = (bf16[8,3584]{1,0:T(8,128)(2,1)}, bf16[8,3584]{1,0:T(8,128)(2,1)S(1)}, u32[]{:S(2)}, u32[]{:S(2)}) collective-permute-start(bf16[8,3584]{1,0:T(8,128)(2,1)} %from_ref.1), channel_id=1, source_target_pairs={{0,6},{2,4},{4,2},{6,0},{8,14},{10,12},{12,10},{14,8},{16,22},{18,... | collective-permute-start | bytes 172040 | tf_op jit(solution)/shard_map/ppermute | solution.py:35
  5.5 0.1 collective-permute-start.1
  5.6 0.0 copy-start.1
  5.6 0.9 %copy-done.1 = bf16[8,3584]{1,0:T(8,128)(2,1)S(1)} copy-done((bf16[8,3584]{1,0:T(8,128)(2,1)S(1)}, bf16[8,3584]{1,0:T(8,128)(2,1)}, u32[]{:S(2)}) %copy-start.1) | copy-done | bytes 57368
  6.5 0.0 copy-start.4
  6.5 1.5 %collective-permute-start.6 = (bf16[8,3584]{1,0:T(8,128)(2,1)S(1)}, bf16[8,3584]{1,0:T(8,128)(2,1)S(1)}, u32[]{:S(2)}, u32[]{:S(2)}) collective-permute-start(bf16[8,3584]{1,0:T(8,128)(2,1)S(1)} %shard_map.64), channel_id=1, source_target_pairs={{0,16},{8,24},{16,0},{24,8},{1,17},{9,25},{17,1},{25,9},{2,18},{10... | collective-permute-start | bytes 172040 | tf_op jit(solution)/shard_map/ppermute | solution.py:21
  8.0 0.0 collective-permute-done
  8.0 0.6 %collective-permute-start.3 = (bf16[8,3584]{1,0:T(8,128)(2,1)S(1)}, bf16[8,3584]{1,0:T(8,128)(2,1)S(1)}, u32[]{:S(2)}, u32[]{:S(2)}) collective-permute-start(bf16[8,3584]{1,0:T(8,128)(2,1)S(1)} %collective-permute-done), channel_id=1, source_target_pairs={{0,16},{8,24},{16,0},{24,8},{1,17},{9,25},{17,1},{25,9},{2,18},{10... | collective-permute-start | bytes 172040 | tf_op jit(solution)/shard_map/ppermute | solution.py:21
  8.6 1.3 %collective-permute-done.2 = bf16[8,3584]{1,0:T(8,128)(2,1)S(1)} collective-permute-done((bf16[8,3584]{1,0:T(8,128)(2,1)}, bf16[8,3584]{1,0:T(8,128)(2,1)S(1)}, u32[]{:S(2)}, u32[]{:S(2)}) %collective-permute-start.2) | collective-permute-done | bytes 57376 | tf_op jit(solution)/shard_map/ppermute | solution.py:35
  9.9 1.5 %collective-permute-start.8 = (bf16[8,3584]{1,0:T(8,128)(2,1)S(1)}, bf16[8,3584]{1,0:T(8,128)(2,1)S(1)}, u32[]{:S(2)}, u32[]{:S(2)}) collective-permute-start(bf16[8,3584]{1,0:T(8,128)(2,1)S(1)} %collective-permute-done.2), channel_id=1, source_target_pairs={{0,16},{8,24},{16,0},{24,8},{1,17},{9,25},{17,1},{25,9},{2,18},{10... | collective-permute-start | bytes 172040 | tf_op jit(solution)/shard_map/ppermute | solution.py:21
  11.4 0.1 collective-permute-done.1
  11.6 1.5 %collective-permute-start.7 = (bf16[8,3584]{1,0:T(8,128)(2,1)S(1)}, bf16[8,3584]{1,0:T(8,128)(2,1)S(1)}, u32[]{:S(2)}, u32[]{:S(2)}) collective-permute-start(bf16[8,3584]{1,0:T(8,128)(2,1)S(1)} %collective-permute-done.1), channel_id=1, source_target_pairs={{0,16},{8,24},{16,0},{24,8},{1,17},{9,25},{17,1},{25,9},{2,18},{10... | collective-permute-start | bytes 172040 | tf_op jit(solution)/shard_map/ppermute | solution.py:21
  13.1 0.0 copy-start.5
  13.1 0.0 collective-permute-done.3.refs_1_
  13.1 0.1 collective-permute-start.4
  13.2 1.5 %collective-permute-done.4 = bf16[32,3584]{1,0:T(8,128)(2,1)S(1)} collective-permute-done((bf16[32,3584]{1,0:T(8,128)(2,1)S(1)}, bf16[32,3584]{1,0:T(8,128)(2,1)S(1)}, u32[]{:S(2)}, u32[]{:S(2)}) %collective-permute-start.4) | collective-permute-done | bytes 229408 | tf_op jit(solution)/shard_map/ppermute | solution.py:39
  14.7 0.0 copy-done.4
  14.7 0.4 %fusion.6 = f32[64,256]{1,0:T(8,128)S(1)} fusion(bf16[64,3584]{1,0:T(8,128)(2,1)S(1)} %constant_dynamic-update-slice_fusion, bf16[1,3584,256]{2,1,0:T(8,128)(2,1)S(1)} %copy-done.4), kind=kOutput, calls=%fused_computation.6 | convolution fusion | flops 117440512 | bytes 2359296 | tf_op jit(solution)/shard_map/dot_general | solution.py:108
  15.2 0.0 copy-done.5
  15.2 0.4 %fusion.10 = f32[64,256]{1,0:T(8,128)S(1)} fusion(bf16[64,3584]{1,0:T(8,128)(2,1)S(1)} %constant_dynamic-update-slice_fusion, bf16[1,3584,256]{2,1,0:T(8,128)(2,1)S(1)} %copy-done.5), kind=kOutput, calls=%fused_computation.10 | convolution fusion | flops 117440512 | bytes 2359296 | tf_op jit(solution)/shard_map/dot_general | solution.py:108
  15.6 1.6 %collective-permute-start.5 = (bf16[64,512]{1,0:T(8,128)(2,1)S(1)}, bf16[64,512]{1,0:T(8,128)(2,1)S(1)}, u32[]{:S(2)}, u32[]{:S(2)}) collective-permute-start(bf16[64,512]{1,0:T(8,128)(2,1)S(1)} %fusion.25.refs_1_), channel_id=1, source_target_pairs={{0,1},{1,0},{2,3},{3,2},{4,5},{5,4},{6,7},{7,6},{8,9},{9,8},{10,11... | collective-permute-start | bytes 196616 | tf_op jit(solution)/shard_map/ppermute | solution.py:16
  17.2 0.0 collective-permute-done.8.refs_0_
  17.2 0.0 collective-permute-done.6
  17.2 0.0 collective-permute-done.7
  17.3 0.1 collective-permute-start.9
  17.4 1.5 %collective-permute-done.9 = bf16[32,3584]{1,0:T(8,128)(2,1)S(1)} collective-permute-done((bf16[32,3584]{1,0:T(8,128)(2,1)S(1)}, bf16[32,3584]{1,0:T(8,128)(2,1)S(1)}, u32[]{:S(2)}, u32[]{:S(2)}) %collective-permute-start.9) | collective-permute-done | bytes 229408 | tf_op jit(solution)/shard_map/ppermute | solution.py:39
  18.8 0.4 %fusion.4 = f32[64,256]{1,0:T(8,128)S(1)} fusion(bf16[1,3584,256]{2,1,0:T(8,128)(2,1)S(1)} %copy-done.4, bf16[32,3584]{1,0:T(8,128)(2,1)S(1)} %collective-permute-done.9, bf16[32,3584]{1,0:T(8,128)(2,1)S(1)} %shard_map.68), kind=kOutput, calls=%fused_computation.4 | convolution fusion | flops 118358016 | bytes 2359296 | tf_op jit(solution)/shard_map/dot_general | solution.py:108
  19.3 0.4 %fusion.8 = f32[64,256]{1,0:T(8,128)S(1)} fusion(bf16[1,3584,256]{2,1,0:T(8,128)(2,1)S(1)} %copy-done.5, bf16[32,3584]{1,0:T(8,128)(2,1)S(1)} %collective-permute-done.9, bf16[32,3584]{1,0:T(8,128)(2,1)S(1)} %shard_map.68), kind=kOutput, calls=%fused_computation.8 | convolution fusion | flops 118358016 | bytes 2359296 | tf_op jit(solution)/shard_map/dot_general | solution.py:108
  19.7 0.6 %collective-permute-start.14 = (bf16[64,512]{1,0:T(8,128)(2,1)S(1)}, bf16[64,512]{1,0:T(8,128)(2,1)S(1)}, u32[]{:S(2)}, u32[]{:S(2)}) collective-permute-start(bf16[64,512]{1,0:T(8,128)(2,1)S(1)} %fusion.14.refs_1_), channel_id=1, source_target_pairs={{0,1},{1,0},{2,3},{3,2},{4,5},{5,4},{6,7},{7,6},{8,9},{9,8},{10,11... | collective-permute-start | bytes 196616 | tf_op jit(solution)/shard_map/ppermute | solution.py:16
  20.3 0.0 collective-permute-done.5.refs_0_
  20.3 0.0 copy-done
  20.3 0.4 %fusion.2.refs_0_ = f32[64,3584]{1,0:T(8,128)S(1)} fusion(bf16[1,256,3584]{2,1,0:T(8,128)(2,1)S(1)} %copy-done, f32[64,512]{1,0:T(8,128)S(1)} %convert_add_fusion.1), kind=kOutput, calls=%fused_computation.2 | convolution fusion | flops 117538816 | bytes 2883584 | tf_op jit(solution)/shard_map/dot_general | solution.py:119
  20.8 0.1 collective-permute-start.10
  20.9 1.5 %collective-permute-done.10 = bf16[32,3584]{1,0:T(8,128)(2,1)S(1)} collective-permute-done((bf16[32,3584]{1,0:T(8,128)(2,1)S(1)}, bf16[32,3584]{1,0:T(8,128)(2,1)S(1)}, u32[]{:S(2)}, u32[]{:S(2)}) %collective-permute-start.10) | collective-permute-done | bytes 229408 | tf_op jit(solution)/shard_map/ppermute | solution.py:39
  22.3 0.1 fusion.26
  22.4 1.6 %collective-permute-done.14.refs_0_ = bf16[64,512]{1,0:T(8,128)(2,1)S(1)} collective-permute-done((bf16[64,512]{1,0:T(8,128)(2,1)S(1)}, bf16[64,512]{1,0:T(8,128)(2,1)S(1)}, u32[]{:S(2)}, u32[]{:S(2)}) %collective-permute-start.14) | collective-permute-done | bytes 65568 | tf_op jit(solution)/shard_map/ppermute | solution.py:16
  24.1 0.4 %fusion = f32[64,3584]{1,0:T(8,128)S(1)} fusion(bf16[1,256,3584]{2,1,0:T(8,128)(2,1)S(1)} %copy-done, f32[64,512]{1,0:T(8,128)S(1)} %convert_add_fusion), kind=kOutput, calls=%fused_computation | convolution fusion | flops 117538816 | bytes 2883584 | tf_op jit(solution)/shard_map/dot_general | solution.py:119
  24.5 0.0 copy-start.2
  24.5 0.0 copy-start.3
  24.6 0.1 collective-permute-start.15
  24.7 2.5 %collective-permute-start.13 = (bf16[8,3584]{1,0:T(8,128)(2,1)S(1)}, bf16[8,3584]{1,0:T(8,128)(2,1)S(1)}, u32[]{:S(2)}, u32[]{:S(2)}) collective-permute-start(bf16[8,3584]{1,0:T(8,128)(2,1)S(1)} %get-tuple-element.11), channel_id=1, source_target_pairs={{0,6},{2,4},{4,2},{6,0},{8,14},{10,12},{12,10},{14,8},{16,22},{18,... | collective-permute-start | bytes 172040 | tf_op jit(solution)/shard_map/ppermute | solution.py:35
  27.1 0.4 collective-permute-start.12
  27.5 1.6 %collective-permute-start.11 = (bf16[8,3584]{1,0:T(8,128)(2,1)S(1)}, bf16[8,3584]{1,0:T(8,128)(2,1)S(1)}, u32[]{:S(2)}, u32[]{:S(2)}) collective-permute-start(bf16[8,3584]{1,0:T(8,128)(2,1)S(1)} %get-tuple-element.13), channel_id=1, source_target_pairs={{0,2},{2,0},{4,6},{6,4},{8,10},{10,8},{12,14},{14,12},{16,18},{18,... | collective-permute-start | bytes 172040 | tf_op jit(solution)/shard_map/ppermute | solution.py:35
  29.1 0.0 collective-permute-done.15
  29.2 2.4 %collective-permute-start.19 = (bf16[8,3584]{1,0:T(8,128)(2,1)S(1)}, bf16[8,3584]{1,0:T(8,128)(2,1)S(1)}, u32[]{:S(2)}, u32[]{:S(2)}) collective-permute-start(bf16[8,3584]{1,0:T(8,128)(2,1)S(1)} %get-tuple-element.7), channel_id=1, source_target_pairs={{0,22},{2,20},{4,18},{6,16},{8,30},{10,28},{12,26},{14,24},{16,6},... | collective-permute-start | bytes 172040 | tf_op jit(solution)/shard_map/ppermute | solution.py:35
  31.6 0.4 %collective-permute-start.18 = (bf16[8,3584]{1,0:T(8,128)(2,1)S(1)}, bf16[8,3584]{1,0:T(8,128)(2,1)S(1)}, u32[]{:S(2)}, u32[]{:S(2)}) collective-permute-start(bf16[8,3584]{1,0:T(8,128)(2,1)S(1)} %get-tuple-element.8), channel_id=1, source_target_pairs={{0,20},{2,22},{4,16},{6,18},{8,28},{10,30},{12,24},{14,26},{16,4},... | collective-permute-start | bytes 172040 | tf_op jit(solution)/shard_map/ppermute | solution.py:35
  32.1 0.0 collective-permute-done.13.refs_3_
  32.1 2.5 %collective-permute-start.17 = (bf16[8,3584]{1,0:T(8,128)(2,1)S(1)}, bf16[8,3584]{1,0:T(8,128)(2,1)S(1)}, u32[]{:S(2)}, u32[]{:S(2)}) collective-permute-start(bf16[8,3584]{1,0:T(8,128)(2,1)S(1)} %get-tuple-element.9), channel_id=1, source_target_pairs={{0,18},{2,16},{4,22},{6,20},{8,26},{10,24},{12,30},{14,28},{16,2},... | collective-permute-start | bytes 172040 | tf_op jit(solution)/shard_map/ppermute | solution.py:35
  34.5 0.0 collective-permute-done.12.refs_2_
  34.5 1.5 %collective-permute-start.16 = (bf16[8,3584]{1,0:T(8,128)(2,1)S(1)}, bf16[8,3584]{1,0:T(8,128)(2,1)S(1)}, u32[]{:S(2)}, u32[]{:S(2)}) collective-permute-start(bf16[8,3584]{1,0:T(8,128)(2,1)S(1)} %get-tuple-element.10), channel_id=1, source_target_pairs={{0,16},{2,18},{4,20},{6,22},{8,24},{10,26},{12,28},{14,30},{16,0},... | collective-permute-start | bytes 172040 | tf_op jit(solution)/shard_map/ppermute | solution.py:35
  36.0 0.0 collective-permute-done.11.refs_1_
  36.0 0.1 collective-permute-done.19.refs_7_
  36.1 2.4 %collective-permute-done.18.refs_6_ = bf16[8,3584]{1,0:T(8,128)(2,1)S(1)} collective-permute-done((bf16[8,3584]{1,0:T(8,128)(2,1)S(1)}, bf16[8,3584]{1,0:T(8,128)(2,1)S(1)}, u32[]{:S(2)}, u32[]{:S(2)}) %collective-permute-start.18) | collective-permute-done | bytes 57376 | tf_op jit(solution)/shard_map/ppermute | solution.py:35
  38.6 0.0 collective-permute-done.17.refs_5_
  38.6 0.8 %collective-permute-done.16.refs_4_ = bf16[8,3584]{1,0:T(8,128)(2,1)S(1)} collective-permute-done((bf16[8,3584]{1,0:T(8,128)(2,1)S(1)}, bf16[8,3584]{1,0:T(8,128)(2,1)S(1)}, u32[]{:S(2)}, u32[]{:S(2)}) %collective-permute-start.16) | collective-permute-done | bytes 57376 | tf_op jit(solution)/shard_map/ppermute | solution.py:35
  39.4 0.0 copy-done.2
  39.4 0.0 copy-done.3
  39.4 0.7 %shard_map.72 = bf16[8,3584]{1,0:T(8,128)(2,1)} custom-call(s32[1,8]{1,0:T(1,128)S(1)} %bitcast.31, s32[1,8]{1,0:T(1,128)S(1)} %bitcast.32, f32[8,3584]{1,0:T(8,128)S(1)} %slice.83.refs_0_, bf16[8,3584]{1,0:T(8,128)(2,1)S(1)} %collective-permute-done.11.refs_1_, bf16[8,3584]{1,0:T(8,128)(2,1)S(1)} %collective-permute-done.12.refs_2_, ...), custom_call_target="tpu_custom_call" | custom-call | tf_op jit(solution)/shard_map/pallas_call | solution.py:92
  (27 shorter events, 0.3 us)
Async XLA Ops:
  0.0 20.3 %copy-start = (bf16[1,256,3584]{2,1,0:T(8,128)(2,1)S(1)}, bf16[1,256,3584]{2,1,0:T(8,128)(2,1)}, u32[]{:S(2)}) copy-start(bf16[1,256,3584]{2,1,0:T(8,128)(2,1)} %param.11) | copy-start | bytes 5505028
  0.0 8.0 %collective-permute-start = (bf16[8,3584]{1,0:T(8,128)(2,1)}, bf16[8,3584]{1,0:T(8,128)(2,1)S(1)}, u32[]{:S(2)}, u32[]{:S(2)}) collective-permute-start(bf16[8,3584]{1,0:T(8,128)(2,1)} %from_ref.1), channel_id=1, source_target_pairs={{0,2},{2,0},{4,6},{6,4},{8,10},{10,8},{12,14},{14,12},{16,18},{18,... | collective-permute-start | bytes 172040 | tf_op jit(solution)/shard_map/ppermute | solution.py:35
  3.0 6.9 %collective-permute-start.2 = (bf16[8,3584]{1,0:T(8,128)(2,1)}, bf16[8,3584]{1,0:T(8,128)(2,1)S(1)}, u32[]{:S(2)}, u32[]{:S(2)}) collective-permute-start(bf16[8,3584]{1,0:T(8,128)(2,1)} %from_ref.1), channel_id=1, source_target_pairs={{0,6},{2,4},{4,2},{6,0},{8,14},{10,12},{12,10},{14,8},{16,22},{18,... | collective-permute-start | bytes 172040 | tf_op jit(solution)/shard_map/ppermute | solution.py:35
  5.5 6.1 %collective-permute-start.1 = (bf16[8,3584]{1,0:T(8,128)(2,1)}, bf16[8,3584]{1,0:T(8,128)(2,1)S(1)}, u32[]{:S(2)}, u32[]{:S(2)}) collective-permute-start(bf16[8,3584]{1,0:T(8,128)(2,1)} %from_ref.1), channel_id=1, source_target_pairs={{0,4},{2,6},{4,0},{6,2},{8,12},{10,14},{12,8},{14,10},{16,20},{18,... | collective-permute-start | bytes 172040 | tf_op jit(solution)/shard_map/ppermute | solution.py:35
  5.6 0.9 %copy-start.1 = (bf16[8,3584]{1,0:T(8,128)(2,1)S(1)}, bf16[8,3584]{1,0:T(8,128)(2,1)}, u32[]{:S(2)}) copy-start(bf16[8,3584]{1,0:T(8,128)(2,1)} %from_ref.1) | copy-start | bytes 172036
  6.5 8.2 %copy-start.4 = (bf16[1,3584,256]{2,1,0:T(8,128)(2,1)S(1)}, bf16[1,3584,256]{2,1,0:T(8,128)(2,1)}, u32[]{:S(2)}) copy-start(bf16[1,3584,256]{2,1,0:T(8,128)(2,1)} %param.10) | copy-start | bytes 5505028
  6.5 10.8 %collective-permute-start.6 = (bf16[8,3584]{1,0:T(8,128)(2,1)S(1)}, bf16[8,3584]{1,0:T(8,128)(2,1)S(1)}, u32[]{:S(2)}, u32[]{:S(2)}) collective-permute-start(bf16[8,3584]{1,0:T(8,128)(2,1)S(1)} %shard_map.64), channel_id=1, source_target_pairs={{0,16},{8,24},{16,0},{24,8},{1,17},{9,25},{17,1},{25,9},{2,18},{10... | collective-permute-start | bytes 172040 | tf_op jit(solution)/shard_map/ppermute | solution.py:21
  8.0 5.1 %collective-permute-start.3 = (bf16[8,3584]{1,0:T(8,128)(2,1)S(1)}, bf16[8,3584]{1,0:T(8,128)(2,1)S(1)}, u32[]{:S(2)}, u32[]{:S(2)}) collective-permute-start(bf16[8,3584]{1,0:T(8,128)(2,1)S(1)} %collective-permute-done), channel_id=1, source_target_pairs={{0,16},{8,24},{16,0},{24,8},{1,17},{9,25},{17,1},{25,9},{2,18},{10... | collective-permute-start | bytes 172040 | tf_op jit(solution)/shard_map/ppermute | solution.py:21
  9.9 7.3 %collective-permute-start.8 = (bf16[8,3584]{1,0:T(8,128)(2,1)S(1)}, bf16[8,3584]{1,0:T(8,128)(2,1)S(1)}, u32[]{:S(2)}, u32[]{:S(2)}) collective-permute-start(bf16[8,3584]{1,0:T(8,128)(2,1)S(1)} %collective-permute-done.2), channel_id=1, source_target_pairs={{0,16},{8,24},{16,0},{24,8},{1,17},{9,25},{17,1},{25,9},{2,18},{10... | collective-permute-start | bytes 172040 | tf_op jit(solution)/shard_map/ppermute | solution.py:21
  11.6 5.7 %collective-permute-start.7 = (bf16[8,3584]{1,0:T(8,128)(2,1)S(1)}, bf16[8,3584]{1,0:T(8,128)(2,1)S(1)}, u32[]{:S(2)}, u32[]{:S(2)}) collective-permute-start(bf16[8,3584]{1,0:T(8,128)(2,1)S(1)} %collective-permute-done.1), channel_id=1, source_target_pairs={{0,16},{8,24},{16,0},{24,8},{1,17},{9,25},{17,1},{25,9},{2,18},{10... | collective-permute-start | bytes 172040 | tf_op jit(solution)/shard_map/ppermute | solution.py:21
  13.1 2.1 %copy-start.5 = (bf16[1,3584,256]{2,1,0:T(8,128)(2,1)S(1)}, bf16[1,3584,256]{2,1,0:T(8,128)(2,1)}, u32[]{:S(2)}) copy-start(bf16[1,3584,256]{2,1,0:T(8,128)(2,1)} %param.9) | copy-start | bytes 5505028
  13.1 1.6 %collective-permute-start.4 = (bf16[32,3584]{1,0:T(8,128)(2,1)S(1)}, bf16[32,3584]{1,0:T(8,128)(2,1)S(1)}, u32[]{:S(2)}, u32[]{:S(2)}) collective-permute-start(bf16[32,3584]{1,0:T(8,128)(2,1)S(1)} %shard_map.65), channel_id=1, source_target_pairs={{0,8},{8,0},{16,24},{24,16},{1,9},{9,1},{17,25},{25,17},{2,10},{10... | collective-permute-start | bytes 688136 | tf_op jit(solution)/shard_map/ppermute | solution.py:39
  15.6 4.7 %collective-permute-start.5 = (bf16[64,512]{1,0:T(8,128)(2,1)S(1)}, bf16[64,512]{1,0:T(8,128)(2,1)S(1)}, u32[]{:S(2)}, u32[]{:S(2)}) collective-permute-start(bf16[64,512]{1,0:T(8,128)(2,1)S(1)} %fusion.25.refs_1_), channel_id=1, source_target_pairs={{0,1},{1,0},{2,3},{3,2},{4,5},{5,4},{6,7},{7,6},{8,9},{9,8},{10,11... | collective-permute-start | bytes 196616 | tf_op jit(solution)/shard_map/ppermute | solution.py:16
  17.3 1.6 %collective-permute-start.9 = (bf16[32,3584]{1,0:T(8,128)(2,1)S(1)}, bf16[32,3584]{1,0:T(8,128)(2,1)S(1)}, u32[]{:S(2)}, u32[]{:S(2)}) collective-permute-start(bf16[32,3584]{1,0:T(8,128)(2,1)S(1)} %pad_maximum_fusion.4.refs_0_), channel_id=1, source_target_pairs={{0,8},{8,0},{16,24},{24,16},{1,9},{9,1},{17,25},{25,17},{2,10},{10... | collective-permute-start | bytes 688136 | tf_op jit(solution)/shard_map/ppermute | solution.py:39
  19.7 4.3 %collective-permute-start.14 = (bf16[64,512]{1,0:T(8,128)(2,1)S(1)}, bf16[64,512]{1,0:T(8,128)(2,1)S(1)}, u32[]{:S(2)}, u32[]{:S(2)}) collective-permute-start(bf16[64,512]{1,0:T(8,128)(2,1)S(1)} %fusion.14.refs_1_), channel_id=1, source_target_pairs={{0,1},{1,0},{2,3},{3,2},{4,5},{5,4},{6,7},{7,6},{8,9},{9,8},{10,11... | collective-permute-start | bytes 196616 | tf_op jit(solution)/shard_map/ppermute | solution.py:16
  20.8 1.6 %collective-permute-start.10 = (bf16[32,3584]{1,0:T(8,128)(2,1)S(1)}, bf16[32,3584]{1,0:T(8,128)(2,1)S(1)}, u32[]{:S(2)}, u32[]{:S(2)}) collective-permute-start(bf16[32,3584]{1,0:T(8,128)(2,1)S(1)} %slice.122), channel_id=1, source_target_pairs={{0,8},{8,0},{16,24},{24,16},{1,9},{9,1},{17,25},{25,17},{2,10},{10... | collective-permute-start | bytes 688136 | tf_op jit(solution)/shard_map/ppermute | solution.py:39
  24.5 14.9 %copy-start.2 = (s32[8,1]{0,1:T(1,128)S(1)}, s32[8,1]{0,1:T(1,128)}, u32[]{:S(2)}) copy-start(s32[8,1]{0,1:T(1,128)} %param.7) | copy-start | bytes 100
  24.5 14.9 %copy-start.3 = (s32[8,1]{0,1:T(1,128)S(1)}, s32[8,1]{0,1:T(1,128)}, u32[]{:S(2)}) copy-start(s32[8,1]{0,1:T(1,128)} %param.8) | copy-start | bytes 100
  24.6 4.6 %collective-permute-start.15 = (bf16[32,3584]{1,0:T(8,128)(2,1)S(1)}, bf16[32,3584]{1,0:T(8,128)(2,1)S(1)}, u32[]{:S(2)}, u32[]{:S(2)}) collective-permute-start(bf16[32,3584]{1,0:T(8,128)(2,1)S(1)} %slice.121), channel_id=1, source_target_pairs={{0,8},{8,0},{16,24},{24,16},{1,9},{9,1},{17,25},{25,17},{2,10},{10... | collective-permute-start | bytes 688136 | tf_op jit(solution)/shard_map/ppermute | solution.py:39
  24.7 7.4 %collective-permute-start.13 = (bf16[8,3584]{1,0:T(8,128)(2,1)S(1)}, bf16[8,3584]{1,0:T(8,128)(2,1)S(1)}, u32[]{:S(2)}, u32[]{:S(2)}) collective-permute-start(bf16[8,3584]{1,0:T(8,128)(2,1)S(1)} %get-tuple-element.11), channel_id=1, source_target_pairs={{0,6},{2,4},{4,2},{6,0},{8,14},{10,12},{12,10},{14,8},{16,22},{18,... | collective-permute-start | bytes 172040 | tf_op jit(solution)/shard_map/ppermute | solution.py:35
  27.1 7.4 %collective-permute-start.12 = (bf16[8,3584]{1,0:T(8,128)(2,1)S(1)}, bf16[8,3584]{1,0:T(8,128)(2,1)S(1)}, u32[]{:S(2)}, u32[]{:S(2)}) collective-permute-start(bf16[8,3584]{1,0:T(8,128)(2,1)S(1)} %get-tuple-element.12), channel_id=1, source_target_pairs={{0,4},{2,6},{4,0},{6,2},{8,12},{10,14},{12,8},{14,10},{16,20},{18,... | collective-permute-start | bytes 172040 | tf_op jit(solution)/shard_map/ppermute | solution.py:35
  27.5 8.5 %collective-permute-start.11 = (bf16[8,3584]{1,0:T(8,128)(2,1)S(1)}, bf16[8,3584]{1,0:T(8,128)(2,1)S(1)}, u32[]{:S(2)}, u32[]{:S(2)}) collective-permute-start(bf16[8,3584]{1,0:T(8,128)(2,1)S(1)} %get-tuple-element.13), channel_id=1, source_target_pairs={{0,2},{2,0},{4,6},{6,4},{8,10},{10,8},{12,14},{14,12},{16,18},{18,... | collective-permute-start | bytes 172040 | tf_op jit(solution)/shard_map/ppermute | solution.py:35
  29.2 6.9 %collective-permute-start.19 = (bf16[8,3584]{1,0:T(8,128)(2,1)S(1)}, bf16[8,3584]{1,0:T(8,128)(2,1)S(1)}, u32[]{:S(2)}, u32[]{:S(2)}) collective-permute-start(bf16[8,3584]{1,0:T(8,128)(2,1)S(1)} %get-tuple-element.7), channel_id=1, source_target_pairs={{0,22},{2,20},{4,18},{6,16},{8,30},{10,28},{12,26},{14,24},{16,6},... | collective-permute-start | bytes 172040 | tf_op jit(solution)/shard_map/ppermute | solution.py:35
  31.6 7.0 %collective-permute-start.18 = (bf16[8,3584]{1,0:T(8,128)(2,1)S(1)}, bf16[8,3584]{1,0:T(8,128)(2,1)S(1)}, u32[]{:S(2)}, u32[]{:S(2)}) collective-permute-start(bf16[8,3584]{1,0:T(8,128)(2,1)S(1)} %get-tuple-element.8), channel_id=1, source_target_pairs={{0,20},{2,22},{4,16},{6,18},{8,28},{10,30},{12,24},{14,26},{16,4},... | collective-permute-start | bytes 172040 | tf_op jit(solution)/shard_map/ppermute | solution.py:35
  32.1 6.5 %collective-permute-start.17 = (bf16[8,3584]{1,0:T(8,128)(2,1)S(1)}, bf16[8,3584]{1,0:T(8,128)(2,1)S(1)}, u32[]{:S(2)}, u32[]{:S(2)}) collective-permute-start(bf16[8,3584]{1,0:T(8,128)(2,1)S(1)} %get-tuple-element.9), channel_id=1, source_target_pairs={{0,18},{2,16},{4,22},{6,20},{8,26},{10,24},{12,30},{14,28},{16,2},... | collective-permute-start | bytes 172040 | tf_op jit(solution)/shard_map/ppermute | solution.py:35
  34.5 4.9 %collective-permute-start.16 = (bf16[8,3584]{1,0:T(8,128)(2,1)S(1)}, bf16[8,3584]{1,0:T(8,128)(2,1)S(1)}, u32[]{:S(2)}, u32[]{:S(2)}) collective-permute-start(bf16[8,3584]{1,0:T(8,128)(2,1)S(1)} %get-tuple-element.10), channel_id=1, source_target_pairs={{0,16},{2,18},{4,20},{6,22},{8,24},{10,26},{12,28},{14,30},{16,0},... | collective-permute-start | bytes 172040 | tf_op jit(solution)/shard_map/ppermute | solution.py:35

commit v9 on v7

--- a/solution.py
+++ b/solution.py
@@ -67,8 +67,14 @@
     )(value)
 
 
+def in_line_order(pieces, n_tp):
+    lines = [pieces[i : i + n_tp] for i in range(0, len(pieces), n_tp)]
+    return [piece for line in lines for piece in (line[0], *line[:0:-1])]
+
+
 def mix_kernel(n_tp, experts, ids_ref, levels_ref, *refs):
     *piece_refs, mixed_ref = refs
+    piece_refs = in_line_order(piece_refs, n_tp)
     count = mixed_ref.shape[0]
     expert = lax.axis_index("grp") // 2
     row = lax.broadcasted_iota(jnp.int32, (count, count), 0)
@@ -144,7 +150,7 @@
     far_out = far_out.reshape(experts - 1, n_tp, count, width).astype(bf16)
     for s in range(1, experts):
         pieces += [exchange(far_out[experts - 1 - s, i], s, -t) for i, t in enumerate(places)]
-    return mix(expert_ids, gate_levels, pieces, n_tp, experts)
+    return mix(expert_ids, gate_levels, in_line_order(pieces, n_tp), n_tp, experts)
 
 
 def solution(mesh):

time: 39.5 us -> 39.8 us (level)
  no operation moved by 1% of the time
where the time goes in v9:
time: 39.8 us; the launch traced here: 39.6 us
  starting transfers between devices  25.3 us (64%)
  waiting for transfers between devices  9.48 us (24%)
  matrix products  2.6 us (7%)
  local copies, waits for them, and re-layouts  1.02 us (3%)
  Pallas kernels  0.75 us (2%)
    ppermute x10, starting transfers between devices, exchange(): return lax.ppermute(value, ('grp', 'tp'), pairs)  16.9 us
    ppermute x10, waiting for transfers between devices, exchange(): return lax.ppermute(value, ('grp', 'tp'), pairs)  5.72 us
    ppermute x4, starting transfers between devices, rotate_experts(): lax.ppermute(value, 'grp', [(i, (i + 2 * by) % groups) for i in range(gro...  5.07 us
    ppermute x2, starting transfers between devices, rotate(): lax.ppermute(value, axis, [(i, (i + by) % size) for i in range(size)])  2.99 us
    ppermute x4, waiting for transfers between devices, swap_half(): lax.ppermute(value, 'grp', [(i, i ^ 1) for i in range(lax.axis_size('grp'...  2.93 us
    dot_general x4, matrix products, partial_sums(): jnp.dot(rows, w, preferred_element_type=f32)  1.76 us
    unnamed x16, local copies, waits for them, and re-layouts  0.9 us
    dot_general x2, matrix products, partial_out(): out = jnp.dot(hidden, w_down, preferred_element_type=f32)  0.83 us
  transfers between devices with their start and end apart: 20, of which 10 were waited for; matrix products, arithmetic and copies ran while one was open for 6% of the time, Pallas kernels for 0%

profile of v9, /device:TPU:0, one launch (start us, length us, event | category | flops | bytes accessed | tf_op | source)
XLA Modules:
  0.0 39.6 jit_solution(17976992975274723112)
XLA Ops:
  0.0 0.0 copy-start
  0.0 3.0 %collective-permute-start = (bf16[8,3584]{1,0:T(8,128)(2,1)}, bf16[8,3584]{1,0:T(8,128)(2,1)S(1)}, u32[]{:S(2)}, u32[]{:S(2)}) collective-permute-start(bf16[8,3584]{1,0:T(8,128)(2,1)} %from_ref.1), channel_id=1, source_target_pairs={{0,2},{2,0},{4,6},{6,4},{8,10},{10,8},{12,14},{14,12},{16,18},{18,... | collective-permute-start | bytes 172040 | tf_op jit(solution)/shard_map/ppermute | solution.py:35
  3.0 2.5 %collective-permute-start.2 = (bf16[8,3584]{1,0:T(8,128)(2,1)}, bf16[8,3584]{1,0:T(8,128)(2,1)S(1)}, u32[]{:S(2)}, u32[]{:S(2)}) collective-permute-start(bf16[8,3584]{1,0:T(8,128)(2,1)} %from_ref.1), channel_id=1, source_target_pairs={{0,6},{2,4},{4,2},{6,0},{8,14},{10,12},{12,10},{14,8},{16,22},{18,... | collective-permute-start | bytes 172040 | tf_op jit(solution)/shard_map/ppermute | solution.py:35
  5.5 0.1 collective-permute-start.1
  5.6 0.0 copy-start.1
  5.6 0.9 %copy-done.1 = bf16[8,3584]{1,0:T(8,128)(2,1)S(1)} copy-done((bf16[8,3584]{1,0:T(8,128)(2,1)S(1)}, bf16[8,3584]{1,0:T(8,128)(2,1)}, u32[]{:S(2)}) %copy-start.1) | copy-done | bytes 57368
  6.5 0.0 copy-start.4
  6.5 1.5 %collective-permute-start.6 = (bf16[8,3584]{1,0:T(8,128)(2,1)S(1)}, bf16[8,3584]{1,0:T(8,128)(2,1)S(1)}, u32[]{:S(2)}, u32[]{:S(2)}) collective-permute-start(bf16[8,3584]{1,0:T(8,128)(2,1)S(1)} %shard_map.64), channel_id=1, source_target_pairs={{0,16},{8,24},{16,0},{24,8},{1,17},{9,25},{17,1},{25,9},{2,18},{10... | collective-permute-start | bytes 172040 | tf_op jit(solution)/shard_map/ppermute | solution.py:21
  8.0 0.0 collective-permute-done
  8.0 0.6 %collective-permute-start.3 = (bf16[8,3584]{1,0:T(8,128)(2,1)S(1)}, bf16[8,3584]{1,0:T(8,128)(2,1)S(1)}, u32[]{:S(2)}, u32[]{:S(2)}) collective-permute-start(bf16[8,3584]{1,0:T(8,128)(2,1)S(1)} %collective-permute-done), channel_id=1, source_target_pairs={{0,16},{8,24},{16,0},{24,8},{1,17},{9,25},{17,1},{25,9},{2,18},{10... | collective-permute-start | bytes 172040 | tf_op jit(solution)/shard_map/ppermute | solution.py:21
  8.6 1.3 %collective-permute-done.2 = bf16[8,3584]{1,0:T(8,128)(2,1)S(1)} collective-permute-done((bf16[8,3584]{1,0:T(8,128)(2,1)}, bf16[8,3584]{1,0:T(8,128)(2,1)S(1)}, u32[]{:S(2)}, u32[]{:S(2)}) %collective-permute-start.2) | collective-permute-done | bytes 57376 | tf_op jit(solution)/shard_map/ppermute | solution.py:35
  9.9 1.5 %collective-permute-start.8 = (bf16[8,3584]{1,0:T(8,128)(2,1)S(1)}, bf16[8,3584]{1,0:T(8,128)(2,1)S(1)}, u32[]{:S(2)}, u32[]{:S(2)}) collective-permute-start(bf16[8,3584]{1,0:T(8,128)(2,1)S(1)} %collective-permute-done.2), channel_id=1, source_target_pairs={{0,16},{8,24},{16,0},{24,8},{1,17},{9,25},{17,1},{25,9},{2,18},{10... | collective-permute-start | bytes 172040 | tf_op jit(solution)/shard_map/ppermute | solution.py:21
  11.4 0.1 collective-permute-done.1
  11.6 1.5 %collective-permute-start.7 = (bf16[8,3584]{1,0:T(8,128)(2,1)S(1)}, bf16[8,3584]{1,0:T(8,128)(2,1)S(1)}, u32[]{:S(2)}, u32[]{:S(2)}) collective-permute-start(bf16[8,3584]{1,0:T(8,128)(2,1)S(1)} %collective-permute-done.1), channel_id=1, source_target_pairs={{0,16},{8,24},{16,0},{24,8},{1,17},{9,25},{17,1},{25,9},{2,18},{10... | collective-permute-start | bytes 172040 | tf_op jit(solution)/shard_map/ppermute | solution.py:21
  13.1 0.0 copy-start.5
  13.1 0.0 collective-permute-done.3.refs_1_
  13.1 0.1 collective-permute-start.4
  13.2 1.5 %collective-permute-done.4 = bf16[32,3584]{1,0:T(8,128)(2,1)S(1)} collective-permute-done((bf16[32,3584]{1,0:T(8,128)(2,1)S(1)}, bf16[32,3584]{1,0:T(8,128)(2,1)S(1)}, u32[]{:S(2)}, u32[]{:S(2)}) %collective-permute-start.4) | collective-permute-done | bytes 229408 | tf_op jit(solution)/shard_map/ppermute | solution.py:39
  14.7 0.0 copy-done.4
  14.7 0.4 %fusion.6 = f32[64,256]{1,0:T(8,128)S(1)} fusion(bf16[64,3584]{1,0:T(8,128)(2,1)S(1)} %constant_dynamic-update-slice_fusion, bf16[1,3584,256]{2,1,0:T(8,128)(2,1)S(1)} %copy-done.4), kind=kOutput, calls=%fused_computation.6 | convolution fusion | flops 117440512 | bytes 2359296 | tf_op jit(solution)/shard_map/dot_general | solution.py:114
  15.2 0.0 copy-done.5
  15.2 0.4 %fusion.10 = f32[64,256]{1,0:T(8,128)S(1)} fusion(bf16[64,3584]{1,0:T(8,128)(2,1)S(1)} %constant_dynamic-update-slice_fusion, bf16[1,3584,256]{2,1,0:T(8,128)(2,1)S(1)} %copy-done.5), kind=kOutput, calls=%fused_computation.10 | convolution fusion | flops 117440512 | bytes 2359296 | tf_op jit(solution)/shard_map/dot_general | solution.py:114
  15.6 0.0 collective-permute-done.8.refs_0_
  15.7 0.0 collective-permute-done.6
  15.7 0.1 collective-permute-done.7
  15.8 0.1 collective-permute-start.9
  15.9 1.5 %collective-permute-start.5 = (bf16[64,512]{1,0:T(8,128)(2,1)S(1)}, bf16[64,512]{1,0:T(8,128)(2,1)S(1)}, u32[]{:S(2)}, u32[]{:S(2)}) collective-permute-start(bf16[64,512]{1,0:T(8,128)(2,1)S(1)} %fusion.15.refs_1_), channel_id=1, source_target_pairs={{0,1},{1,0},{2,3},{3,2},{4,5},{5,4},{6,7},{7,6},{8,9},{9,8},{10,11... | collective-permute-start | bytes 196616 | tf_op jit(solution)/shard_map/ppermute | solution.py:16
  17.4 0.0 collective-permute-done.9
  17.4 0.4 %fusion.4 = f32[64,256]{1,0:T(8,128)S(1)} fusion(bf16[1,3584,256]{2,1,0:T(8,128)(2,1)S(1)} %copy-done.4, bf16[32,3584]{1,0:T(8,128)(2,1)S(1)} %collective-permute-done.9, bf16[32,3584]{1,0:T(8,128)(2,1)S(1)} %shard_map.67), kind=kOutput, calls=%fused_computation.4 | convolution fusion | flops 118358016 | bytes 2359296 | tf_op jit(solution)/shard_map/dot_general | solution.py:114
  17.9 0.4 %fusion.8 = f32[64,256]{1,0:T(8,128)S(1)} fusion(bf16[1,3584,256]{2,1,0:T(8,128)(2,1)S(1)} %copy-done.5, bf16[32,3584]{1,0:T(8,128)(2,1)S(1)} %collective-permute-done.9, bf16[32,3584]{1,0:T(8,128)(2,1)S(1)} %shard_map.67), kind=kOutput, calls=%fused_computation.8 | convolution fusion | flops 118358016 | bytes 2359296 | tf_op jit(solution)/shard_map/dot_general | solution.py:114
  18.3 1.5 %collective-permute-start.14 = (bf16[64,512]{1,0:T(8,128)(2,1)S(1)}, bf16[64,512]{1,0:T(8,128)(2,1)S(1)}, u32[]{:S(2)}, u32[]{:S(2)}) collective-permute-start(bf16[64,512]{1,0:T(8,128)(2,1)S(1)} %fusion.14.refs_1_), channel_id=1, source_target_pairs={{0,1},{1,0},{2,3},{3,2},{4,5},{5,4},{6,7},{7,6},{8,9},{9,8},{10,11... | collective-permute-start | bytes 196616 | tf_op jit(solution)/shard_map/ppermute | solution.py:16
  19.8 0.5 %collective-permute-done.5.refs_0_ = bf16[64,512]{1,0:T(8,128)(2,1)S(1)} collective-permute-done((bf16[64,512]{1,0:T(8,128)(2,1)S(1)}, bf16[64,512]{1,0:T(8,128)(2,1)S(1)}, u32[]{:S(2)}, u32[]{:S(2)}) %collective-permute-start.5) | collective-permute-done | bytes 65568 | tf_op jit(solution)/shard_map/ppermute | solution.py:16
  20.4 0.0 copy-done
  20.4 0.4 %fusion.2.refs_0_ = f32[64,3584]{1,0:T(8,128)S(1)} fusion(bf16[1,256,3584]{2,1,0:T(8,128)(2,1)S(1)} %copy-done, f32[64,512]{1,0:T(8,128)S(1)} %convert_add_fusion.1), kind=kOutput, calls=%fused_computation.2 | convolution fusion | flops 117538816 | bytes 2883584 | tf_op jit(solution)/shard_map/dot_general | solution.py:125
  20.8 0.1 collective-permute-start.10
  20.9 1.5 %collective-permute-done.10 = bf16[32,3584]{1,0:T(8,128)(2,1)S(1)} collective-permute-done((bf16[32,3584]{1,0:T(8,128)(2,1)S(1)}, bf16[32,3584]{1,0:T(8,128)(2,1)S(1)}, u32[]{:S(2)}, u32[]{:S(2)}) %collective-permute-start.10) | collective-permute-done | bytes 229408 | tf_op jit(solution)/shard_map/ppermute | solution.py:39
  22.4 0.1 fusion.26
  22.5 0.2 collective-permute-done.14.refs_0_
  22.7 0.4 %fusion = f32[64,3584]{1,0:T(8,128)S(1)} fusion(bf16[1,256,3584]{2,1,0:T(8,128)(2,1)S(1)} %copy-done, f32[64,512]{1,0:T(8,128)S(1)} %convert_add_fusion), kind=kOutput, calls=%fused_computation | convolution fusion | flops 117538816 | bytes 2883584 | tf_op jit(solution)/shard_map/dot_general | solution.py:125
  23.1 0.0 copy-start.2
  23.1 0.0 copy-start.3
  23.2 0.1 collective-permute-start.15
  23.3 1.4 %collective-permute-start.13 = (bf16[8,3584]{1,0:T(8,128)(2,1)S(1)}, bf16[8,3584]{1,0:T(8,128)(2,1)S(1)}, u32[]{:S(2)}, u32[]{:S(2)}) collective-permute-start(bf16[8,3584]{1,0:T(8,128)(2,1)S(1)} %get-tuple-element.11), channel_id=1, source_target_pairs={{0,2},{2,0},{4,6},{6,4},{8,10},{10,8},{12,14},{14,12},{16,18},{18,... | collective-permute-start | bytes 172040 | tf_op jit(solution)/shard_map/ppermute | solution.py:35
  24.7 1.6 %collective-permute-start.12 = (bf16[8,3584]{1,0:T(8,128)(2,1)S(1)}, bf16[8,3584]{1,0:T(8,128)(2,1)S(1)}, u32[]{:S(2)}, u32[]{:S(2)}) collective-permute-start(bf16[8,3584]{1,0:T(8,128)(2,1)S(1)} %get-tuple-element.12), channel_id=1, source_target_pairs={{0,4},{2,6},{4,0},{6,2},{8,12},{10,14},{12,8},{14,10},{16,20},{18,... | collective-permute-start | bytes 172040 | tf_op jit(solution)/shard_map/ppermute | solution.py:35
  26.3 1.4 %collective-permute-start.11 = (bf16[8,3584]{1,0:T(8,128)(2,1)S(1)}, bf16[8,3584]{1,0:T(8,128)(2,1)S(1)}, u32[]{:S(2)}, u32[]{:S(2)}) collective-permute-start(bf16[8,3584]{1,0:T(8,128)(2,1)S(1)} %get-tuple-element.13), channel_id=1, source_target_pairs={{0,6},{2,4},{4,2},{6,0},{8,14},{10,12},{12,10},{14,8},{16,22},{18,... | collective-permute-start | bytes 172040 | tf_op jit(solution)/shard_map/ppermute | solution.py:35
  27.7 0.0 collective-permute-done.15
  27.8 0.3 collective-permute-start.19
  28.1 3.6 %collective-permute-start.18 = (bf16[8,3584]{1,0:T(8,128)(2,1)S(1)}, bf16[8,3584]{1,0:T(8,128)(2,1)S(1)}, u32[]{:S(2)}, u32[]{:S(2)}) collective-permute-start(bf16[8,3584]{1,0:T(8,128)(2,1)S(1)} %get-tuple-element.8), channel_id=1, source_target_pairs={{0,20},{2,22},{4,16},{6,18},{8,28},{10,30},{12,24},{14,26},{16,4},... | collective-permute-start | bytes 172040 | tf_op jit(solution)/shard_map/ppermute | solution.py:35
  31.7 0.0 collective-permute-done.13.refs_3_
  31.7 2.4 %collective-permute-start.17 = (bf16[8,3584]{1,0:T(8,128)(2,1)S(1)}, bf16[8,3584]{1,0:T(8,128)(2,1)S(1)}, u32[]{:S(2)}, u32[]{:S(2)}) collective-permute-start(bf16[8,3584]{1,0:T(8,128)(2,1)S(1)} %get-tuple-element.9), channel_id=1, source_target_pairs={{0,22},{2,20},{4,18},{6,16},{8,30},{10,28},{12,26},{14,24},{16,6},... | collective-permute-start | bytes 172040 | tf_op jit(solution)/shard_map/ppermute | solution.py:35
  34.1 0.0 collective-permute-done.12.refs_2_
  34.1 0.5 %collective-permute-start.16 = (bf16[8,3584]{1,0:T(8,128)(2,1)S(1)}, bf16[8,3584]{1,0:T(8,128)(2,1)S(1)}, u32[]{:S(2)}, u32[]{:S(2)}) collective-permute-start(bf16[8,3584]{1,0:T(8,128)(2,1)S(1)} %get-tuple-element.10), channel_id=1, source_target_pairs={{0,16},{2,18},{4,20},{6,22},{8,24},{10,26},{12,28},{14,30},{16,0},... | collective-permute-start | bytes 172040 | tf_op jit(solution)/shard_map/ppermute | solution.py:35
  34.6 0.0 collective-permute-done.11.refs_1_
  34.6 0.0 collective-permute-done.19.refs_7_
  34.7 0.7 %collective-permute-done.18.refs_6_ = bf16[8,3584]{1,0:T(8,128)(2,1)S(1)} collective-permute-done((bf16[8,3584]{1,0:T(8,128)(2,1)S(1)}, bf16[8,3584]{1,0:T(8,128)(2,1)S(1)}, u32[]{:S(2)}, u32[]{:S(2)}) %collective-permute-start.18) | collective-permute-done | bytes 57376 | tf_op jit(solution)/shard_map/ppermute | solution.py:35
  35.4 3.3 %collective-permute-done.17.refs_5_ = bf16[8,3584]{1,0:T(8,128)(2,1)S(1)} collective-permute-done((bf16[8,3584]{1,0:T(8,128)(2,1)S(1)}, bf16[8,3584]{1,0:T(8,128)(2,1)S(1)}, u32[]{:S(2)}, u32[]{:S(2)}) %collective-permute-start.17) | collective-permute-done | bytes 57376 | tf_op jit(solution)/shard_map/ppermute | solution.py:35
  38.7 0.2 collective-permute-done.16.refs_4_
  38.9 0.0 copy-done.2
  38.9 0.0 copy-done.3
  38.9 0.7 %shard_map.71 = bf16[8,3584]{1,0:T(8,128)(2,1)} custom-call(s32[1,8]{1,0:T(1,128)S(1)} %bitcast.31, s32[1,8]{1,0:T(1,128)S(1)} %bitcast.32, f32[8,3584]{1,0:T(8,128)S(1)} %slice.83.refs_0_, bf16[8,3584]{1,0:T(8,128)(2,1)S(1)} %collective-permute-done.11.refs_1_, bf16[8,3584]{1,0:T(8,128)(2,1)S(1)} %collective-permute-done.12.refs_2_, ...), custom_call_target="tpu_custom_call" | custom-call | tf_op jit(solution)/shard_map/pallas_call | solution.py:98
  (25 shorter events, 0.3 us)
Async XLA Ops:
  0.0 20.4 %copy-start = (bf16[1,256,3584]{2,1,0:T(8,128)(2,1)S(1)}, bf16[1,256,3584]{2,1,0:T(8,128)(2,1)}, u32[]{:S(2)}) copy-start(bf16[1,256,3584]{2,1,0:T(8,128)(2,1)} %param.11) | copy-start | bytes 5505028
  0.0 8.0 %collective-permute-start = (bf16[8,3584]{1,0:T(8,128)(2,1)}, bf16[8,3584]{1,0:T(8,128)(2,1)S(1)}, u32[]{:S(2)}, u32[]{:S(2)}) collective-permute-start(bf16[8,3584]{1,0:T(8,128)(2,1)} %from_ref.1), channel_id=1, source_target_pairs={{0,2},{2,0},{4,6},{6,4},{8,10},{10,8},{12,14},{14,12},{16,18},{18,... | collective-permute-start | bytes 172040 | tf_op jit(solution)/shard_map/ppermute | solution.py:35
  3.0 6.9 %collective-permute-start.2 = (bf16[8,3584]{1,0:T(8,128)(2,1)}, bf16[8,3584]{1,0:T(8,128)(2,1)S(1)}, u32[]{:S(2)}, u32[]{:S(2)}) collective-permute-start(bf16[8,3584]{1,0:T(8,128)(2,1)} %from_ref.1), channel_id=1, source_target_pairs={{0,6},{2,4},{4,2},{6,0},{8,14},{10,12},{12,10},{14,8},{16,22},{18,... | collective-permute-start | bytes 172040 | tf_op jit(solution)/shard_map/ppermute | solution.py:35
  5.5 6.1 %collective-permute-start.1 = (bf16[8,3584]{1,0:T(8,128)(2,1)}, bf16[8,3584]{1,0:T(8,128)(2,1)S(1)}, u32[]{:S(2)}, u32[]{:S(2)}) collective-permute-start(bf16[8,3584]{1,0:T(8,128)(2,1)} %from_ref.1), channel_id=1, source_target_pairs={{0,4},{2,6},{4,0},{6,2},{8,12},{10,14},{12,8},{14,10},{16,20},{18,... | collective-permute-start | bytes 172040 | tf_op jit(solution)/shard_map/ppermute | solution.py:35
  5.6 0.9 %copy-start.1 = (bf16[8,3584]{1,0:T(8,128)(2,1)S(1)}, bf16[8,3584]{1,0:T(8,128)(2,1)}, u32[]{:S(2)}) copy-start(bf16[8,3584]{1,0:T(8,128)(2,1)} %from_ref.1) | copy-start | bytes 172036
  6.5 8.2 %copy-start.4 = (bf16[1,3584,256]{2,1,0:T(8,128)(2,1)S(1)}, bf16[1,3584,256]{2,1,0:T(8,128)(2,1)}, u32[]{:S(2)}) copy-start(bf16[1,3584,256]{2,1,0:T(8,128)(2,1)} %param.10) | copy-start | bytes 5505028
  6.5 9.2 %collective-permute-start.6 = (bf16[8,3584]{1,0:T(8,128)(2,1)S(1)}, bf16[8,3584]{1,0:T(8,128)(2,1)S(1)}, u32[]{:S(2)}, u32[]{:S(2)}) collective-permute-start(bf16[8,3584]{1,0:T(8,128)(2,1)S(1)} %shard_map.64), channel_id=1, source_target_pairs={{0,16},{8,24},{16,0},{24,8},{1,17},{9,25},{17,1},{25,9},{2,18},{10... | collective-permute-start | bytes 172040 | tf_op jit(solution)/shard_map/ppermute | solution.py:21
  8.0 5.1 %collective-permute-start.3 = (bf16[8,3584]{1,0:T(8,128)(2,1)S(1)}, bf16[8,3584]{1,0:T(8,128)(2,1)S(1)}, u32[]{:S(2)}, u32[]{:S(2)}) collective-permute-start(bf16[8,3584]{1,0:T(8,128)(2,1)S(1)} %collective-permute-done), channel_id=1, source_target_pairs={{0,16},{8,24},{16,0},{24,8},{1,17},{9,25},{17,1},{25,9},{2,18},{10... | collective-permute-start | bytes 172040 | tf_op jit(solution)/shard_map/ppermute | solution.py:21
  9.9 5.7 %collective-permute-start.8 = (bf16[8,3584]{1,0:T(8,128)(2,1)S(1)}, bf16[8,3584]{1,0:T(8,128)(2,1)S(1)}, u32[]{:S(2)}, u32[]{:S(2)}) collective-permute-start(bf16[8,3584]{1,0:T(8,128)(2,1)S(1)} %collective-permute-done.2), channel_id=1, source_target_pairs={{0,16},{8,24},{16,0},{24,8},{1,17},{9,25},{17,1},{25,9},{2,18},{10... | collective-permute-start | bytes 172040 | tf_op jit(solution)/shard_map/ppermute | solution.py:21
  11.6 4.2 %collective-permute-start.7 = (bf16[8,3584]{1,0:T(8,128)(2,1)S(1)}, bf16[8,3584]{1,0:T(8,128)(2,1)S(1)}, u32[]{:S(2)}, u32[]{:S(2)}) collective-permute-start(bf16[8,3584]{1,0:T(8,128)(2,1)S(1)} %collective-permute-done.1), channel_id=1, source_target_pairs={{0,16},{8,24},{16,0},{24,8},{1,17},{9,25},{17,1},{25,9},{2,18},{10... | collective-permute-start | bytes 172040 | tf_op jit(solution)/shard_map/ppermute | solution.py:21
  13.1 2.1 %copy-start.5 = (bf16[1,3584,256]{2,1,0:T(8,128)(2,1)S(1)}, bf16[1,3584,256]{2,1,0:T(8,128)(2,1)}, u32[]{:S(2)}) copy-start(bf16[1,3584,256]{2,1,0:T(8,128)(2,1)} %param.9) | copy-start | bytes 5505028
  13.1 1.6 %collective-permute-start.4 = (bf16[32,3584]{1,0:T(8,128)(2,1)S(1)}, bf16[32,3584]{1,0:T(8,128)(2,1)S(1)}, u32[]{:S(2)}, u32[]{:S(2)}) collective-permute-start(bf16[32,3584]{1,0:T(8,128)(2,1)S(1)} %shard_map.65), channel_id=1, source_target_pairs={{0,8},{8,0},{16,24},{24,16},{1,9},{9,1},{17,25},{25,17},{2,10},{10... | collective-permute-start | bytes 688136 | tf_op jit(solution)/shard_map/ppermute | solution.py:39
  15.8 1.7 %collective-permute-start.9 = (bf16[32,3584]{1,0:T(8,128)(2,1)S(1)}, bf16[32,3584]{1,0:T(8,128)(2,1)S(1)}, u32[]{:S(2)}, u32[]{:S(2)}) collective-permute-start(bf16[32,3584]{1,0:T(8,128)(2,1)S(1)} %pad_maximum_fusion.4.refs_0_), channel_id=1, source_target_pairs={{0,8},{8,0},{16,24},{24,16},{1,9},{9,1},{17,25},{25,17},{2,10},{10... | collective-permute-start | bytes 688136 | tf_op jit(solution)/shard_map/ppermute | solution.py:39
  15.9 4.4 %collective-permute-start.5 = (bf16[64,512]{1,0:T(8,128)(2,1)S(1)}, bf16[64,512]{1,0:T(8,128)(2,1)S(1)}, u32[]{:S(2)}, u32[]{:S(2)}) collective-permute-start(bf16[64,512]{1,0:T(8,128)(2,1)S(1)} %fusion.15.refs_1_), channel_id=1, source_target_pairs={{0,1},{1,0},{2,3},{3,2},{4,5},{5,4},{6,7},{7,6},{8,9},{9,8},{10,11... | collective-permute-start | bytes 196616 | tf_op jit(solution)/shard_map/ppermute | solution.py:16
  18.3 4.3 %collective-permute-start.14 = (bf16[64,512]{1,0:T(8,128)(2,1)S(1)}, bf16[64,512]{1,0:T(8,128)(2,1)S(1)}, u32[]{:S(2)}, u32[]{:S(2)}) collective-permute-start(bf16[64,512]{1,0:T(8,128)(2,1)S(1)} %fusion.14.refs_1_), channel_id=1, source_target_pairs={{0,1},{1,0},{2,3},{3,2},{4,5},{5,4},{6,7},{7,6},{8,9},{9,8},{10,11... | collective-permute-start | bytes 196616 | tf_op jit(solution)/shard_map/ppermute | solution.py:16
  20.8 1.6 %collective-permute-start.10 = (bf16[32,3584]{1,0:T(8,128)(2,1)S(1)}, bf16[32,3584]{1,0:T(8,128)(2,1)S(1)}, u32[]{:S(2)}, u32[]{:S(2)}) collective-permute-start(bf16[32,3584]{1,0:T(8,128)(2,1)S(1)} %slice.122), channel_id=1, source_target_pairs={{0,8},{8,0},{16,24},{24,16},{1,9},{9,1},{17,25},{25,17},{2,10},{10... | collective-permute-start | bytes 688136 | tf_op jit(solution)/shard_map/ppermute | solution.py:39
  23.1 15.8 %copy-start.2 = (s32[8,1]{0,1:T(1,128)S(1)}, s32[8,1]{0,1:T(1,128)}, u32[]{:S(2)}) copy-start(s32[8,1]{0,1:T(1,128)} %param.7) | copy-start | bytes 100
  23.1 15.8 %copy-start.3 = (s32[8,1]{0,1:T(1,128)S(1)}, s32[8,1]{0,1:T(1,128)}, u32[]{:S(2)}) copy-start(s32[8,1]{0,1:T(1,128)} %param.8) | copy-start | bytes 100
  23.2 4.6 %collective-permute-start.15 = (bf16[32,3584]{1,0:T(8,128)(2,1)S(1)}, bf16[32,3584]{1,0:T(8,128)(2,1)S(1)}, u32[]{:S(2)}, u32[]{:S(2)}) collective-permute-start(bf16[32,3584]{1,0:T(8,128)(2,1)S(1)} %slice.121), channel_id=1, source_target_pairs={{0,8},{8,0},{16,24},{24,16},{1,9},{9,1},{17,25},{25,17},{2,10},{10... | collective-permute-start | bytes 688136 | tf_op jit(solution)/shard_map/ppermute | solution.py:39
  23.3 8.5 %collective-permute-start.13 = (bf16[8,3584]{1,0:T(8,128)(2,1)S(1)}, bf16[8,3584]{1,0:T(8,128)(2,1)S(1)}, u32[]{:S(2)}, u32[]{:S(2)}) collective-permute-start(bf16[8,3584]{1,0:T(8,128)(2,1)S(1)} %get-tuple-element.11), channel_id=1, source_target_pairs={{0,2},{2,0},{4,6},{6,4},{8,10},{10,8},{12,14},{14,12},{16,18},{18,... | collective-permute-start | bytes 172040 | tf_op jit(solution)/shard_map/ppermute | solution.py:35
  24.7 9.4 %collective-permute-start.12 = (bf16[8,3584]{1,0:T(8,128)(2,1)S(1)}, bf16[8,3584]{1,0:T(8,128)(2,1)S(1)}, u32[]{:S(2)}, u32[]{:S(2)}) collective-permute-start(bf16[8,3584]{1,0:T(8,128)(2,1)S(1)} %get-tuple-element.12), channel_id=1, source_target_pairs={{0,4},{2,6},{4,0},{6,2},{8,12},{10,14},{12,8},{14,10},{16,20},{18,... | collective-permute-start | bytes 172040 | tf_op jit(solution)/shard_map/ppermute | solution.py:35
  26.3 8.3 %collective-permute-start.11 = (bf16[8,3584]{1,0:T(8,128)(2,1)S(1)}, bf16[8,3584]{1,0:T(8,128)(2,1)S(1)}, u32[]{:S(2)}, u32[]{:S(2)}) collective-permute-start(bf16[8,3584]{1,0:T(8,128)(2,1)S(1)} %get-tuple-element.13), channel_id=1, source_target_pairs={{0,6},{2,4},{4,2},{6,0},{8,14},{10,12},{12,10},{14,8},{16,22},{18,... | collective-permute-start | bytes 172040 | tf_op jit(solution)/shard_map/ppermute | solution.py:35
  27.8 6.8 %collective-permute-start.19 = (bf16[8,3584]{1,0:T(8,128)(2,1)S(1)}, bf16[8,3584]{1,0:T(8,128)(2,1)S(1)}, u32[]{:S(2)}, u32[]{:S(2)}) collective-permute-start(bf16[8,3584]{1,0:T(8,128)(2,1)S(1)} %get-tuple-element.7), channel_id=1, source_target_pairs={{0,18},{2,16},{4,22},{6,20},{8,26},{10,24},{12,30},{14,28},{16,2},... | collective-permute-start | bytes 172040 | tf_op jit(solution)/shard_map/ppermute | solution.py:35
  28.1 7.3 %collective-permute-start.18 = (bf16[8,3584]{1,0:T(8,128)(2,1)S(1)}, bf16[8,3584]{1,0:T(8,128)(2,1)S(1)}, u32[]{:S(2)}, u32[]{:S(2)}) collective-permute-start(bf16[8,3584]{1,0:T(8,128)(2,1)S(1)} %get-tuple-element.8), channel_id=1, source_target_pairs={{0,20},{2,22},{4,16},{6,18},{8,28},{10,30},{12,24},{14,26},{16,4},... | collective-permute-start | bytes 172040 | tf_op jit(solution)/shard_map/ppermute | solution.py:35
  31.7 7.0 %collective-permute-start.17 = (bf16[8,3584]{1,0:T(8,128)(2,1)S(1)}, bf16[8,3584]{1,0:T(8,128)(2,1)S(1)}, u32[]{:S(2)}, u32[]{:S(2)}) collective-permute-start(bf16[8,3584]{1,0:T(8,128)(2,1)S(1)} %get-tuple-element.9), channel_id=1, source_target_pairs={{0,22},{2,20},{4,18},{6,16},{8,30},{10,28},{12,26},{14,24},{16,6},... | collective-permute-start | bytes 172040 | tf_op jit(solution)/shard_map/ppermute | solution.py:35
  34.1 4.8 %collective-permute-start.16 = (bf16[8,3584]{1,0:T(8,128)(2,1)S(1)}, bf16[8,3584]{1,0:T(8,128)(2,1)S(1)}, u32[]{:S(2)}, u32[]{:S(2)}) collective-permute-start(bf16[8,3584]{1,0:T(8,128)(2,1)S(1)} %get-tuple-element.10), channel_id=1, source_target_pairs={{0,16},{2,18},{4,20},{6,22},{8,24},{10,26},{12,28},{14,30},{16,0},... | collective-permute-start | bytes 172040 | tf_op jit(solution)/shard_map/ppermute | solution.py:35

commit v10 on v7

--- a/solution.py
+++ b/solution.py
@@ -25,12 +25,12 @@
     return place ^ abs(step) if size & (size - 1) == 0 else (place + step) % size
 
 
-def exchange(value, by_expert, step):
+def exchange(value, by_expert, *steps):
     groups, n_tp = lax.axis_size("grp"), lax.axis_size("tp")
     pairs = []
     for g in range(groups):
         for t in range(n_tp):
-            to = (g + 2 * by_expert) % groups * n_tp + partner(t, step, n_tp)
+            to = (g + 2 * by_expert) % groups * n_tp + partner(t, steps[g % len(steps)], n_tp)
             pairs.append((g * n_tp + t, to))
     return lax.ppermute(value, ("grp", "tp"), pairs)
 
@@ -117,14 +117,36 @@
             part = part + other.astype(f32)
         hidden = (jax.nn.silu(part[:, :inner]) * part[:, inner:]).astype(bf16)
         out = jnp.dot(hidden, w_down, preferred_element_type=f32)
-        kept = out.shape[0] // 2
-        swapped = swap_half(out[kept:].astype(bf16)).astype(f32)
+        out = out.reshape(2, -1, n_tp, count, width)
+        kept, sent = [], []
+        for line in range(out.shape[1]):
+            own, other = out[0, line], out[1, line]
+            for t in (0, half):
+                kept.append(own[places.index(t)])
+                sent.append(other[places.index(t)])
+            for t in range(1, half):
+                low, high = places.index(t), places.index(n_tp - t)
+                for mine, theirs in ((own, other), (other, own)):
+                    kept.append(jnp.where(odd, mine[high], mine[low]))
+                    sent.append(jnp.where(odd, theirs[low], theirs[high]))
+        swapped = swap_half(jnp.concatenate(sent, axis=0).astype(bf16)).astype(f32)
+        kept = jnp.concatenate(kept, axis=0)
         if kept_flops:
-            out = after(after(out, *earlier) if earlier else out, flops=kept_flops)
-        return out[:kept] + swapped
+            kept = after(kept, flops=kept_flops)
+        return (kept + swapped).reshape(-1, n_tp * count, width)
 
+    def send_back(rows, by_expert):
+        rows = rows.astype(bf16)
+        pieces = [exchange(rows[2 * i * count : 2 * (i + 1) * count], by_expert, -i, i - n_tp) for i in range(1, half)]
+        pieces.append(exchange(rows[count : 2 * count], by_expert, -half))
+        if by_expert:
+            pieces.append(exchange(rows[:count], by_expert, 0))
+        return pieces
+
+    half = n_tp // 2
+    odd = lax.axis_index("grp") % 2 == 1
+    places = tuple(range(n_tp))
     held = copied(tokens)
-    places = tuple(range(n_tp))
     blocks = [held] + [exchange(tokens, 0, t) for t in places[1:]]
     far = [[rotate_experts(rows, s) for rows in blocks] for s in range(1, experts)]
     near = jnp.concatenate(blocks, axis=0)
@@ -137,13 +159,20 @@
     far = jnp.concatenate([after(far, flops=3450000000), far_swapped], axis=0)
     far_part, far_sent, far_others = partial_sums(far)
     near_out = partial_out(near_part, [after(other, far_sent) for other in near_others], 3450000000, 0)
-    near_out = near_out.reshape(n_tp, count, width)
-    near_sent = near_out[1:].astype(bf16)
-    pieces = [near_out[0]] + [exchange(near_sent[i], 0, -t) for i, t in enumerate(places[1:])]
-    far_out = partial_out(far_part, [after(other, near_sent) for other in far_others], 0, 0)
-    far_out = far_out.reshape(experts - 1, n_tp, count, width).astype(bf16)
-    for s in range(1, experts):
-        pieces += [exchange(far_out[experts - 1 - s, i], s, -t) for i, t in enumerate(places)]
+    backs = [send_back(near_out[0], 0)]
+    far_out = partial_out(far_part, [after(other, near_out) for other in far_others], 0, 0)
+    backs += [send_back(far_out[experts - 1 - s], s) for s in range(1, experts)]
+    late = [piece for back in backs[1:] for piece in back]
+    backs[0] = [after(piece, *late) for piece in backs[0]]
+    pairs = [back[i] for back in backs for i in range(half - 1)]
+    handed = jnp.concatenate([pair[count:] for pair in pairs], axis=0)
+    handed = swap_half(after(handed, *(piece for back in backs[1:] for piece in back[half - 1 :])))
+    handed = handed.reshape(experts, half - 1, count, width)
+    pieces = []
+    for s, back in enumerate(backs):
+        pieces += [back[half] if s else near_out[0, :count], back[half - 1]]
+        for i in range(half - 1):
+            pieces += [back[i][:count], handed[s, i]]
     return mix(expert_ids, gate_levels, pieces, n_tp, experts)
 
 

time: 39.5 us -> 40.8 us (1.033)
  waiting for transfers between devices: 9.18 us -> 12.7 us
  starting transfers between devices: 25.3 us -> 21.8 us
  local copies, waits for them, and re-layouts: 1.02 us -> 2.05 us
    ppermute x10 -> x8, starting transfers between devices: 16.9 us -> 13.1 us  [exchange(): return lax.ppermute(value, ('grp', 'tp'), pairs)]
    ppermute x10 -> x8, waiting for transfers between devices: 5.41 us -> 8.44 us  [exchange(): return lax.ppermute(value, ('grp', 'tp'), pairs)]
    unnamed x16 -> x20, local copies, waits for them, and re-layouts: 0.9 us -> 1.96 us
    ppermute x4 -> x5, waiting for transfers between devices: 2.93 us -> 3.43 us  [swap_half(): lax.ppermute(value, 'grp', [(i, i ^ 1) for i in range(lax.axis_size('grp'...]
  transfers between devices with their start and end apart: 20 -> 19, of which waited for: 10 -> 11; matrix products, arithmetic and copies ran while one was open for 6% -> 6% of each run, Pallas kernels for 0% -> 0%
where the time goes in v10:
time: 40.8 us; the launch traced here: 40.6 us
  starting transfers between devices  21.8 us (53%)
  waiting for transfers between devices  12.7 us (31%)
  matrix products  2.59 us (6%)
  local copies, waits for them, and re-layouts  2.05 us (5%)
  Pallas kernels  0.76 us (2%)
  other arithmetic  0.41 us (1%)
    ppermute x8, starting transfers between devices, exchange(): return lax.ppermute(value, ('grp', 'tp'), pairs)  13.1 us
    ppermute x8, waiting for transfers between devices, exchange(): return lax.ppermute(value, ('grp', 'tp'), pairs)  8.44 us
    ppermute x4, starting transfers between devices, rotate_experts(): lax.ppermute(value, 'grp', [(i, (i + 2 * by) % groups) for i in range(gro...  5.07 us
    ppermute x5, waiting for transfers between devices, swap_half(): lax.ppermute(value, 'grp', [(i, i ^ 1) for i in range(lax.axis_size('grp'...  3.43 us
    ppermute x2, starting transfers between devices, rotate(): lax.ppermute(value, axis, [(i, (i + by) % size) for i in range(size)])  3.08 us
    unnamed x20, local copies, waits for them, and re-layouts  1.96 us
    dot_general x4, matrix products, partial_sums(): jnp.dot(rows, w, preferred_element_type=f32)  1.76 us
    dot_general x2, matrix products, partial_out(): out = jnp.dot(hidden, w_down, preferred_element_type=f32)  0.83 us
  transfers between devices with their start and end apart: 19, of which 11 were waited for; matrix products, arithmetic and copies ran while one was open for 6% of the time, Pallas kernels for 0%

profile of v10, /device:TPU:0, one launch (start us, length us, event | category | flops | bytes accessed | tf_op | source)
XLA Modules:
  0.0 40.6 jit_solution(3277415537623996059)
XLA Ops:
  0.0 0.0 copy-start
  0.0 3.0 %collective-permute-start = (bf16[8,3584]{1,0:T(8,128)(2,1)}, bf16[8,3584]{1,0:T(8,128)(2,1)S(1)}, u32[]{:S(2)}, u32[]{:S(2)}) collective-permute-start(bf16[8,3584]{1,0:T(8,128)(2,1)} %from_ref.1), channel_id=1, source_target_pairs={{0,2},{2,0},{4,6},{6,4},{8,10},{10,8},{12,14},{14,12},{16,18},{18,... | collective-permute-start | bytes 172040 | tf_op jit(solution)/shard_map/ppermute | solution.py:35
  3.0 2.5 %collective-permute-start.2 = (bf16[8,3584]{1,0:T(8,128)(2,1)}, bf16[8,3584]{1,0:T(8,128)(2,1)S(1)}, u32[]{:S(2)}, u32[]{:S(2)}) collective-permute-start(bf16[8,3584]{1,0:T(8,128)(2,1)} %from_ref.1), channel_id=1, source_target_pairs={{0,6},{2,4},{4,2},{6,0},{8,14},{10,12},{12,10},{14,8},{16,22},{18,... | collective-permute-start | bytes 172040 | tf_op jit(solution)/shard_map/ppermute | solution.py:35
  5.5 0.1 collective-permute-start.1
  5.6 0.0 copy-start.1
  5.6 0.9 %copy-done.1 = bf16[8,3584]{1,0:T(8,128)(2,1)S(1)} copy-done((bf16[8,3584]{1,0:T(8,128)(2,1)S(1)}, bf16[8,3584]{1,0:T(8,128)(2,1)}, u32[]{:S(2)}) %copy-start.1) | copy-done | bytes 57368
  6.5 0.0 copy-start.4
  6.5 1.5 %collective-permute-start.6 = (bf16[8,3584]{1,0:T(8,128)(2,1)S(1)}, bf16[8,3584]{1,0:T(8,128)(2,1)S(1)}, u32[]{:S(2)}, u32[]{:S(2)}) collective-permute-start(bf16[8,3584]{1,0:T(8,128)(2,1)S(1)} %shard_map.64), channel_id=1, source_target_pairs={{0,16},{8,24},{16,0},{24,8},{1,17},{9,25},{17,1},{25,9},{2,18},{10... | collective-permute-start | bytes 172040 | tf_op jit(solution)/shard_map/ppermute | solution.py:21
  8.0 0.0 collective-permute-done
  8.0 0.6 %collective-permute-start.3 = (bf16[8,3584]{1,0:T(8,128)(2,1)S(1)}, bf16[8,3584]{1,0:T(8,128)(2,1)S(1)}, u32[]{:S(2)}, u32[]{:S(2)}) collective-permute-start(bf16[8,3584]{1,0:T(8,128)(2,1)S(1)} %collective-permute-done), channel_id=1, source_target_pairs={{0,16},{8,24},{16,0},{24,8},{1,17},{9,25},{17,1},{25,9},{2,18},{10... | collective-permute-start | bytes 172040 | tf_op jit(solution)/shard_map/ppermute | solution.py:21
  8.6 1.3 %collective-permute-done.2 = bf16[8,3584]{1,0:T(8,128)(2,1)S(1)} collective-permute-done((bf16[8,3584]{1,0:T(8,128)(2,1)}, bf16[8,3584]{1,0:T(8,128)(2,1)S(1)}, u32[]{:S(2)}, u32[]{:S(2)}) %collective-permute-start.2) | collective-permute-done | bytes 57376 | tf_op jit(solution)/shard_map/ppermute | solution.py:35
  9.9 1.5 %collective-permute-start.8 = (bf16[8,3584]{1,0:T(8,128)(2,1)S(1)}, bf16[8,3584]{1,0:T(8,128)(2,1)S(1)}, u32[]{:S(2)}, u32[]{:S(2)}) collective-permute-start(bf16[8,3584]{1,0:T(8,128)(2,1)S(1)} %collective-permute-done.2), channel_id=1, source_target_pairs={{0,16},{8,24},{16,0},{24,8},{1,17},{9,25},{17,1},{25,9},{2,18},{10... | collective-permute-start | bytes 172040 | tf_op jit(solution)/shard_map/ppermute | solution.py:21
  11.4 0.1 collective-permute-done.1
  11.6 1.5 %collective-permute-start.7 = (bf16[8,3584]{1,0:T(8,128)(2,1)S(1)}, bf16[8,3584]{1,0:T(8,128)(2,1)S(1)}, u32[]{:S(2)}, u32[]{:S(2)}) collective-permute-start(bf16[8,3584]{1,0:T(8,128)(2,1)S(1)} %collective-permute-done.1), channel_id=1, source_target_pairs={{0,16},{8,24},{16,0},{24,8},{1,17},{9,25},{17,1},{25,9},{2,18},{10... | collective-permute-start | bytes 172040 | tf_op jit(solution)/shard_map/ppermute | solution.py:21
  13.1 0.0 copy-start.6
  13.1 0.0 collective-permute-done.3.refs_1_
  13.1 0.1 collective-permute-start.4
  13.2 1.5 %collective-permute-done.4 = bf16[32,3584]{1,0:T(8,128)(2,1)S(1)} collective-permute-done((bf16[32,3584]{1,0:T(8,128)(2,1)S(1)}, bf16[32,3584]{1,0:T(8,128)(2,1)S(1)}, u32[]{:S(2)}, u32[]{:S(2)}) %collective-permute-start.4) | collective-permute-done | bytes 229408 | tf_op jit(solution)/shard_map/ppermute | solution.py:39
  14.7 0.0 copy-done.4
  14.7 0.4 %fusion.6 = f32[64,256]{1,0:T(8,128)S(1)} fusion(bf16[64,3584]{1,0:T(8,128)(2,1)S(1)} %constant_dynamic-update-slice_fusion, bf16[1,3584,256]{2,1,0:T(8,128)(2,1)S(1)} %copy-done.4), kind=kOutput, calls=%fused_computation.6 | convolution fusion | flops 117440512 | bytes 2359296 | tf_op jit(solution)/shard_map/dot_general | solution.py:108
  15.2 0.0 copy-done.6
  15.2 0.4 %fusion.10 = f32[64,256]{1,0:T(8,128)S(1)} fusion(bf16[64,3584]{1,0:T(8,128)(2,1)S(1)} %constant_dynamic-update-slice_fusion, bf16[1,3584,256]{2,1,0:T(8,128)(2,1)S(1)} %copy-done.6), kind=kOutput, calls=%fused_computation.10 | convolution fusion | flops 117440512 | bytes 2359296 | tf_op jit(solution)/shard_map/dot_general | solution.py:108
  15.6 0.0 collective-permute-done.8.refs_0_
  15.6 0.0 collective-permute-done.6
  15.7 0.1 collective-permute-done.7
  15.8 0.1 collective-permute-start.9
  15.9 0.0 copy-start.5
  15.9 1.6 %collective-permute-start.5 = (bf16[64,512]{1,0:T(8,128)(2,1)S(1)}, bf16[64,512]{1,0:T(8,128)(2,1)S(1)}, u32[]{:S(2)}, u32[]{:S(2)}) collective-permute-start(bf16[64,512]{1,0:T(8,128)(2,1)S(1)} %fusion.16.refs_1_), channel_id=1, source_target_pairs={{0,1},{1,0},{2,3},{3,2},{4,5},{5,4},{6,7},{7,6},{8,9},{9,8},{10,11... | collective-permute-start | bytes 196616 | tf_op jit(solution)/shard_map/ppermute | solution.py:16
  17.5 0.0 collective-permute-done.9
  17.5 0.0 copy-done.5
  17.5 0.0 copy-start.7
  17.5 0.4 %fusion.4 = f32[64,256]{1,0:T(8,128)S(1)} fusion(bf16[1,3584,256]{2,1,0:T(8,128)(2,1)S(1)} %copy-done.5, bf16[32,3584]{1,0:T(8,128)(2,1)S(1)} %collective-permute-done.9, bf16[32,3584]{1,0:T(8,128)(2,1)S(1)} %shard_map.67), kind=kOutput, calls=%fused_computation.4 | convolution fusion | flops 118358016 | bytes 2359296 | tf_op jit(solution)/shard_map/dot_general | solution.py:108
  17.9 1.1 %copy-done.7 = bf16[1,3584,256]{2,1,0:T(8,128)(2,1)S(1)} copy-done((bf16[1,3584,256]{2,1,0:T(8,128)(2,1)S(1)}, bf16[1,3584,256]{2,1,0:T(8,128)(2,1)}, u32[]{:S(2)}) %copy-start.7) | copy-done | bytes 1835032
  19.0 0.4 %fusion.8 = f32[64,256]{1,0:T(8,128)S(1)} fusion(bf16[1,3584,256]{2,1,0:T(8,128)(2,1)S(1)} %copy-done.7, bf16[32,3584]{1,0:T(8,128)(2,1)S(1)} %collective-permute-done.9, bf16[32,3584]{1,0:T(8,128)(2,1)S(1)} %shard_map.67), kind=kOutput, calls=%fused_computation.8 | convolution fusion | flops 118358016 | bytes 2359296 | tf_op jit(solution)/shard_map/dot_general | solution.py:108
  19.4 1.5 %collective-permute-start.12 = (bf16[64,512]{1,0:T(8,128)(2,1)S(1)}, bf16[64,512]{1,0:T(8,128)(2,1)S(1)}, u32[]{:S(2)}, u32[]{:S(2)}) collective-permute-start(bf16[64,512]{1,0:T(8,128)(2,1)S(1)} %fusion.15.refs_1_), channel_id=1, source_target_pairs={{0,1},{1,0},{2,3},{3,2},{4,5},{5,4},{6,7},{7,6},{8,9},{9,8},{10,11... | collective-permute-start | bytes 196616 | tf_op jit(solution)/shard_map/ppermute | solution.py:16
  20.9 0.0 collective-permute-done.5.refs_0_
  21.0 0.0 copy-done
  21.0 0.4 %fusion.35 = (bf16[64,3584]{1,0:T(8,128)(2,1)S(1)}, f32[64,3584]{1,0:T(8,128)S(1)}) fusion(bf16[1,256,3584]{2,1,0:T(8,128)(2,1)S(1)} %copy-done, f32[64,512]{1,0:T(8,128)S(1)} %convert_add_fusion.2), kind=kOutput, calls=%fused_computation.62 | convolution fusion | flops 117768192 | bytes 3342336 | tf_op jit(solution)/shard_map/dot_general | solution.py:119
  21.5 0.2 collective-permute-start.10
  21.8 1.3 %collective-permute-done.10 = bf16[32,3584]{1,0:T(8,128)(2,1)S(1)} collective-permute-done((bf16[32,3584]{1,0:T(8,128)(2,1)S(1)}, bf16[32,3584]{1,0:T(8,128)(2,1)S(1)}, u32[]{:S(2)}, u32[]{:S(2)}) %collective-permute-start.10) | collective-permute-done | bytes 229408 | tf_op jit(solution)/shard_map/ppermute | solution.py:39
  23.1 0.1 fusion.13
  23.1 0.7 %collective-permute-done.12.refs_0_ = bf16[64,512]{1,0:T(8,128)(2,1)S(1)} collective-permute-done((bf16[64,512]{1,0:T(8,128)(2,1)S(1)}, bf16[64,512]{1,0:T(8,128)(2,1)S(1)}, u32[]{:S(2)}, u32[]{:S(2)}) %collective-permute-start.12) | collective-permute-done | bytes 65568 | tf_op jit(solution)/shard_map/ppermute | solution.py:16
  23.9 0.4 %fusion.36 = (bf16[64,3584]{1,0:T(8,128)(2,1)S(1)}, f32[64,3584]{1,0:T(8,128)S(1)}) fusion(bf16[1,256,3584]{2,1,0:T(8,128)(2,1)S(1)} %copy-done, f32[64,512]{1,0:T(8,128)S(1)} %convert_add_fusion.1), kind=kOutput, calls=%fused_computation.63 | convolution fusion | flops 117768192 | bytes 3342336 | tf_op jit(solution)/shard_map/dot_general | solution.py:119
  24.4 0.1 collective-permute-start.13
  24.5 1.3 %collective-permute-start.17 = (bf16[16,3584]{1,0:T(8,128)(2,1)S(1)}, bf16[16,3584]{1,0:T(8,128)(2,1)S(1)}, u32[]{:S(2)}, u32[]{:S(2)}) collective-permute-start(bf16[16,3584]{1,0:T(8,128)(2,1)S(1)} %slice.207), channel_id=1, source_target_pairs={{0,2},{2,0},{4,6},{6,4},{8,14},{10,12},{12,10},{14,8},{16,18},{18,... | collective-permute-start | bytes 344072 | tf_op jit(solution)/shard_map/ppermute | solution.py:35
  25.9 0.1 collective-permute-done.13
  25.9 0.0 copy-start.2
  25.9 0.0 copy-start.3
  26.0 1.7 %collective-permute-start.14 = (bf16[16,3584]{1,0:T(8,128)(2,1)S(1)}, bf16[16,3584]{1,0:T(8,128)(2,1)S(1)}, u32[]{:S(2)}, u32[]{:S(2)}) collective-permute-start(bf16[16,3584]{1,0:T(8,128)(2,1)S(1)} %slice.204), channel_id=1, source_target_pairs={{0,18},{2,16},{4,22},{6,20},{8,30},{10,28},{12,26},{14,24},{16,2},... | collective-permute-start | bytes 344072 | tf_op jit(solution)/shard_map/ppermute | solution.py:35
  27.7 1.2 %collective-permute-start.16 = (bf16[8,3584]{1,0:T(8,128)(2,1)S(1)}, bf16[8,3584]{1,0:T(8,128)(2,1)S(1)}, u32[]{:S(2)}, u32[]{:S(2)}) collective-permute-start(bf16[8,3584]{1,0:T(8,128)(2,1)S(1)} %get-tuple-element.23), channel_id=1, source_target_pairs={{0,16},{2,18},{4,20},{6,22},{8,24},{10,26},{12,28},{14,30},{16,0},... | collective-permute-start | bytes 172040 | tf_op jit(solution)/shard_map/ppermute | solution.py:35
  28.9 2.6 %collective-permute-start.15 = (bf16[8,3584]{1,0:T(8,128)(2,1)S(1)}, bf16[8,3584]{1,0:T(8,128)(2,1)S(1)}, u32[]{:S(2)}, u32[]{:S(2)}) collective-permute-start(bf16[8,3584]{1,0:T(8,128)(2,1)S(1)} %get-tuple-element.24), channel_id=1, source_target_pairs={{0,20},{2,22},{4,16},{6,18},{8,28},{10,30},{12,24},{14,26},{16,4},... | collective-permute-start | bytes 172040 | tf_op jit(solution)/shard_map/ppermute | solution.py:35
  31.5 0.7 %collective-permute-start.11 = (bf16[8,3584]{1,0:T(8,128)(2,1)S(1)}, bf16[8,3584]{1,0:T(8,128)(2,1)S(1)}, u32[]{:S(2)}, u32[]{:S(2)}) collective-permute-start(bf16[8,3584]{1,0:T(8,128)(2,1)S(1)} %slice.193), channel_id=1, source_target_pairs={{0,4},{2,6},{4,0},{6,2},{8,12},{10,14},{12,8},{14,10},{16,20},{18,... | collective-permute-start | bytes 172040 | tf_op jit(solution)/shard_map/ppermute | solution.py:35
  32.2 0.0 collective-permute-done.17.refs_0_
  32.2 1.1 %collective-permute-done.16.refs_3_.refs_2_.refs_4_ = bf16[8,3584]{1,0:T(8,128)(2,1)S(1)} collective-permute-done((bf16[8,3584]{1,0:T(8,128)(2,1)S(1)}, bf16[8,3584]{1,0:T(8,128)(2,1)S(1)}, u32[]{:S(2)}, u32[]{:S(2)}) %collective-permute-start.16) | collective-permute-done | bytes 57376 | tf_op jit(solution)/shard_map/ppermute | solution.py:35
  33.3 5.1 %collective-permute-done.15.refs_2_.refs_1_.refs_5_ = bf16[8,3584]{1,0:T(8,128)(2,1)S(1)} collective-permute-done((bf16[8,3584]{1,0:T(8,128)(2,1)S(1)}, bf16[8,3584]{1,0:T(8,128)(2,1)S(1)}, u32[]{:S(2)}, u32[]{:S(2)}) %collective-permute-start.15) | collective-permute-done | bytes 57376 | tf_op jit(solution)/shard_map/ppermute | solution.py:35
  38.4 0.0 collective-permute-done.14.refs_1_
  38.5 0.1 collective-permute-start.18
  38.6 0.7 %collective-permute-done.11.refs_0_ = bf16[8,3584]{1,0:T(8,128)(2,1)S(1)} collective-permute-done((bf16[8,3584]{1,0:T(8,128)(2,1)S(1)}, bf16[8,3584]{1,0:T(8,128)(2,1)S(1)}, u32[]{:S(2)}, u32[]{:S(2)}) %collective-permute-start.11) | collective-permute-done | bytes 57376 | tf_op jit(solution)/shard_map/ppermute | solution.py:35
  39.3 0.6 %collective-permute-done.18 = bf16[16,3584]{1,0:T(8,128)(2,1)S(1)} collective-permute-done((bf16[16,3584]{1,0:T(8,128)(2,1)S(1)}, bf16[16,3584]{1,0:T(8,128)(2,1)S(1)}, u32[]{:S(2)}, u32[]{:S(2)}) %collective-permute-start.18) | collective-permute-done | bytes 114720 | tf_op jit(solution)/shard_map/ppermute | solution.py:39
  39.9 0.0 copy-done.2
  39.9 0.0 copy-done.3
  39.9 0.7 %shard_map.74 = bf16[8,3584]{1,0:T(8,128)(2,1)} custom-call(s32[1,8]{1,0:T(1,128)S(1)} %bitcast.27, s32[1,8]{1,0:T(1,128)S(1)} %bitcast.28, f32[8,3584]{1,0:T(8,128)S(1)} %slice_bitcast_fusion.refs_0_, bf16[8,3584]{1,0:T(8,128)(2,1)S(1)} %shard_map.71.refs_1_, bf16[8,3584]{1,0:T(8,128)(2,1)S(1)} %get-tuple-element.30.refs_2_, ...), custom_call_target="tpu_custom_call" | custom-call | tf_op jit(solution)/shard_map/pallas_call | solution.py:92
  (39 shorter events, 0.5 us)
Async XLA Ops:
  0.0 21.0 %copy-start = (bf16[1,256,3584]{2,1,0:T(8,128)(2,1)S(1)}, bf16[1,256,3584]{2,1,0:T(8,128)(2,1)}, u32[]{:S(2)}) copy-start(bf16[1,256,3584]{2,1,0:T(8,128)(2,1)} %param.11) | copy-start | bytes 5505028
  0.0 8.0 %collective-permute-start = (bf16[8,3584]{1,0:T(8,128)(2,1)}, bf16[8,3584]{1,0:T(8,128)(2,1)S(1)}, u32[]{:S(2)}, u32[]{:S(2)}) collective-permute-start(bf16[8,3584]{1,0:T(8,128)(2,1)} %from_ref.1), channel_id=1, source_target_pairs={{0,2},{2,0},{4,6},{6,4},{8,10},{10,8},{12,14},{14,12},{16,18},{18,... | collective-permute-start | bytes 172040 | tf_op jit(solution)/shard_map/ppermute | solution.py:35
  3.0 6.9 %collective-permute-start.2 = (bf16[8,3584]{1,0:T(8,128)(2,1)}, bf16[8,3584]{1,0:T(8,128)(2,1)S(1)}, u32[]{:S(2)}, u32[]{:S(2)}) collective-permute-start(bf16[8,3584]{1,0:T(8,128)(2,1)} %from_ref.1), channel_id=1, source_target_pairs={{0,6},{2,4},{4,2},{6,0},{8,14},{10,12},{12,10},{14,8},{16,22},{18,... | collective-permute-start | bytes 172040 | tf_op jit(solution)/shard_map/ppermute | solution.py:35
  5.5 6.1 %collective-permute-start.1 = (bf16[8,3584]{1,0:T(8,128)(2,1)}, bf16[8,3584]{1,0:T(8,128)(2,1)S(1)}, u32[]{:S(2)}, u32[]{:S(2)}) collective-permute-start(bf16[8,3584]{1,0:T(8,128)(2,1)} %from_ref.1), channel_id=1, source_target_pairs={{0,4},{2,6},{4,0},{6,2},{8,12},{10,14},{12,8},{14,10},{16,20},{18,... | collective-permute-start | bytes 172040 | tf_op jit(solution)/shard_map/ppermute | solution.py:35
  5.6 0.9 %copy-start.1 = (bf16[8,3584]{1,0:T(8,128)(2,1)S(1)}, bf16[8,3584]{1,0:T(8,128)(2,1)}, u32[]{:S(2)}) copy-start(bf16[8,3584]{1,0:T(8,128)(2,1)} %from_ref.1) | copy-start | bytes 172036
  6.5 8.2 %copy-start.4 = (bf16[1,3584,256]{2,1,0:T(8,128)(2,1)S(1)}, bf16[1,3584,256]{2,1,0:T(8,128)(2,1)}, u32[]{:S(2)}) copy-start(bf16[1,3584,256]{2,1,0:T(8,128)(2,1)} %param.10) | copy-start | bytes 5505028
  6.5 9.2 %collective-permute-start.6 = (bf16[8,3584]{1,0:T(8,128)(2,1)S(1)}, bf16[8,3584]{1,0:T(8,128)(2,1)S(1)}, u32[]{:S(2)}, u32[]{:S(2)}) collective-permute-start(bf16[8,3584]{1,0:T(8,128)(2,1)S(1)} %shard_map.64), channel_id=1, source_target_pairs={{0,16},{8,24},{16,0},{24,8},{1,17},{9,25},{17,1},{25,9},{2,18},{10... | collective-permute-start | bytes 172040 | tf_op jit(solution)/shard_map/ppermute | solution.py:21
  8.0 5.1 %collective-permute-start.3 = (bf16[8,3584]{1,0:T(8,128)(2,1)S(1)}, bf16[8,3584]{1,0:T(8,128)(2,1)S(1)}, u32[]{:S(2)}, u32[]{:S(2)}) collective-permute-start(bf16[8,3584]{1,0:T(8,128)(2,1)S(1)} %collective-permute-done), channel_id=1, source_target_pairs={{0,16},{8,24},{16,0},{24,8},{1,17},{9,25},{17,1},{25,9},{2,18},{10... | collective-permute-start | bytes 172040 | tf_op jit(solution)/shard_map/ppermute | solution.py:21
  9.9 5.7 %collective-permute-start.8 = (bf16[8,3584]{1,0:T(8,128)(2,1)S(1)}, bf16[8,3584]{1,0:T(8,128)(2,1)S(1)}, u32[]{:S(2)}, u32[]{:S(2)}) collective-permute-start(bf16[8,3584]{1,0:T(8,128)(2,1)S(1)} %collective-permute-done.2), channel_id=1, source_target_pairs={{0,16},{8,24},{16,0},{24,8},{1,17},{9,25},{17,1},{25,9},{2,18},{10... | collective-permute-start | bytes 172040 | tf_op jit(solution)/shard_map/ppermute | solution.py:21
  11.6 4.2 %collective-permute-start.7 = (bf16[8,3584]{1,0:T(8,128)(2,1)S(1)}, bf16[8,3584]{1,0:T(8,128)(2,1)S(1)}, u32[]{:S(2)}, u32[]{:S(2)}) collective-permute-start(bf16[8,3584]{1,0:T(8,128)(2,1)S(1)} %collective-permute-done.1), channel_id=1, source_target_pairs={{0,16},{8,24},{16,0},{24,8},{1,17},{9,25},{17,1},{25,9},{2,18},{10... | collective-permute-start | bytes 172040 | tf_op jit(solution)/shard_map/ppermute | solution.py:21
  13.1 2.1 %copy-start.6 = (bf16[1,3584,256]{2,1,0:T(8,128)(2,1)S(1)}, bf16[1,3584,256]{2,1,0:T(8,128)(2,1)}, u32[]{:S(2)}) copy-start(bf16[1,3584,256]{2,1,0:T(8,128)(2,1)} %param.9) | copy-start | bytes 5505028
  13.1 1.6 %collective-permute-start.4 = (bf16[32,3584]{1,0:T(8,128)(2,1)S(1)}, bf16[32,3584]{1,0:T(8,128)(2,1)S(1)}, u32[]{:S(2)}, u32[]{:S(2)}) collective-permute-start(bf16[32,3584]{1,0:T(8,128)(2,1)S(1)} %shard_map.65), channel_id=1, source_target_pairs={{0,8},{8,0},{16,24},{24,16},{1,9},{9,1},{17,25},{25,17},{2,10},{10... | collective-permute-start | bytes 688136 | tf_op jit(solution)/shard_map/ppermute | solution.py:39
  15.8 1.7 %collective-permute-start.9 = (bf16[32,3584]{1,0:T(8,128)(2,1)S(1)}, bf16[32,3584]{1,0:T(8,128)(2,1)S(1)}, u32[]{:S(2)}, u32[]{:S(2)}) collective-permute-start(bf16[32,3584]{1,0:T(8,128)(2,1)S(1)} %pad_maximum_fusion.5.refs_0_), channel_id=1, source_target_pairs={{0,8},{8,0},{16,24},{24,16},{1,9},{9,1},{17,25},{25,17},{2,10},{10... | collective-permute-start | bytes 688136 | tf_op jit(solution)/shard_map/ppermute | solution.py:39
  15.9 1.6 %copy-start.5 = (bf16[1,3584,256]{2,1,0:T(8,128)(2,1)S(1)}, bf16[1,3584,256]{2,1,0:T(8,128)(2,1)}, u32[]{:S(2)}) copy-start(bf16[1,3584,256]{2,1,0:T(8,128)(2,1)} %param.10) | copy-start | bytes 5505028
  15.9 5.0 %collective-permute-start.5 = (bf16[64,512]{1,0:T(8,128)(2,1)S(1)}, bf16[64,512]{1,0:T(8,128)(2,1)S(1)}, u32[]{:S(2)}, u32[]{:S(2)}) collective-permute-start(bf16[64,512]{1,0:T(8,128)(2,1)S(1)} %fusion.16.refs_1_), channel_id=1, source_target_pairs={{0,1},{1,0},{2,3},{3,2},{4,5},{5,4},{6,7},{7,6},{8,9},{9,8},{10,11... | collective-permute-start | bytes 196616 | tf_op jit(solution)/shard_map/ppermute | solution.py:16
  17.5 1.5 %copy-start.7 = (bf16[1,3584,256]{2,1,0:T(8,128)(2,1)S(1)}, bf16[1,3584,256]{2,1,0:T(8,128)(2,1)}, u32[]{:S(2)}) copy-start(bf16[1,3584,256]{2,1,0:T(8,128)(2,1)} %param.9) | copy-start | bytes 5505028
  19.4 4.4 %collective-permute-start.12 = (bf16[64,512]{1,0:T(8,128)(2,1)S(1)}, bf16[64,512]{1,0:T(8,128)(2,1)S(1)}, u32[]{:S(2)}, u32[]{:S(2)}) collective-permute-start(bf16[64,512]{1,0:T(8,128)(2,1)S(1)} %fusion.15.refs_1_), channel_id=1, source_target_pairs={{0,1},{1,0},{2,3},{3,2},{4,5},{5,4},{6,7},{7,6},{8,9},{9,8},{10,11... | collective-permute-start | bytes 196616 | tf_op jit(solution)/shard_map/ppermute | solution.py:16
  21.5 1.6 %collective-permute-start.10 = (bf16[32,3584]{1,0:T(8,128)(2,1)S(1)}, bf16[32,3584]{1,0:T(8,128)(2,1)S(1)}, u32[]{:S(2)}, u32[]{:S(2)}) collective-permute-start(bf16[32,3584]{1,0:T(8,128)(2,1)S(1)} %pad_maximum_fusion.6), channel_id=1, source_target_pairs={{0,8},{8,0},{16,24},{24,16},{1,9},{9,1},{17,25},{25,17},{2,10},{10... | collective-permute-start | bytes 688136 | tf_op jit(solution)/shard_map/ppermute | solution.py:39
  24.4 1.6 %collective-permute-start.13 = (bf16[32,3584]{1,0:T(8,128)(2,1)S(1)}, bf16[32,3584]{1,0:T(8,128)(2,1)S(1)}, u32[]{:S(2)}, u32[]{:S(2)}) collective-permute-start(bf16[32,3584]{1,0:T(8,128)(2,1)S(1)} %pad_maximum_fusion.7), channel_id=1, source_target_pairs={{0,8},{8,0},{16,24},{24,16},{1,9},{9,1},{17,25},{25,17},{2,10},{10... | collective-permute-start | bytes 688136 | tf_op jit(solution)/shard_map/ppermute | solution.py:39
  24.5 7.6 %collective-permute-start.17 = (bf16[16,3584]{1,0:T(8,128)(2,1)S(1)}, bf16[16,3584]{1,0:T(8,128)(2,1)S(1)}, u32[]{:S(2)}, u32[]{:S(2)}) collective-permute-start(bf16[16,3584]{1,0:T(8,128)(2,1)S(1)} %slice.207), channel_id=1, source_target_pairs={{0,2},{2,0},{4,6},{6,4},{8,14},{10,12},{12,10},{14,8},{16,18},{18,... | collective-permute-start | bytes 344072 | tf_op jit(solution)/shard_map/ppermute | solution.py:35
  25.9 13.9 %copy-start.2 = (s32[8,1]{0,1:T(1,128)S(1)}, s32[8,1]{0,1:T(1,128)}, u32[]{:S(2)}) copy-start(s32[8,1]{0,1:T(1,128)} %param.7) | copy-start | bytes 100
  25.9 14.0 %copy-start.3 = (s32[8,1]{0,1:T(1,128)S(1)}, s32[8,1]{0,1:T(1,128)}, u32[]{:S(2)}) copy-start(s32[8,1]{0,1:T(1,128)} %param.8) | copy-start | bytes 100
  26.0 12.4 %collective-permute-start.14 = (bf16[16,3584]{1,0:T(8,128)(2,1)S(1)}, bf16[16,3584]{1,0:T(8,128)(2,1)S(1)}, u32[]{:S(2)}, u32[]{:S(2)}) collective-permute-start(bf16[16,3584]{1,0:T(8,128)(2,1)S(1)} %slice.204), channel_id=1, source_target_pairs={{0,18},{2,16},{4,22},{6,20},{8,30},{10,28},{12,26},{14,24},{16,2},... | collective-permute-start | bytes 344072 | tf_op jit(solution)/shard_map/ppermute | solution.py:35
  27.7 5.6 %collective-permute-start.16 = (bf16[8,3584]{1,0:T(8,128)(2,1)S(1)}, bf16[8,3584]{1,0:T(8,128)(2,1)S(1)}, u32[]{:S(2)}, u32[]{:S(2)}) collective-permute-start(bf16[8,3584]{1,0:T(8,128)(2,1)S(1)} %get-tuple-element.23), channel_id=1, source_target_pairs={{0,16},{2,18},{4,20},{6,22},{8,24},{10,26},{12,28},{14,30},{16,0},... | collective-permute-start | bytes 172040 | tf_op jit(solution)/shard_map/ppermute | solution.py:35
  28.9 9.5 %collective-permute-start.15 = (bf16[8,3584]{1,0:T(8,128)(2,1)S(1)}, bf16[8,3584]{1,0:T(8,128)(2,1)S(1)}, u32[]{:S(2)}, u32[]{:S(2)}) collective-permute-start(bf16[8,3584]{1,0:T(8,128)(2,1)S(1)} %get-tuple-element.24), channel_id=1, source_target_pairs={{0,20},{2,22},{4,16},{6,18},{8,28},{10,30},{12,24},{14,26},{16,4},... | collective-permute-start | bytes 172040 | tf_op jit(solution)/shard_map/ppermute | solution.py:35
  31.5 7.8 %collective-permute-start.11 = (bf16[8,3584]{1,0:T(8,128)(2,1)S(1)}, bf16[8,3584]{1,0:T(8,128)(2,1)S(1)}, u32[]{:S(2)}, u32[]{:S(2)}) collective-permute-start(bf16[8,3584]{1,0:T(8,128)(2,1)S(1)} %slice.193), channel_id=1, source_target_pairs={{0,4},{2,6},{4,0},{6,2},{8,12},{10,14},{12,8},{14,10},{16,20},{18,... | collective-permute-start | bytes 172040 | tf_op jit(solution)/shard_map/ppermute | solution.py:35
  38.5 1.4 %collective-permute-start.18 = (bf16[16,3584]{1,0:T(8,128)(2,1)S(1)}, bf16[16,3584]{1,0:T(8,128)(2,1)S(1)}, u32[]{:S(2)}, u32[]{:S(2)}) collective-permute-start(bf16[16,3584]{1,0:T(8,128)(2,1)S(1)} %shard_map.73), channel_id=1, source_target_pairs={{0,8},{8,0},{16,24},{24,16},{1,9},{9,1},{17,25},{25,17},{2,10},{10... | collective-permute-start | bytes 344072 | tf_op jit(solution)/shard_map/ppermute | solution.py:39

commit v11 on v8

--- a/solution.py
+++ b/solution.py
@@ -25,12 +25,12 @@
     return place ^ abs(step) if size & (size - 1) == 0 else (place + step) % size
 
 
-def exchange(value, by_expert, step):
+def exchange(value, by_expert, *steps):
     groups, n_tp = lax.axis_size("grp"), lax.axis_size("tp")
     pairs = []
     for g in range(groups):
         for t in range(n_tp):
-            to = (g + 2 * by_expert) % groups * n_tp + partner(t, step, n_tp)
+            to = (g + 2 * by_expert) % groups * n_tp + partner(t, steps[g % len(steps)], n_tp)
             pairs.append((g * n_tp + t, to))
     return lax.ppermute(value, ("grp", "tp"), pairs)
 
@@ -110,21 +110,33 @@
         sent = part.astype(bf16)
         return part, sent, [rotate(sent, "ex", s) for s in range(1, n_ex)]
 
-    def partial_out(part, others, kept_flops, part_flops=0, *earlier):
+    def partial_out(part, others, paired, kept_flops, part_flops=0):
         if part_flops:
             part = after(part, flops=part_flops)
         for other in others:
             part = part + other.astype(f32)
         hidden = (jax.nn.silu(part[:, :inner]) * part[:, inner:]).astype(bf16)
         out = jnp.dot(hidden, w_down, preferred_element_type=f32)
-        kept = out.shape[0] // 2
-        swapped = swap_half(out[kept:].astype(bf16)).astype(f32)
+        kept, sent = jnp.split(out, 2, axis=0)
+        if paired:
+            own, other = kept.reshape(n_tp, count, width), sent.reshape(n_tp, count, width)
+            kept = [own[places.index(t)] for t in (0, half)]
+            sent = [other[places.index(t)] for t in (0, half)]
+            for t in range(1, half):
+                low, high = places.index(t), places.index(n_tp - t)
+                for mine, theirs in ((own, other), (other, own)):
+                    kept.append(jnp.where(odd, mine[high], mine[low]))
+                    sent.append(jnp.where(odd, theirs[low], theirs[high]))
+            kept, sent = jnp.concatenate(kept, axis=0), jnp.concatenate(sent, axis=0)
+        swapped = swap_half(sent.astype(bf16)).astype(f32)
         if kept_flops:
-            out = after(after(out, *earlier) if earlier else out, flops=kept_flops)
-        return out[:kept] + swapped
+            kept = after(kept, flops=kept_flops)
+        return kept + swapped
 
+    half = n_tp // 2
+    odd = lax.axis_index("grp") % 2 == 1
+    places = tuple(range(n_tp))
     held = copied(tokens)
-    places = tuple(range(n_tp))
     blocks = [held] + [exchange(tokens, 0, t) for t in places[1:]]
     far = [[rotate_experts(rows, s) for rows in blocks] for s in range(1, experts)]
     near = jnp.concatenate(blocks, axis=0)
@@ -136,14 +148,21 @@
     far_swapped = swap_half(far)
     far = jnp.concatenate([after(far, flops=3450000000), far_swapped], axis=0)
     far_part, far_sent, far_others = partial_sums(far)
-    near_out = partial_out(near_part, [after(other, far_sent) for other in near_others], 3450000000, 3450000000)
-    near_out = near_out.reshape(n_tp, count, width)
-    near_sent = near_out[1:].astype(bf16)
-    pieces = [near_out[0]] + [exchange(near_sent[i], 0, -t) for i, t in enumerate(places[1:])]
-    far_out = partial_out(far_part, [after(other, near_sent) for other in far_others], 0, 0)
+    near_out = partial_out(near_part, [after(other, far_sent) for other in near_others], True, 3450000000, 0)
+    near_sent = near_out[count:].astype(bf16)
+    middle = exchange(near_sent[:count], 0, -half)
+    pairs = [exchange(near_sent[(2 * i - 1) * count : (2 * i + 1) * count], 0, -i, i - n_tp) for i in range(1, half)]
+    far_out = partial_out(far_part, [after(other, near_out) for other in far_others], False, 0, 0)
     far_out = far_out.reshape(experts - 1, n_tp, count, width).astype(bf16)
+    far_back = []
     for s in range(1, experts):
-        pieces += [exchange(far_out[experts - 1 - s, i], s, -t) for i, t in enumerate(places)]
+        far_back += [exchange(far_out[experts - 1 - s, i], s, -t) for i, t in enumerate(places)]
+    pairs = [after(pair, far_back[n_tp - 1]) for pair in pairs]
+    handed = swap_half(jnp.concatenate([pair[count:] for pair in pairs], axis=0))
+    pieces = [near_out[:count], middle]
+    for i, pair in enumerate(pairs):
+        pieces += [pair[:count], handed[i * count : (i + 1) * count]]
+    pieces += far_back
     return mix(expert_ids, gate_levels, pieces, n_tp, experts)
 
 

time: 40.3 us -> 40.3 us (level)
  local copies, waits for them, and re-layouts: 1.02 us -> 2.06 us
  waiting for transfers between devices: 10.9 us -> 10.2 us
    ppermute x10 -> x9, starting transfers between devices: 16.9 us -> 15.2 us  [exchange(): return lax.ppermute(value, ('grp', 'tp'), pairs)]
    ppermute x10 -> x9, waiting for transfers between devices: 4.86 us -> 6.45 us  [exchange(): return lax.ppermute(value, ('grp', 'tp'), pairs)]
    ppermute x4 -> x5, waiting for transfers between devices: 4.39 us -> 2.88 us  [swap_half(): lax.ppermute(value, 'grp', [(i, i ^ 1) for i in range(lax.axis_size('grp'...]
    unnamed x16 -> x20, local copies, waits for them, and re-layouts: 0.9 us -> 1.96 us
    ppermute x2, starting transfers between devices: 2.16 us -> 3.08 us  [rotate(): lax.ppermute(value, axis, [(i, (i + by) % size) for i in range(size)])]
    ppermute x2, waiting for transfers between devices: 1.64 us -> 0.74 us  [rotate(): lax.ppermute(value, axis, [(i, (i + by) % size) for i in range(size)])]
  transfers between devices with their start and end apart: 20 -> 20, of which waited for: 9 -> 10; matrix products, arithmetic and copies ran while one was open for 6% -> 6% of each run, Pallas kernels for 0% -> 0%
where the time goes in v11:
time: 40.3 us; the launch traced here: 40.1 us
  starting transfers between devices  24 us (60%)
  waiting for transfers between devices  10.2 us (25%)
  matrix products  2.59 us (6%)
  local copies, waits for them, and re-layouts  2.06 us (5%)
  Pallas kernels  0.75 us (2%)
    ppermute x9, starting transfers between devices, exchange(): return lax.ppermute(value, ('grp', 'tp'), pairs)  15.2 us
    ppermute x9, waiting for transfers between devices, exchange(): return lax.ppermute(value, ('grp', 'tp'), pairs)  6.45 us
    ppermute x4, starting transfers between devices, rotate_experts(): lax.ppermute(value, 'grp', [(i, (i + 2 * by) % groups) for i in range(gro...  5.07 us
    ppermute x2, starting transfers between devices, rotate(): lax.ppermute(value, axis, [(i, (i + by) % size) for i in range(size)])  3.08 us
    ppermute x5, waiting for transfers between devices, swap_half(): lax.ppermute(value, 'grp', [(i, i ^ 1) for i in range(lax.axis_size('grp'...  2.88 us
    unnamed x20, local copies, waits for them, and re-layouts  1.96 us
    dot_general x4, matrix products, partial_sums(): jnp.dot(rows, w, preferred_element_type=f32)  1.76 us
    dot_general x2, matrix products, partial_out(): out = jnp.dot(hidden, w_down, preferred_element_type=f32)  0.83 us
  transfers between devices with their start and end apart: 20, of which 10 were waited for; matrix products, arithmetic and copies ran while one was open for 6% of the time, Pallas kernels for 0%

profile of v11, /device:TPU:0, one launch (start us, length us, event | category | flops | bytes accessed | tf_op | source)
XLA Modules:
  0.0 40.1 jit_solution(16584098890776319832)
XLA Ops:
  0.0 0.0 copy-start
  0.0 3.0 %collective-permute-start = (bf16[8,3584]{1,0:T(8,128)(2,1)}, bf16[8,3584]{1,0:T(8,128)(2,1)S(1)}, u32[]{:S(2)}, u32[]{:S(2)}) collective-permute-start(bf16[8,3584]{1,0:T(8,128)(2,1)} %from_ref.1), channel_id=1, source_target_pairs={{0,2},{2,0},{4,6},{6,4},{8,10},{10,8},{12,14},{14,12},{16,18},{18,... | collective-permute-start | bytes 172040 | tf_op jit(solution)/shard_map/ppermute | solution.py:35
  3.0 2.5 %collective-permute-start.2 = (bf16[8,3584]{1,0:T(8,128)(2,1)}, bf16[8,3584]{1,0:T(8,128)(2,1)S(1)}, u32[]{:S(2)}, u32[]{:S(2)}) collective-permute-start(bf16[8,3584]{1,0:T(8,128)(2,1)} %from_ref.1), channel_id=1, source_target_pairs={{0,6},{2,4},{4,2},{6,0},{8,14},{10,12},{12,10},{14,8},{16,22},{18,... | collective-permute-start | bytes 172040 | tf_op jit(solution)/shard_map/ppermute | solution.py:35
  5.5 0.1 collective-permute-start.1
  5.6 0.0 copy-start.1
  5.6 0.9 %copy-done.1 = bf16[8,3584]{1,0:T(8,128)(2,1)S(1)} copy-done((bf16[8,3584]{1,0:T(8,128)(2,1)S(1)}, bf16[8,3584]{1,0:T(8,128)(2,1)}, u32[]{:S(2)}) %copy-start.1) | copy-done | bytes 57368
  6.5 0.0 copy-start.4
  6.5 1.5 %collective-permute-start.6 = (bf16[8,3584]{1,0:T(8,128)(2,1)S(1)}, bf16[8,3584]{1,0:T(8,128)(2,1)S(1)}, u32[]{:S(2)}, u32[]{:S(2)}) collective-permute-start(bf16[8,3584]{1,0:T(8,128)(2,1)S(1)} %shard_map.64), channel_id=1, source_target_pairs={{0,16},{8,24},{16,0},{24,8},{1,17},{9,25},{17,1},{25,9},{2,18},{10... | collective-permute-start | bytes 172040 | tf_op jit(solution)/shard_map/ppermute | solution.py:21
  8.0 0.0 collective-permute-done
  8.0 0.6 %collective-permute-start.3 = (bf16[8,3584]{1,0:T(8,128)(2,1)S(1)}, bf16[8,3584]{1,0:T(8,128)(2,1)S(1)}, u32[]{:S(2)}, u32[]{:S(2)}) collective-permute-start(bf16[8,3584]{1,0:T(8,128)(2,1)S(1)} %collective-permute-done), channel_id=1, source_target_pairs={{0,16},{8,24},{16,0},{24,8},{1,17},{9,25},{17,1},{25,9},{2,18},{10... | collective-permute-start | bytes 172040 | tf_op jit(solution)/shard_map/ppermute | solution.py:21
  8.6 1.3 %collective-permute-done.2 = bf16[8,3584]{1,0:T(8,128)(2,1)S(1)} collective-permute-done((bf16[8,3584]{1,0:T(8,128)(2,1)}, bf16[8,3584]{1,0:T(8,128)(2,1)S(1)}, u32[]{:S(2)}, u32[]{:S(2)}) %collective-permute-start.2) | collective-permute-done | bytes 57376 | tf_op jit(solution)/shard_map/ppermute | solution.py:35
  9.9 1.5 %collective-permute-start.8 = (bf16[8,3584]{1,0:T(8,128)(2,1)S(1)}, bf16[8,3584]{1,0:T(8,128)(2,1)S(1)}, u32[]{:S(2)}, u32[]{:S(2)}) collective-permute-start(bf16[8,3584]{1,0:T(8,128)(2,1)S(1)} %collective-permute-done.2), channel_id=1, source_target_pairs={{0,16},{8,24},{16,0},{24,8},{1,17},{9,25},{17,1},{25,9},{2,18},{10... | collective-permute-start | bytes 172040 | tf_op jit(solution)/shard_map/ppermute | solution.py:21
  11.4 0.1 collective-permute-done.1
  11.6 1.5 %collective-permute-start.7 = (bf16[8,3584]{1,0:T(8,128)(2,1)S(1)}, bf16[8,3584]{1,0:T(8,128)(2,1)S(1)}, u32[]{:S(2)}, u32[]{:S(2)}) collective-permute-start(bf16[8,3584]{1,0:T(8,128)(2,1)S(1)} %collective-permute-done.1), channel_id=1, source_target_pairs={{0,16},{8,24},{16,0},{24,8},{1,17},{9,25},{17,1},{25,9},{2,18},{10... | collective-permute-start | bytes 172040 | tf_op jit(solution)/shard_map/ppermute | solution.py:21
  13.1 0.0 copy-start.6
  13.1 0.0 collective-permute-done.3.refs_1_
  13.1 0.1 collective-permute-start.4
  13.2 1.5 %collective-permute-done.4 = bf16[32,3584]{1,0:T(8,128)(2,1)S(1)} collective-permute-done((bf16[32,3584]{1,0:T(8,128)(2,1)S(1)}, bf16[32,3584]{1,0:T(8,128)(2,1)S(1)}, u32[]{:S(2)}, u32[]{:S(2)}) %collective-permute-start.4) | collective-permute-done | bytes 229408 | tf_op jit(solution)/shard_map/ppermute | solution.py:39
  14.7 0.0 copy-done.4
  14.7 0.4 %fusion.6 = f32[64,256]{1,0:T(8,128)S(1)} fusion(bf16[64,3584]{1,0:T(8,128)(2,1)S(1)} %constant_dynamic-update-slice_fusion, bf16[1,3584,256]{2,1,0:T(8,128)(2,1)S(1)} %copy-done.4), kind=kOutput, calls=%fused_computation.6 | convolution fusion | flops 117440512 | bytes 2359296 | tf_op jit(solution)/shard_map/dot_general | solution.py:108
  15.2 0.0 copy-done.6
  15.2 0.4 %fusion.10 = f32[64,256]{1,0:T(8,128)S(1)} fusion(bf16[64,3584]{1,0:T(8,128)(2,1)S(1)} %constant_dynamic-update-slice_fusion, bf16[1,3584,256]{2,1,0:T(8,128)(2,1)S(1)} %copy-done.6), kind=kOutput, calls=%fused_computation.10 | convolution fusion | flops 117440512 | bytes 2359296 | tf_op jit(solution)/shard_map/dot_general | solution.py:108
  15.6 0.0 collective-permute-done.8.refs_0_
  15.6 0.0 collective-permute-done.6
  15.7 0.1 collective-permute-done.7
  15.8 0.1 collective-permute-start.9
  15.9 0.0 copy-start.5
  15.9 1.6 %collective-permute-start.5 = (bf16[64,512]{1,0:T(8,128)(2,1)S(1)}, bf16[64,512]{1,0:T(8,128)(2,1)S(1)}, u32[]{:S(2)}, u32[]{:S(2)}) collective-permute-start(bf16[64,512]{1,0:T(8,128)(2,1)S(1)} %fusion.15.refs_1_), channel_id=1, source_target_pairs={{0,1},{1,0},{2,3},{3,2},{4,5},{5,4},{6,7},{7,6},{8,9},{9,8},{10,11... | collective-permute-start | bytes 196616 | tf_op jit(solution)/shard_map/ppermute | solution.py:16
  17.5 0.0 collective-permute-done.9
  17.5 0.0 copy-done.5
  17.5 0.0 copy-start.7
  17.5 0.4 %fusion.4 = f32[64,256]{1,0:T(8,128)S(1)} fusion(bf16[1,3584,256]{2,1,0:T(8,128)(2,1)S(1)} %copy-done.5, bf16[32,3584]{1,0:T(8,128)(2,1)S(1)} %collective-permute-done.9, bf16[32,3584]{1,0:T(8,128)(2,1)S(1)} %shard_map.67), kind=kOutput, calls=%fused_computation.4 | convolution fusion | flops 118358016 | bytes 2359296 | tf_op jit(solution)/shard_map/dot_general | solution.py:108
  17.9 1.1 %copy-done.7 = bf16[1,3584,256]{2,1,0:T(8,128)(2,1)S(1)} copy-done((bf16[1,3584,256]{2,1,0:T(8,128)(2,1)S(1)}, bf16[1,3584,256]{2,1,0:T(8,128)(2,1)}, u32[]{:S(2)}) %copy-start.7) | copy-done | bytes 1835032
  19.0 0.4 %fusion.8 = f32[64,256]{1,0:T(8,128)S(1)} fusion(bf16[1,3584,256]{2,1,0:T(8,128)(2,1)S(1)} %copy-done.7, bf16[32,3584]{1,0:T(8,128)(2,1)S(1)} %collective-permute-done.9, bf16[32,3584]{1,0:T(8,128)(2,1)S(1)} %shard_map.67), kind=kOutput, calls=%fused_computation.8 | convolution fusion | flops 118358016 | bytes 2359296 | tf_op jit(solution)/shard_map/dot_general | solution.py:108
  19.4 1.5 %collective-permute-start.13 = (bf16[64,512]{1,0:T(8,128)(2,1)S(1)}, bf16[64,512]{1,0:T(8,128)(2,1)S(1)}, u32[]{:S(2)}, u32[]{:S(2)}) collective-permute-start(bf16[64,512]{1,0:T(8,128)(2,1)S(1)} %fusion.14.refs_1_), channel_id=1, source_target_pairs={{0,1},{1,0},{2,3},{3,2},{4,5},{5,4},{6,7},{7,6},{8,9},{9,8},{10,11... | collective-permute-start | bytes 196616 | tf_op jit(solution)/shard_map/ppermute | solution.py:16
  20.9 0.0 collective-permute-done.5.refs_0_
  21.0 0.0 copy-done
  21.0 0.4 %fusion.30 = (bf16[64,3584]{1,0:T(8,128)(2,1)S(1)}, f32[64,3584]{1,0:T(8,128)S(1)}) fusion(bf16[1,256,3584]{2,1,0:T(8,128)(2,1)S(1)} %copy-done, f32[64,512]{1,0:T(8,128)S(1)} %convert_add_fusion.2), kind=kOutput, calls=%fused_computation.55 | convolution fusion | flops 117768192 | bytes 3342336 | tf_op jit(solution)/shard_map/dot_general | solution.py:119
  21.5 0.2 collective-permute-start.10
  21.8 1.3 %collective-permute-done.10 = bf16[32,3584]{1,0:T(8,128)(2,1)S(1)} collective-permute-done((bf16[32,3584]{1,0:T(8,128)(2,1)S(1)}, bf16[32,3584]{1,0:T(8,128)(2,1)S(1)}, u32[]{:S(2)}, u32[]{:S(2)}) %collective-permute-start.10) | collective-permute-done | bytes 229408 | tf_op jit(solution)/shard_map/ppermute | solution.py:39
  23.1 0.1 fusion.26
  23.1 0.7 %collective-permute-done.13.refs_0_ = bf16[64,512]{1,0:T(8,128)(2,1)S(1)} collective-permute-done((bf16[64,512]{1,0:T(8,128)(2,1)S(1)}, bf16[64,512]{1,0:T(8,128)(2,1)S(1)}, u32[]{:S(2)}, u32[]{:S(2)}) %collective-permute-start.13) | collective-permute-done | bytes 65568 | tf_op jit(solution)/shard_map/ppermute | solution.py:16
  23.9 0.4 %fusion = f32[64,3584]{1,0:T(8,128)S(1)} fusion(bf16[1,256,3584]{2,1,0:T(8,128)(2,1)S(1)} %copy-done, f32[64,512]{1,0:T(8,128)S(1)} %convert_add_fusion.1), kind=kOutput, calls=%fused_computation | convolution fusion | flops 117538816 | bytes 2883584 | tf_op jit(solution)/shard_map/dot_general | solution.py:119
  24.3 0.0 copy-start.2
  24.3 0.0 copy-start.3
  24.4 0.1 collective-permute-start.14
  24.5 1.3 %collective-permute-start.12 = (bf16[16,3584]{1,0:T(8,128)(2,1)S(1)}, bf16[16,3584]{1,0:T(8,128)(2,1)S(1)}, u32[]{:S(2)}, u32[]{:S(2)}) collective-permute-start(bf16[16,3584]{1,0:T(8,128)(2,1)S(1)} %slice.122), channel_id=1, source_target_pairs={{0,2},{2,0},{4,6},{6,4},{8,14},{10,12},{12,10},{14,8},{16,18},{18,... | collective-permute-start | bytes 344072 | tf_op jit(solution)/shard_map/ppermute | solution.py:35
  25.8 0.1 collective-permute-done.14
  26.0 3.4 %collective-permute-start.15 = (bf16[8,3584]{1,0:T(8,128)(2,1)S(1)}, bf16[8,3584]{1,0:T(8,128)(2,1)S(1)}, u32[]{:S(2)}, u32[]{:S(2)}) collective-permute-start(bf16[8,3584]{1,0:T(8,128)(2,1)S(1)} %get-tuple-element.18), channel_id=1, source_target_pairs={{0,22},{2,20},{4,18},{6,16},{8,30},{10,28},{12,26},{14,24},{16,6},... | collective-permute-start | bytes 172040 | tf_op jit(solution)/shard_map/ppermute | solution.py:35
  29.4 0.0 collective-permute-start.11
  29.4 2.9 %collective-permute-start.19 = (bf16[8,3584]{1,0:T(8,128)(2,1)S(1)}, bf16[8,3584]{1,0:T(8,128)(2,1)S(1)}, u32[]{:S(2)}, u32[]{:S(2)}) collective-permute-start(bf16[8,3584]{1,0:T(8,128)(2,1)S(1)} %get-tuple-element.15), channel_id=1, source_target_pairs={{0,20},{2,22},{4,16},{6,18},{8,28},{10,30},{12,24},{14,26},{16,4},... | collective-permute-start | bytes 172040 | tf_op jit(solution)/shard_map/ppermute | solution.py:35
  32.3 0.7 %collective-permute-start.18 = (bf16[8,3584]{1,0:T(8,128)(2,1)S(1)}, bf16[8,3584]{1,0:T(8,128)(2,1)S(1)}, u32[]{:S(2)}, u32[]{:S(2)}) collective-permute-start(bf16[8,3584]{1,0:T(8,128)(2,1)S(1)} %get-tuple-element.16), channel_id=1, source_target_pairs={{0,18},{2,16},{4,22},{6,20},{8,26},{10,24},{12,30},{14,28},{16,2},... | collective-permute-start | bytes 172040 | tf_op jit(solution)/shard_map/ppermute | solution.py:35
  33.0 0.0 collective-permute-done.12.refs_0_
  33.0 1.3 %collective-permute-start.17 = (bf16[8,3584]{1,0:T(8,128)(2,1)S(1)}, bf16[8,3584]{1,0:T(8,128)(2,1)S(1)}, u32[]{:S(2)}, u32[]{:S(2)}) collective-permute-start(bf16[8,3584]{1,0:T(8,128)(2,1)S(1)} %get-tuple-element.17), channel_id=1, source_target_pairs={{0,16},{2,18},{4,20},{6,22},{8,24},{10,26},{12,28},{14,30},{16,0},... | collective-permute-start | bytes 172040 | tf_op jit(solution)/shard_map/ppermute | solution.py:35
  34.3 0.0 collective-permute-done.15.refs_1_.refs_7_
  34.3 0.1 collective-permute-start.16
  34.4 3.0 %collective-permute-done.11.refs_1_ = bf16[8,3584]{1,0:T(8,128)(2,1)S(1)} collective-permute-done((bf16[8,3584]{1,0:T(8,128)(2,1)S(1)}, bf16[8,3584]{1,0:T(8,128)(2,1)S(1)}, u32[]{:S(2)}, u32[]{:S(2)}) %collective-permute-start.11) | collective-permute-done | bytes 57376 | tf_op jit(solution)/shard_map/ppermute | solution.py:35
  37.4 1.8 %collective-permute-done.19.refs_6_ = bf16[8,3584]{1,0:T(8,128)(2,1)S(1)} collective-permute-done((bf16[8,3584]{1,0:T(8,128)(2,1)S(1)}, bf16[8,3584]{1,0:T(8,128)(2,1)S(1)}, u32[]{:S(2)}, u32[]{:S(2)}) %collective-permute-start.19) | collective-permute-done | bytes 57376 | tf_op jit(solution)/shard_map/ppermute | solution.py:35
  39.2 0.2 collective-permute-done.18.refs_5_
  39.4 0.0 collective-permute-done.17.refs_4_
  39.4 0.0 collective-permute-done.16.refs_3_
  39.4 0.0 copy-done.2
  39.4 0.0 copy-done.3
  39.4 0.7 %shard_map.72 = bf16[8,3584]{1,0:T(8,128)(2,1)} custom-call(s32[1,8]{1,0:T(1,128)S(1)} %bitcast.31, s32[1,8]{1,0:T(1,128)S(1)} %bitcast.32, f32[8,3584]{1,0:T(8,128)S(1)} %slice.120.refs_0_, bf16[8,3584]{1,0:T(8,128)(2,1)S(1)} %collective-permute-done.11.refs_1_, bf16[8,3584]{1,0:T(8,128)(2,1)S(1)} %get-tuple-element.20.refs_2_, ...), custom_call_target="tpu_custom_call" | custom-call | tf_op jit(solution)/shard_map/pallas_call | solution.py:92
  (30 shorter events, 0.4 us)
Async XLA Ops:
  0.0 21.0 %copy-start = (bf16[1,256,3584]{2,1,0:T(8,128)(2,1)S(1)}, bf16[1,256,3584]{2,1,0:T(8,128)(2,1)}, u32[]{:S(2)}) copy-start(bf16[1,256,3584]{2,1,0:T(8,128)(2,1)} %param.11) | copy-start | bytes 5505028
  0.0 8.0 %collective-permute-start = (bf16[8,3584]{1,0:T(8,128)(2,1)}, bf16[8,3584]{1,0:T(8,128)(2,1)S(1)}, u32[]{:S(2)}, u32[]{:S(2)}) collective-permute-start(bf16[8,3584]{1,0:T(8,128)(2,1)} %from_ref.1), channel_id=1, source_target_pairs={{0,2},{2,0},{4,6},{6,4},{8,10},{10,8},{12,14},{14,12},{16,18},{18,... | collective-permute-start | bytes 172040 | tf_op jit(solution)/shard_map/ppermute | solution.py:35
  3.0 6.9 %collective-permute-start.2 = (bf16[8,3584]{1,0:T(8,128)(2,1)}, bf16[8,3584]{1,0:T(8,128)(2,1)S(1)}, u32[]{:S(2)}, u32[]{:S(2)}) collective-permute-start(bf16[8,3584]{1,0:T(8,128)(2,1)} %from_ref.1), channel_id=1, source_target_pairs={{0,6},{2,4},{4,2},{6,0},{8,14},{10,12},{12,10},{14,8},{16,22},{18,... | collective-permute-start | bytes 172040 | tf_op jit(solution)/shard_map/ppermute | solution.py:35
  5.5 6.1 %collective-permute-start.1 = (bf16[8,3584]{1,0:T(8,128)(2,1)}, bf16[8,3584]{1,0:T(8,128)(2,1)S(1)}, u32[]{:S(2)}, u32[]{:S(2)}) collective-permute-start(bf16[8,3584]{1,0:T(8,128)(2,1)} %from_ref.1), channel_id=1, source_target_pairs={{0,4},{2,6},{4,0},{6,2},{8,12},{10,14},{12,8},{14,10},{16,20},{18,... | collective-permute-start | bytes 172040 | tf_op jit(solution)/shard_map/ppermute | solution.py:35
  5.6 0.9 %copy-start.1 = (bf16[8,3584]{1,0:T(8,128)(2,1)S(1)}, bf16[8,3584]{1,0:T(8,128)(2,1)}, u32[]{:S(2)}) copy-start(bf16[8,3584]{1,0:T(8,128)(2,1)} %from_ref.1) | copy-start | bytes 172036
  6.5 8.2 %copy-start.4 = (bf16[1,3584,256]{2,1,0:T(8,128)(2,1)S(1)}, bf16[1,3584,256]{2,1,0:T(8,128)(2,1)}, u32[]{:S(2)}) copy-start(bf16[1,3584,256]{2,1,0:T(8,128)(2,1)} %param.10) | copy-start | bytes 5505028
  6.5 9.2 %collective-permute-start.6 = (bf16[8,3584]{1,0:T(8,128)(2,1)S(1)}, bf16[8,3584]{1,0:T(8,128)(2,1)S(1)}, u32[]{:S(2)}, u32[]{:S(2)}) collective-permute-start(bf16[8,3584]{1,0:T(8,128)(2,1)S(1)} %shard_map.64), channel_id=1, source_target_pairs={{0,16},{8,24},{16,0},{24,8},{1,17},{9,25},{17,1},{25,9},{2,18},{10... | collective-permute-start | bytes 172040 | tf_op jit(solution)/shard_map/ppermute | solution.py:21
  8.0 5.1 %collective-permute-start.3 = (bf16[8,3584]{1,0:T(8,128)(2,1)S(1)}, bf16[8,3584]{1,0:T(8,128)(2,1)S(1)}, u32[]{:S(2)}, u32[]{:S(2)}) collective-permute-start(bf16[8,3584]{1,0:T(8,128)(2,1)S(1)} %collective-permute-done), channel_id=1, source_target_pairs={{0,16},{8,24},{16,0},{24,8},{1,17},{9,25},{17,1},{25,9},{2,18},{10... | collective-permute-start | bytes 172040 | tf_op jit(solution)/shard_map/ppermute | solution.py:21
  9.9 5.7 %collective-permute-start.8 = (bf16[8,3584]{1,0:T(8,128)(2,1)S(1)}, bf16[8,3584]{1,0:T(8,128)(2,1)S(1)}, u32[]{:S(2)}, u32[]{:S(2)}) collective-permute-start(bf16[8,3584]{1,0:T(8,128)(2,1)S(1)} %collective-permute-done.2), channel_id=1, source_target_pairs={{0,16},{8,24},{16,0},{24,8},{1,17},{9,25},{17,1},{25,9},{2,18},{10... | collective-permute-start | bytes 172040 | tf_op jit(solution)/shard_map/ppermute | solution.py:21
  11.6 4.2 %collective-permute-start.7 = (bf16[8,3584]{1,0:T(8,128)(2,1)S(1)}, bf16[8,3584]{1,0:T(8,128)(2,1)S(1)}, u32[]{:S(2)}, u32[]{:S(2)}) collective-permute-start(bf16[8,3584]{1,0:T(8,128)(2,1)S(1)} %collective-permute-done.1), channel_id=1, source_target_pairs={{0,16},{8,24},{16,0},{24,8},{1,17},{9,25},{17,1},{25,9},{2,18},{10... | collective-permute-start | bytes 172040 | tf_op jit(solution)/shard_map/ppermute | solution.py:21
  13.1 2.1 %copy-start.6 = (bf16[1,3584,256]{2,1,0:T(8,128)(2,1)S(1)}, bf16[1,3584,256]{2,1,0:T(8,128)(2,1)}, u32[]{:S(2)}) copy-start(bf16[1,3584,256]{2,1,0:T(8,128)(2,1)} %param.9) | copy-start | bytes 5505028
  13.1 1.6 %collective-permute-start.4 = (bf16[32,3584]{1,0:T(8,128)(2,1)S(1)}, bf16[32,3584]{1,0:T(8,128)(2,1)S(1)}, u32[]{:S(2)}, u32[]{:S(2)}) collective-permute-start(bf16[32,3584]{1,0:T(8,128)(2,1)S(1)} %shard_map.65), channel_id=1, source_target_pairs={{0,8},{8,0},{16,24},{24,16},{1,9},{9,1},{17,25},{25,17},{2,10},{10... | collective-permute-start | bytes 688136 | tf_op jit(solution)/shard_map/ppermute | solution.py:39
  15.8 1.7 %collective-permute-start.9 = (bf16[32,3584]{1,0:T(8,128)(2,1)S(1)}, bf16[32,3584]{1,0:T(8,128)(2,1)S(1)}, u32[]{:S(2)}, u32[]{:S(2)}) collective-permute-start(bf16[32,3584]{1,0:T(8,128)(2,1)S(1)} %pad_maximum_fusion.5.refs_0_), channel_id=1, source_target_pairs={{0,8},{8,0},{16,24},{24,16},{1,9},{9,1},{17,25},{25,17},{2,10},{10... | collective-permute-start | bytes 688136 | tf_op jit(solution)/shard_map/ppermute | solution.py:39
  15.9 1.6 %copy-start.5 = (bf16[1,3584,256]{2,1,0:T(8,128)(2,1)S(1)}, bf16[1,3584,256]{2,1,0:T(8,128)(2,1)}, u32[]{:S(2)}) copy-start(bf16[1,3584,256]{2,1,0:T(8,128)(2,1)} %param.10) | copy-start | bytes 5505028
  15.9 5.0 %collective-permute-start.5 = (bf16[64,512]{1,0:T(8,128)(2,1)S(1)}, bf16[64,512]{1,0:T(8,128)(2,1)S(1)}, u32[]{:S(2)}, u32[]{:S(2)}) collective-permute-start(bf16[64,512]{1,0:T(8,128)(2,1)S(1)} %fusion.15.refs_1_), channel_id=1, source_target_pairs={{0,1},{1,0},{2,3},{3,2},{4,5},{5,4},{6,7},{7,6},{8,9},{9,8},{10,11... | collective-permute-start | bytes 196616 | tf_op jit(solution)/shard_map/ppermute | solution.py:16
  17.5 1.5 %copy-start.7 = (bf16[1,3584,256]{2,1,0:T(8,128)(2,1)S(1)}, bf16[1,3584,256]{2,1,0:T(8,128)(2,1)}, u32[]{:S(2)}) copy-start(bf16[1,3584,256]{2,1,0:T(8,128)(2,1)} %param.9) | copy-start | bytes 5505028
  19.4 4.4 %collective-permute-start.13 = (bf16[64,512]{1,0:T(8,128)(2,1)S(1)}, bf16[64,512]{1,0:T(8,128)(2,1)S(1)}, u32[]{:S(2)}, u32[]{:S(2)}) collective-permute-start(bf16[64,512]{1,0:T(8,128)(2,1)S(1)} %fusion.14.refs_1_), channel_id=1, source_target_pairs={{0,1},{1,0},{2,3},{3,2},{4,5},{5,4},{6,7},{7,6},{8,9},{9,8},{10,11... | collective-permute-start | bytes 196616 | tf_op jit(solution)/shard_map/ppermute | solution.py:16
  21.5 1.6 %collective-permute-start.10 = (bf16[32,3584]{1,0:T(8,128)(2,1)S(1)}, bf16[32,3584]{1,0:T(8,128)(2,1)S(1)}, u32[]{:S(2)}, u32[]{:S(2)}) collective-permute-start(bf16[32,3584]{1,0:T(8,128)(2,1)S(1)} %pad_maximum_fusion.6), channel_id=1, source_target_pairs={{0,8},{8,0},{16,24},{24,16},{1,9},{9,1},{17,25},{25,17},{2,10},{10... | collective-permute-start | bytes 688136 | tf_op jit(solution)/shard_map/ppermute | solution.py:39
  24.3 15.1 %copy-start.2 = (s32[8,1]{0,1:T(1,128)S(1)}, s32[8,1]{0,1:T(1,128)}, u32[]{:S(2)}) copy-start(s32[8,1]{0,1:T(1,128)} %param.7) | copy-start | bytes 100
  24.3 15.1 %copy-start.3 = (s32[8,1]{0,1:T(1,128)S(1)}, s32[8,1]{0,1:T(1,128)}, u32[]{:S(2)}) copy-start(s32[8,1]{0,1:T(1,128)} %param.8) | copy-start | bytes 100
  24.4 1.6 %collective-permute-start.14 = (bf16[32,3584]{1,0:T(8,128)(2,1)S(1)}, bf16[32,3584]{1,0:T(8,128)(2,1)S(1)}, u32[]{:S(2)}, u32[]{:S(2)}) collective-permute-start(bf16[32,3584]{1,0:T(8,128)(2,1)S(1)} %split.19), channel_id=1, source_target_pairs={{0,8},{8,0},{16,24},{24,16},{1,9},{9,1},{17,25},{25,17},{2,10},{10... | collective-permute-start | bytes 688136 | tf_op jit(solution)/shard_map/ppermute | solution.py:39
  24.5 8.5 %collective-permute-start.12 = (bf16[16,3584]{1,0:T(8,128)(2,1)S(1)}, bf16[16,3584]{1,0:T(8,128)(2,1)S(1)}, u32[]{:S(2)}, u32[]{:S(2)}) collective-permute-start(bf16[16,3584]{1,0:T(8,128)(2,1)S(1)} %slice.122), channel_id=1, source_target_pairs={{0,2},{2,0},{4,6},{6,4},{8,14},{10,12},{12,10},{14,8},{16,18},{18,... | collective-permute-start | bytes 344072 | tf_op jit(solution)/shard_map/ppermute | solution.py:35
  26.0 8.3 %collective-permute-start.15 = (bf16[8,3584]{1,0:T(8,128)(2,1)S(1)}, bf16[8,3584]{1,0:T(8,128)(2,1)S(1)}, u32[]{:S(2)}, u32[]{:S(2)}) collective-permute-start(bf16[8,3584]{1,0:T(8,128)(2,1)S(1)} %get-tuple-element.18), channel_id=1, source_target_pairs={{0,22},{2,20},{4,18},{6,16},{8,30},{10,28},{12,26},{14,24},{16,6},... | collective-permute-start | bytes 172040 | tf_op jit(solution)/shard_map/ppermute | solution.py:35
  29.4 8.0 %collective-permute-start.11 = (bf16[8,3584]{1,0:T(8,128)(2,1)S(1)}, bf16[8,3584]{1,0:T(8,128)(2,1)S(1)}, u32[]{:S(2)}, u32[]{:S(2)}) collective-permute-start(bf16[8,3584]{1,0:T(8,128)(2,1)S(1)} %slice.121), channel_id=1, source_target_pairs={{0,4},{2,6},{4,0},{6,2},{8,12},{10,14},{12,8},{14,10},{16,20},{18,... | collective-permute-start | bytes 172040 | tf_op jit(solution)/shard_map/ppermute | solution.py:35
  29.4 9.8 %collective-permute-start.19 = (bf16[8,3584]{1,0:T(8,128)(2,1)S(1)}, bf16[8,3584]{1,0:T(8,128)(2,1)S(1)}, u32[]{:S(2)}, u32[]{:S(2)}) collective-permute-start(bf16[8,3584]{1,0:T(8,128)(2,1)S(1)} %get-tuple-element.15), channel_id=1, source_target_pairs={{0,20},{2,22},{4,16},{6,18},{8,28},{10,30},{12,24},{14,26},{16,4},... | collective-permute-start | bytes 172040 | tf_op jit(solution)/shard_map/ppermute | solution.py:35
  32.3 7.0 %collective-permute-start.18 = (bf16[8,3584]{1,0:T(8,128)(2,1)S(1)}, bf16[8,3584]{1,0:T(8,128)(2,1)S(1)}, u32[]{:S(2)}, u32[]{:S(2)}) collective-permute-start(bf16[8,3584]{1,0:T(8,128)(2,1)S(1)} %get-tuple-element.16), channel_id=1, source_target_pairs={{0,18},{2,16},{4,22},{6,20},{8,26},{10,24},{12,30},{14,28},{16,2},... | collective-permute-start | bytes 172040 | tf_op jit(solution)/shard_map/ppermute | solution.py:35
  33.0 6.4 %collective-permute-start.17 = (bf16[8,3584]{1,0:T(8,128)(2,1)S(1)}, bf16[8,3584]{1,0:T(8,128)(2,1)S(1)}, u32[]{:S(2)}, u32[]{:S(2)}) collective-permute-start(bf16[8,3584]{1,0:T(8,128)(2,1)S(1)} %get-tuple-element.17), channel_id=1, source_target_pairs={{0,16},{2,18},{4,20},{6,22},{8,24},{10,26},{12,28},{14,30},{16,0},... | collective-permute-start | bytes 172040 | tf_op jit(solution)/shard_map/ppermute | solution.py:35
  34.3 5.1 %collective-permute-start.16 = (bf16[8,3584]{1,0:T(8,128)(2,1)S(1)}, bf16[8,3584]{1,0:T(8,128)(2,1)S(1)}, u32[]{:S(2)}, u32[]{:S(2)}) collective-permute-start(bf16[8,3584]{1,0:T(8,128)(2,1)S(1)} %get-tuple-element.19), channel_id=1, source_target_pairs={{0,8},{8,0},{16,24},{24,16},{1,9},{9,1},{17,25},{25,17},{2,10},{10... | collective-permute-start | bytes 172040 | tf_op jit(solution)/shard_map/ppermute | solution.py:39

commit v12 on v11

--- a/solution.py
+++ b/solution.py
@@ -146,9 +146,9 @@
     far = [after(rows, near_sent) if i == n_tp - 1 else rows for line in far for i, rows in enumerate(line)]
     far = jnp.concatenate(far, axis=0)
     far_swapped = swap_half(far)
-    far = jnp.concatenate([after(far, flops=3450000000), far_swapped], axis=0)
+    far = jnp.concatenate([after(far, flops=1725000000), far_swapped], axis=0)
     far_part, far_sent, far_others = partial_sums(far)
-    near_out = partial_out(near_part, [after(other, far_sent) for other in near_others], True, 3450000000, 0)
+    near_out = partial_out(near_part, [after(other, far_sent) for other in near_others], True, 1725000000, 0)
     near_sent = near_out[count:].astype(bf16)
     middle = exchange(near_sent[:count], 0, -half)
     pairs = [exchange(near_sent[(2 * i - 1) * count : (2 * i + 1) * count], 0, -i, i - n_tp) for i in range(1, half)]

time: 40.3 us -> 40.3 us (level)
  no operation moved by 1% of the time
where the time goes in v12:
time: 40.3 us; the launch traced here: 40.1 us
  starting transfers between devices  24 us (60%)
  waiting for transfers between devices  10.2 us (25%)
  matrix products  2.59 us (6%)
  local copies, waits for them, and re-layouts  2.06 us (5%)
  Pallas kernels  0.75 us (2%)
    ppermute x9, starting transfers between devices, exchange(): return lax.ppermute(value, ('grp', 'tp'), pairs)  15.2 us
    ppermute x9, waiting for transfers between devices, exchange(): return lax.ppermute(value, ('grp', 'tp'), pairs)  6.45 us
    ppermute x4, starting transfers between devices, rotate_experts(): lax.ppermute(value, 'grp', [(i, (i + 2 * by) % groups) for i in range(gro...  5.07 us
    ppermute x2, starting transfers between devices, rotate(): lax.ppermute(value, axis, [(i, (i + by) % size) for i in range(size)])  3.08 us
    ppermute x5, waiting for transfers between devices, swap_half(): lax.ppermute(value, 'grp', [(i, i ^ 1) for i in range(lax.axis_size('grp'...  2.88 us
    unnamed x20, local copies, waits for them, and re-layouts  1.96 us
    dot_general x4, matrix products, partial_sums(): jnp.dot(rows, w, preferred_element_type=f32)  1.76 us
    dot_general x2, matrix products, partial_out(): out = jnp.dot(hidden, w_down, preferred_element_type=f32)  0.83 us
  transfers between devices with their start and end apart: 20, of which 10 were waited for; matrix products, arithmetic and copies ran while one was open for 6% of the time, Pallas kernels for 0%

profile of v12, /device:TPU:0, one launch (start us, length us, event | category | flops | bytes accessed | tf_op | source)
XLA Modules:
  0.0 40.1 jit_solution(16584098890776319832)
XLA Ops:
  0.0 0.0 copy-start
  0.0 3.0 %collective-permute-start = (bf16[8,3584]{1,0:T(8,128)(2,1)}, bf16[8,3584]{1,0:T(8,128)(2,1)S(1)}, u32[]{:S(2)}, u32[]{:S(2)}) collective-permute-start(bf16[8,3584]{1,0:T(8,128)(2,1)} %from_ref.1), channel_id=1, source_target_pairs={{0,2},{2,0},{4,6},{6,4},{8,10},{10,8},{12,14},{14,12},{16,18},{18,... | collective-permute-start | bytes 172040 | tf_op jit(solution)/shard_map/ppermute | solution.py:35
  3.0 2.5 %collective-permute-start.2 = (bf16[8,3584]{1,0:T(8,128)(2,1)}, bf16[8,3584]{1,0:T(8,128)(2,1)S(1)}, u32[]{:S(2)}, u32[]{:S(2)}) collective-permute-start(bf16[8,3584]{1,0:T(8,128)(2,1)} %from_ref.1), channel_id=1, source_target_pairs={{0,6},{2,4},{4,2},{6,0},{8,14},{10,12},{12,10},{14,8},{16,22},{18,... | collective-permute-start | bytes 172040 | tf_op jit(solution)/shard_map/ppermute | solution.py:35
  5.5 0.1 collective-permute-start.1
  5.6 0.0 copy-start.1
  5.6 0.9 %copy-done.1 = bf16[8,3584]{1,0:T(8,128)(2,1)S(1)} copy-done((bf16[8,3584]{1,0:T(8,128)(2,1)S(1)}, bf16[8,3584]{1,0:T(8,128)(2,1)}, u32[]{:S(2)}) %copy-start.1) | copy-done | bytes 57368
  6.5 0.0 copy-start.4
  6.5 1.5 %collective-permute-start.6 = (bf16[8,3584]{1,0:T(8,128)(2,1)S(1)}, bf16[8,3584]{1,0:T(8,128)(2,1)S(1)}, u32[]{:S(2)}, u32[]{:S(2)}) collective-permute-start(bf16[8,3584]{1,0:T(8,128)(2,1)S(1)} %shard_map.64), channel_id=1, source_target_pairs={{0,16},{8,24},{16,0},{24,8},{1,17},{9,25},{17,1},{25,9},{2,18},{10... | collective-permute-start | bytes 172040 | tf_op jit(solution)/shard_map/ppermute | solution.py:21
  8.0 0.0 collective-permute-done
  8.0 0.6 %collective-permute-start.3 = (bf16[8,3584]{1,0:T(8,128)(2,1)S(1)}, bf16[8,3584]{1,0:T(8,128)(2,1)S(1)}, u32[]{:S(2)}, u32[]{:S(2)}) collective-permute-start(bf16[8,3584]{1,0:T(8,128)(2,1)S(1)} %collective-permute-done), channel_id=1, source_target_pairs={{0,16},{8,24},{16,0},{24,8},{1,17},{9,25},{17,1},{25,9},{2,18},{10... | collective-permute-start | bytes 172040 | tf_op jit(solution)/shard_map/ppermute | solution.py:21
  8.6 1.3 %collective-permute-done.2 = bf16[8,3584]{1,0:T(8,128)(2,1)S(1)} collective-permute-done((bf16[8,3584]{1,0:T(8,128)(2,1)}, bf16[8,3584]{1,0:T(8,128)(2,1)S(1)}, u32[]{:S(2)}, u32[]{:S(2)}) %collective-permute-start.2) | collective-permute-done | bytes 57376 | tf_op jit(solution)/shard_map/ppermute | solution.py:35
  9.9 1.5 %collective-permute-start.8 = (bf16[8,3584]{1,0:T(8,128)(2,1)S(1)}, bf16[8,3584]{1,0:T(8,128)(2,1)S(1)}, u32[]{:S(2)}, u32[]{:S(2)}) collective-permute-start(bf16[8,3584]{1,0:T(8,128)(2,1)S(1)} %collective-permute-done.2), channel_id=1, source_target_pairs={{0,16},{8,24},{16,0},{24,8},{1,17},{9,25},{17,1},{25,9},{2,18},{10... | collective-permute-start | bytes 172040 | tf_op jit(solution)/shard_map/ppermute | solution.py:21
  11.4 0.1 collective-permute-done.1
  11.6 1.5 %collective-permute-start.7 = (bf16[8,3584]{1,0:T(8,128)(2,1)S(1)}, bf16[8,3584]{1,0:T(8,128)(2,1)S(1)}, u32[]{:S(2)}, u32[]{:S(2)}) collective-permute-start(bf16[8,3584]{1,0:T(8,128)(2,1)S(1)} %collective-permute-done.1), channel_id=1, source_target_pairs={{0,16},{8,24},{16,0},{24,8},{1,17},{9,25},{17,1},{25,9},{2,18},{10... | collective-permute-start | bytes 172040 | tf_op jit(solution)/shard_map/ppermute | solution.py:21
  13.1 0.0 copy-start.6
  13.1 0.0 collective-permute-done.3.refs_1_
  13.1 0.1 collective-permute-start.4
  13.2 1.5 %collective-permute-done.4 = bf16[32,3584]{1,0:T(8,128)(2,1)S(1)} collective-permute-done((bf16[32,3584]{1,0:T(8,128)(2,1)S(1)}, bf16[32,3584]{1,0:T(8,128)(2,1)S(1)}, u32[]{:S(2)}, u32[]{:S(2)}) %collective-permute-start.4) | collective-permute-done | bytes 229408 | tf_op jit(solution)/shard_map/ppermute | solution.py:39
  14.7 0.0 copy-done.4
  14.7 0.4 %fusion.6 = f32[64,256]{1,0:T(8,128)S(1)} fusion(bf16[64,3584]{1,0:T(8,128)(2,1)S(1)} %constant_dynamic-update-slice_fusion, bf16[1,3584,256]{2,1,0:T(8,128)(2,1)S(1)} %copy-done.4), kind=kOutput, calls=%fused_computation.6 | convolution fusion | flops 117440512 | bytes 2359296 | tf_op jit(solution)/shard_map/dot_general | solution.py:108
  15.2 0.0 copy-done.6
  15.2 0.4 %fusion.10 = f32[64,256]{1,0:T(8,128)S(1)} fusion(bf16[64,3584]{1,0:T(8,128)(2,1)S(1)} %constant_dynamic-update-slice_fusion, bf16[1,3584,256]{2,1,0:T(8,128)(2,1)S(1)} %copy-done.6), kind=kOutput, calls=%fused_computation.10 | convolution fusion | flops 117440512 | bytes 2359296 | tf_op jit(solution)/shard_map/dot_general | solution.py:108
  15.6 0.0 collective-permute-done.8.refs_0_
  15.6 0.0 collective-permute-done.6
  15.7 0.1 collective-permute-done.7
  15.8 0.1 collective-permute-start.9
  15.9 0.0 copy-start.5
  15.9 1.6 %collective-permute-start.5 = (bf16[64,512]{1,0:T(8,128)(2,1)S(1)}, bf16[64,512]{1,0:T(8,128)(2,1)S(1)}, u32[]{:S(2)}, u32[]{:S(2)}) collective-permute-start(bf16[64,512]{1,0:T(8,128)(2,1)S(1)} %fusion.15.refs_1_), channel_id=1, source_target_pairs={{0,1},{1,0},{2,3},{3,2},{4,5},{5,4},{6,7},{7,6},{8,9},{9,8},{10,11... | collective-permute-start | bytes 196616 | tf_op jit(solution)/shard_map/ppermute | solution.py:16
  17.5 0.0 collective-permute-done.9
  17.5 0.0 copy-done.5
  17.5 0.0 copy-start.7
  17.5 0.4 %fusion.4 = f32[64,256]{1,0:T(8,128)S(1)} fusion(bf16[1,3584,256]{2,1,0:T(8,128)(2,1)S(1)} %copy-done.5, bf16[32,3584]{1,0:T(8,128)(2,1)S(1)} %collective-permute-done.9, bf16[32,3584]{1,0:T(8,128)(2,1)S(1)} %shard_map.67), kind=kOutput, calls=%fused_computation.4 | convolution fusion | flops 118358016 | bytes 2359296 | tf_op jit(solution)/shard_map/dot_general | solution.py:108
  17.9 1.1 %copy-done.7 = bf16[1,3584,256]{2,1,0:T(8,128)(2,1)S(1)} copy-done((bf16[1,3584,256]{2,1,0:T(8,128)(2,1)S(1)}, bf16[1,3584,256]{2,1,0:T(8,128)(2,1)}, u32[]{:S(2)}) %copy-start.7) | copy-done | bytes 1835032
  19.0 0.4 %fusion.8 = f32[64,256]{1,0:T(8,128)S(1)} fusion(bf16[1,3584,256]{2,1,0:T(8,128)(2,1)S(1)} %copy-done.7, bf16[32,3584]{1,0:T(8,128)(2,1)S(1)} %collective-permute-done.9, bf16[32,3584]{1,0:T(8,128)(2,1)S(1)} %shard_map.67), kind=kOutput, calls=%fused_computation.8 | convolution fusion | flops 118358016 | bytes 2359296 | tf_op jit(solution)/shard_map/dot_general | solution.py:108
  19.4 1.5 %collective-permute-start.13 = (bf16[64,512]{1,0:T(8,128)(2,1)S(1)}, bf16[64,512]{1,0:T(8,128)(2,1)S(1)}, u32[]{:S(2)}, u32[]{:S(2)}) collective-permute-start(bf16[64,512]{1,0:T(8,128)(2,1)S(1)} %fusion.14.refs_1_), channel_id=1, source_target_pairs={{0,1},{1,0},{2,3},{3,2},{4,5},{5,4},{6,7},{7,6},{8,9},{9,8},{10,11... | collective-permute-start | bytes 196616 | tf_op jit(solution)/shard_map/ppermute | solution.py:16
  20.9 0.0 collective-permute-done.5.refs_0_
  21.0 0.0 copy-done
  21.0 0.4 %fusion.30 = (bf16[64,3584]{1,0:T(8,128)(2,1)S(1)}, f32[64,3584]{1,0:T(8,128)S(1)}) fusion(bf16[1,256,3584]{2,1,0:T(8,128)(2,1)S(1)} %copy-done, f32[64,512]{1,0:T(8,128)S(1)} %convert_add_fusion.2), kind=kOutput, calls=%fused_computation.55 | convolution fusion | flops 117768192 | bytes 3342336 | tf_op jit(solution)/shard_map/dot_general | solution.py:119
  21.5 0.2 collective-permute-start.10
  21.8 1.3 %collective-permute-done.10 = bf16[32,3584]{1,0:T(8,128)(2,1)S(1)} collective-permute-done((bf16[32,3584]{1,0:T(8,128)(2,1)S(1)}, bf16[32,3584]{1,0:T(8,128)(2,1)S(1)}, u32[]{:S(2)}, u32[]{:S(2)}) %collective-permute-start.10) | collective-permute-done | bytes 229408 | tf_op jit(solution)/shard_map/ppermute | solution.py:39
  23.1 0.1 fusion.26
  23.1 0.7 %collective-permute-done.13.refs_0_ = bf16[64,512]{1,0:T(8,128)(2,1)S(1)} collective-permute-done((bf16[64,512]{1,0:T(8,128)(2,1)S(1)}, bf16[64,512]{1,0:T(8,128)(2,1)S(1)}, u32[]{:S(2)}, u32[]{:S(2)}) %collective-permute-start.13) | collective-permute-done | bytes 65568 | tf_op jit(solution)/shard_map/ppermute | solution.py:16
  23.9 0.4 %fusion = f32[64,3584]{1,0:T(8,128)S(1)} fusion(bf16[1,256,3584]{2,1,0:T(8,128)(2,1)S(1)} %copy-done, f32[64,512]{1,0:T(8,128)S(1)} %convert_add_fusion.1), kind=kOutput, calls=%fused_computation | convolution fusion | flops 117538816 | bytes 2883584 | tf_op jit(solution)/shard_map/dot_general | solution.py:119
  24.3 0.0 copy-start.2
  24.3 0.0 copy-start.3
  24.4 0.1 collective-permute-start.14
  24.5 1.3 %collective-permute-start.12 = (bf16[16,3584]{1,0:T(8,128)(2,1)S(1)}, bf16[16,3584]{1,0:T(8,128)(2,1)S(1)}, u32[]{:S(2)}, u32[]{:S(2)}) collective-permute-start(bf16[16,3584]{1,0:T(8,128)(2,1)S(1)} %slice.122), channel_id=1, source_target_pairs={{0,2},{2,0},{4,6},{6,4},{8,14},{10,12},{12,10},{14,8},{16,18},{18,... | collective-permute-start | bytes 344072 | tf_op jit(solution)/shard_map/ppermute | solution.py:35
  25.8 0.1 collective-permute-done.14
  26.0 3.4 %collective-permute-start.15 = (bf16[8,3584]{1,0:T(8,128)(2,1)S(1)}, bf16[8,3584]{1,0:T(8,128)(2,1)S(1)}, u32[]{:S(2)}, u32[]{:S(2)}) collective-permute-start(bf16[8,3584]{1,0:T(8,128)(2,1)S(1)} %get-tuple-element.18), channel_id=1, source_target_pairs={{0,22},{2,20},{4,18},{6,16},{8,30},{10,28},{12,26},{14,24},{16,6},... | collective-permute-start | bytes 172040 | tf_op jit(solution)/shard_map/ppermute | solution.py:35
  29.4 0.0 collective-permute-start.11
  29.4 2.9 %collective-permute-start.19 = (bf16[8,3584]{1,0:T(8,128)(2,1)S(1)}, bf16[8,3584]{1,0:T(8,128)(2,1)S(1)}, u32[]{:S(2)}, u32[]{:S(2)}) collective-permute-start(bf16[8,3584]{1,0:T(8,128)(2,1)S(1)} %get-tuple-element.15), channel_id=1, source_target_pairs={{0,20},{2,22},{4,16},{6,18},{8,28},{10,30},{12,24},{14,26},{16,4},... | collective-permute-start | bytes 172040 | tf_op jit(solution)/shard_map/ppermute | solution.py:35
  32.3 0.7 %collective-permute-start.18 = (bf16[8,3584]{1,0:T(8,128)(2,1)S(1)}, bf16[8,3584]{1,0:T(8,128)(2,1)S(1)}, u32[]{:S(2)}, u32[]{:S(2)}) collective-permute-start(bf16[8,3584]{1,0:T(8,128)(2,1)S(1)} %get-tuple-element.16), channel_id=1, source_target_pairs={{0,18},{2,16},{4,22},{6,20},{8,26},{10,24},{12,30},{14,28},{16,2},... | collective-permute-start | bytes 172040 | tf_op jit(solution)/shard_map/ppermute | solution.py:35
  33.0 0.0 collective-permute-done.12.refs_0_
  33.0 1.3 %collective-permute-start.17 = (bf16[8,3584]{1,0:T(8,128)(2,1)S(1)}, bf16[8,3584]{1,0:T(8,128)(2,1)S(1)}, u32[]{:S(2)}, u32[]{:S(2)}) collective-permute-start(bf16[8,3584]{1,0:T(8,128)(2,1)S(1)} %get-tuple-element.17), channel_id=1, source_target_pairs={{0,16},{2,18},{4,20},{6,22},{8,24},{10,26},{12,28},{14,30},{16,0},... | collective-permute-start | bytes 172040 | tf_op jit(solution)/shard_map/ppermute | solution.py:35
  34.3 0.0 collective-permute-done.15.refs_1_.refs_7_
  34.3 0.1 collective-permute-start.16
  34.4 3.0 %collective-permute-done.11.refs_1_ = bf16[8,3584]{1,0:T(8,128)(2,1)S(1)} collective-permute-done((bf16[8,3584]{1,0:T(8,128)(2,1)S(1)}, bf16[8,3584]{1,0:T(8,128)(2,1)S(1)}, u32[]{:S(2)}, u32[]{:S(2)}) %collective-permute-start.11) | collective-permute-done | bytes 57376 | tf_op jit(solution)/shard_map/ppermute | solution.py:35
  37.4 1.8 %collective-permute-done.19.refs_6_ = bf16[8,3584]{1,0:T(8,128)(2,1)S(1)} collective-permute-done((bf16[8,3584]{1,0:T(8,128)(2,1)S(1)}, bf16[8,3584]{1,0:T(8,128)(2,1)S(1)}, u32[]{:S(2)}, u32[]{:S(2)}) %collective-permute-start.19) | collective-permute-done | bytes 57376 | tf_op jit(solution)/shard_map/ppermute | solution.py:35
  39.2 0.2 collective-permute-done.18.refs_5_
  39.4 0.0 collective-permute-done.17.refs_4_
  39.4 0.0 collective-permute-done.16.refs_3_
  39.4 0.0 copy-done.2
  39.4 0.0 copy-done.3
  39.4 0.7 %shard_map.72 = bf16[8,3584]{1,0:T(8,128)(2,1)} custom-call(s32[1,8]{1,0:T(1,128)S(1)} %bitcast.31, s32[1,8]{1,0:T(1,128)S(1)} %bitcast.32, f32[8,3584]{1,0:T(8,128)S(1)} %slice.120.refs_0_, bf16[8,3584]{1,0:T(8,128)(2,1)S(1)} %collective-permute-done.11.refs_1_, bf16[8,3584]{1,0:T(8,128)(2,1)S(1)} %get-tuple-element.20.refs_2_, ...), custom_call_target="tpu_custom_call" | custom-call | tf_op jit(solution)/shard_map/pallas_call | solution.py:92
  (30 shorter events, 0.4 us)
Async XLA Ops:
  0.0 21.0 %copy-start = (bf16[1,256,3584]{2,1,0:T(8,128)(2,1)S(1)}, bf16[1,256,3584]{2,1,0:T(8,128)(2,1)}, u32[]{:S(2)}) copy-start(bf16[1,256,3584]{2,1,0:T(8,128)(2,1)} %param.11) | copy-start | bytes 5505028
  0.0 8.0 %collective-permute-start = (bf16[8,3584]{1,0:T(8,128)(2,1)}, bf16[8,3584]{1,0:T(8,128)(2,1)S(1)}, u32[]{:S(2)}, u32[]{:S(2)}) collective-permute-start(bf16[8,3584]{1,0:T(8,128)(2,1)} %from_ref.1), channel_id=1, source_target_pairs={{0,2},{2,0},{4,6},{6,4},{8,10},{10,8},{12,14},{14,12},{16,18},{18,... | collective-permute-start | bytes 172040 | tf_op jit(solution)/shard_map/ppermute | solution.py:35
  3.0 6.9 %collective-permute-start.2 = (bf16[8,3584]{1,0:T(8,128)(2,1)}, bf16[8,3584]{1,0:T(8,128)(2,1)S(1)}, u32[]{:S(2)}, u32[]{:S(2)}) collective-permute-start(bf16[8,3584]{1,0:T(8,128)(2,1)} %from_ref.1), channel_id=1, source_target_pairs={{0,6},{2,4},{4,2},{6,0},{8,14},{10,12},{12,10},{14,8},{16,22},{18,... | collective-permute-start | bytes 172040 | tf_op jit(solution)/shard_map/ppermute | solution.py:35
  5.5 6.1 %collective-permute-start.1 = (bf16[8,3584]{1,0:T(8,128)(2,1)}, bf16[8,3584]{1,0:T(8,128)(2,1)S(1)}, u32[]{:S(2)}, u32[]{:S(2)}) collective-permute-start(bf16[8,3584]{1,0:T(8,128)(2,1)} %from_ref.1), channel_id=1, source_target_pairs={{0,4},{2,6},{4,0},{6,2},{8,12},{10,14},{12,8},{14,10},{16,20},{18,... | collective-permute-start | bytes 172040 | tf_op jit(solution)/shard_map/ppermute | solution.py:35
  5.6 0.9 %copy-start.1 = (bf16[8,3584]{1,0:T(8,128)(2,1)S(1)}, bf16[8,3584]{1,0:T(8,128)(2,1)}, u32[]{:S(2)}) copy-start(bf16[8,3584]{1,0:T(8,128)(2,1)} %from_ref.1) | copy-start | bytes 172036
  6.5 8.2 %copy-start.4 = (bf16[1,3584,256]{2,1,0:T(8,128)(2,1)S(1)}, bf16[1,3584,256]{2,1,0:T(8,128)(2,1)}, u32[]{:S(2)}) copy-start(bf16[1,3584,256]{2,1,0:T(8,128)(2,1)} %param.10) | copy-start | bytes 5505028
  6.5 9.2 %collective-permute-start.6 = (bf16[8,3584]{1,0:T(8,128)(2,1)S(1)}, bf16[8,3584]{1,0:T(8,128)(2,1)S(1)}, u32[]{:S(2)}, u32[]{:S(2)}) collective-permute-start(bf16[8,3584]{1,0:T(8,128)(2,1)S(1)} %shard_map.64), channel_id=1, source_target_pairs={{0,16},{8,24},{16,0},{24,8},{1,17},{9,25},{17,1},{25,9},{2,18},{10... | collective-permute-start | bytes 172040 | tf_op jit(solution)/shard_map/ppermute | solution.py:21
  8.0 5.1 %collective-permute-start.3 = (bf16[8,3584]{1,0:T(8,128)(2,1)S(1)}, bf16[8,3584]{1,0:T(8,128)(2,1)S(1)}, u32[]{:S(2)}, u32[]{:S(2)}) collective-permute-start(bf16[8,3584]{1,0:T(8,128)(2,1)S(1)} %collective-permute-done), channel_id=1, source_target_pairs={{0,16},{8,24},{16,0},{24,8},{1,17},{9,25},{17,1},{25,9},{2,18},{10... | collective-permute-start | bytes 172040 | tf_op jit(solution)/shard_map/ppermute | solution.py:21
  9.9 5.7 %collective-permute-start.8 = (bf16[8,3584]{1,0:T(8,128)(2,1)S(1)}, bf16[8,3584]{1,0:T(8,128)(2,1)S(1)}, u32[]{:S(2)}, u32[]{:S(2)}) collective-permute-start(bf16[8,3584]{1,0:T(8,128)(2,1)S(1)} %collective-permute-done.2), channel_id=1, source_target_pairs={{0,16},{8,24},{16,0},{24,8},{1,17},{9,25},{17,1},{25,9},{2,18},{10... | collective-permute-start | bytes 172040 | tf_op jit(solution)/shard_map/ppermute | solution.py:21
  11.6 4.2 %collective-permute-start.7 = (bf16[8,3584]{1,0:T(8,128)(2,1)S(1)}, bf16[8,3584]{1,0:T(8,128)(2,1)S(1)}, u32[]{:S(2)}, u32[]{:S(2)}) collective-permute-start(bf16[8,3584]{1,0:T(8,128)(2,1)S(1)} %collective-permute-done.1), channel_id=1, source_target_pairs={{0,16},{8,24},{16,0},{24,8},{1,17},{9,25},{17,1},{25,9},{2,18},{10... | collective-permute-start | bytes 172040 | tf_op jit(solution)/shard_map/ppermute | solution.py:21
  13.1 2.1 %copy-start.6 = (bf16[1,3584,256]{2,1,0:T(8,128)(2,1)S(1)}, bf16[1,3584,256]{2,1,0:T(8,128)(2,1)}, u32[]{:S(2)}) copy-start(bf16[1,3584,256]{2,1,0:T(8,128)(2,1)} %param.9) | copy-start | bytes 5505028
  13.1 1.6 %collective-permute-start.4 = (bf16[32,3584]{1,0:T(8,128)(2,1)S(1)}, bf16[32,3584]{1,0:T(8,128)(2,1)S(1)}, u32[]{:S(2)}, u32[]{:S(2)}) collective-permute-start(bf16[32,3584]{1,0:T(8,128)(2,1)S(1)} %shard_map.65), channel_id=1, source_target_pairs={{0,8},{8,0},{16,24},{24,16},{1,9},{9,1},{17,25},{25,17},{2,10},{10... | collective-permute-start | bytes 688136 | tf_op jit(solution)/shard_map/ppermute | solution.py:39
  15.8 1.7 %collective-permute-start.9 = (bf16[32,3584]{1,0:T(8,128)(2,1)S(1)}, bf16[32,3584]{1,0:T(8,128)(2,1)S(1)}, u32[]{:S(2)}, u32[]{:S(2)}) collective-permute-start(bf16[32,3584]{1,0:T(8,128)(2,1)S(1)} %pad_maximum_fusion.5.refs_0_), channel_id=1, source_target_pairs={{0,8},{8,0},{16,24},{24,16},{1,9},{9,1},{17,25},{25,17},{2,10},{10... | collective-permute-start | bytes 688136 | tf_op jit(solution)/shard_map/ppermute | solution.py:39
  15.9 1.6 %copy-start.5 = (bf16[1,3584,256]{2,1,0:T(8,128)(2,1)S(1)}, bf16[1,3584,256]{2,1,0:T(8,128)(2,1)}, u32[]{:S(2)}) copy-start(bf16[1,3584,256]{2,1,0:T(8,128)(2,1)} %param.10) | copy-start | bytes 5505028
  15.9 5.0 %collective-permute-start.5 = (bf16[64,512]{1,0:T(8,128)(2,1)S(1)}, bf16[64,512]{1,0:T(8,128)(2,1)S(1)}, u32[]{:S(2)}, u32[]{:S(2)}) collective-permute-start(bf16[64,512]{1,0:T(8,128)(2,1)S(1)} %fusion.15.refs_1_), channel_id=1, source_target_pairs={{0,1},{1,0},{2,3},{3,2},{4,5},{5,4},{6,7},{7,6},{8,9},{9,8},{10,11... | collective-permute-start | bytes 196616 | tf_op jit(solution)/shard_map/ppermute | solution.py:16
  17.5 1.5 %copy-start.7 = (bf16[1,3584,256]{2,1,0:T(8,128)(2,1)S(1)}, bf16[1,3584,256]{2,1,0:T(8,128)(2,1)}, u32[]{:S(2)}) copy-start(bf16[1,3584,256]{2,1,0:T(8,128)(2,1)} %param.9) | copy-start | bytes 5505028
  19.4 4.4 %collective-permute-start.13 = (bf16[64,512]{1,0:T(8,128)(2,1)S(1)}, bf16[64,512]{1,0:T(8,128)(2,1)S(1)}, u32[]{:S(2)}, u32[]{:S(2)}) collective-permute-start(bf16[64,512]{1,0:T(8,128)(2,1)S(1)} %fusion.14.refs_1_), channel_id=1, source_target_pairs={{0,1},{1,0},{2,3},{3,2},{4,5},{5,4},{6,7},{7,6},{8,9},{9,8},{10,11... | collective-permute-start | bytes 196616 | tf_op jit(solution)/shard_map/ppermute | solution.py:16
  21.5 1.6 %collective-permute-start.10 = (bf16[32,3584]{1,0:T(8,128)(2,1)S(1)}, bf16[32,3584]{1,0:T(8,128)(2,1)S(1)}, u32[]{:S(2)}, u32[]{:S(2)}) collective-permute-start(bf16[32,3584]{1,0:T(8,128)(2,1)S(1)} %pad_maximum_fusion.6), channel_id=1, source_target_pairs={{0,8},{8,0},{16,24},{24,16},{1,9},{9,1},{17,25},{25,17},{2,10},{10... | collective-permute-start | bytes 688136 | tf_op jit(solution)/shard_map/ppermute | solution.py:39
  24.3 15.1 %copy-start.2 = (s32[8,1]{0,1:T(1,128)S(1)}, s32[8,1]{0,1:T(1,128)}, u32[]{:S(2)}) copy-start(s32[8,1]{0,1:T(1,128)} %param.7) | copy-start | bytes 100
  24.3 15.1 %copy-start.3 = (s32[8,1]{0,1:T(1,128)S(1)}, s32[8,1]{0,1:T(1,128)}, u32[]{:S(2)}) copy-start(s32[8,1]{0,1:T(1,128)} %param.8) | copy-start | bytes 100
  24.4 1.6 %collective-permute-start.14 = (bf16[32,3584]{1,0:T(8,128)(2,1)S(1)}, bf16[32,3584]{1,0:T(8,128)(2,1)S(1)}, u32[]{:S(2)}, u32[]{:S(2)}) collective-permute-start(bf16[32,3584]{1,0:T(8,128)(2,1)S(1)} %split.19), channel_id=1, source_target_pairs={{0,8},{8,0},{16,24},{24,16},{1,9},{9,1},{17,25},{25,17},{2,10},{10... | collective-permute-start | bytes 688136 | tf_op jit(solution)/shard_map/ppermute | solution.py:39
  24.5 8.5 %collective-permute-start.12 = (bf16[16,3584]{1,0:T(8,128)(2,1)S(1)}, bf16[16,3584]{1,0:T(8,128)(2,1)S(1)}, u32[]{:S(2)}, u32[]{:S(2)}) collective-permute-start(bf16[16,3584]{1,0:T(8,128)(2,1)S(1)} %slice.122), channel_id=1, source_target_pairs={{0,2},{2,0},{4,6},{6,4},{8,14},{10,12},{12,10},{14,8},{16,18},{18,... | collective-permute-start | bytes 344072 | tf_op jit(solution)/shard_map/ppermute | solution.py:35
  26.0 8.3 %collective-permute-start.15 = (bf16[8,3584]{1,0:T(8,128)(2,1)S(1)}, bf16[8,3584]{1,0:T(8,128)(2,1)S(1)}, u32[]{:S(2)}, u32[]{:S(2)}) collective-permute-start(bf16[8,3584]{1,0:T(8,128)(2,1)S(1)} %get-tuple-element.18), channel_id=1, source_target_pairs={{0,22},{2,20},{4,18},{6,16},{8,30},{10,28},{12,26},{14,24},{16,6},... | collective-permute-start | bytes 172040 | tf_op jit(solution)/shard_map/ppermute | solution.py:35
  29.4 8.0 %collective-permute-start.11 = (bf16[8,3584]{1,0:T(8,128)(2,1)S(1)}, bf16[8,3584]{1,0:T(8,128)(2,1)S(1)}, u32[]{:S(2)}, u32[]{:S(2)}) collective-permute-start(bf16[8,3584]{1,0:T(8,128)(2,1)S(1)} %slice.121), channel_id=1, source_target_pairs={{0,4},{2,6},{4,0},{6,2},{8,12},{10,14},{12,8},{14,10},{16,20},{18,... | collective-permute-start | bytes 172040 | tf_op jit(solution)/shard_map/ppermute | solution.py:35
  29.4 9.8 %collective-permute-start.19 = (bf16[8,3584]{1,0:T(8,128)(2,1)S(1)}, bf16[8,3584]{1,0:T(8,128)(2,1)S(1)}, u32[]{:S(2)}, u32[]{:S(2)}) collective-permute-start(bf16[8,3584]{1,0:T(8,128)(2,1)S(1)} %get-tuple-element.15), channel_id=1, source_target_pairs={{0,20},{2,22},{4,16},{6,18},{8,28},{10,30},{12,24},{14,26},{16,4},... | collective-permute-start | bytes 172040 | tf_op jit(solution)/shard_map/ppermute | solution.py:35
  32.3 7.0 %collective-permute-start.18 = (bf16[8,3584]{1,0:T(8,128)(2,1)S(1)}, bf16[8,3584]{1,0:T(8,128)(2,1)S(1)}, u32[]{:S(2)}, u32[]{:S(2)}) collective-permute-start(bf16[8,3584]{1,0:T(8,128)(2,1)S(1)} %get-tuple-element.16), channel_id=1, source_target_pairs={{0,18},{2,16},{4,22},{6,20},{8,26},{10,24},{12,30},{14,28},{16,2},... | collective-permute-start | bytes 172040 | tf_op jit(solution)/shard_map/ppermute | solution.py:35
  33.0 6.4 %collective-permute-start.17 = (bf16[8,3584]{1,0:T(8,128)(2,1)S(1)}, bf16[8,3584]{1,0:T(8,128)(2,1)S(1)}, u32[]{:S(2)}, u32[]{:S(2)}) collective-permute-start(bf16[8,3584]{1,0:T(8,128)(2,1)S(1)} %get-tuple-element.17), channel_id=1, source_target_pairs={{0,16},{2,18},{4,20},{6,22},{8,24},{10,26},{12,28},{14,30},{16,0},... | collective-permute-start | bytes 172040 | tf_op jit(solution)/shard_map/ppermute | solution.py:35
  34.3 5.1 %collective-permute-start.16 = (bf16[8,3584]{1,0:T(8,128)(2,1)S(1)}, bf16[8,3584]{1,0:T(8,128)(2,1)S(1)}, u32[]{:S(2)}, u32[]{:S(2)}) collective-permute-start(bf16[8,3584]{1,0:T(8,128)(2,1)S(1)} %get-tuple-element.19), channel_id=1, source_target_pairs={{0,8},{8,0},{16,24},{24,16},{1,9},{9,1},{17,25},{25,17},{2,10},{10... | collective-permute-start | bytes 172040 | tf_op jit(solution)/shard_map/ppermute | solution.py:39

commit v13 on v7

--- a/solution.py
+++ b/solution.py
@@ -124,7 +124,7 @@
         return out[:kept] + swapped
 
     held = copied(tokens)
-    places = tuple(range(n_tp))
+    places = (0, 1, *range(n_tp - 1, 1, -1))
     blocks = [held] + [exchange(tokens, 0, t) for t in places[1:]]
     far = [[rotate_experts(rows, s) for rows in blocks] for s in range(1, experts)]
     near = jnp.concatenate(blocks, axis=0)

time: 39.5 us -> 39.8 us (level)
  waiting for transfers between devices: 9.18 us -> 11.2 us
  starting transfers between devices: 25.3 us -> 23.6 us
    ppermute x10, waiting for transfers between devices: 5.41 us -> 7.43 us  [exchange(): return lax.ppermute(value, ('grp', 'tp'), pairs)]
    ppermute x10, starting transfers between devices: 16.9 us -> 15.1 us  [exchange(): return lax.ppermute(value, ('grp', 'tp'), pairs)]
where the time goes in v13:
time: 39.8 us; the launch traced here: 39.6 us
  starting transfers between devices  23.6 us (59%)
  waiting for transfers between devices  11.2 us (28%)
  matrix products  2.59 us (7%)
  local copies, waits for them, and re-layouts  1.05 us (3%)
  Pallas kernels  0.75 us (2%)
    ppermute x10, starting transfers between devices, exchange(): return lax.ppermute(value, ('grp', 'tp'), pairs)  15.1 us
    ppermute x10, waiting for transfers between devices, exchange(): return lax.ppermute(value, ('grp', 'tp'), pairs)  7.43 us
    ppermute x4, starting transfers between devices, rotate_experts(): lax.ppermute(value, 'grp', [(i, (i + 2 * by) % groups) for i in range(gro...  5.07 us
    ppermute x2, starting transfers between devices, rotate(): lax.ppermute(value, axis, [(i, (i + by) % size) for i in range(size)])  3 us
    ppermute x4, waiting for transfers between devices, swap_half(): lax.ppermute(value, 'grp', [(i, i ^ 1) for i in range(lax.axis_size('grp'...  2.93 us
    dot_general x4, matrix products, partial_sums(): jnp.dot(rows, w, preferred_element_type=f32)  1.76 us
    unnamed x16, local copies, waits for them, and re-layouts  0.93 us
    dot_general x2, matrix products, partial_out(): out = jnp.dot(hidden, w_down, preferred_element_type=f32)  0.83 us
  transfers between devices with their start and end apart: 20, of which 10 were waited for; matrix products, arithmetic and copies ran while one was open for 6% of the time, Pallas kernels for 0%

profile of v13, /device:TPU:0, one launch (start us, length us, event | category | flops | bytes accessed | tf_op | source)
XLA Modules:
  0.0 39.6 jit_solution(16055384781734569686)
XLA Ops:
  0.0 0.0 copy-start
  0.0 3.0 %collective-permute-start = (bf16[8,3584]{1,0:T(8,128)(2,1)}, bf16[8,3584]{1,0:T(8,128)(2,1)S(1)}, u32[]{:S(2)}, u32[]{:S(2)}) collective-permute-start(bf16[8,3584]{1,0:T(8,128)(2,1)} %from_ref.1), channel_id=1, source_target_pairs={{0,2},{2,0},{4,6},{6,4},{8,10},{10,8},{12,14},{14,12},{16,18},{18,... | collective-permute-start | bytes 172040 | tf_op jit(solution)/shard_map/ppermute | solution.py:35
  3.0 2.6 %collective-permute-start.2 = (bf16[8,3584]{1,0:T(8,128)(2,1)}, bf16[8,3584]{1,0:T(8,128)(2,1)S(1)}, u32[]{:S(2)}, u32[]{:S(2)}) collective-permute-start(bf16[8,3584]{1,0:T(8,128)(2,1)} %from_ref.1), channel_id=1, source_target_pairs={{0,4},{2,6},{4,0},{6,2},{8,12},{10,14},{12,8},{14,10},{16,20},{18,... | collective-permute-start | bytes 172040 | tf_op jit(solution)/shard_map/ppermute | solution.py:35
  5.6 0.0 collective-permute-start.1
  5.6 0.0 copy-start.1
  5.6 0.9 %copy-done.1 = bf16[8,3584]{1,0:T(8,128)(2,1)S(1)} copy-done((bf16[8,3584]{1,0:T(8,128)(2,1)S(1)}, bf16[8,3584]{1,0:T(8,128)(2,1)}, u32[]{:S(2)}) %copy-start.1) | copy-done | bytes 57368
  6.5 0.0 copy-start.4
  6.5 1.7 %collective-permute-start.6 = (bf16[8,3584]{1,0:T(8,128)(2,1)S(1)}, bf16[8,3584]{1,0:T(8,128)(2,1)S(1)}, u32[]{:S(2)}, u32[]{:S(2)}) collective-permute-start(bf16[8,3584]{1,0:T(8,128)(2,1)S(1)} %shard_map.64), channel_id=1, source_target_pairs={{0,16},{8,24},{16,0},{24,8},{1,17},{9,25},{17,1},{25,9},{2,18},{10... | collective-permute-start | bytes 172040 | tf_op jit(solution)/shard_map/ppermute | solution.py:21
  8.2 0.0 collective-permute-done
  8.2 0.4 %collective-permute-start.3 = (bf16[8,3584]{1,0:T(8,128)(2,1)S(1)}, bf16[8,3584]{1,0:T(8,128)(2,1)S(1)}, u32[]{:S(2)}, u32[]{:S(2)}) collective-permute-start(bf16[8,3584]{1,0:T(8,128)(2,1)S(1)} %collective-permute-done), channel_id=1, source_target_pairs={{0,16},{8,24},{16,0},{24,8},{1,17},{9,25},{17,1},{25,9},{2,18},{10... | collective-permute-start | bytes 172040 | tf_op jit(solution)/shard_map/ppermute | solution.py:21
  8.6 0.8 %collective-permute-done.2 = bf16[8,3584]{1,0:T(8,128)(2,1)S(1)} collective-permute-done((bf16[8,3584]{1,0:T(8,128)(2,1)}, bf16[8,3584]{1,0:T(8,128)(2,1)S(1)}, u32[]{:S(2)}, u32[]{:S(2)}) %collective-permute-start.2) | collective-permute-done | bytes 57376 | tf_op jit(solution)/shard_map/ppermute | solution.py:35
  9.4 1.5 %collective-permute-start.8 = (bf16[8,3584]{1,0:T(8,128)(2,1)S(1)}, bf16[8,3584]{1,0:T(8,128)(2,1)S(1)}, u32[]{:S(2)}, u32[]{:S(2)}) collective-permute-start(bf16[8,3584]{1,0:T(8,128)(2,1)S(1)} %collective-permute-done.2), channel_id=1, source_target_pairs={{0,16},{8,24},{16,0},{24,8},{1,17},{9,25},{17,1},{25,9},{2,18},{10... | collective-permute-start | bytes 172040 | tf_op jit(solution)/shard_map/ppermute | solution.py:21
  10.9 0.9 %collective-permute-done.1 = bf16[8,3584]{1,0:T(8,128)(2,1)S(1)} collective-permute-done((bf16[8,3584]{1,0:T(8,128)(2,1)}, bf16[8,3584]{1,0:T(8,128)(2,1)S(1)}, u32[]{:S(2)}, u32[]{:S(2)}) %collective-permute-start.1) | collective-permute-done | bytes 57376 | tf_op jit(solution)/shard_map/ppermute | solution.py:35
  11.8 1.5 %collective-permute-start.7 = (bf16[8,3584]{1,0:T(8,128)(2,1)S(1)}, bf16[8,3584]{1,0:T(8,128)(2,1)S(1)}, u32[]{:S(2)}, u32[]{:S(2)}) collective-permute-start(bf16[8,3584]{1,0:T(8,128)(2,1)S(1)} %collective-permute-done.1), channel_id=1, source_target_pairs={{0,16},{8,24},{16,0},{24,8},{1,17},{9,25},{17,1},{25,9},{2,18},{10... | collective-permute-start | bytes 172040 | tf_op jit(solution)/shard_map/ppermute | solution.py:21
  13.3 0.0 copy-start.5
  13.4 0.0 collective-permute-done.3.refs_1_
  13.4 0.1 collective-permute-start.4
  13.5 1.5 %collective-permute-done.4 = bf16[32,3584]{1,0:T(8,128)(2,1)S(1)} collective-permute-done((bf16[32,3584]{1,0:T(8,128)(2,1)S(1)}, bf16[32,3584]{1,0:T(8,128)(2,1)S(1)}, u32[]{:S(2)}, u32[]{:S(2)}) %collective-permute-start.4) | collective-permute-done | bytes 229408 | tf_op jit(solution)/shard_map/ppermute | solution.py:39
  15.0 0.0 copy-done.4
  15.0 0.4 %fusion.6 = f32[64,256]{1,0:T(8,128)S(1)} fusion(bf16[64,3584]{1,0:T(8,128)(2,1)S(1)} %constant_dynamic-update-slice_fusion, bf16[1,3584,256]{2,1,0:T(8,128)(2,1)S(1)} %copy-done.4), kind=kOutput, calls=%fused_computation.6 | convolution fusion | flops 117440512 | bytes 2359296 | tf_op jit(solution)/shard_map/dot_general | solution.py:108
  15.4 0.0 copy-done.5
  15.4 0.4 %fusion.10 = f32[64,256]{1,0:T(8,128)S(1)} fusion(bf16[64,3584]{1,0:T(8,128)(2,1)S(1)} %constant_dynamic-update-slice_fusion, bf16[1,3584,256]{2,1,0:T(8,128)(2,1)S(1)} %copy-done.5), kind=kOutput, calls=%fused_computation.10 | convolution fusion | flops 117440512 | bytes 2359296 | tf_op jit(solution)/shard_map/dot_general | solution.py:108
  15.9 0.0 collective-permute-done.8.refs_0_
  15.9 0.0 collective-permute-done.6
  15.9 0.1 collective-permute-done.7
  16.0 0.1 collective-permute-start.9
  16.1 1.5 %collective-permute-start.5 = (bf16[64,512]{1,0:T(8,128)(2,1)S(1)}, bf16[64,512]{1,0:T(8,128)(2,1)S(1)}, u32[]{:S(2)}, u32[]{:S(2)}) collective-permute-start(bf16[64,512]{1,0:T(8,128)(2,1)S(1)} %fusion.15.refs_1_), channel_id=1, source_target_pairs={{0,1},{1,0},{2,3},{3,2},{4,5},{5,4},{6,7},{7,6},{8,9},{9,8},{10,11... | collective-permute-start | bytes 196616 | tf_op jit(solution)/shard_map/ppermute | solution.py:16
  17.7 0.0 collective-permute-done.9
  17.7 0.4 %fusion.4 = f32[64,256]{1,0:T(8,128)S(1)} fusion(bf16[1,3584,256]{2,1,0:T(8,128)(2,1)S(1)} %copy-done.4, bf16[32,3584]{1,0:T(8,128)(2,1)S(1)} %collective-permute-done.9, bf16[32,3584]{1,0:T(8,128)(2,1)S(1)} %shard_map.67), kind=kOutput, calls=%fused_computation.4 | convolution fusion | flops 118358016 | bytes 2359296 | tf_op jit(solution)/shard_map/dot_general | solution.py:108
  18.1 0.4 %fusion.8 = f32[64,256]{1,0:T(8,128)S(1)} fusion(bf16[1,3584,256]{2,1,0:T(8,128)(2,1)S(1)} %copy-done.5, bf16[32,3584]{1,0:T(8,128)(2,1)S(1)} %collective-permute-done.9, bf16[32,3584]{1,0:T(8,128)(2,1)S(1)} %shard_map.67), kind=kOutput, calls=%fused_computation.8 | convolution fusion | flops 118358016 | bytes 2359296 | tf_op jit(solution)/shard_map/dot_general | solution.py:108
  18.6 1.5 %collective-permute-start.14 = (bf16[64,512]{1,0:T(8,128)(2,1)S(1)}, bf16[64,512]{1,0:T(8,128)(2,1)S(1)}, u32[]{:S(2)}, u32[]{:S(2)}) collective-permute-start(bf16[64,512]{1,0:T(8,128)(2,1)S(1)} %fusion.14.refs_1_), channel_id=1, source_target_pairs={{0,1},{1,0},{2,3},{3,2},{4,5},{5,4},{6,7},{7,6},{8,9},{9,8},{10,11... | collective-permute-start | bytes 196616 | tf_op jit(solution)/shard_map/ppermute | solution.py:16
  20.0 0.5 %collective-permute-done.5.refs_0_ = bf16[64,512]{1,0:T(8,128)(2,1)S(1)} collective-permute-done((bf16[64,512]{1,0:T(8,128)(2,1)S(1)}, bf16[64,512]{1,0:T(8,128)(2,1)S(1)}, u32[]{:S(2)}, u32[]{:S(2)}) %collective-permute-start.5) | collective-permute-done | bytes 65568 | tf_op jit(solution)/shard_map/ppermute | solution.py:16
  20.6 0.0 copy-done
  20.6 0.4 %fusion.2.refs_0_ = f32[64,3584]{1,0:T(8,128)S(1)} fusion(bf16[1,256,3584]{2,1,0:T(8,128)(2,1)S(1)} %copy-done, f32[64,512]{1,0:T(8,128)S(1)} %convert_add_fusion.1), kind=kOutput, calls=%fused_computation.2 | convolution fusion | flops 117538816 | bytes 2883584 | tf_op jit(solution)/shard_map/dot_general | solution.py:119
  21.1 0.1 collective-permute-start.10
  21.2 1.5 %collective-permute-done.10 = bf16[32,3584]{1,0:T(8,128)(2,1)S(1)} collective-permute-done((bf16[32,3584]{1,0:T(8,128)(2,1)S(1)}, bf16[32,3584]{1,0:T(8,128)(2,1)S(1)}, u32[]{:S(2)}, u32[]{:S(2)}) %collective-permute-start.10) | collective-permute-done | bytes 229408 | tf_op jit(solution)/shard_map/ppermute | solution.py:39
  22.6 0.1 fusion.26
  22.7 0.2 collective-permute-done.14.refs_0_
  22.9 0.4 %fusion = f32[64,3584]{1,0:T(8,128)S(1)} fusion(bf16[1,256,3584]{2,1,0:T(8,128)(2,1)S(1)} %copy-done, f32[64,512]{1,0:T(8,128)S(1)} %convert_add_fusion), kind=kOutput, calls=%fused_computation | convolution fusion | flops 117538816 | bytes 2883584 | tf_op jit(solution)/shard_map/dot_general | solution.py:119
  23.3 0.0 copy-start.2
  23.4 0.0 copy-start.3
  23.4 0.1 collective-permute-start.15
  23.5 1.0 %collective-permute-start.13 = (bf16[8,3584]{1,0:T(8,128)(2,1)S(1)}, bf16[8,3584]{1,0:T(8,128)(2,1)S(1)}, u32[]{:S(2)}, u32[]{:S(2)}) collective-permute-start(bf16[8,3584]{1,0:T(8,128)(2,1)S(1)} %get-tuple-element.11), channel_id=1, source_target_pairs={{0,4},{2,6},{4,0},{6,2},{8,12},{10,14},{12,8},{14,10},{16,20},{18,... | collective-permute-start | bytes 172040 | tf_op jit(solution)/shard_map/ppermute | solution.py:35
  24.5 1.9 %collective-permute-start.12 = (bf16[8,3584]{1,0:T(8,128)(2,1)S(1)}, bf16[8,3584]{1,0:T(8,128)(2,1)S(1)}, u32[]{:S(2)}, u32[]{:S(2)}) collective-permute-start(bf16[8,3584]{1,0:T(8,128)(2,1)S(1)} %get-tuple-element.12), channel_id=1, source_target_pairs={{0,6},{2,4},{4,2},{6,0},{8,14},{10,12},{12,10},{14,8},{16,22},{18,... | collective-permute-start | bytes 172040 | tf_op jit(solution)/shard_map/ppermute | solution.py:35
  26.5 0.6 %collective-permute-start.11 = (bf16[8,3584]{1,0:T(8,128)(2,1)S(1)}, bf16[8,3584]{1,0:T(8,128)(2,1)S(1)}, u32[]{:S(2)}, u32[]{:S(2)}) collective-permute-start(bf16[8,3584]{1,0:T(8,128)(2,1)S(1)} %get-tuple-element.13), channel_id=1, source_target_pairs={{0,2},{2,0},{4,6},{6,4},{8,10},{10,8},{12,14},{14,12},{16,18},{18,... | collective-permute-start | bytes 172040 | tf_op jit(solution)/shard_map/ppermute | solution.py:35
  27.1 0.0 collective-permute-done.15
  27.1 2.9 %collective-permute-start.19 = (bf16[8,3584]{1,0:T(8,128)(2,1)S(1)}, bf16[8,3584]{1,0:T(8,128)(2,1)S(1)}, u32[]{:S(2)}, u32[]{:S(2)}) collective-permute-start(bf16[8,3584]{1,0:T(8,128)(2,1)S(1)} %get-tuple-element.7), channel_id=1, source_target_pairs={{0,20},{2,22},{4,16},{6,18},{8,28},{10,30},{12,24},{14,26},{16,4},... | collective-permute-start | bytes 172040 | tf_op jit(solution)/shard_map/ppermute | solution.py:35
  30.0 1.9 %collective-permute-start.18 = (bf16[8,3584]{1,0:T(8,128)(2,1)S(1)}, bf16[8,3584]{1,0:T(8,128)(2,1)S(1)}, u32[]{:S(2)}, u32[]{:S(2)}) collective-permute-start(bf16[8,3584]{1,0:T(8,128)(2,1)S(1)} %get-tuple-element.8), channel_id=1, source_target_pairs={{0,22},{2,20},{4,18},{6,16},{8,30},{10,28},{12,26},{14,24},{16,6},... | collective-permute-start | bytes 172040 | tf_op jit(solution)/shard_map/ppermute | solution.py:35
  31.9 0.0 collective-permute-done.13.refs_3_
  31.9 0.6 %collective-permute-start.17 = (bf16[8,3584]{1,0:T(8,128)(2,1)S(1)}, bf16[8,3584]{1,0:T(8,128)(2,1)S(1)}, u32[]{:S(2)}, u32[]{:S(2)}) collective-permute-start(bf16[8,3584]{1,0:T(8,128)(2,1)S(1)} %get-tuple-element.9), channel_id=1, source_target_pairs={{0,18},{2,16},{4,22},{6,20},{8,26},{10,24},{12,30},{14,28},{16,2},... | collective-permute-start | bytes 172040 | tf_op jit(solution)/shard_map/ppermute | solution.py:35
  32.5 0.0 collective-permute-done.12.refs_2_
  32.5 0.6 %collective-permute-start.16 = (bf16[8,3584]{1,0:T(8,128)(2,1)S(1)}, bf16[8,3584]{1,0:T(8,128)(2,1)S(1)}, u32[]{:S(2)}, u32[]{:S(2)}) collective-permute-start(bf16[8,3584]{1,0:T(8,128)(2,1)S(1)} %get-tuple-element.10), channel_id=1, source_target_pairs={{0,16},{2,18},{4,20},{6,22},{8,24},{10,26},{12,28},{14,30},{16,0},... | collective-permute-start | bytes 172040 | tf_op jit(solution)/shard_map/ppermute | solution.py:35
  33.1 0.0 collective-permute-done.11.refs_1_
  33.1 4.0 %collective-permute-done.19.refs_7_ = bf16[8,3584]{1,0:T(8,128)(2,1)S(1)} collective-permute-done((bf16[8,3584]{1,0:T(8,128)(2,1)S(1)}, bf16[8,3584]{1,0:T(8,128)(2,1)S(1)}, u32[]{:S(2)}, u32[]{:S(2)}) %collective-permute-start.19) | collective-permute-done | bytes 57376 | tf_op jit(solution)/shard_map/ppermute | solution.py:35
  37.1 0.0 collective-permute-done.18.refs_6_
  37.1 1.1 %collective-permute-done.17.refs_5_ = bf16[8,3584]{1,0:T(8,128)(2,1)S(1)} collective-permute-done((bf16[8,3584]{1,0:T(8,128)(2,1)S(1)}, bf16[8,3584]{1,0:T(8,128)(2,1)S(1)}, u32[]{:S(2)}, u32[]{:S(2)}) %collective-permute-start.17) | collective-permute-done | bytes 57376 | tf_op jit(solution)/shard_map/ppermute | solution.py:35
  38.3 0.6 %collective-permute-done.16.refs_4_ = bf16[8,3584]{1,0:T(8,128)(2,1)S(1)} collective-permute-done((bf16[8,3584]{1,0:T(8,128)(2,1)S(1)}, bf16[8,3584]{1,0:T(8,128)(2,1)S(1)}, u32[]{:S(2)}, u32[]{:S(2)}) %collective-permute-start.16) | collective-permute-done | bytes 57376 | tf_op jit(solution)/shard_map/ppermute | solution.py:35
  38.9 0.0 copy-done.2
  38.9 0.0 copy-done.3
  38.9 0.7 %shard_map.71 = bf16[8,3584]{1,0:T(8,128)(2,1)} custom-call(s32[1,8]{1,0:T(1,128)S(1)} %bitcast.31, s32[1,8]{1,0:T(1,128)S(1)} %bitcast.32, f32[8,3584]{1,0:T(8,128)S(1)} %slice.83.refs_0_, bf16[8,3584]{1,0:T(8,128)(2,1)S(1)} %collective-permute-done.11.refs_1_, bf16[8,3584]{1,0:T(8,128)(2,1)S(1)} %collective-permute-done.12.refs_2_, ...), custom_call_target="tpu_custom_call" | custom-call | tf_op jit(solution)/shard_map/pallas_call | solution.py:92
  (25 shorter events, 0.3 us)
Async XLA Ops:
  0.0 20.6 %copy-start = (bf16[1,256,3584]{2,1,0:T(8,128)(2,1)S(1)}, bf16[1,256,3584]{2,1,0:T(8,128)(2,1)}, u32[]{:S(2)}) copy-start(bf16[1,256,3584]{2,1,0:T(8,128)(2,1)} %param.11) | copy-start | bytes 5505028
  0.0 8.2 %collective-permute-start = (bf16[8,3584]{1,0:T(8,128)(2,1)}, bf16[8,3584]{1,0:T(8,128)(2,1)S(1)}, u32[]{:S(2)}, u32[]{:S(2)}) collective-permute-start(bf16[8,3584]{1,0:T(8,128)(2,1)} %from_ref.1), channel_id=1, source_target_pairs={{0,2},{2,0},{4,6},{6,4},{8,10},{10,8},{12,14},{14,12},{16,18},{18,... | collective-permute-start | bytes 172040 | tf_op jit(solution)/shard_map/ppermute | solution.py:35
  3.0 6.4 %collective-permute-start.2 = (bf16[8,3584]{1,0:T(8,128)(2,1)}, bf16[8,3584]{1,0:T(8,128)(2,1)S(1)}, u32[]{:S(2)}, u32[]{:S(2)}) collective-permute-start(bf16[8,3584]{1,0:T(8,128)(2,1)} %from_ref.1), channel_id=1, source_target_pairs={{0,4},{2,6},{4,0},{6,2},{8,12},{10,14},{12,8},{14,10},{16,20},{18,... | collective-permute-start | bytes 172040 | tf_op jit(solution)/shard_map/ppermute | solution.py:35
  5.6 6.2 %collective-permute-start.1 = (bf16[8,3584]{1,0:T(8,128)(2,1)}, bf16[8,3584]{1,0:T(8,128)(2,1)S(1)}, u32[]{:S(2)}, u32[]{:S(2)}) collective-permute-start(bf16[8,3584]{1,0:T(8,128)(2,1)} %from_ref.1), channel_id=1, source_target_pairs={{0,6},{2,4},{4,2},{6,0},{8,14},{10,12},{12,10},{14,8},{16,22},{18,... | collective-permute-start | bytes 172040 | tf_op jit(solution)/shard_map/ppermute | solution.py:35
  5.6 0.9 %copy-start.1 = (bf16[8,3584]{1,0:T(8,128)(2,1)S(1)}, bf16[8,3584]{1,0:T(8,128)(2,1)}, u32[]{:S(2)}) copy-start(bf16[8,3584]{1,0:T(8,128)(2,1)} %from_ref.1) | copy-start | bytes 172036
  6.5 8.4 %copy-start.4 = (bf16[1,3584,256]{2,1,0:T(8,128)(2,1)S(1)}, bf16[1,3584,256]{2,1,0:T(8,128)(2,1)}, u32[]{:S(2)}) copy-start(bf16[1,3584,256]{2,1,0:T(8,128)(2,1)} %param.10) | copy-start | bytes 5505028
  6.5 9.4 %collective-permute-start.6 = (bf16[8,3584]{1,0:T(8,128)(2,1)S(1)}, bf16[8,3584]{1,0:T(8,128)(2,1)S(1)}, u32[]{:S(2)}, u32[]{:S(2)}) collective-permute-start(bf16[8,3584]{1,0:T(8,128)(2,1)S(1)} %shard_map.64), channel_id=1, source_target_pairs={{0,16},{8,24},{16,0},{24,8},{1,17},{9,25},{17,1},{25,9},{2,18},{10... | collective-permute-start | bytes 172040 | tf_op jit(solution)/shard_map/ppermute | solution.py:21
  8.2 5.2 %collective-permute-start.3 = (bf16[8,3584]{1,0:T(8,128)(2,1)S(1)}, bf16[8,3584]{1,0:T(8,128)(2,1)S(1)}, u32[]{:S(2)}, u32[]{:S(2)}) collective-permute-start(bf16[8,3584]{1,0:T(8,128)(2,1)S(1)} %collective-permute-done), channel_id=1, source_target_pairs={{0,16},{8,24},{16,0},{24,8},{1,17},{9,25},{17,1},{25,9},{2,18},{10... | collective-permute-start | bytes 172040 | tf_op jit(solution)/shard_map/ppermute | solution.py:21
  9.4 6.4 %collective-permute-start.8 = (bf16[8,3584]{1,0:T(8,128)(2,1)S(1)}, bf16[8,3584]{1,0:T(8,128)(2,1)S(1)}, u32[]{:S(2)}, u32[]{:S(2)}) collective-permute-start(bf16[8,3584]{1,0:T(8,128)(2,1)S(1)} %collective-permute-done.2), channel_id=1, source_target_pairs={{0,16},{8,24},{16,0},{24,8},{1,17},{9,25},{17,1},{25,9},{2,18},{10... | collective-permute-start | bytes 172040 | tf_op jit(solution)/shard_map/ppermute | solution.py:21
  11.8 4.2 %collective-permute-start.7 = (bf16[8,3584]{1,0:T(8,128)(2,1)S(1)}, bf16[8,3584]{1,0:T(8,128)(2,1)S(1)}, u32[]{:S(2)}, u32[]{:S(2)}) collective-permute-start(bf16[8,3584]{1,0:T(8,128)(2,1)S(1)} %collective-permute-done.1), channel_id=1, source_target_pairs={{0,16},{8,24},{16,0},{24,8},{1,17},{9,25},{17,1},{25,9},{2,18},{10... | collective-permute-start | bytes 172040 | tf_op jit(solution)/shard_map/ppermute | solution.py:21
  13.3 2.1 %copy-start.5 = (bf16[1,3584,256]{2,1,0:T(8,128)(2,1)S(1)}, bf16[1,3584,256]{2,1,0:T(8,128)(2,1)}, u32[]{:S(2)}) copy-start(bf16[1,3584,256]{2,1,0:T(8,128)(2,1)} %param.9) | copy-start | bytes 5505028
  13.4 1.6 %collective-permute-start.4 = (bf16[32,3584]{1,0:T(8,128)(2,1)S(1)}, bf16[32,3584]{1,0:T(8,128)(2,1)S(1)}, u32[]{:S(2)}, u32[]{:S(2)}) collective-permute-start(bf16[32,3584]{1,0:T(8,128)(2,1)S(1)} %shard_map.65), channel_id=1, source_target_pairs={{0,8},{8,0},{16,24},{24,16},{1,9},{9,1},{17,25},{25,17},{2,10},{10... | collective-permute-start | bytes 688136 | tf_op jit(solution)/shard_map/ppermute | solution.py:39
  16.0 1.7 %collective-permute-start.9 = (bf16[32,3584]{1,0:T(8,128)(2,1)S(1)}, bf16[32,3584]{1,0:T(8,128)(2,1)S(1)}, u32[]{:S(2)}, u32[]{:S(2)}) collective-permute-start(bf16[32,3584]{1,0:T(8,128)(2,1)S(1)} %pad_maximum_fusion.4.refs_0_), channel_id=1, source_target_pairs={{0,8},{8,0},{16,24},{24,16},{1,9},{9,1},{17,25},{25,17},{2,10},{10... | collective-permute-start | bytes 688136 | tf_op jit(solution)/shard_map/ppermute | solution.py:39
  16.1 4.4 %collective-permute-start.5 = (bf16[64,512]{1,0:T(8,128)(2,1)S(1)}, bf16[64,512]{1,0:T(8,128)(2,1)S(1)}, u32[]{:S(2)}, u32[]{:S(2)}) collective-permute-start(bf16[64,512]{1,0:T(8,128)(2,1)S(1)} %fusion.15.refs_1_), channel_id=1, source_target_pairs={{0,1},{1,0},{2,3},{3,2},{4,5},{5,4},{6,7},{7,6},{8,9},{9,8},{10,11... | collective-permute-start | bytes 196616 | tf_op jit(solution)/shard_map/ppermute | solution.py:16
  18.6 4.3 %collective-permute-start.14 = (bf16[64,512]{1,0:T(8,128)(2,1)S(1)}, bf16[64,512]{1,0:T(8,128)(2,1)S(1)}, u32[]{:S(2)}, u32[]{:S(2)}) collective-permute-start(bf16[64,512]{1,0:T(8,128)(2,1)S(1)} %fusion.14.refs_1_), channel_id=1, source_target_pairs={{0,1},{1,0},{2,3},{3,2},{4,5},{5,4},{6,7},{7,6},{8,9},{9,8},{10,11... | collective-permute-start | bytes 196616 | tf_op jit(solution)/shard_map/ppermute | solution.py:16
  21.1 1.6 %collective-permute-start.10 = (bf16[32,3584]{1,0:T(8,128)(2,1)S(1)}, bf16[32,3584]{1,0:T(8,128)(2,1)S(1)}, u32[]{:S(2)}, u32[]{:S(2)}) collective-permute-start(bf16[32,3584]{1,0:T(8,128)(2,1)S(1)} %slice.122), channel_id=1, source_target_pairs={{0,8},{8,0},{16,24},{24,16},{1,9},{9,1},{17,25},{25,17},{2,10},{10... | collective-permute-start | bytes 688136 | tf_op jit(solution)/shard_map/ppermute | solution.py:39
  23.3 15.5 %copy-start.2 = (s32[8,1]{0,1:T(1,128)S(1)}, s32[8,1]{0,1:T(1,128)}, u32[]{:S(2)}) copy-start(s32[8,1]{0,1:T(1,128)} %param.7) | copy-start | bytes 100
  23.4 15.5 %copy-start.3 = (s32[8,1]{0,1:T(1,128)S(1)}, s32[8,1]{0,1:T(1,128)}, u32[]{:S(2)}) copy-start(s32[8,1]{0,1:T(1,128)} %param.8) | copy-start | bytes 100
  23.4 3.7 %collective-permute-start.15 = (bf16[32,3584]{1,0:T(8,128)(2,1)S(1)}, bf16[32,3584]{1,0:T(8,128)(2,1)S(1)}, u32[]{:S(2)}, u32[]{:S(2)}) collective-permute-start(bf16[32,3584]{1,0:T(8,128)(2,1)S(1)} %slice.121), channel_id=1, source_target_pairs={{0,8},{8,0},{16,24},{24,16},{1,9},{9,1},{17,25},{25,17},{2,10},{10... | collective-permute-start | bytes 688136 | tf_op jit(solution)/shard_map/ppermute | solution.py:39
  23.5 8.4 %collective-permute-start.13 = (bf16[8,3584]{1,0:T(8,128)(2,1)S(1)}, bf16[8,3584]{1,0:T(8,128)(2,1)S(1)}, u32[]{:S(2)}, u32[]{:S(2)}) collective-permute-start(bf16[8,3584]{1,0:T(8,128)(2,1)S(1)} %get-tuple-element.11), channel_id=1, source_target_pairs={{0,4},{2,6},{4,0},{6,2},{8,12},{10,14},{12,8},{14,10},{16,20},{18,... | collective-permute-start | bytes 172040 | tf_op jit(solution)/shard_map/ppermute | solution.py:35
  24.5 8.0 %collective-permute-start.12 = (bf16[8,3584]{1,0:T(8,128)(2,1)S(1)}, bf16[8,3584]{1,0:T(8,128)(2,1)S(1)}, u32[]{:S(2)}, u32[]{:S(2)}) collective-permute-start(bf16[8,3584]{1,0:T(8,128)(2,1)S(1)} %get-tuple-element.12), channel_id=1, source_target_pairs={{0,6},{2,4},{4,2},{6,0},{8,14},{10,12},{12,10},{14,8},{16,22},{18,... | collective-permute-start | bytes 172040 | tf_op jit(solution)/shard_map/ppermute | solution.py:35
  26.5 6.7 %collective-permute-start.11 = (bf16[8,3584]{1,0:T(8,128)(2,1)S(1)}, bf16[8,3584]{1,0:T(8,128)(2,1)S(1)}, u32[]{:S(2)}, u32[]{:S(2)}) collective-permute-start(bf16[8,3584]{1,0:T(8,128)(2,1)S(1)} %get-tuple-element.13), channel_id=1, source_target_pairs={{0,2},{2,0},{4,6},{6,4},{8,10},{10,8},{12,14},{14,12},{16,18},{18,... | collective-permute-start | bytes 172040 | tf_op jit(solution)/shard_map/ppermute | solution.py:35
  27.1 10.0 %collective-permute-start.19 = (bf16[8,3584]{1,0:T(8,128)(2,1)S(1)}, bf16[8,3584]{1,0:T(8,128)(2,1)S(1)}, u32[]{:S(2)}, u32[]{:S(2)}) collective-permute-start(bf16[8,3584]{1,0:T(8,128)(2,1)S(1)} %get-tuple-element.7), channel_id=1, source_target_pairs={{0,20},{2,22},{4,16},{6,18},{8,28},{10,30},{12,24},{14,26},{16,4},... | collective-permute-start | bytes 172040 | tf_op jit(solution)/shard_map/ppermute | solution.py:35
  30.0 7.1 %collective-permute-start.18 = (bf16[8,3584]{1,0:T(8,128)(2,1)S(1)}, bf16[8,3584]{1,0:T(8,128)(2,1)S(1)}, u32[]{:S(2)}, u32[]{:S(2)}) collective-permute-start(bf16[8,3584]{1,0:T(8,128)(2,1)S(1)} %get-tuple-element.8), channel_id=1, source_target_pairs={{0,22},{2,20},{4,18},{6,16},{8,30},{10,28},{12,26},{14,24},{16,6},... | collective-permute-start | bytes 172040 | tf_op jit(solution)/shard_map/ppermute | solution.py:35
  31.9 6.4 %collective-permute-start.17 = (bf16[8,3584]{1,0:T(8,128)(2,1)S(1)}, bf16[8,3584]{1,0:T(8,128)(2,1)S(1)}, u32[]{:S(2)}, u32[]{:S(2)}) collective-permute-start(bf16[8,3584]{1,0:T(8,128)(2,1)S(1)} %get-tuple-element.9), channel_id=1, source_target_pairs={{0,18},{2,16},{4,22},{6,20},{8,26},{10,24},{12,30},{14,28},{16,2},... | collective-permute-start | bytes 172040 | tf_op jit(solution)/shard_map/ppermute | solution.py:35
  32.5 6.3 %collective-permute-start.16 = (bf16[8,3584]{1,0:T(8,128)(2,1)S(1)}, bf16[8,3584]{1,0:T(8,128)(2,1)S(1)}, u32[]{:S(2)}, u32[]{:S(2)}) collective-permute-start(bf16[8,3584]{1,0:T(8,128)(2,1)S(1)} %get-tuple-element.10), channel_id=1, source_target_pairs={{0,16},{2,18},{4,20},{6,22},{8,24},{10,26},{12,28},{14,30},{16,0},... | collective-permute-start | bytes 172040 | tf_op jit(solution)/shard_map/ppermute | solution.py:35

commit v14 on v7

--- a/solution.py
+++ b/solution.py
@@ -126,7 +126,7 @@
     held = copied(tokens)
     places = tuple(range(n_tp))
     blocks = [held] + [exchange(tokens, 0, t) for t in places[1:]]
-    far = [[rotate_experts(rows, s) for rows in blocks] for s in range(1, experts)]
+    far = [[rotate_experts(rows, s) for rows in (tokens, *blocks[1:])] for s in range(1, experts)]
     near = jnp.concatenate(blocks, axis=0)
     near_swapped = swap_half(after(near, *(line[1] for line in far)))
     near = jnp.concatenate([near, near_swapped], axis=0)

time: 39.5 us -> 41.2 us (1.043)
  waiting for transfers between devices: 9.18 us -> 11.7 us
  starting transfers between devices: 25.3 us -> 24.6 us
    ppermute x10, waiting for transfers between devices: 5.41 us -> 6.92 us  [exchange(): return lax.ppermute(value, ('grp', 'tp'), pairs)]
    ppermute x4, waiting for transfers between devices: 0.09 us -> 1.07 us  [rotate_experts(): lax.ppermute(value, 'grp', [(i, (i + 2 * by) % groups) for i in range(gro...]
    ppermute x4, starting transfers between devices: 5.07 us -> 4.12 us  [rotate_experts(): lax.ppermute(value, 'grp', [(i, (i + 2 * by) % groups) for i in range(gro...]
where the time goes in v14:
time: 41.2 us; the launch traced here: 41 us
  starting transfers between devices  24.6 us (60%)
  waiting for transfers between devices  11.7 us (28%)
  matrix products  2.6 us (6%)
  local copies, waits for them, and re-layouts  1.02 us (2%)
  Pallas kernels  0.74 us (2%)
    ppermute x10, starting transfers between devices, exchange(): return lax.ppermute(value, ('grp', 'tp'), pairs)  17.1 us
    ppermute x10, waiting for transfers between devices, exchange(): return lax.ppermute(value, ('grp', 'tp'), pairs)  6.92 us
    ppermute x4, starting transfers between devices, rotate_experts(): lax.ppermute(value, 'grp', [(i, (i + 2 * by) % groups) for i in range(gro...  4.12 us
    ppermute x2, starting transfers between devices, rotate(): lax.ppermute(value, axis, [(i, (i + by) % size) for i in range(size)])  3.06 us
    ppermute x4, waiting for transfers between devices, swap_half(): lax.ppermute(value, 'grp', [(i, i ^ 1) for i in range(lax.axis_size('grp'...  2.93 us
    dot_general x4, matrix products, partial_sums(): jnp.dot(rows, w, preferred_element_type=f32)  1.76 us
    ppermute x4, waiting for transfers between devices, rotate_experts(): lax.ppermute(value, 'grp', [(i, (i + 2 * by) % groups) for i in range(gro...  1.07 us
    unnamed x16, local copies, waits for them, and re-layouts  0.9 us
  transfers between devices with their start and end apart: 20, of which 10 were waited for; matrix products, arithmetic and copies ran while one was open for 6% of the time, Pallas kernels for 0%

profile of v14, /device:TPU:0, one launch (start us, length us, event | category | flops | bytes accessed | tf_op | source)
XLA Modules:
  0.0 41.0 jit_solution(8804504761663126268)
XLA Ops:
  0.0 0.0 copy-start
  0.0 4.0 %collective-permute-start.1 = (bf16[8,3584]{1,0:T(8,128)(2,1)}, bf16[8,3584]{1,0:T(8,128)(2,1)S(1)}, u32[]{:S(2)}, u32[]{:S(2)}) collective-permute-start(bf16[8,3584]{1,0:T(8,128)(2,1)} %from_ref.1), channel_id=1, source_target_pairs={{0,4},{2,6},{4,0},{6,2},{8,12},{10,14},{12,8},{14,10},{16,20},{18,... | collective-permute-start | bytes 172040 | tf_op jit(solution)/shard_map/ppermute | solution.py:35
  4.0 1.6 %collective-permute-start = (bf16[8,3584]{1,0:T(8,128)(2,1)}, bf16[8,3584]{1,0:T(8,128)(2,1)S(1)}, u32[]{:S(2)}, u32[]{:S(2)}) collective-permute-start(bf16[8,3584]{1,0:T(8,128)(2,1)} %from_ref.1), channel_id=1, source_target_pairs={{0,2},{2,0},{4,6},{6,4},{8,10},{10,8},{12,14},{14,12},{16,18},{18,... | collective-permute-start | bytes 172040 | tf_op jit(solution)/shard_map/ppermute | solution.py:35
  5.6 1.5 %collective-permute-start.6 = (bf16[8,3584]{1,0:T(8,128)(2,1)}, bf16[8,3584]{1,0:T(8,128)(2,1)S(1)}, u32[]{:S(2)}, u32[]{:S(2)}) collective-permute-start(bf16[8,3584]{1,0:T(8,128)(2,1)} %from_ref.1), channel_id=1, source_target_pairs={{0,16},{8,24},{16,0},{24,8},{1,17},{9,25},{17,1},{25,9},{2,18},{10... | collective-permute-start | bytes 172040 | tf_op jit(solution)/shard_map/ppermute | solution.py:21
  7.1 0.2 collective-permute-start.2
  7.3 0.0 copy-start.1
  7.3 0.9 %copy-done.1 = bf16[8,3584]{1,0:T(8,128)(2,1)S(1)} copy-done((bf16[8,3584]{1,0:T(8,128)(2,1)S(1)}, bf16[8,3584]{1,0:T(8,128)(2,1)}, u32[]{:S(2)}) %copy-start.1) | copy-done | bytes 57368
  8.2 0.0 copy-start.4
  8.2 0.0 collective-permute-done.1
  8.2 0.6 %collective-permute-start.7 = (bf16[8,3584]{1,0:T(8,128)(2,1)S(1)}, bf16[8,3584]{1,0:T(8,128)(2,1)S(1)}, u32[]{:S(2)}, u32[]{:S(2)}) collective-permute-start(bf16[8,3584]{1,0:T(8,128)(2,1)S(1)} %collective-permute-done.1), channel_id=1, source_target_pairs={{0,16},{8,24},{16,0},{24,8},{1,17},{9,25},{17,1},{25,9},{2,18},{10... | collective-permute-start | bytes 172040 | tf_op jit(solution)/shard_map/ppermute | solution.py:21
  8.8 0.0 collective-permute-done
  8.8 1.5 %collective-permute-start.3 = (bf16[8,3584]{1,0:T(8,128)(2,1)S(1)}, bf16[8,3584]{1,0:T(8,128)(2,1)S(1)}, u32[]{:S(2)}, u32[]{:S(2)}) collective-permute-start(bf16[8,3584]{1,0:T(8,128)(2,1)S(1)} %collective-permute-done), channel_id=1, source_target_pairs={{0,16},{8,24},{16,0},{24,8},{1,17},{9,25},{17,1},{25,9},{2,18},{10... | collective-permute-start | bytes 172040 | tf_op jit(solution)/shard_map/ppermute | solution.py:21
  10.3 3.0 %collective-permute-done.2 = bf16[8,3584]{1,0:T(8,128)(2,1)S(1)} collective-permute-done((bf16[8,3584]{1,0:T(8,128)(2,1)}, bf16[8,3584]{1,0:T(8,128)(2,1)S(1)}, u32[]{:S(2)}, u32[]{:S(2)}) %collective-permute-start.2) | collective-permute-done | bytes 57376 | tf_op jit(solution)/shard_map/ppermute | solution.py:35
  13.3 0.5 %collective-permute-start.8 = (bf16[8,3584]{1,0:T(8,128)(2,1)S(1)}, bf16[8,3584]{1,0:T(8,128)(2,1)S(1)}, u32[]{:S(2)}, u32[]{:S(2)}) collective-permute-start(bf16[8,3584]{1,0:T(8,128)(2,1)S(1)} %collective-permute-done.2), channel_id=1, source_target_pairs={{0,16},{8,24},{16,0},{24,8},{1,17},{9,25},{17,1},{25,9},{2,18},{10... | collective-permute-start | bytes 172040 | tf_op jit(solution)/shard_map/ppermute | solution.py:21
  13.9 0.0 copy-start.5
  13.9 0.0 collective-permute-done.3.refs_1_
  13.9 0.1 collective-permute-start.4
  14.0 1.5 %collective-permute-done.4 = bf16[32,3584]{1,0:T(8,128)(2,1)S(1)} collective-permute-done((bf16[32,3584]{1,0:T(8,128)(2,1)S(1)}, bf16[32,3584]{1,0:T(8,128)(2,1)S(1)}, u32[]{:S(2)}, u32[]{:S(2)}) %collective-permute-start.4) | collective-permute-done | bytes 229408 | tf_op jit(solution)/shard_map/ppermute | solution.py:39
  15.5 0.0 copy-done.4
  15.5 0.4 %fusion.6 = f32[64,256]{1,0:T(8,128)S(1)} fusion(bf16[64,3584]{1,0:T(8,128)(2,1)S(1)} %constant_dynamic-update-slice_fusion, bf16[1,3584,256]{2,1,0:T(8,128)(2,1)S(1)} %copy-done.4), kind=kOutput, calls=%fused_computation.6 | convolution fusion | flops 117440512 | bytes 2359296 | tf_op jit(solution)/shard_map/dot_general | solution.py:108
  15.9 0.0 copy-done.5
  15.9 0.4 %fusion.10 = f32[64,256]{1,0:T(8,128)S(1)} fusion(bf16[64,3584]{1,0:T(8,128)(2,1)S(1)} %constant_dynamic-update-slice_fusion, bf16[1,3584,256]{2,1,0:T(8,128)(2,1)S(1)} %copy-done.5), kind=kOutput, calls=%fused_computation.10 | convolution fusion | flops 117440512 | bytes 2359296 | tf_op jit(solution)/shard_map/dot_general | solution.py:108
  16.4 1.1 %collective-permute-done.8.refs_0_ = bf16[8,3584]{1,0:T(8,128)(2,1)S(1)} collective-permute-done((bf16[8,3584]{1,0:T(8,128)(2,1)S(1)}, bf16[8,3584]{1,0:T(8,128)(2,1)S(1)}, u32[]{:S(2)}, u32[]{:S(2)}) %collective-permute-start.8) | collective-permute-done | bytes 57376 | tf_op jit(solution)/shard_map/ppermute | solution.py:21
  17.5 0.0 collective-permute-done.6
  17.5 0.0 collective-permute-done.7
  17.5 0.1 collective-permute-start.9
  17.6 1.6 %collective-permute-start.5 = (bf16[64,512]{1,0:T(8,128)(2,1)S(1)}, bf16[64,512]{1,0:T(8,128)(2,1)S(1)}, u32[]{:S(2)}, u32[]{:S(2)}) collective-permute-start(bf16[64,512]{1,0:T(8,128)(2,1)S(1)} %fusion.15.refs_1_), channel_id=1, source_target_pairs={{0,1},{1,0},{2,3},{3,2},{4,5},{5,4},{6,7},{7,6},{8,9},{9,8},{10,11... | collective-permute-start | bytes 196616 | tf_op jit(solution)/shard_map/ppermute | solution.py:16
  19.2 0.0 collective-permute-done.9
  19.2 0.4 %fusion.4 = f32[64,256]{1,0:T(8,128)S(1)} fusion(bf16[1,3584,256]{2,1,0:T(8,128)(2,1)S(1)} %copy-done.4, bf16[32,3584]{1,0:T(8,128)(2,1)S(1)} %collective-permute-done.9, bf16[32,3584]{1,0:T(8,128)(2,1)S(1)} %shard_map.67), kind=kOutput, calls=%fused_computation.4 | convolution fusion | flops 118358016 | bytes 2359296 | tf_op jit(solution)/shard_map/dot_general | solution.py:108
  19.6 0.4 %fusion.8 = f32[64,256]{1,0:T(8,128)S(1)} fusion(bf16[1,3584,256]{2,1,0:T(8,128)(2,1)S(1)} %copy-done.5, bf16[32,3584]{1,0:T(8,128)(2,1)S(1)} %collective-permute-done.9, bf16[32,3584]{1,0:T(8,128)(2,1)S(1)} %shard_map.67), kind=kOutput, calls=%fused_computation.8 | convolution fusion | flops 118358016 | bytes 2359296 | tf_op jit(solution)/shard_map/dot_general | solution.py:108
  20.1 1.5 %collective-permute-start.14 = (bf16[64,512]{1,0:T(8,128)(2,1)S(1)}, bf16[64,512]{1,0:T(8,128)(2,1)S(1)}, u32[]{:S(2)}, u32[]{:S(2)}) collective-permute-start(bf16[64,512]{1,0:T(8,128)(2,1)S(1)} %fusion.14.refs_1_), channel_id=1, source_target_pairs={{0,1},{1,0},{2,3},{3,2},{4,5},{5,4},{6,7},{7,6},{8,9},{9,8},{10,11... | collective-permute-start | bytes 196616 | tf_op jit(solution)/shard_map/ppermute | solution.py:16
  21.6 0.5 %collective-permute-done.5.refs_0_ = bf16[64,512]{1,0:T(8,128)(2,1)S(1)} collective-permute-done((bf16[64,512]{1,0:T(8,128)(2,1)S(1)}, bf16[64,512]{1,0:T(8,128)(2,1)S(1)}, u32[]{:S(2)}, u32[]{:S(2)}) %collective-permute-start.5) | collective-permute-done | bytes 65568 | tf_op jit(solution)/shard_map/ppermute | solution.py:16
  22.1 0.0 copy-done
  22.1 0.4 %fusion.2.refs_0_ = f32[64,3584]{1,0:T(8,128)S(1)} fusion(bf16[1,256,3584]{2,1,0:T(8,128)(2,1)S(1)} %copy-done, f32[64,512]{1,0:T(8,128)S(1)} %convert_add_fusion.1), kind=kOutput, calls=%fused_computation.2 | convolution fusion | flops 117538816 | bytes 2883584 | tf_op jit(solution)/shard_map/dot_general | solution.py:119
  22.6 0.1 collective-permute-start.10
  22.7 1.5 %collective-permute-done.10 = bf16[32,3584]{1,0:T(8,128)(2,1)S(1)} collective-permute-done((bf16[32,3584]{1,0:T(8,128)(2,1)S(1)}, bf16[32,3584]{1,0:T(8,128)(2,1)S(1)}, u32[]{:S(2)}, u32[]{:S(2)}) %collective-permute-start.10) | collective-permute-done | bytes 229408 | tf_op jit(solution)/shard_map/ppermute | solution.py:39
  24.1 0.1 fusion.26
  24.2 0.2 collective-permute-done.14.refs_0_
  24.4 0.4 %fusion = f32[64,3584]{1,0:T(8,128)S(1)} fusion(bf16[1,256,3584]{2,1,0:T(8,128)(2,1)S(1)} %copy-done, f32[64,512]{1,0:T(8,128)S(1)} %convert_add_fusion), kind=kOutput, calls=%fused_computation | convolution fusion | flops 117538816 | bytes 2883584 | tf_op jit(solution)/shard_map/dot_general | solution.py:119
  24.8 0.0 copy-start.2
  24.9 0.0 copy-start.3
  24.9 0.1 collective-permute-start.15
  25.0 3.6 %collective-permute-start.13 = (bf16[8,3584]{1,0:T(8,128)(2,1)S(1)}, bf16[8,3584]{1,0:T(8,128)(2,1)S(1)}, u32[]{:S(2)}, u32[]{:S(2)}) collective-permute-start(bf16[8,3584]{1,0:T(8,128)(2,1)S(1)} %get-tuple-element.11), channel_id=1, source_target_pairs={{0,6},{2,4},{4,2},{6,0},{8,14},{10,12},{12,10},{14,8},{16,22},{18,... | collective-permute-start | bytes 172040 | tf_op jit(solution)/shard_map/ppermute | solution.py:35
  28.6 0.0 collective-permute-start.12
  28.6 0.9 %collective-permute-start.11 = (bf16[8,3584]{1,0:T(8,128)(2,1)S(1)}, bf16[8,3584]{1,0:T(8,128)(2,1)S(1)}, u32[]{:S(2)}, u32[]{:S(2)}) collective-permute-start(bf16[8,3584]{1,0:T(8,128)(2,1)S(1)} %get-tuple-element.13), channel_id=1, source_target_pairs={{0,2},{2,0},{4,6},{6,4},{8,10},{10,8},{12,14},{14,12},{16,18},{18,... | collective-permute-start | bytes 172040 | tf_op jit(solution)/shard_map/ppermute | solution.py:35
  29.5 0.0 collective-permute-done.15
  29.5 3.6 %collective-permute-start.19 = (bf16[8,3584]{1,0:T(8,128)(2,1)S(1)}, bf16[8,3584]{1,0:T(8,128)(2,1)S(1)}, u32[]{:S(2)}, u32[]{:S(2)}) collective-permute-start(bf16[8,3584]{1,0:T(8,128)(2,1)S(1)} %get-tuple-element.7), channel_id=1, source_target_pairs={{0,22},{2,20},{4,18},{6,16},{8,30},{10,28},{12,26},{14,24},{16,6},... | collective-permute-start | bytes 172040 | tf_op jit(solution)/shard_map/ppermute | solution.py:35
  33.2 0.0 collective-permute-start.18
  33.2 0.0 collective-permute-done.13.refs_3_
  33.2 1.7 %collective-permute-start.17 = (bf16[8,3584]{1,0:T(8,128)(2,1)S(1)}, bf16[8,3584]{1,0:T(8,128)(2,1)S(1)}, u32[]{:S(2)}, u32[]{:S(2)}) collective-permute-start(bf16[8,3584]{1,0:T(8,128)(2,1)S(1)} %get-tuple-element.9), channel_id=1, source_target_pairs={{0,18},{2,16},{4,22},{6,20},{8,26},{10,24},{12,30},{14,28},{16,2},... | collective-permute-start | bytes 172040 | tf_op jit(solution)/shard_map/ppermute | solution.py:35
  34.9 0.0 collective-permute-done.12.refs_2_
  34.9 1.5 %collective-permute-start.16 = (bf16[8,3584]{1,0:T(8,128)(2,1)S(1)}, bf16[8,3584]{1,0:T(8,128)(2,1)S(1)}, u32[]{:S(2)}, u32[]{:S(2)}) collective-permute-start(bf16[8,3584]{1,0:T(8,128)(2,1)S(1)} %get-tuple-element.10), channel_id=1, source_target_pairs={{0,16},{2,18},{4,20},{6,22},{8,24},{10,26},{12,28},{14,30},{16,0},... | collective-permute-start | bytes 172040 | tf_op jit(solution)/shard_map/ppermute | solution.py:35
  36.4 0.0 collective-permute-done.11.refs_1_
  36.4 0.9 %collective-permute-done.19.refs_7_ = bf16[8,3584]{1,0:T(8,128)(2,1)S(1)} collective-permute-done((bf16[8,3584]{1,0:T(8,128)(2,1)S(1)}, bf16[8,3584]{1,0:T(8,128)(2,1)S(1)}, u32[]{:S(2)}, u32[]{:S(2)}) %collective-permute-start.19) | collective-permute-done | bytes 57376 | tf_op jit(solution)/shard_map/ppermute | solution.py:35
  37.3 1.9 %collective-permute-done.18.refs_6_ = bf16[8,3584]{1,0:T(8,128)(2,1)S(1)} collective-permute-done((bf16[8,3584]{1,0:T(8,128)(2,1)S(1)}, bf16[8,3584]{1,0:T(8,128)(2,1)S(1)}, u32[]{:S(2)}, u32[]{:S(2)}) %collective-permute-start.18) | collective-permute-done | bytes 57376 | tf_op jit(solution)/shard_map/ppermute | solution.py:35
  39.2 0.3 collective-permute-done.17.refs_5_
  39.5 0.8 %collective-permute-done.16.refs_4_ = bf16[8,3584]{1,0:T(8,128)(2,1)S(1)} collective-permute-done((bf16[8,3584]{1,0:T(8,128)(2,1)S(1)}, bf16[8,3584]{1,0:T(8,128)(2,1)S(1)}, u32[]{:S(2)}, u32[]{:S(2)}) %collective-permute-start.16) | collective-permute-done | bytes 57376 | tf_op jit(solution)/shard_map/ppermute | solution.py:35
  40.3 0.0 copy-done.2
  40.3 0.0 copy-done.3
  40.3 0.7 %shard_map.71 = bf16[8,3584]{1,0:T(8,128)(2,1)} custom-call(s32[1,8]{1,0:T(1,128)S(1)} %bitcast.31, s32[1,8]{1,0:T(1,128)S(1)} %bitcast.32, f32[8,3584]{1,0:T(8,128)S(1)} %slice.83.refs_0_, bf16[8,3584]{1,0:T(8,128)(2,1)S(1)} %collective-permute-done.11.refs_1_, bf16[8,3584]{1,0:T(8,128)(2,1)S(1)} %collective-permute-done.12.refs_2_, ...), custom_call_target="tpu_custom_call" | custom-call | tf_op jit(solution)/shard_map/pallas_call | solution.py:92
  (25 shorter events, 0.3 us)
Async XLA Ops:
  0.0 22.1 %copy-start = (bf16[1,256,3584]{2,1,0:T(8,128)(2,1)S(1)}, bf16[1,256,3584]{2,1,0:T(8,128)(2,1)}, u32[]{:S(2)}) copy-start(bf16[1,256,3584]{2,1,0:T(8,128)(2,1)} %param.11) | copy-start | bytes 5505028
  0.0 8.2 %collective-permute-start.1 = (bf16[8,3584]{1,0:T(8,128)(2,1)}, bf16[8,3584]{1,0:T(8,128)(2,1)S(1)}, u32[]{:S(2)}, u32[]{:S(2)}) collective-permute-start(bf16[8,3584]{1,0:T(8,128)(2,1)} %from_ref.1), channel_id=1, source_target_pairs={{0,4},{2,6},{4,0},{6,2},{8,12},{10,14},{12,8},{14,10},{16,20},{18,... | collective-permute-start | bytes 172040 | tf_op jit(solution)/shard_map/ppermute | solution.py:35
  4.0 4.8 %collective-permute-start = (bf16[8,3584]{1,0:T(8,128)(2,1)}, bf16[8,3584]{1,0:T(8,128)(2,1)S(1)}, u32[]{:S(2)}, u32[]{:S(2)}) collective-permute-start(bf16[8,3584]{1,0:T(8,128)(2,1)} %from_ref.1), channel_id=1, source_target_pairs={{0,2},{2,0},{4,6},{6,4},{8,10},{10,8},{12,14},{14,12},{16,18},{18,... | collective-permute-start | bytes 172040 | tf_op jit(solution)/shard_map/ppermute | solution.py:35
  5.6 11.9 %collective-permute-start.6 = (bf16[8,3584]{1,0:T(8,128)(2,1)}, bf16[8,3584]{1,0:T(8,128)(2,1)S(1)}, u32[]{:S(2)}, u32[]{:S(2)}) collective-permute-start(bf16[8,3584]{1,0:T(8,128)(2,1)} %from_ref.1), channel_id=1, source_target_pairs={{0,16},{8,24},{16,0},{24,8},{1,17},{9,25},{17,1},{25,9},{2,18},{10... | collective-permute-start | bytes 172040 | tf_op jit(solution)/shard_map/ppermute | solution.py:21
  7.1 6.2 %collective-permute-start.2 = (bf16[8,3584]{1,0:T(8,128)(2,1)}, bf16[8,3584]{1,0:T(8,128)(2,1)S(1)}, u32[]{:S(2)}, u32[]{:S(2)}) collective-permute-start(bf16[8,3584]{1,0:T(8,128)(2,1)} %from_ref.1), channel_id=1, source_target_pairs={{0,6},{2,4},{4,2},{6,0},{8,14},{10,12},{12,10},{14,8},{16,22},{18,... | collective-permute-start | bytes 172040 | tf_op jit(solution)/shard_map/ppermute | solution.py:35
  7.3 0.9 %copy-start.1 = (bf16[8,3584]{1,0:T(8,128)(2,1)S(1)}, bf16[8,3584]{1,0:T(8,128)(2,1)}, u32[]{:S(2)}) copy-start(bf16[8,3584]{1,0:T(8,128)(2,1)} %from_ref.1) | copy-start | bytes 172036
  8.2 7.3 %copy-start.4 = (bf16[1,3584,256]{2,1,0:T(8,128)(2,1)S(1)}, bf16[1,3584,256]{2,1,0:T(8,128)(2,1)}, u32[]{:S(2)}) copy-start(bf16[1,3584,256]{2,1,0:T(8,128)(2,1)} %param.10) | copy-start | bytes 5505028
  8.2 9.3 %collective-permute-start.7 = (bf16[8,3584]{1,0:T(8,128)(2,1)S(1)}, bf16[8,3584]{1,0:T(8,128)(2,1)S(1)}, u32[]{:S(2)}, u32[]{:S(2)}) collective-permute-start(bf16[8,3584]{1,0:T(8,128)(2,1)S(1)} %collective-permute-done.1), channel_id=1, source_target_pairs={{0,16},{8,24},{16,0},{24,8},{1,17},{9,25},{17,1},{25,9},{2,18},{10... | collective-permute-start | bytes 172040 | tf_op jit(solution)/shard_map/ppermute | solution.py:21
  8.8 5.1 %collective-permute-start.3 = (bf16[8,3584]{1,0:T(8,128)(2,1)S(1)}, bf16[8,3584]{1,0:T(8,128)(2,1)S(1)}, u32[]{:S(2)}, u32[]{:S(2)}) collective-permute-start(bf16[8,3584]{1,0:T(8,128)(2,1)S(1)} %collective-permute-done), channel_id=1, source_target_pairs={{0,16},{8,24},{16,0},{24,8},{1,17},{9,25},{17,1},{25,9},{2,18},{10... | collective-permute-start | bytes 172040 | tf_op jit(solution)/shard_map/ppermute | solution.py:21
  13.3 4.2 %collective-permute-start.8 = (bf16[8,3584]{1,0:T(8,128)(2,1)S(1)}, bf16[8,3584]{1,0:T(8,128)(2,1)S(1)}, u32[]{:S(2)}, u32[]{:S(2)}) collective-permute-start(bf16[8,3584]{1,0:T(8,128)(2,1)S(1)} %collective-permute-done.2), channel_id=1, source_target_pairs={{0,16},{8,24},{16,0},{24,8},{1,17},{9,25},{17,1},{25,9},{2,18},{10... | collective-permute-start | bytes 172040 | tf_op jit(solution)/shard_map/ppermute | solution.py:21
  13.9 2.1 %copy-start.5 = (bf16[1,3584,256]{2,1,0:T(8,128)(2,1)S(1)}, bf16[1,3584,256]{2,1,0:T(8,128)(2,1)}, u32[]{:S(2)}) copy-start(bf16[1,3584,256]{2,1,0:T(8,128)(2,1)} %param.9) | copy-start | bytes 5505028
  13.9 1.6 %collective-permute-start.4 = (bf16[32,3584]{1,0:T(8,128)(2,1)S(1)}, bf16[32,3584]{1,0:T(8,128)(2,1)S(1)}, u32[]{:S(2)}, u32[]{:S(2)}) collective-permute-start(bf16[32,3584]{1,0:T(8,128)(2,1)S(1)} %shard_map.65), channel_id=1, source_target_pairs={{0,8},{8,0},{16,24},{24,16},{1,9},{9,1},{17,25},{25,17},{2,10},{10... | collective-permute-start | bytes 688136 | tf_op jit(solution)/shard_map/ppermute | solution.py:39
  17.5 1.7 %collective-permute-start.9 = (bf16[32,3584]{1,0:T(8,128)(2,1)S(1)}, bf16[32,3584]{1,0:T(8,128)(2,1)S(1)}, u32[]{:S(2)}, u32[]{:S(2)}) collective-permute-start(bf16[32,3584]{1,0:T(8,128)(2,1)S(1)} %pad_maximum_fusion.4.refs_0_), channel_id=1, source_target_pairs={{0,8},{8,0},{16,24},{24,16},{1,9},{9,1},{17,25},{25,17},{2,10},{10... | collective-permute-start | bytes 688136 | tf_op jit(solution)/shard_map/ppermute | solution.py:39
  17.6 4.5 %collective-permute-start.5 = (bf16[64,512]{1,0:T(8,128)(2,1)S(1)}, bf16[64,512]{1,0:T(8,128)(2,1)S(1)}, u32[]{:S(2)}, u32[]{:S(2)}) collective-permute-start(bf16[64,512]{1,0:T(8,128)(2,1)S(1)} %fusion.15.refs_1_), channel_id=1, source_target_pairs={{0,1},{1,0},{2,3},{3,2},{4,5},{5,4},{6,7},{7,6},{8,9},{9,8},{10,11... | collective-permute-start | bytes 196616 | tf_op jit(solution)/shard_map/ppermute | solution.py:16
  20.1 4.3 %collective-permute-start.14 = (bf16[64,512]{1,0:T(8,128)(2,1)S(1)}, bf16[64,512]{1,0:T(8,128)(2,1)S(1)}, u32[]{:S(2)}, u32[]{:S(2)}) collective-permute-start(bf16[64,512]{1,0:T(8,128)(2,1)S(1)} %fusion.14.refs_1_), channel_id=1, source_target_pairs={{0,1},{1,0},{2,3},{3,2},{4,5},{5,4},{6,7},{7,6},{8,9},{9,8},{10,11... | collective-permute-start | bytes 196616 | tf_op jit(solution)/shard_map/ppermute | solution.py:16
  22.6 1.6 %collective-permute-start.10 = (bf16[32,3584]{1,0:T(8,128)(2,1)S(1)}, bf16[32,3584]{1,0:T(8,128)(2,1)S(1)}, u32[]{:S(2)}, u32[]{:S(2)}) collective-permute-start(bf16[32,3584]{1,0:T(8,128)(2,1)S(1)} %slice.122), channel_id=1, source_target_pairs={{0,8},{8,0},{16,24},{24,16},{1,9},{9,1},{17,25},{25,17},{2,10},{10... | collective-permute-start | bytes 688136 | tf_op jit(solution)/shard_map/ppermute | solution.py:39
  24.8 15.5 %copy-start.2 = (s32[8,1]{0,1:T(1,128)S(1)}, s32[8,1]{0,1:T(1,128)}, u32[]{:S(2)}) copy-start(s32[8,1]{0,1:T(1,128)} %param.7) | copy-start | bytes 100
  24.9 15.5 %copy-start.3 = (s32[8,1]{0,1:T(1,128)S(1)}, s32[8,1]{0,1:T(1,128)}, u32[]{:S(2)}) copy-start(s32[8,1]{0,1:T(1,128)} %param.8) | copy-start | bytes 100
  24.9 4.6 %collective-permute-start.15 = (bf16[32,3584]{1,0:T(8,128)(2,1)S(1)}, bf16[32,3584]{1,0:T(8,128)(2,1)S(1)}, u32[]{:S(2)}, u32[]{:S(2)}) collective-permute-start(bf16[32,3584]{1,0:T(8,128)(2,1)S(1)} %slice.121), channel_id=1, source_target_pairs={{0,8},{8,0},{16,24},{24,16},{1,9},{9,1},{17,25},{25,17},{2,10},{10... | collective-permute-start | bytes 688136 | tf_op jit(solution)/shard_map/ppermute | solution.py:39
  25.0 8.2 %collective-permute-start.13 = (bf16[8,3584]{1,0:T(8,128)(2,1)S(1)}, bf16[8,3584]{1,0:T(8,128)(2,1)S(1)}, u32[]{:S(2)}, u32[]{:S(2)}) collective-permute-start(bf16[8,3584]{1,0:T(8,128)(2,1)S(1)} %get-tuple-element.11), channel_id=1, source_target_pairs={{0,6},{2,4},{4,2},{6,0},{8,14},{10,12},{12,10},{14,8},{16,22},{18,... | collective-permute-start | bytes 172040 | tf_op jit(solution)/shard_map/ppermute | solution.py:35
  28.6 6.3 %collective-permute-start.12 = (bf16[8,3584]{1,0:T(8,128)(2,1)S(1)}, bf16[8,3584]{1,0:T(8,128)(2,1)S(1)}, u32[]{:S(2)}, u32[]{:S(2)}) collective-permute-start(bf16[8,3584]{1,0:T(8,128)(2,1)S(1)} %get-tuple-element.12), channel_id=1, source_target_pairs={{0,4},{2,6},{4,0},{6,2},{8,12},{10,14},{12,8},{14,10},{16,20},{18,... | collective-permute-start | bytes 172040 | tf_op jit(solution)/shard_map/ppermute | solution.py:35
  28.6 7.8 %collective-permute-start.11 = (bf16[8,3584]{1,0:T(8,128)(2,1)S(1)}, bf16[8,3584]{1,0:T(8,128)(2,1)S(1)}, u32[]{:S(2)}, u32[]{:S(2)}) collective-permute-start(bf16[8,3584]{1,0:T(8,128)(2,1)S(1)} %get-tuple-element.13), channel_id=1, source_target_pairs={{0,2},{2,0},{4,6},{6,4},{8,10},{10,8},{12,14},{14,12},{16,18},{18,... | collective-permute-start | bytes 172040 | tf_op jit(solution)/shard_map/ppermute | solution.py:35
  29.5 7.8 %collective-permute-start.19 = (bf16[8,3584]{1,0:T(8,128)(2,1)S(1)}, bf16[8,3584]{1,0:T(8,128)(2,1)S(1)}, u32[]{:S(2)}, u32[]{:S(2)}) collective-permute-start(bf16[8,3584]{1,0:T(8,128)(2,1)S(1)} %get-tuple-element.7), channel_id=1, source_target_pairs={{0,22},{2,20},{4,18},{6,16},{8,30},{10,28},{12,26},{14,24},{16,6},... | collective-permute-start | bytes 172040 | tf_op jit(solution)/shard_map/ppermute | solution.py:35
  33.2 6.0 %collective-permute-start.18 = (bf16[8,3584]{1,0:T(8,128)(2,1)S(1)}, bf16[8,3584]{1,0:T(8,128)(2,1)S(1)}, u32[]{:S(2)}, u32[]{:S(2)}) collective-permute-start(bf16[8,3584]{1,0:T(8,128)(2,1)S(1)} %get-tuple-element.8), channel_id=1, source_target_pairs={{0,20},{2,22},{4,16},{6,18},{8,28},{10,30},{12,24},{14,26},{16,4},... | collective-permute-start | bytes 172040 | tf_op jit(solution)/shard_map/ppermute | solution.py:35
  33.2 6.3 %collective-permute-start.17 = (bf16[8,3584]{1,0:T(8,128)(2,1)S(1)}, bf16[8,3584]{1,0:T(8,128)(2,1)S(1)}, u32[]{:S(2)}, u32[]{:S(2)}) collective-permute-start(bf16[8,3584]{1,0:T(8,128)(2,1)S(1)} %get-tuple-element.9), channel_id=1, source_target_pairs={{0,18},{2,16},{4,22},{6,20},{8,26},{10,24},{12,30},{14,28},{16,2},... | collective-permute-start | bytes 172040 | tf_op jit(solution)/shard_map/ppermute | solution.py:35
  34.9 5.4 %collective-permute-start.16 = (bf16[8,3584]{1,0:T(8,128)(2,1)S(1)}, bf16[8,3584]{1,0:T(8,128)(2,1)S(1)}, u32[]{:S(2)}, u32[]{:S(2)}) collective-permute-start(bf16[8,3584]{1,0:T(8,128)(2,1)S(1)} %get-tuple-element.10), channel_id=1, source_target_pairs={{0,16},{2,18},{4,20},{6,22},{8,24},{10,26},{12,28},{14,30},{16,0},... | collective-permute-start | bytes 172040 | tf_op jit(solution)/shard_map/ppermute | solution.py:35

commit v15 on v14

--- a/solution.py
+++ b/solution.py
@@ -124,11 +124,11 @@
         return out[:kept] + swapped
 
     held = copied(tokens)
-    places = tuple(range(n_tp))
+    places = (0, n_tp - 1, *range(1, n_tp - 1))
     blocks = [held] + [exchange(tokens, 0, t) for t in places[1:]]
     far = [[rotate_experts(rows, s) for rows in (tokens, *blocks[1:])] for s in range(1, experts)]
     near = jnp.concatenate(blocks, axis=0)
-    near_swapped = swap_half(after(near, *(line[1] for line in far)))
+    near_swapped = swap_half(after(near, *(line[places.index(1)] for line in far)))
     near = jnp.concatenate([near, near_swapped], axis=0)
     near_part, near_sent, near_others = partial_sums(near)
     far = [after(rows, near_sent) if i == n_tp - 1 else rows for line in far for i, rows in enumerate(line)]

time: 41.2 us -> 40.2 us (0.976)
  waiting for transfers between devices: 11.7 us -> 10.4 us
    ppermute x10, waiting for transfers between devices: 6.92 us -> 5.64 us  [exchange(): return lax.ppermute(value, ('grp', 'tp'), pairs)]
    ppermute x4, starting transfers between devices: 4.12 us -> 4.57 us  [rotate_experts(): lax.ppermute(value, 'grp', [(i, (i + 2 * by) % groups) for i in range(gro...]
  transfers between devices with their start and end apart: 20 -> 20, of which waited for: 10 -> 9; matrix products, arithmetic and copies ran while one was open for 6% -> 6% of each run, Pallas kernels for 0% -> 0%
where the time goes in v15:
time: 40.2 us; the launch traced here: 40 us
  starting transfers between devices  24.8 us (62%)
  waiting for transfers between devices  10.4 us (26%)
  matrix products  2.6 us (6%)
  local copies, waits for them, and re-layouts  1.02 us (3%)
  Pallas kernels  0.74 us (2%)
    ppermute x10, starting transfers between devices, exchange(): return lax.ppermute(value, ('grp', 'tp'), pairs)  16.9 us
    ppermute x10, waiting for transfers between devices, exchange(): return lax.ppermute(value, ('grp', 'tp'), pairs)  5.64 us
    ppermute x4, starting transfers between devices, rotate_experts(): lax.ppermute(value, 'grp', [(i, (i + 2 * by) % groups) for i in range(gro...  4.57 us
    ppermute x2, starting transfers between devices, rotate(): lax.ppermute(value, axis, [(i, (i + by) % size) for i in range(size)])  3.06 us
    ppermute x4, waiting for transfers between devices, swap_half(): lax.ppermute(value, 'grp', [(i, i ^ 1) for i in range(lax.axis_size('grp'...  2.93 us
    dot_general x4, matrix products, partial_sums(): jnp.dot(rows, w, preferred_element_type=f32)  1.77 us
    ppermute x4, waiting for transfers between devices, rotate_experts(): lax.ppermute(value, 'grp', [(i, (i + 2 * by) % groups) for i in range(gro...  1.08 us
    unnamed x16, local copies, waits for them, and re-layouts  0.9 us
  transfers between devices with their start and end apart: 20, of which 9 were waited for; matrix products, arithmetic and copies ran while one was open for 6% of the time, Pallas kernels for 0%

profile of v15, /device:TPU:0, one launch (start us, length us, event | category | flops | bytes accessed | tf_op | source)
XLA Modules:
  0.0 40.0 jit_solution(7124357020956952205)
XLA Ops:
  0.0 0.0 copy-start
  0.0 3.0 %collective-permute-start.1 = (bf16[8,3584]{1,0:T(8,128)(2,1)}, bf16[8,3584]{1,0:T(8,128)(2,1)S(1)}, u32[]{:S(2)}, u32[]{:S(2)}) collective-permute-start(bf16[8,3584]{1,0:T(8,128)(2,1)} %from_ref.1), channel_id=1, source_target_pairs={{0,2},{2,0},{4,6},{6,4},{8,10},{10,8},{12,14},{14,12},{16,18},{18,... | collective-permute-start | bytes 172040 | tf_op jit(solution)/shard_map/ppermute | solution.py:35
  3.0 2.5 %collective-permute-start = (bf16[8,3584]{1,0:T(8,128)(2,1)}, bf16[8,3584]{1,0:T(8,128)(2,1)S(1)}, u32[]{:S(2)}, u32[]{:S(2)}) collective-permute-start(bf16[8,3584]{1,0:T(8,128)(2,1)} %from_ref.1), channel_id=1, source_target_pairs={{0,6},{2,4},{4,2},{6,0},{8,14},{10,12},{12,10},{14,8},{16,22},{18,... | collective-permute-start | bytes 172040 | tf_op jit(solution)/shard_map/ppermute | solution.py:35
  5.5 1.5 %collective-permute-start.6 = (bf16[8,3584]{1,0:T(8,128)(2,1)}, bf16[8,3584]{1,0:T(8,128)(2,1)S(1)}, u32[]{:S(2)}, u32[]{:S(2)}) collective-permute-start(bf16[8,3584]{1,0:T(8,128)(2,1)} %from_ref.1), channel_id=1, source_target_pairs={{0,16},{8,24},{16,0},{24,8},{1,17},{9,25},{17,1},{25,9},{2,18},{10... | collective-permute-start | bytes 172040 | tf_op jit(solution)/shard_map/ppermute | solution.py:21
  7.0 0.1 collective-permute-start.2
  7.1 0.0 copy-start.1
  7.1 0.9 %copy-done.1 = bf16[8,3584]{1,0:T(8,128)(2,1)S(1)} copy-done((bf16[8,3584]{1,0:T(8,128)(2,1)S(1)}, bf16[8,3584]{1,0:T(8,128)(2,1)}, u32[]{:S(2)}) %copy-start.1) | copy-done | bytes 57368
  8.0 0.0 copy-start.4
  8.0 0.0 collective-permute-done.1
  8.0 0.6 %collective-permute-start.3 = (bf16[8,3584]{1,0:T(8,128)(2,1)S(1)}, bf16[8,3584]{1,0:T(8,128)(2,1)S(1)}, u32[]{:S(2)}, u32[]{:S(2)}) collective-permute-start(bf16[8,3584]{1,0:T(8,128)(2,1)S(1)} %collective-permute-done.1), channel_id=1, source_target_pairs={{0,16},{8,24},{16,0},{24,8},{1,17},{9,25},{17,1},{25,9},{2,18},{10... | collective-permute-start | bytes 172040 | tf_op jit(solution)/shard_map/ppermute | solution.py:21
  8.6 0.6 %collective-permute-done = bf16[8,3584]{1,0:T(8,128)(2,1)S(1)} collective-permute-done((bf16[8,3584]{1,0:T(8,128)(2,1)}, bf16[8,3584]{1,0:T(8,128)(2,1)S(1)}, u32[]{:S(2)}, u32[]{:S(2)}) %collective-permute-start) | collective-permute-done | bytes 57376 | tf_op jit(solution)/shard_map/ppermute | solution.py:35
  9.2 1.9 %collective-permute-start.7 = (bf16[8,3584]{1,0:T(8,128)(2,1)S(1)}, bf16[8,3584]{1,0:T(8,128)(2,1)S(1)}, u32[]{:S(2)}, u32[]{:S(2)}) collective-permute-start(bf16[8,3584]{1,0:T(8,128)(2,1)S(1)} %collective-permute-done), channel_id=1, source_target_pairs={{0,16},{8,24},{16,0},{24,8},{1,17},{9,25},{17,1},{25,9},{2,18},{10... | collective-permute-start | bytes 172040 | tf_op jit(solution)/shard_map/ppermute | solution.py:21
  11.2 1.7 %collective-permute-done.2 = bf16[8,3584]{1,0:T(8,128)(2,1)S(1)} collective-permute-done((bf16[8,3584]{1,0:T(8,128)(2,1)}, bf16[8,3584]{1,0:T(8,128)(2,1)S(1)}, u32[]{:S(2)}, u32[]{:S(2)}) %collective-permute-start.2) | collective-permute-done | bytes 57376 | tf_op jit(solution)/shard_map/ppermute | solution.py:35
  12.9 0.5 %collective-permute-start.8 = (bf16[8,3584]{1,0:T(8,128)(2,1)S(1)}, bf16[8,3584]{1,0:T(8,128)(2,1)S(1)}, u32[]{:S(2)}, u32[]{:S(2)}) collective-permute-start(bf16[8,3584]{1,0:T(8,128)(2,1)S(1)} %collective-permute-done.2), channel_id=1, source_target_pairs={{0,16},{8,24},{16,0},{24,8},{1,17},{9,25},{17,1},{25,9},{2,18},{10... | collective-permute-start | bytes 172040 | tf_op jit(solution)/shard_map/ppermute | solution.py:21
  13.5 0.0 copy-start.5
  13.5 0.0 collective-permute-done.3.refs_1_
  13.5 0.1 collective-permute-start.4
  13.6 1.5 %collective-permute-done.4 = bf16[32,3584]{1,0:T(8,128)(2,1)S(1)} collective-permute-done((bf16[32,3584]{1,0:T(8,128)(2,1)S(1)}, bf16[32,3584]{1,0:T(8,128)(2,1)S(1)}, u32[]{:S(2)}, u32[]{:S(2)}) %collective-permute-start.4) | collective-permute-done | bytes 229408 | tf_op jit(solution)/shard_map/ppermute | solution.py:39
  15.1 0.0 copy-done.4
  15.1 0.4 %fusion.6 = f32[64,256]{1,0:T(8,128)S(1)} fusion(bf16[64,3584]{1,0:T(8,128)(2,1)S(1)} %constant_dynamic-update-slice_fusion, bf16[1,3584,256]{2,1,0:T(8,128)(2,1)S(1)} %copy-done.4), kind=kOutput, calls=%fused_computation.6 | convolution fusion | flops 117440512 | bytes 2359296 | tf_op jit(solution)/shard_map/dot_general | solution.py:108
  15.5 0.0 copy-done.5
  15.5 0.4 %fusion.10 = f32[64,256]{1,0:T(8,128)S(1)} fusion(bf16[64,3584]{1,0:T(8,128)(2,1)S(1)} %constant_dynamic-update-slice_fusion, bf16[1,3584,256]{2,1,0:T(8,128)(2,1)S(1)} %copy-done.5), kind=kOutput, calls=%fused_computation.10 | convolution fusion | flops 117440512 | bytes 2359296 | tf_op jit(solution)/shard_map/dot_general | solution.py:108
  16.0 1.1 %collective-permute-done.8.refs_0_ = bf16[8,3584]{1,0:T(8,128)(2,1)S(1)} collective-permute-done((bf16[8,3584]{1,0:T(8,128)(2,1)S(1)}, bf16[8,3584]{1,0:T(8,128)(2,1)S(1)}, u32[]{:S(2)}, u32[]{:S(2)}) %collective-permute-start.8) | collective-permute-done | bytes 57376 | tf_op jit(solution)/shard_map/ppermute | solution.py:21
  17.1 0.0 collective-permute-done.6
  17.1 0.0 collective-permute-done.7
  17.1 0.1 collective-permute-start.9
  17.2 1.6 %collective-permute-start.5 = (bf16[64,512]{1,0:T(8,128)(2,1)S(1)}, bf16[64,512]{1,0:T(8,128)(2,1)S(1)}, u32[]{:S(2)}, u32[]{:S(2)}) collective-permute-start(bf16[64,512]{1,0:T(8,128)(2,1)S(1)} %fusion.15.refs_1_), channel_id=1, source_target_pairs={{0,1},{1,0},{2,3},{3,2},{4,5},{5,4},{6,7},{7,6},{8,9},{9,8},{10,11... | collective-permute-start | bytes 196616 | tf_op jit(solution)/shard_map/ppermute | solution.py:16
  18.8 0.0 collective-permute-done.9
  18.8 0.4 %fusion.4 = f32[64,256]{1,0:T(8,128)S(1)} fusion(bf16[1,3584,256]{2,1,0:T(8,128)(2,1)S(1)} %copy-done.4, bf16[32,3584]{1,0:T(8,128)(2,1)S(1)} %collective-permute-done.9, bf16[32,3584]{1,0:T(8,128)(2,1)S(1)} %shard_map.67), kind=kOutput, calls=%fused_computation.4 | convolution fusion | flops 118358016 | bytes 2359296 | tf_op jit(solution)/shard_map/dot_general | solution.py:108
  19.2 0.4 %fusion.8 = f32[64,256]{1,0:T(8,128)S(1)} fusion(bf16[1,3584,256]{2,1,0:T(8,128)(2,1)S(1)} %copy-done.5, bf16[32,3584]{1,0:T(8,128)(2,1)S(1)} %collective-permute-done.9, bf16[32,3584]{1,0:T(8,128)(2,1)S(1)} %shard_map.67), kind=kOutput, calls=%fused_computation.8 | convolution fusion | flops 118358016 | bytes 2359296 | tf_op jit(solution)/shard_map/dot_general | solution.py:108
  19.7 1.5 %collective-permute-start.14 = (bf16[64,512]{1,0:T(8,128)(2,1)S(1)}, bf16[64,512]{1,0:T(8,128)(2,1)S(1)}, u32[]{:S(2)}, u32[]{:S(2)}) collective-permute-start(bf16[64,512]{1,0:T(8,128)(2,1)S(1)} %fusion.14.refs_1_), channel_id=1, source_target_pairs={{0,1},{1,0},{2,3},{3,2},{4,5},{5,4},{6,7},{7,6},{8,9},{9,8},{10,11... | collective-permute-start | bytes 196616 | tf_op jit(solution)/shard_map/ppermute | solution.py:16
  21.1 0.5 %collective-permute-done.5.refs_0_ = bf16[64,512]{1,0:T(8,128)(2,1)S(1)} collective-permute-done((bf16[64,512]{1,0:T(8,128)(2,1)S(1)}, bf16[64,512]{1,0:T(8,128)(2,1)S(1)}, u32[]{:S(2)}, u32[]{:S(2)}) %collective-permute-start.5) | collective-permute-done | bytes 65568 | tf_op jit(solution)/shard_map/ppermute | solution.py:16
  21.7 0.0 copy-done
  21.7 0.4 %fusion.2.refs_0_ = f32[64,3584]{1,0:T(8,128)S(1)} fusion(bf16[1,256,3584]{2,1,0:T(8,128)(2,1)S(1)} %copy-done, f32[64,512]{1,0:T(8,128)S(1)} %convert_add_fusion.1), kind=kOutput, calls=%fused_computation.2 | convolution fusion | flops 117538816 | bytes 2883584 | tf_op jit(solution)/shard_map/dot_general | solution.py:119
  22.2 0.1 collective-permute-start.10
  22.3 1.5 %collective-permute-done.10 = bf16[32,3584]{1,0:T(8,128)(2,1)S(1)} collective-permute-done((bf16[32,3584]{1,0:T(8,128)(2,1)S(1)}, bf16[32,3584]{1,0:T(8,128)(2,1)S(1)}, u32[]{:S(2)}, u32[]{:S(2)}) %collective-permute-start.10) | collective-permute-done | bytes 229408 | tf_op jit(solution)/shard_map/ppermute | solution.py:39
  23.7 0.1 fusion.26
  23.8 0.2 collective-permute-done.14.refs_0_
  24.0 0.4 %fusion = f32[64,3584]{1,0:T(8,128)S(1)} fusion(bf16[1,256,3584]{2,1,0:T(8,128)(2,1)S(1)} %copy-done, f32[64,512]{1,0:T(8,128)S(1)} %convert_add_fusion), kind=kOutput, calls=%fused_computation | convolution fusion | flops 117538816 | bytes 2883584 | tf_op jit(solution)/shard_map/dot_general | solution.py:119
  24.4 0.0 copy-start.2
  24.5 0.0 copy-start.3
  24.5 0.1 collective-permute-start.15
  24.6 1.1 %collective-permute-start.13 = (bf16[8,3584]{1,0:T(8,128)(2,1)S(1)}, bf16[8,3584]{1,0:T(8,128)(2,1)S(1)}, u32[]{:S(2)}, u32[]{:S(2)}) collective-permute-start(bf16[8,3584]{1,0:T(8,128)(2,1)S(1)} %get-tuple-element.11), channel_id=1, source_target_pairs={{0,4},{2,6},{4,0},{6,2},{8,12},{10,14},{12,8},{14,10},{16,20},{18,... | collective-permute-start | bytes 172040 | tf_op jit(solution)/shard_map/ppermute | solution.py:35
  25.7 0.7 %collective-permute-start.12 = (bf16[8,3584]{1,0:T(8,128)(2,1)S(1)}, bf16[8,3584]{1,0:T(8,128)(2,1)S(1)}, u32[]{:S(2)}, u32[]{:S(2)}) collective-permute-start(bf16[8,3584]{1,0:T(8,128)(2,1)S(1)} %get-tuple-element.12), channel_id=1, source_target_pairs={{0,2},{2,0},{4,6},{6,4},{8,10},{10,8},{12,14},{14,12},{16,18},{18,... | collective-permute-start | bytes 172040 | tf_op jit(solution)/shard_map/ppermute | solution.py:35
  26.4 2.7 %collective-permute-start.11 = (bf16[8,3584]{1,0:T(8,128)(2,1)S(1)}, bf16[8,3584]{1,0:T(8,128)(2,1)S(1)}, u32[]{:S(2)}, u32[]{:S(2)}) collective-permute-start(bf16[8,3584]{1,0:T(8,128)(2,1)S(1)} %get-tuple-element.13), channel_id=1, source_target_pairs={{0,6},{2,4},{4,2},{6,0},{8,14},{10,12},{12,10},{14,8},{16,22},{18,... | collective-permute-start | bytes 172040 | tf_op jit(solution)/shard_map/ppermute | solution.py:35
  29.1 0.0 collective-permute-done.15
  29.1 0.3 collective-permute-start.19
  29.4 2.4 %collective-permute-start.18 = (bf16[8,3584]{1,0:T(8,128)(2,1)S(1)}, bf16[8,3584]{1,0:T(8,128)(2,1)S(1)}, u32[]{:S(2)}, u32[]{:S(2)}) collective-permute-start(bf16[8,3584]{1,0:T(8,128)(2,1)S(1)} %get-tuple-element.8), channel_id=1, source_target_pairs={{0,18},{2,16},{4,22},{6,20},{8,26},{10,24},{12,30},{14,28},{16,2},... | collective-permute-start | bytes 172040 | tf_op jit(solution)/shard_map/ppermute | solution.py:35
  31.8 0.0 collective-permute-done.13.refs_3_
  31.8 2.6 %collective-permute-start.17 = (bf16[8,3584]{1,0:T(8,128)(2,1)S(1)}, bf16[8,3584]{1,0:T(8,128)(2,1)S(1)}, u32[]{:S(2)}, u32[]{:S(2)}) collective-permute-start(bf16[8,3584]{1,0:T(8,128)(2,1)S(1)} %get-tuple-element.9), channel_id=1, source_target_pairs={{0,22},{2,20},{4,18},{6,16},{8,30},{10,28},{12,26},{14,24},{16,6},... | collective-permute-start | bytes 172040 | tf_op jit(solution)/shard_map/ppermute | solution.py:35
  34.5 0.0 collective-permute-done.12.refs_2_
  34.5 1.5 %collective-permute-start.16 = (bf16[8,3584]{1,0:T(8,128)(2,1)S(1)}, bf16[8,3584]{1,0:T(8,128)(2,1)S(1)}, u32[]{:S(2)}, u32[]{:S(2)}) collective-permute-start(bf16[8,3584]{1,0:T(8,128)(2,1)S(1)} %get-tuple-element.10), channel_id=1, source_target_pairs={{0,16},{2,18},{4,20},{6,22},{8,24},{10,26},{12,28},{14,30},{16,0},... | collective-permute-start | bytes 172040 | tf_op jit(solution)/shard_map/ppermute | solution.py:35
  36.0 0.0 collective-permute-done.11.refs_1_
  36.0 0.0 collective-permute-done.19.refs_7_
  36.0 0.0 collective-permute-done.18.refs_6_
  36.0 2.8 %collective-permute-done.17.refs_5_ = bf16[8,3584]{1,0:T(8,128)(2,1)S(1)} collective-permute-done((bf16[8,3584]{1,0:T(8,128)(2,1)S(1)}, bf16[8,3584]{1,0:T(8,128)(2,1)S(1)}, u32[]{:S(2)}, u32[]{:S(2)}) %collective-permute-start.17) | collective-permute-done | bytes 57376 | tf_op jit(solution)/shard_map/ppermute | solution.py:35
  38.8 0.4 %collective-permute-done.16.refs_4_ = bf16[8,3584]{1,0:T(8,128)(2,1)S(1)} collective-permute-done((bf16[8,3584]{1,0:T(8,128)(2,1)S(1)}, bf16[8,3584]{1,0:T(8,128)(2,1)S(1)}, u32[]{:S(2)}, u32[]{:S(2)}) %collective-permute-start.16) | collective-permute-done | bytes 57376 | tf_op jit(solution)/shard_map/ppermute | solution.py:35
  39.3 0.0 copy-done.2
  39.3 0.0 copy-done.3
  39.3 0.7 %shard_map.71 = bf16[8,3584]{1,0:T(8,128)(2,1)} custom-call(s32[1,8]{1,0:T(1,128)S(1)} %bitcast.31, s32[1,8]{1,0:T(1,128)S(1)} %bitcast.32, f32[8,3584]{1,0:T(8,128)S(1)} %slice.83.refs_0_, bf16[8,3584]{1,0:T(8,128)(2,1)S(1)} %collective-permute-done.11.refs_1_, bf16[8,3584]{1,0:T(8,128)(2,1)S(1)} %collective-permute-done.12.refs_2_, ...), custom_call_target="tpu_custom_call" | custom-call | tf_op jit(solution)/shard_map/pallas_call | solution.py:92
  (25 shorter events, 0.3 us)
Async XLA Ops:
  0.0 21.7 %copy-start = (bf16[1,256,3584]{2,1,0:T(8,128)(2,1)S(1)}, bf16[1,256,3584]{2,1,0:T(8,128)(2,1)}, u32[]{:S(2)}) copy-start(bf16[1,256,3584]{2,1,0:T(8,128)(2,1)} %param.11) | copy-start | bytes 5505028
  0.0 8.0 %collective-permute-start.1 = (bf16[8,3584]{1,0:T(8,128)(2,1)}, bf16[8,3584]{1,0:T(8,128)(2,1)S(1)}, u32[]{:S(2)}, u32[]{:S(2)}) collective-permute-start(bf16[8,3584]{1,0:T(8,128)(2,1)} %from_ref.1), channel_id=1, source_target_pairs={{0,2},{2,0},{4,6},{6,4},{8,10},{10,8},{12,14},{14,12},{16,18},{18,... | collective-permute-start | bytes 172040 | tf_op jit(solution)/shard_map/ppermute | solution.py:35
  3.0 6.2 %collective-permute-start = (bf16[8,3584]{1,0:T(8,128)(2,1)}, bf16[8,3584]{1,0:T(8,128)(2,1)S(1)}, u32[]{:S(2)}, u32[]{:S(2)}) collective-permute-start(bf16[8,3584]{1,0:T(8,128)(2,1)} %from_ref.1), channel_id=1, source_target_pairs={{0,6},{2,4},{4,2},{6,0},{8,14},{10,12},{12,10},{14,8},{16,22},{18,... | collective-permute-start | bytes 172040 | tf_op jit(solution)/shard_map/ppermute | solution.py:35
  5.5 11.6 %collective-permute-start.6 = (bf16[8,3584]{1,0:T(8,128)(2,1)}, bf16[8,3584]{1,0:T(8,128)(2,1)S(1)}, u32[]{:S(2)}, u32[]{:S(2)}) collective-permute-start(bf16[8,3584]{1,0:T(8,128)(2,1)} %from_ref.1), channel_id=1, source_target_pairs={{0,16},{8,24},{16,0},{24,8},{1,17},{9,25},{17,1},{25,9},{2,18},{10... | collective-permute-start | bytes 172040 | tf_op jit(solution)/shard_map/ppermute | solution.py:21
  7.0 5.9 %collective-permute-start.2 = (bf16[8,3584]{1,0:T(8,128)(2,1)}, bf16[8,3584]{1,0:T(8,128)(2,1)S(1)}, u32[]{:S(2)}, u32[]{:S(2)}) collective-permute-start(bf16[8,3584]{1,0:T(8,128)(2,1)} %from_ref.1), channel_id=1, source_target_pairs={{0,4},{2,6},{4,0},{6,2},{8,12},{10,14},{12,8},{14,10},{16,20},{18,... | collective-permute-start | bytes 172040 | tf_op jit(solution)/shard_map/ppermute | solution.py:35
  7.1 0.9 %copy-start.1 = (bf16[8,3584]{1,0:T(8,128)(2,1)S(1)}, bf16[8,3584]{1,0:T(8,128)(2,1)}, u32[]{:S(2)}) copy-start(bf16[8,3584]{1,0:T(8,128)(2,1)} %from_ref.1) | copy-start | bytes 172036
  8.0 7.1 %copy-start.4 = (bf16[1,3584,256]{2,1,0:T(8,128)(2,1)S(1)}, bf16[1,3584,256]{2,1,0:T(8,128)(2,1)}, u32[]{:S(2)}) copy-start(bf16[1,3584,256]{2,1,0:T(8,128)(2,1)} %param.10) | copy-start | bytes 5505028
  8.0 5.5 %collective-permute-start.3 = (bf16[8,3584]{1,0:T(8,128)(2,1)S(1)}, bf16[8,3584]{1,0:T(8,128)(2,1)S(1)}, u32[]{:S(2)}, u32[]{:S(2)}) collective-permute-start(bf16[8,3584]{1,0:T(8,128)(2,1)S(1)} %collective-permute-done.1), channel_id=1, source_target_pairs={{0,16},{8,24},{16,0},{24,8},{1,17},{9,25},{17,1},{25,9},{2,18},{10... | collective-permute-start | bytes 172040 | tf_op jit(solution)/shard_map/ppermute | solution.py:21
  9.2 7.9 %collective-permute-start.7 = (bf16[8,3584]{1,0:T(8,128)(2,1)S(1)}, bf16[8,3584]{1,0:T(8,128)(2,1)S(1)}, u32[]{:S(2)}, u32[]{:S(2)}) collective-permute-start(bf16[8,3584]{1,0:T(8,128)(2,1)S(1)} %collective-permute-done), channel_id=1, source_target_pairs={{0,16},{8,24},{16,0},{24,8},{1,17},{9,25},{17,1},{25,9},{2,18},{10... | collective-permute-start | bytes 172040 | tf_op jit(solution)/shard_map/ppermute | solution.py:21
  12.9 4.2 %collective-permute-start.8 = (bf16[8,3584]{1,0:T(8,128)(2,1)S(1)}, bf16[8,3584]{1,0:T(8,128)(2,1)S(1)}, u32[]{:S(2)}, u32[]{:S(2)}) collective-permute-start(bf16[8,3584]{1,0:T(8,128)(2,1)S(1)} %collective-permute-done.2), channel_id=1, source_target_pairs={{0,16},{8,24},{16,0},{24,8},{1,17},{9,25},{17,1},{25,9},{2,18},{10... | collective-permute-start | bytes 172040 | tf_op jit(solution)/shard_map/ppermute | solution.py:21
  13.5 2.1 %copy-start.5 = (bf16[1,3584,256]{2,1,0:T(8,128)(2,1)S(1)}, bf16[1,3584,256]{2,1,0:T(8,128)(2,1)}, u32[]{:S(2)}) copy-start(bf16[1,3584,256]{2,1,0:T(8,128)(2,1)} %param.9) | copy-start | bytes 5505028
  13.5 1.6 %collective-permute-start.4 = (bf16[32,3584]{1,0:T(8,128)(2,1)S(1)}, bf16[32,3584]{1,0:T(8,128)(2,1)S(1)}, u32[]{:S(2)}, u32[]{:S(2)}) collective-permute-start(bf16[32,3584]{1,0:T(8,128)(2,1)S(1)} %shard_map.65), channel_id=1, source_target_pairs={{0,8},{8,0},{16,24},{24,16},{1,9},{9,1},{17,25},{25,17},{2,10},{10... | collective-permute-start | bytes 688136 | tf_op jit(solution)/shard_map/ppermute | solution.py:39
  17.1 1.7 %collective-permute-start.9 = (bf16[32,3584]{1,0:T(8,128)(2,1)S(1)}, bf16[32,3584]{1,0:T(8,128)(2,1)S(1)}, u32[]{:S(2)}, u32[]{:S(2)}) collective-permute-start(bf16[32,3584]{1,0:T(8,128)(2,1)S(1)} %pad_maximum_fusion.4.refs_0_), channel_id=1, source_target_pairs={{0,8},{8,0},{16,24},{24,16},{1,9},{9,1},{17,25},{25,17},{2,10},{10... | collective-permute-start | bytes 688136 | tf_op jit(solution)/shard_map/ppermute | solution.py:39
  17.2 4.5 %collective-permute-start.5 = (bf16[64,512]{1,0:T(8,128)(2,1)S(1)}, bf16[64,512]{1,0:T(8,128)(2,1)S(1)}, u32[]{:S(2)}, u32[]{:S(2)}) collective-permute-start(bf16[64,512]{1,0:T(8,128)(2,1)S(1)} %fusion.15.refs_1_), channel_id=1, source_target_pairs={{0,1},{1,0},{2,3},{3,2},{4,5},{5,4},{6,7},{7,6},{8,9},{9,8},{10,11... | collective-permute-start | bytes 196616 | tf_op jit(solution)/shard_map/ppermute | solution.py:16
  19.7 4.3 %collective-permute-start.14 = (bf16[64,512]{1,0:T(8,128)(2,1)S(1)}, bf16[64,512]{1,0:T(8,128)(2,1)S(1)}, u32[]{:S(2)}, u32[]{:S(2)}) collective-permute-start(bf16[64,512]{1,0:T(8,128)(2,1)S(1)} %fusion.14.refs_1_), channel_id=1, source_target_pairs={{0,1},{1,0},{2,3},{3,2},{4,5},{5,4},{6,7},{7,6},{8,9},{9,8},{10,11... | collective-permute-start | bytes 196616 | tf_op jit(solution)/shard_map/ppermute | solution.py:16
  22.2 1.6 %collective-permute-start.10 = (bf16[32,3584]{1,0:T(8,128)(2,1)S(1)}, bf16[32,3584]{1,0:T(8,128)(2,1)S(1)}, u32[]{:S(2)}, u32[]{:S(2)}) collective-permute-start(bf16[32,3584]{1,0:T(8,128)(2,1)S(1)} %slice.122), channel_id=1, source_target_pairs={{0,8},{8,0},{16,24},{24,16},{1,9},{9,1},{17,25},{25,17},{2,10},{10... | collective-permute-start | bytes 688136 | tf_op jit(solution)/shard_map/ppermute | solution.py:39
  24.4 14.8 %copy-start.2 = (s32[8,1]{0,1:T(1,128)S(1)}, s32[8,1]{0,1:T(1,128)}, u32[]{:S(2)}) copy-start(s32[8,1]{0,1:T(1,128)} %param.7) | copy-start | bytes 100
  24.5 14.8 %copy-start.3 = (s32[8,1]{0,1:T(1,128)S(1)}, s32[8,1]{0,1:T(1,128)}, u32[]{:S(2)}) copy-start(s32[8,1]{0,1:T(1,128)} %param.8) | copy-start | bytes 100
  24.5 4.6 %collective-permute-start.15 = (bf16[32,3584]{1,0:T(8,128)(2,1)S(1)}, bf16[32,3584]{1,0:T(8,128)(2,1)S(1)}, u32[]{:S(2)}, u32[]{:S(2)}) collective-permute-start(bf16[32,3584]{1,0:T(8,128)(2,1)S(1)} %slice.121), channel_id=1, source_target_pairs={{0,8},{8,0},{16,24},{24,16},{1,9},{9,1},{17,25},{25,17},{2,10},{10... | collective-permute-start | bytes 688136 | tf_op jit(solution)/shard_map/ppermute | solution.py:39
  24.6 7.2 %collective-permute-start.13 = (bf16[8,3584]{1,0:T(8,128)(2,1)S(1)}, bf16[8,3584]{1,0:T(8,128)(2,1)S(1)}, u32[]{:S(2)}, u32[]{:S(2)}) collective-permute-start(bf16[8,3584]{1,0:T(8,128)(2,1)S(1)} %get-tuple-element.11), channel_id=1, source_target_pairs={{0,4},{2,6},{4,0},{6,2},{8,12},{10,14},{12,8},{14,10},{16,20},{18,... | collective-permute-start | bytes 172040 | tf_op jit(solution)/shard_map/ppermute | solution.py:35
  25.7 8.8 %collective-permute-start.12 = (bf16[8,3584]{1,0:T(8,128)(2,1)S(1)}, bf16[8,3584]{1,0:T(8,128)(2,1)S(1)}, u32[]{:S(2)}, u32[]{:S(2)}) collective-permute-start(bf16[8,3584]{1,0:T(8,128)(2,1)S(1)} %get-tuple-element.12), channel_id=1, source_target_pairs={{0,2},{2,0},{4,6},{6,4},{8,10},{10,8},{12,14},{14,12},{16,18},{18,... | collective-permute-start | bytes 172040 | tf_op jit(solution)/shard_map/ppermute | solution.py:35
  26.4 9.6 %collective-permute-start.11 = (bf16[8,3584]{1,0:T(8,128)(2,1)S(1)}, bf16[8,3584]{1,0:T(8,128)(2,1)S(1)}, u32[]{:S(2)}, u32[]{:S(2)}) collective-permute-start(bf16[8,3584]{1,0:T(8,128)(2,1)S(1)} %get-tuple-element.13), channel_id=1, source_target_pairs={{0,6},{2,4},{4,2},{6,0},{8,14},{10,12},{12,10},{14,8},{16,22},{18,... | collective-permute-start | bytes 172040 | tf_op jit(solution)/shard_map/ppermute | solution.py:35
  29.1 6.8 %collective-permute-start.19 = (bf16[8,3584]{1,0:T(8,128)(2,1)S(1)}, bf16[8,3584]{1,0:T(8,128)(2,1)S(1)}, u32[]{:S(2)}, u32[]{:S(2)}) collective-permute-start(bf16[8,3584]{1,0:T(8,128)(2,1)S(1)} %get-tuple-element.7), channel_id=1, source_target_pairs={{0,20},{2,22},{4,16},{6,18},{8,28},{10,30},{12,24},{14,26},{16,4},... | collective-permute-start | bytes 172040 | tf_op jit(solution)/shard_map/ppermute | solution.py:35
  29.4 6.6 %collective-permute-start.18 = (bf16[8,3584]{1,0:T(8,128)(2,1)S(1)}, bf16[8,3584]{1,0:T(8,128)(2,1)S(1)}, u32[]{:S(2)}, u32[]{:S(2)}) collective-permute-start(bf16[8,3584]{1,0:T(8,128)(2,1)S(1)} %get-tuple-element.8), channel_id=1, source_target_pairs={{0,18},{2,16},{4,22},{6,20},{8,26},{10,24},{12,30},{14,28},{16,2},... | collective-permute-start | bytes 172040 | tf_op jit(solution)/shard_map/ppermute | solution.py:35
  31.8 7.0 %collective-permute-start.17 = (bf16[8,3584]{1,0:T(8,128)(2,1)S(1)}, bf16[8,3584]{1,0:T(8,128)(2,1)S(1)}, u32[]{:S(2)}, u32[]{:S(2)}) collective-permute-start(bf16[8,3584]{1,0:T(8,128)(2,1)S(1)} %get-tuple-element.9), channel_id=1, source_target_pairs={{0,22},{2,20},{4,18},{6,16},{8,30},{10,28},{12,26},{14,24},{16,6},... | collective-permute-start | bytes 172040 | tf_op jit(solution)/shard_map/ppermute | solution.py:35
  34.5 4.8 %collective-permute-start.16 = (bf16[8,3584]{1,0:T(8,128)(2,1)S(1)}, bf16[8,3584]{1,0:T(8,128)(2,1)S(1)}, u32[]{:S(2)}, u32[]{:S(2)}) collective-permute-start(bf16[8,3584]{1,0:T(8,128)(2,1)S(1)} %get-tuple-element.10), channel_id=1, source_target_pairs={{0,16},{2,18},{4,20},{6,22},{8,24},{10,26},{12,28},{14,30},{16,0},... | collective-permute-start | bytes 172040 | tf_op jit(solution)/shard_map/ppermute | solution.py:35
